TPU v7x, 32 devices: a whole 2x2x4 slice. The times are simulated.
32 devices in a mesh: groups: 2 (over y), seq: 8 (over z, x), cache: 2 (over core).
Axes of the slice: x: 2, y: 2, z: 4, core: 2. Of those that a mesh axis runs over, the one named last changes fastest.
Arguments:
- queries: bfloat16 [128, 2048, 128], P('groups', ('seq', 'cache')), parts along dimension 0, may hold values from -8 to 8
- stretch_keys: bfloat16 [128, 2048, 128], P('groups', 'seq'), parts along dimension 0, may hold values from -8 to 8
- stretch_values: bfloat16 [128, 2048, 128], P('groups', 'seq'), parts along dimension 0, may hold values from -6 to 6
- cache_keys: bfloat16 [128, 2048, 128], P(('groups', 'seq'), 'cache'), parts along dimension 0, may hold values from -6 to 6
- cache_values: bfloat16 [128, 2048, 128], P(('groups', 'seq'), 'cache'), parts along dimension 0, may hold values from -6 to 6
- rand_blocks: int32 [32, 3], P('groups'), parts along dimension 0, may hold values from 2 to 28, as said below
Outputs:
- attended: bfloat16 [128, 2048, 128], P('groups', ('seq', 'cache')), parts along dimension 0
There are 2 independent parts, one for each index of `groups`. A program takes and returns all parts, laid end to end along the dimension named above; each array names one. Nothing has to cross between parts.
Inputs may be any that keep to these rules, and one draw needn't show every extreme that they name: `rand_blocks`: row i holds 3 different block numbers, each at least 2 and below 16 + i - 2.
All inputs are finite; a program needn't handle non-finite values.
Results may differ from a plain program's by a relative error of at most 0.0049.
Values may be sent and summed in bfloat16 or wider, within the bound.
No kernel may reach another device: no remote copies, remote signals or barrier semaphores. Data moves between devices by JAX's collectives and lax.ppermute only.
A program may use at most 128 MiB of HBM per device.

v0:
```python
import math

import jax
import jax.numpy as jnp
from jax import lax
from jax.sharding import PartitionSpec as P

BLK = 128
CB = 16


def block_lists(rand_blocks):
    block_count = rand_blocks.shape[0]
    starts = jnp.arange(block_count, dtype=jnp.int32)[:, None] + CB
    window = starts + jnp.array([-2, -1, 0], jnp.int32)[None, :]
    anchors = jnp.broadcast_to(jnp.array([0, 1], jnp.int32)[None, :], (block_count, 2))
    return jnp.concatenate([window, anchors, rand_blocks], axis=1)


def attend_blocks(query_blocks, key_lists, key_blocks, value_blocks):
    groups, block_width, head_width = query_blocks.shape
    listed = key_lists.shape[1]
    chosen_keys = jnp.take(key_blocks, key_lists, axis=0).reshape(
        groups, listed * block_width, head_width
    )
    chosen_values = jnp.take(value_blocks, key_lists, axis=0).reshape(
        groups, listed * block_width, head_width
    )
    scores = jnp.einsum(
        "gqd,gkd->gqk", query_blocks, chosen_keys, preferred_element_type=jnp.float32
    )
    scores = scores * (1.0 / math.sqrt(head_width))
    key_slot = jnp.arange(listed * block_width, dtype=jnp.int32)
    query_slot = jnp.arange(block_width, dtype=jnp.int32)
    blocked = (key_slot // block_width == 2)[None, :] & (
        (key_slot % block_width)[None, :] > query_slot[:, None]
    )
    scores = jnp.where(blocked[None], -jnp.inf, scores)
    row_max = jnp.max(scores, axis=2, keepdims=True)
    weights = jnp.exp(scores - row_max)
    row_probs = (weights / jnp.sum(weights, axis=2, keepdims=True)).astype(jnp.bfloat16)
    result = jnp.einsum(
        "gqk,gkd->gqd", row_probs, chosen_values, preferred_element_type=jnp.float32
    )
    return result.astype(jnp.bfloat16)


def per_device(queries, stretch_keys, stretch_values, cache_keys, cache_values, rand_blocks):
    local_rows = queries.shape[1]
    head_width = queries.shape[2]
    seq_devices = lax.axis_size("seq")
    cache_devices = lax.axis_size("cache")
    cache_side = lax.axis_index("cache")
    query_heads, key_heads, value_heads = (
        lax.all_to_all(queries, "seq", split_axis=0, concat_axis=1, tiled=True),
        lax.all_to_all(stretch_keys, "seq", split_axis=0, concat_axis=1, tiled=True),
        lax.all_to_all(stretch_values, "seq", split_axis=0, concat_axis=1, tiled=True),
    )
    prefix_keys, prefix_values = (
        lax.all_gather(cache_keys, "cache", axis=1, tiled=True),
        lax.all_gather(cache_values, "cache", axis=1, tiled=True),
    )
    all_lists = block_lists(rand_blocks)
    per_segment = local_rows // BLK
    my_blocks = seq_devices * per_segment
    block_order = jnp.arange(my_blocks, dtype=jnp.int32)
    global_block = (
        block_order // per_segment * cache_devices + cache_side
    ) * per_segment + block_order % per_segment
    my_lists = jnp.take(all_lists, global_block, axis=0)
    group_size = math.gcd(my_blocks, max(1, 2048 // BLK))
    group_count = my_blocks // group_size
    lists_grouped = my_lists.reshape(group_count, group_size, my_lists.shape[1])

    def one_pair(operands):
        query_rows, key_rows, value_rows, prefix_key, prefix_value = operands
        key_blocks = jnp.concatenate([prefix_key, key_rows], axis=0).reshape(-1, BLK, head_width)
        value_blocks = jnp.concatenate([prefix_value, value_rows], axis=0).reshape(
            -1, BLK, head_width
        )
        query_groups = query_rows.reshape(group_count, group_size, BLK, head_width)

        def one_group(group_operands):
            query_group, list_group = group_operands
            return attend_blocks(query_group, list_group, key_blocks, value_blocks)

        result = lax.map(one_group, (query_groups, lists_grouped))
        return result.reshape(my_blocks * BLK, head_width)

    attended_heads = lax.map(
        one_pair, (query_heads, key_heads, value_heads, prefix_keys, prefix_values)
    )
    return lax.all_to_all(attended_heads, "seq", split_axis=1, concat_axis=0, tiled=True)


def solution(mesh):
    placed = (
        P("groups", ("seq", "cache"), None),
        P("groups", "seq", None),
        P("groups", "seq", None),
        P(("groups", "seq"), "cache", None),
        P(("groups", "seq"), "cache", None),
        P("groups", None),
    )
    return jax.shard_map(
        per_device,
        mesh=mesh,
        in_specs=placed,
        out_specs=P("groups", ("seq", "cache"), None),
        check_vma=False,
    )
```

profile of v0, /device:TPU:0, one launch (start us, length us, event | category | flops | bytes accessed | tf_op | source)
XLA Modules:
  0.0 483.7 jit_solution(15000138229564814692)
XLA Ops:
  6.5 55.5 %all_to_all.72 = bf16[64,128,128]{2,1,0:T(8,128)(2,1)S(1)} all-to-all(bf16[64,128,128]{2,1,0:T(8,128)(2,1)} %param.12), channel_id=1, replica_groups=mesh['groups'=2,'seq'=8,'cache'=2] {'seq'}, dimensions={0} | all-to-all | bytes 4194304 | tf_op jit(solution)/shard_map/all_to_all | solution.py:55
  62.0 4.6 all-to-all-start.1
  67.3 91.6 %all-to-all-done.1 = bf16[64,256,128]{2,1,0:T(8,128)(2,1)} async-done(((bf16[64,256,128]{2,1,0:T(8,128)(2,1)}), bf16[64,256,128]{2,1,0:T(8,128)(2,1)}, u32[]{:S(2)}, u32[]{:S(2)}) %all-to-all-start.1) | async-done | bytes 4194336 | tf_op jit(solution)/shard_map/all_to_all | solution.py:56
  158.9 4.6 all-to-all-start.2
  165.2 1.5 copy.14
  166.7 4.6 copy.15
  171.3 84.7 %all-to-all-done.2 = bf16[64,256,128]{2,1,0:T(8,128)(2,1)} async-done(((bf16[64,256,128]{2,1,0:T(8,128)(2,1)}), bf16[64,256,128]{2,1,0:T(8,128)(2,1)}, u32[]{:S(2)}, u32[]{:S(2)}) %all-to-all-start.2) | async-done | bytes 4194336 | tf_op jit(solution)/shard_map/all_to_all | solution.py:57
  256.0 4.6 copy.17
  260.6 159.6 %while.16 = (s32[]{:T(128)}, bf16[8,1024,128]{2,1,0:T(8,128)(2,1)}, bf16[8,1024,128]{2,1,0:T(8,128)(2,1)}, bf16[8,2048,128]{2,1,0:T(8,128)(2,1)}, bf16[8,2048,12...) while((s32[]{:T(128)}, bf16[8,1024,128]{2,1,0:T(8,128)(2,1)}, ...), condition=%wide.region_3.5_spmd, body=%wide.region_0.4_spmd.sunk | while | flops 549865024 | bytes 47997700 | solution.py:90
  260.6 1.3 dynamic-slice_bitcast_fusion.7
  263.1 1.3 dynamic-slice_bitcast_fusion.6
  264.4 2.1 gather_fusion
  266.6 4.1 broadcast_select_fusion.3
  270.6 1.0 constant_dynamic-slice_fusion.2
  271.7 5.2 %fusion.41 = (f32[8,128]{1,0:T(8,128)S(1)}, f32[8,128,1024]{2,1,0:T(8,128)}) fusion(pred[128,1024]{1,0:T(8,128)(4,1)S(1)} %fusion.40, bf16[8,128,128]{2,1,0:T(8,128)(2,1)S(1)} %bitcast.87, bf16[8,1024,128]{2,1,0:T(8,128)(2,1)} %bitcast.82), kind=kOutput, calls=%fused_computation.52.clone.1 | convolution fusion | flops 272630784 | bytes 6688768 | tf_op jit(solution)/shard_map/while/body/eval_jaxpr/while/body/eval_jaxpr/sub | solution.py:40
  276.9 3.0 fusion.42
  280.6 1.3 dynamic-slice_bitcast_fusion.7
  283.0 1.3 dynamic-slice_bitcast_fusion.6
  284.4 2.1 gather_fusion
  286.5 4.1 broadcast_select_fusion.3
  290.6 1.0 constant_dynamic-slice_fusion.2
  291.7 5.2 %fusion.41 = (f32[8,128]{1,0:T(8,128)S(1)}, f32[8,128,1024]{2,1,0:T(8,128)}) fusion(pred[128,1024]{1,0:T(8,128)(4,1)S(1)} %fusion.40, bf16[8,128,128]{2,1,0:T(8,128)(2,1)S(1)} %bitcast.87, bf16[8,1024,128]{2,1,0:T(8,128)(2,1)} %bitcast.82), kind=kOutput, calls=%fused_computation.52.clone.1 | convolution fusion | flops 272630784 | bytes 6688768 | tf_op jit(solution)/shard_map/while/body/eval_jaxpr/while/body/eval_jaxpr/sub | solution.py:40
  296.8 3.0 fusion.42
  300.5 1.3 dynamic-slice_bitcast_fusion.7
  302.9 1.3 dynamic-slice_bitcast_fusion.6
  304.3 2.1 gather_fusion
  306.4 4.1 broadcast_select_fusion.3
  310.5 1.0 constant_dynamic-slice_fusion.2
  311.6 5.2 %fusion.41 = (f32[8,128]{1,0:T(8,128)S(1)}, f32[8,128,1024]{2,1,0:T(8,128)}) fusion(pred[128,1024]{1,0:T(8,128)(4,1)S(1)} %fusion.40, bf16[8,128,128]{2,1,0:T(8,128)(2,1)S(1)} %bitcast.87, bf16[8,1024,128]{2,1,0:T(8,128)(2,1)} %bitcast.82), kind=kOutput, calls=%fused_computation.52.clone.1 | convolution fusion | flops 272630784 | bytes 6688768 | tf_op jit(solution)/shard_map/while/body/eval_jaxpr/while/body/eval_jaxpr/sub | solution.py:40
  316.8 3.0 fusion.42
  320.5 1.3 dynamic-slice_bitcast_fusion.7
  322.9 1.3 dynamic-slice_bitcast_fusion.6
  324.2 2.1 gather_fusion
  326.4 4.1 broadcast_select_fusion.3
  330.4 1.0 constant_dynamic-slice_fusion.2
  331.6 5.2 %fusion.41 = (f32[8,128]{1,0:T(8,128)S(1)}, f32[8,128,1024]{2,1,0:T(8,128)}) fusion(pred[128,1024]{1,0:T(8,128)(4,1)S(1)} %fusion.40, bf16[8,128,128]{2,1,0:T(8,128)(2,1)S(1)} %bitcast.87, bf16[8,1024,128]{2,1,0:T(8,128)(2,1)} %bitcast.82), kind=kOutput, calls=%fused_computation.52.clone.1 | convolution fusion | flops 272630784 | bytes 6688768 | tf_op jit(solution)/shard_map/while/body/eval_jaxpr/while/body/eval_jaxpr/sub | solution.py:40
  336.7 3.0 fusion.42
  340.4 1.3 dynamic-slice_bitcast_fusion.7
  342.8 1.3 dynamic-slice_bitcast_fusion.6
  344.2 2.1 gather_fusion
  346.3 4.1 broadcast_select_fusion.3
  351.5 5.2 %fusion.41 = (f32[8,128]{1,0:T(8,128)S(1)}, f32[8,128,1024]{2,1,0:T(8,128)}) fusion(pred[128,1024]{1,0:T(8,128)(4,1)S(1)} %fusion.40, bf16[8,128,128]{2,1,0:T(8,128)(2,1)S(1)} %bitcast.87, bf16[8,1024,128]{2,1,0:T(8,128)(2,1)} %bitcast.82), kind=kOutput, calls=%fused_computation.52.clone.1 | convolution fusion | flops 272630784 | bytes 6688768 | tf_op jit(solution)/shard_map/while/body/eval_jaxpr/while/body/eval_jaxpr/sub | solution.py:40
  356.7 3.0 fusion.42
  360.4 1.3 dynamic-slice_bitcast_fusion.7
  362.8 1.3 dynamic-slice_bitcast_fusion.6
  364.1 2.1 gather_fusion
  366.3 4.1 broadcast_select_fusion.3
  371.4 5.2 %fusion.41 = (f32[8,128]{1,0:T(8,128)S(1)}, f32[8,128,1024]{2,1,0:T(8,128)}) fusion(pred[128,1024]{1,0:T(8,128)(4,1)S(1)} %fusion.40, bf16[8,128,128]{2,1,0:T(8,128)(2,1)S(1)} %bitcast.87, bf16[8,1024,128]{2,1,0:T(8,128)(2,1)} %bitcast.82), kind=kOutput, calls=%fused_computation.52.clone.1 | convolution fusion | flops 272630784 | bytes 6688768 | tf_op jit(solution)/shard_map/while/body/eval_jaxpr/while/body/eval_jaxpr/sub | solution.py:40
  376.6 3.0 fusion.42
  380.3 1.3 dynamic-slice_bitcast_fusion.7
  382.7 1.3 dynamic-slice_bitcast_fusion.6
  384.1 2.1 gather_fusion
  386.2 4.1 broadcast_select_fusion.3
  391.4 5.2 %fusion.41 = (f32[8,128]{1,0:T(8,128)S(1)}, f32[8,128,1024]{2,1,0:T(8,128)}) fusion(pred[128,1024]{1,0:T(8,128)(4,1)S(1)} %fusion.40, bf16[8,128,128]{2,1,0:T(8,128)(2,1)S(1)} %bitcast.87, bf16[8,1024,128]{2,1,0:T(8,128)(2,1)} %bitcast.82), kind=kOutput, calls=%fused_computation.52.clone.1 | convolution fusion | flops 272630784 | bytes 6688768 | tf_op jit(solution)/shard_map/while/body/eval_jaxpr/while/body/eval_jaxpr/sub | solution.py:40
  396.6 3.0 fusion.42
  400.3 1.3 dynamic-slice_bitcast_fusion.7
  402.7 1.3 dynamic-slice_bitcast_fusion.6
  404.0 2.1 gather_fusion
  406.2 4.1 broadcast_select_fusion.3
  411.3 5.2 %fusion.41 = (f32[8,128]{1,0:T(8,128)S(1)}, f32[8,128,1024]{2,1,0:T(8,128)}) fusion(pred[128,1024]{1,0:T(8,128)(4,1)S(1)} %fusion.40, bf16[8,128,128]{2,1,0:T(8,128)(2,1)S(1)} %bitcast.87, bf16[8,1024,128]{2,1,0:T(8,128)(2,1)} %bitcast.82), kind=kOutput, calls=%fused_computation.52.clone.1 | convolution fusion | flops 272630784 | bytes 6688768 | tf_op jit(solution)/shard_map/while/body/eval_jaxpr/while/body/eval_jaxpr/sub | solution.py:40
  416.5 3.0 fusion.42
  420.2 2.9 copy.18
  423.1 51.8 %all_to_all.73 = bf16[8,1024,128]{2,0,1:T(8,128)(2,1)S(1)} all-to-all(bf16[8,1024,128]{2,0,1:T(8,128)(2,1)S(1)} %copy.18), channel_id=1, replica_groups=mesh['groups'=2,'seq'=8,'cache'=2] {'seq'}, dimensions={1} | all-to-all | bytes 4194304 | tf_op jit(solution)/shard_map/all_to_all | solution.py:93
  474.9 1.9 copy.19
  (129 shorter events, 22.5 us)
Async XLA Ops:
  62.0 96.9 %all-to-all-start.1 = ((bf16[64,256,128]{2,1,0:T(8,128)(2,1)}), bf16[64,256,128]{2,1,0:T(8,128)(2,1)}, u32[]{:S(2)}, u32[]{:S(2)}) async-start(bf16[64,256,128]{2,1,0:T(8,128)(2,1)} %param.13), calls=%async_computation.1 | async-start | bytes 8388608 | tf_op jit(solution)/shard_map/all_to_all | solution.py:56
  66.6 194.0 %all-gather.3.cloned.1.call-start = ((), (), s32[]{:S(2)}) async-start(), calls=%async_computation.4 | async-start | bytes 6291456 | tf_op jit(solution)/shard_map/all_gather | solution.py:60
  158.9 97.1 %all-to-all-start.2 = ((bf16[64,256,128]{2,1,0:T(8,128)(2,1)}), bf16[64,256,128]{2,1,0:T(8,128)(2,1)}, u32[]{:S(2)}, u32[]{:S(2)}) async-start(bf16[64,256,128]{2,1,0:T(8,128)(2,1)} %param.14), calls=%async_computation.2 | async-start | bytes 8388608 | tf_op jit(solution)/shard_map/all_to_all | solution.py:57
  163.5 0.8 copy-start.1
  163.5 0.9 copy-start.2
  163.5 97.1 %all-gather.5.cloned.1.call-start = ((), (), s32[]{:S(2)}) async-start(), calls=%async_computation.5 | async-start | bytes 6291456 | tf_op jit(solution)/shard_map/all_gather | solution.py:61
  271.7 5.2 %copy-start = (bf16[8,8,128,128]{3,2,1,0:T(8,128)(2,1)S(1)}, bf16[8,8,128,128]{3,2,1,0:T(8,128)(2,1)}, u32[]{:S(2)}) copy-start(bf16[8,8,128,128]{3,2,1,0:T(8,128)(2,1)} %get-tuple-element.214) | copy-start | bytes 6291460 | tf_op jit(solution)/shard_map/while
  291.7 5.2 %copy-start = (bf16[8,8,128,128]{3,2,1,0:T(8,128)(2,1)S(1)}, bf16[8,8,128,128]{3,2,1,0:T(8,128)(2,1)}, u32[]{:S(2)}) copy-start(bf16[8,8,128,128]{3,2,1,0:T(8,128)(2,1)} %get-tuple-element.214) | copy-start | bytes 6291460 | tf_op jit(solution)/shard_map/while
  311.6 5.2 %copy-start = (bf16[8,8,128,128]{3,2,1,0:T(8,128)(2,1)S(1)}, bf16[8,8,128,128]{3,2,1,0:T(8,128)(2,1)}, u32[]{:S(2)}) copy-start(bf16[8,8,128,128]{3,2,1,0:T(8,128)(2,1)} %get-tuple-element.214) | copy-start | bytes 6291460 | tf_op jit(solution)/shard_map/while
  331.5 5.2 %copy-start = (bf16[8,8,128,128]{3,2,1,0:T(8,128)(2,1)S(1)}, bf16[8,8,128,128]{3,2,1,0:T(8,128)(2,1)}, u32[]{:S(2)}) copy-start(bf16[8,8,128,128]{3,2,1,0:T(8,128)(2,1)} %get-tuple-element.214) | copy-start | bytes 6291460 | tf_op jit(solution)/shard_map/while
  351.5 5.2 %copy-start = (bf16[8,8,128,128]{3,2,1,0:T(8,128)(2,1)S(1)}, bf16[8,8,128,128]{3,2,1,0:T(8,128)(2,1)}, u32[]{:S(2)}) copy-start(bf16[8,8,128,128]{3,2,1,0:T(8,128)(2,1)} %get-tuple-element.214) | copy-start | bytes 6291460 | tf_op jit(solution)/shard_map/while
  371.4 5.2 %copy-start = (bf16[8,8,128,128]{3,2,1,0:T(8,128)(2,1)S(1)}, bf16[8,8,128,128]{3,2,1,0:T(8,128)(2,1)}, u32[]{:S(2)}) copy-start(bf16[8,8,128,128]{3,2,1,0:T(8,128)(2,1)} %get-tuple-element.214) | copy-start | bytes 6291460 | tf_op jit(solution)/shard_map/while
  391.4 5.2 %copy-start = (bf16[8,8,128,128]{3,2,1,0:T(8,128)(2,1)S(1)}, bf16[8,8,128,128]{3,2,1,0:T(8,128)(2,1)}, u32[]{:S(2)}) copy-start(bf16[8,8,128,128]{3,2,1,0:T(8,128)(2,1)} %get-tuple-element.214) | copy-start | bytes 6291460 | tf_op jit(solution)/shard_map/while
  411.3 5.2 %copy-start = (bf16[8,8,128,128]{3,2,1,0:T(8,128)(2,1)S(1)}, bf16[8,8,128,128]{3,2,1,0:T(8,128)(2,1)}, u32[]{:S(2)}) copy-start(bf16[8,8,128,128]{3,2,1,0:T(8,128)(2,1)} %get-tuple-element.214) | copy-start | bytes 6291460 | tf_op jit(solution)/shard_map/while
Sparse Core Ops, SparseCore 0:
  69.0 14.9 all-gather.2
  165.9 14.9 all-gather.4
where the time goes:
time: 485 us; the launch traced here: 484 us
  waiting for transfers between devices  178 us (37%)
  blocking collectives  107 us (22%)
  local copies, waits for them, and re-layouts  75.5 us (16%)
  matrix products  65.1 us (13%)
  other arithmetic  34.8 us (7%)
  between operations  13.5 us (3%)
  starting transfers between devices  9.23 us (2%)
    all_to_all x1, waiting for transfers between devices, per_device(): lax.all_to_all(stretch_keys, 'seq', split_axis=0, concat_axis=1, tiled=True)  91.6 us
    all_to_all x1, waiting for transfers between devices, per_device(): lax.all_to_all(stretch_values, 'seq', split_axis=0, concat_axis=1, tiled=...  84.7 us
    all_to_all x1, blocking collectives, per_device(): lax.all_to_all(queries, 'seq', split_axis=0, concat_axis=1, tiled=True)  55.5 us
    all_to_all x1, blocking collectives, per_device(): lax.all_to_all(attended_heads, 'seq', split_axis=1, concat_axis=0, tiled=...  51.8 us
    sub x8, matrix products, attend_blocks(): weights = jnp.exp(scores - row_max)  41.3 us
    select_n x16, other arithmetic, attend_blocks(): jnp.take(key_blocks, key_lists, axis=0)  32.5 us
    dot_general x8, matrix products, attend_blocks(): jnp.einsum('gqk,gkd->gqd', row_probs, chosen_values, preferred_element_ty...  23.7 us
    squeeze x16, local copies, waits for them, and re-layouts, per_device(): lax.map(one_pair, (query_heads, key_heads, value_heads, prefix_keys, pref...  20.4 us
  transfers between devices with their start and end apart: 4, of which 2 were waited for; matrix products, arithmetic and copies ran while one was open for 2% of the time, Pallas kernels for 0%

commit v1 on v0

v1 whole, which is shorter than its diff:
```python
import math
import functools

import jax
import jax.numpy as jnp
from jax import lax
from jax.experimental import pallas as pl
from jax.experimental.pallas import tpu as pltpu
from jax.sharding import PartitionSpec as P

BLK = 128
LISTED = 8


def attention_kernel(place, rand, mine, theirs, ck_mine, ck_theirs, cv_mine, cv_theirs, out, keys, values):
    sources = mine.shape[0]
    cached = ck_mine.shape[1] // BLK
    prefix = 2 * cached
    side = place[0]
    other = 1 - side
    for index in range(cached):
        rows = pl.ds(index * BLK, BLK)
        keys[side * cached + index] = ck_mine[0, rows, :]
        values[side * cached + index] = cv_mine[0, rows, :]
        keys[other * cached + index] = ck_theirs[0, rows, :]
        values[other * cached + index] = cv_theirs[0, rows, :]

    def place_source(source, carry):
        block = prefix + 2 * source
        keys[block + side] = mine[source, 1, 0]
        values[block + side] = mine[source, 2, 0]
        keys[block + other] = theirs[source, 0, 0]
        values[block + other] = theirs[source, 1, 0]
        return carry

    lax.fori_loop(0, sources, place_source, 0, unroll=min(8, sources))
    scale = 1.0 / math.sqrt(mine.shape[-1])
    query_slot = lax.broadcasted_iota(jnp.int32, (BLK, BLK), 0)
    key_slot = lax.broadcasted_iota(jnp.int32, (BLK, BLK), 1)
    blocked = key_slot > query_slot

    def one_block(source, carry):
        block = 2 * source + side
        own = prefix + block
        listed = [own - 2, own - 1, own, 0, 1] + [rand[block, column] for column in range(3)]
        query = mine[source, 0, 0]
        parts = []
        for slot, key_block in enumerate(listed):
            part = lax.dot_general(
                query, keys[key_block], (((1,), (1,)), ((), ())), preferred_element_type=jnp.float32
            )
            part = part * scale
            if slot == 2:
                part = jnp.where(blocked, -jnp.inf, part)
            parts.append(part)
        scores = jnp.concatenate(parts, axis=1)
        row_max = jnp.max(scores, axis=1, keepdims=True)
        weights = jnp.exp(scores - row_max)
        inverse = 1.0 / jnp.sum(weights, axis=1, keepdims=True)
        probs = (weights * inverse).astype(jnp.bfloat16)
        total = jnp.zeros((BLK, mine.shape[-1]), jnp.float32)
        for slot, key_block in enumerate(listed):
            total += jnp.dot(
                probs[:, slot * BLK : (slot + 1) * BLK],
                values[key_block],
                preferred_element_type=jnp.float32,
            )
        out[source, 0] = total.astype(out.dtype)
        return carry

    lax.fori_loop(0, sources, one_block, 0, unroll=2)


def attend(place, rand, mine, theirs, caches, first):
    sources, _, heads, _, width = mine.shape
    cached_rows = caches[0].shape[1]
    key_blocks = 2 * cached_rows // BLK + 2 * sources
    cache_spec = pl.BlockSpec((1, cached_rows, width), lambda head, *_: (first + head, 0, 0))
    work = heads * sources * BLK * LISTED * BLK
    return pl.pallas_call(
        attention_kernel,
        grid_spec=pltpu.PrefetchScalarGridSpec(
            num_scalar_prefetch=2,
            grid=(heads,),
            in_specs=[
                pl.BlockSpec((sources, 3, 1, BLK, width), lambda head, *_: (0, 0, head, 0, 0)),
                pl.BlockSpec((sources, 2, 1, BLK, width), lambda head, *_: (0, 0, head, 0, 0)),
            ]
            + [cache_spec] * 4,
            out_specs=pl.BlockSpec((sources, 1, BLK, width), lambda head, *_: (0, head, 0, 0)),
            scratch_shapes=[
                pltpu.VMEM((key_blocks, BLK, width), jnp.bfloat16),
                pltpu.VMEM((key_blocks, BLK, width), jnp.bfloat16),
            ],
        ),
        out_shape=jax.ShapeDtypeStruct((sources, heads, BLK, width), jnp.bfloat16),
        compiler_params=pltpu.CompilerParams(vmem_limit_bytes=48 * 1024 * 1024),
        cost_estimate=pl.CostEstimate(
            flops=4 * work * width,
            bytes_accessed=2 * heads * width * BLK * (6 * sources + 2 * key_blocks),
            transcendentals=work,
        ),
    )(place, rand, mine, theirs, *caches)


def per_device(queries, stretch_keys, stretch_values, cache_keys, cache_values, rand_blocks):
    heads, local_rows, width = queries.shape
    seq_devices = lax.axis_size("seq")
    side = lax.axis_index("cache")
    owned = heads // seq_devices
    swap = [(0, 1), (1, 0)]
    assert local_rows == BLK and lax.axis_size("cache") == 2

    def own_rows(rows):
        return lax.dynamic_slice_in_dim(rows, side * local_rows, local_rows, axis=1)

    def by_owner(rows):
        return rows.reshape(seq_devices, owned, local_rows, width)

    packed = jnp.stack(
        [by_owner(queries), by_owner(own_rows(stretch_keys)), by_owner(own_rows(stretch_values))], axis=1
    )
    caches = (
        cache_keys,
        lax.ppermute(cache_keys, "cache", swap),
        cache_values,
        lax.ppermute(cache_values, "cache", swap),
    )
    place = jnp.reshape(side, (1,)).astype(jnp.int32)
    chunk = max(1, owned // 2)
    results = []
    for first in range(0, owned, chunk):
        mine = lax.all_to_all(
            packed[:, :, first : first + chunk], "seq", split_axis=0, concat_axis=0, tiled=True
        )
        theirs = lax.ppermute(mine[:, 1:], "cache", swap)
        attended = attend(place, rand_blocks, mine, theirs, caches, first)
        results.append(lax.all_to_all(attended, "seq", split_axis=0, concat_axis=0, tiled=True))
    return jnp.concatenate(results, axis=1).reshape(heads, local_rows, width)


def solution(mesh):
    placed = (
        P("groups", ("seq", "cache"), None),
        P("groups", "seq", None),
        P("groups", "seq", None),
        P(("groups", "seq"), "cache", None),
        P(("groups", "seq"), "cache", None),
        P("groups", None),
    )
    return jax.shard_map(
        per_device,
        mesh=mesh,
        in_specs=placed,
        out_specs=P("groups", ("seq", "cache"), None),
        check_vma=False,
    )
```

time: 485 us -> 252 us (0.52)
  waiting for transfers between devices: 178 us -> 67.6 us
  matrix products: 65.1 us -> 0 us
  local copies, waits for them, and re-layouts: 75.5 us -> 12.3 us
  Pallas kernels: 0 us -> 51 us
  other arithmetic: 34.8 us -> 3.4 us
  between operations: 13.5 us -> 0.07 us
    all_to_all x2, waiting for transfers between devices: 176 us -> 67.5 us  [the longest x1 66 us: per_device(): lax.all_to_all(packed[:, :, first:first + chunk], 'seq', split_axis=0, co...]
    pallas_call x0 -> x2, Pallas kernels: none -> 51 us  [attend(): pl.pallas_call(attention_kernel, grid_spec=pltpu.PrefetchScalarGridSpec(n...]
    sub x8 -> x0, matrix products: 41.3 us -> none  [attend_blocks(): weights = jnp.exp(scores - row_max)]
    select_n x26 -> x0, other arithmetic: 32.6 us -> none  [the longest x16 32.5 us: attend_blocks(): jnp.take(key_blocks, key_lists, axis=0)]
    gather x17 -> x0, local copies, waits for them, and re-layouts: 25.3 us -> none  [the longest x8 17.2 us: attend_blocks(): jnp.take(key_blocks, key_lists, axis=0)]
    dot_general x8 -> x0, matrix products: 23.7 us -> none  [attend_blocks(): jnp.einsum('gqk,gkd->gqd', row_probs, chosen_values, preferred_element_ty...]
    squeeze x16 -> x0, local copies, waits for them, and re-layouts: 20.4 us -> none  [per_device(): lax.map(one_pair, (query_heads, key_heads, value_heads, prefix_keys, pref...]
    all_to_all x4 -> x0, local copies, waits for them, and re-layouts: 12.6 us -> none  [the longest x1 4.64 us: per_device(): lax.all_to_all(stretch_keys, 'seq', split_axis=0, concat_axis=1, tiled=True)]
  transfers between devices with their start and end apart: 4 -> 6, of which waited for: 2 -> 2; matrix products, arithmetic and copies ran while one was open for 2% -> 3% of each run, Pallas kernels for 0% -> 20%
where the time goes in v1:
time: 252 us
  blocking collectives  108 us (43%)
  waiting for transfers between devices  67.6 us (27%)
  Pallas kernels  51 us (20%)
  local copies, waits for them, and re-layouts  12.3 us (5%)
  starting transfers between devices  9.46 us (4%)
  other arithmetic  3.4 us (1%)
    all_to_all x1, blocking collectives, per_device(): lax.all_to_all(packed[:, :, first:first + chunk], 'seq', split_axis=0, co...  77.9 us
    all_to_all x1, waiting for transfers between devices, per_device(): lax.all_to_all(packed[:, :, first:first + chunk], 'seq', split_axis=0, co...  66 us
    pallas_call x2, Pallas kernels, attend(): pl.pallas_call(attention_kernel, grid_spec=pltpu.PrefetchScalarGridSpec(n...  51 us
    all_to_all x1, blocking collectives, per_device(): lax.all_to_all(attended, 'seq', split_axis=0, concat_axis=0, tiled=True)  30.3 us
    slice x2, local copies, waits for them, and re-layouts, per_device(): theirs = lax.ppermute(mine[:, 1:], 'cache', swap)  6.3 us
  transfers between devices with their start and end apart: 6, of which 2 were waited for; matrix products, arithmetic and copies ran while one was open for 3% of the time, Pallas kernels for 20%

profile of v1, /device:TPU:0, one launch (start us, length us, event | category | flops | bytes accessed | tf_op | source)
XLA Modules:
  0.0 252.0 jit_solution(5269946469716508104)
XLA Ops:
  0.0 0.0 copy-start.1
  0.0 2.7 %constant_dynamic-slice_fusion = (bf16[64,128,128]{2,1,0:T(8,128)(2,1)S(1)}, bf16[64,128,128]{2,1,0:T(8,128)(2,1)S(1)}) fusion(bf16[64,256,128]{2,1,0:T(8,128)(2,1)} %param.8, s32[]{:T(128)S(6)} %select_n.4, bf16[64,256,128]{2,1,0:T(8,128)(2,1)} %param.7), kind=kLoop, calls=%fused_computation.2 | loop fusion | bytes 8388612 | tf_op jit(solution)/shard_map/dynamic_slice | solution.py:115
  2.7 0.2 copy-done.1
  2.9 0.7 pad_maximum_fusion
  3.5 3.1 %fusion = (bf16[8,3,4,128,128]{4,3,2,1,0:T(8,128)(2,1)S(1)}, bf16[8,3,4,128,128]{4,3,2,1,0:T(8,128)(2,1)}) fusion(bf16[8,3,8,128,128]{4,3,2,1,0:T(8,128)(2,1)S(1)} %pad_maximum_fusion), kind=kLoop, calls=%fused_computation.4 | loop fusion | bytes 12582912 | tf_op jit(solution)/shard_map/slice | solution.py:134
  6.6 77.9 %all_to_all.20.mine = bf16[8,3,4,128,128]{4,3,2,1,0:T(8,128)(2,1)} all-to-all(bf16[8,3,4,128,128]{4,3,2,1,0:T(8,128)(2,1)S(1)} %get-tuple-element.5), channel_id=1, replica_groups=mesh['groups'=2,'seq'=8,'cache'=2] {'seq'}, dimensions={0} | all-to-all | bytes 6291456 | tf_op jit(solution)/shard_map/all_to_all | solution.py:133
  84.5 0.0 copy-start
  84.5 4.6 %all-to-all-start.2 = ((bf16[8,3,4,128,128]{4,3,2,1,0:T(8,128)(2,1)}), bf16[8,3,4,128,128]{4,3,2,1,0:T(8,128)(2,1)}, u32[]{:S(2)}, u32[]{:S(2)}) async-start(bf16[8,3,4,128,128]{4,3,2,1,0:T(8,128)(2,1)} %get-tuple-element.6), calls=%async_computation.2 | async-start | bytes 6291456 | tf_op jit(solution)/shard_map/all_to_all | solution.py:133
  89.0 0.0 copy-done
  89.1 0.1 collective-permute-start.1
  89.1 0.5 collective-permute-start.2
  89.6 3.1 %slice.17 = bf16[8,2,4,128,128]{4,3,2,1,0:T(8,128)(2,1)} slice(bf16[8,3,4,128,128]{4,3,2,1,0:T(8,128)(2,1)} %all_to_all.20.mine), slice={[0:8], [1:3], [0:4], [0:128], [0:128]} | slice | bytes 4194304 | tf_op jit(solution)/shard_map/slice | solution.py:136
  92.8 0.0 copy-start.2
  92.8 0.1 collective-permute-start
  92.9 66.0 %all-to-all-done.2.mine = bf16[8,3,4,128,128]{4,3,2,1,0:T(8,128)(2,1)} async-done(((bf16[8,3,4,128,128]{4,3,2,1,0:T(8,128)(2,1)}), bf16[8,3,4,128,128]{4,3,2,1,0:T(8,128)(2,1)}, u32[]{:S(2)}, u32[]{:S(2)}) %all-to-all-start.2) | async-done | bytes 3145760 | tf_op jit(solution)/shard_map/all_to_all | solution.py:133
  158.9 3.2 %slice.19 = bf16[8,2,4,128,128]{4,3,2,1,0:T(8,128)(2,1)} slice(bf16[8,3,4,128,128]{4,3,2,1,0:T(8,128)(2,1)} %all-to-all-done.2.mine), slice={[0:8], [1:3], [0:4], [0:128], [0:128]} | slice | bytes 4194304 | tf_op jit(solution)/shard_map/slice | solution.py:136
  162.1 0.0 collective-permute-start.3
  162.1 0.0 copy-done.2
  162.1 0.1 copy.7.rand
  162.2 0.0 collective-permute-done.1.ck_theirs
  162.2 0.0 collective-permute-done.2.cv_theirs
  162.2 0.0 collective-permute-done.theirs
  162.2 25.8 %shard_map.64 = bf16[8,4,128,128]{3,2,1,0:T(8,128)(2,1)} custom-call(s32[1]{0:T(128)} %bitcast.place, s32[16,3]{1,0:T(8,128)S(1)} %copy.7.rand, bf16[8,3,4,128,128]{4,3,2,1,0:T(8,128)(2,1)} %all_to_all.20.mine, bf16[8,2,4,128,128]{4,3,2,1,0:T(8,128)(2,1)} %collective-permute-done.theirs, bf16[8,1024,128]{2,1,0:T(8,128)(2,1)S(1)} %copy-done, ...), custom_call_target="tpu_custom_call" | custom-call | flops 2147483648 | bytes 14680064 | tf_op jit(solution)/shard_map/pallas_call | solution.py:80
  188.0 4.2 %all-to-all-start.1 = ((bf16[8,4,128,128]{3,2,1,0:T(8,128)(2,1)}), bf16[8,4,128,128]{3,2,1,0:T(8,128)(2,1)}, u32[]{:S(2)}, u32[]{:S(2)}) async-start(bf16[8,4,128,128]{3,2,1,0:T(8,128)(2,1)} %shard_map.64), calls=%async_computation.1 | async-start | bytes 2097152 | tf_op jit(solution)/shard_map/all_to_all | solution.py:138
  192.3 0.0 collective-permute-done.3.theirs
  192.3 25.2 %shard_map.65 = bf16[8,4,128,128]{3,2,1,0:T(8,128)(2,1)S(1)} custom-call(s32[1]{0:T(128)} %bitcast.place, s32[16,3]{1,0:T(8,128)S(1)} %copy.7.rand, bf16[8,3,4,128,128]{4,3,2,1,0:T(8,128)(2,1)} %all-to-all-done.2.mine, bf16[8,2,4,128,128]{4,3,2,1,0:T(8,128)(2,1)} %collective-permute-done.3.theirs, bf16[8,1024,128]{2,1,0:T(8,128)(2,1)S(1)} %copy-done, ...), custom_call_target="tpu_custom_call" | custom-call | flops 2147483648 | bytes 14680064 | tf_op jit(solution)/shard_map/pallas_call | solution.py:80
  217.5 1.5 all-to-all-done.1
  219.0 30.3 %all_to_all.21 = bf16[8,4,128,128]{3,2,1,0:T(8,128)(2,1)S(1)} all-to-all(bf16[8,4,128,128]{3,2,1,0:T(8,128)(2,1)S(1)} %shard_map.65), channel_id=1, replica_groups=mesh['groups'=2,'seq'=8,'cache'=2] {'seq'}, dimensions={0} | all-to-all | bytes 2097152 | tf_op jit(solution)/shard_map/all_to_all | solution.py:138
  249.3 2.7 %pad_maximum_fusion.1 = bf16[8,8,128,128]{3,2,1,0:T(8,128)(2,1)} fusion(bf16[8,4,128,128]{3,2,1,0:T(8,128)(2,1)S(1)} %all_to_all.21, bf16[8,4,128,128]{3,2,1,0:T(8,128)(2,1)} %all-to-all-done.1), kind=kLoop, calls=%fused_computation.1 | loop fusion | flops 1048576 | bytes 4194304 | tf_op jit(solution)/shard_map/concatenate | solution.py:139
Async XLA Ops:
  0.0 2.9 %copy-start.1 = (bf16[64,128,128]{2,1,0:T(8,128)(2,1)S(1)}, bf16[64,128,128]{2,1,0:T(8,128)(2,1)}, u32[]{:S(2)}) copy-start(bf16[64,128,128]{2,1,0:T(8,128)(2,1)} %param.6) | copy-start | bytes 6291460
  84.5 4.6 %copy-start = (bf16[8,1024,128]{2,1,0:T(8,128)(2,1)S(1)}, bf16[8,1024,128]{2,1,0:T(8,128)(2,1)}, u32[]{:S(2)}) copy-start(bf16[8,1024,128]{2,1,0:T(8,128)(2,1)} %ck_mine.3) | copy-start | bytes 6291460
  84.5 74.4 %all-to-all-start.2 = ((bf16[8,3,4,128,128]{4,3,2,1,0:T(8,128)(2,1)}), bf16[8,3,4,128,128]{4,3,2,1,0:T(8,128)(2,1)}, u32[]{:S(2)}, u32[]{:S(2)}) async-start(bf16[8,3,4,128,128]{4,3,2,1,0:T(8,128)(2,1)} %get-tuple-element.6), calls=%async_computation.2 | async-start | bytes 6291456 | tf_op jit(solution)/shard_map/all_to_all | solution.py:133
  89.1 73.1 %collective-permute-start.1 = (bf16[8,1024,128]{2,1,0:T(8,128)(2,1)S(1)}, bf16[8,1024,128]{2,1,0:T(8,128)(2,1)}, u32[]{:S(2)}, u32[]{:S(2)}) collective-permute-start(bf16[8,1024,128]{2,1,0:T(8,128)(2,1)S(1)} %copy-done), channel_id=1, source_target_pairs={{0,1},{1,0},{2,3},{3,2},{4,5},{5,4},{6,7},{7,6},{8,9},{9,8},{10,11... | collective-permute-start | bytes 6291464 | tf_op jit(solution)/shard_map/ppermute | solution.py:125
  89.1 73.0 %collective-permute-start.2 = (bf16[8,1024,128]{2,1,0:T(8,128)(2,1)}, bf16[8,1024,128]{2,1,0:T(8,128)(2,1)}, u32[]{:S(2)}, u32[]{:S(2)}) collective-permute-start(bf16[8,1024,128]{2,1,0:T(8,128)(2,1)} %cv_mine.3), channel_id=1, source_target_pairs={{0,1},{1,0},{2,3},{3,2},{4,5},{5,4},{6,7},{7,6},{8,9},{9,8},{10,11... | collective-permute-start | bytes 6291464 | tf_op jit(solution)/shard_map/ppermute | solution.py:127
  92.8 69.3 %copy-start.2 = (s32[16,3]{0,1:T(4,128)S(1)}, s32[16,3]{0,1:T(4,128)}, u32[]{:S(2)}) copy-start(s32[16,3]{0,1:T(4,128)} %param.11) | copy-start | bytes 580
  92.8 69.4 %collective-permute-start = (bf16[8,2,4,128,128]{4,3,2,1,0:T(8,128)(2,1)}, bf16[8,2,4,128,128]{4,3,2,1,0:T(8,128)(2,1)}, u32[]{:S(2)}, u32[]{:S(2)}) collective-permute-start(bf16[8,2,4,128,128]{4,3,2,1,0:T(8,128)(2,1)} %slice.17), channel_id=1, source_target_pairs={{0,1},{1,0},{2,3},{3,2},{4,5},{5,4},{6,7},{7,6},{8,9},{9,8},{10,11... | collective-permute-start | bytes 6291464 | tf_op jit(solution)/shard_map/ppermute | solution.py:136
  162.1 30.2 %collective-permute-start.3 = (bf16[8,2,4,128,128]{4,3,2,1,0:T(8,128)(2,1)}, bf16[8,2,4,128,128]{4,3,2,1,0:T(8,128)(2,1)}, u32[]{:S(2)}, u32[]{:S(2)}) collective-permute-start(bf16[8,2,4,128,128]{4,3,2,1,0:T(8,128)(2,1)} %slice.19), channel_id=1, source_target_pairs={{0,1},{1,0},{2,3},{3,2},{4,5},{5,4},{6,7},{7,6},{8,9},{9,8},{10,11... | collective-permute-start | bytes 6291464 | tf_op jit(solution)/shard_map/ppermute | solution.py:136
  188.0 31.0 %all-to-all-start.1 = ((bf16[8,4,128,128]{3,2,1,0:T(8,128)(2,1)}), bf16[8,4,128,128]{3,2,1,0:T(8,128)(2,1)}, u32[]{:S(2)}, u32[]{:S(2)}) async-start(bf16[8,4,128,128]{3,2,1,0:T(8,128)(2,1)} %shard_map.64), calls=%async_computation.1 | async-start | bytes 2097152 | tf_op jit(solution)/shard_map/all_to_all | solution.py:138

commit v2 on v1

v2 whole, which is shorter than its diff:
```python
import math

import jax
import jax.numpy as jnp
from jax import lax
from jax.experimental import pallas as pl
from jax.experimental.pallas import tpu as pltpu
from jax.sharding import PartitionSpec as P

BLK = 128
LISTED = 8
CHUNKS = 2
WINDOW = 4


def attention_kernel(pieces, place, rand, *refs):
    mine, refs = refs[:pieces], refs[pieces:]
    theirs, refs = refs[:pieces], refs[pieces:]
    (ck_mine, ck_theirs, cv_mine, cv_theirs), refs = refs[:4], refs[4:]
    outs, (queries, results, keys, values) = refs[:pieces], refs[pieces:]
    per_piece = mine[0].shape[0]
    sources = pieces * per_piece
    cached = ck_mine.shape[1] // BLK
    prefix = 2 * cached
    side = place[sources]
    other = 1 - side
    for index in range(cached):
        rows = pl.ds(index * BLK, BLK)
        keys[side * cached + index] = ck_mine[0, rows, :]
        values[side * cached + index] = cv_mine[0, rows, :]
        keys[other * cached + index] = ck_theirs[0, rows, :]
        values[other * cached + index] = cv_theirs[0, rows, :]

    for piece in range(pieces):
        for index in range(per_piece):
            slot = piece * per_piece + index
            block = prefix + 2 * place[slot]
            queries[slot] = mine[piece][index, 0, 0]
            keys[block + side] = mine[piece][index, 1, 0]
            values[block + side] = mine[piece][index, 2, 0]
            keys[block + other] = theirs[piece][index, 1, 0]
            values[block + other] = theirs[piece][index, 2, 0]

    width = queries.shape[-1]
    scale = 1.0 / math.sqrt(width)
    query_slot = lax.broadcasted_iota(jnp.int32, (BLK, BLK), 0)
    key_slot = lax.broadcasted_iota(jnp.int32, (BLK, BLK), 1)
    blocked = key_slot > query_slot

    def one_block(slot, carry):
        block = 2 * place[slot] + side
        own = prefix + block
        listed = [own - 2, own - 1, own, 0, 1] + [rand[block, column] for column in range(3)]
        query = queries[slot]
        parts = []
        for position, key_block in enumerate(listed):
            part = lax.dot_general(
                query, keys[key_block], (((1,), (1,)), ((), ())), preferred_element_type=jnp.float32
            )
            part = part * scale
            if position == 2:
                part = jnp.where(blocked, -jnp.inf, part)
            parts.append(part)
        scores = jnp.concatenate(parts, axis=1)
        row_max = jnp.max(scores, axis=1, keepdims=True)
        weights = jnp.exp(scores - row_max)
        inverse = 1.0 / jnp.sum(weights, axis=1, keepdims=True)
        probs = (weights * inverse).astype(jnp.bfloat16)
        total = jnp.zeros((BLK, width), jnp.float32)
        for position, key_block in enumerate(listed):
            total += jnp.dot(
                probs[:, position * BLK : (position + 1) * BLK],
                values[key_block],
                preferred_element_type=jnp.float32,
            )
        results[slot] = total.astype(jnp.bfloat16)
        return carry

    lax.fori_loop(0, sources, one_block, 0, unroll=2)
    for piece in range(pieces):
        for index in range(per_piece):
            outs[piece][index, 0] = results[piece * per_piece + index]


def attend(place, rand, mine, theirs, caches, first):
    pieces = len(mine)
    per_piece, parts, heads, _, width = mine[0].shape
    sources = pieces * per_piece
    cached_rows = caches[0].shape[1]
    key_blocks = 2 * cached_rows // BLK + 2 * sources
    cache_spec = pl.BlockSpec((1, cached_rows, width), lambda head, *_: (first + head, 0, 0))
    piece_spec = pl.BlockSpec((per_piece, parts, 1, BLK, width), lambda head, *_: (0, 0, head, 0, 0))
    out_spec = pl.BlockSpec((per_piece, 1, BLK, width), lambda head, *_: (0, head, 0, 0))
    work = heads * sources * BLK * LISTED * BLK

    def kernel(*refs):
        attention_kernel(pieces, *refs)

    return pl.pallas_call(
        kernel,
        grid_spec=pltpu.PrefetchScalarGridSpec(
            num_scalar_prefetch=2,
            grid=(heads,),
            in_specs=[piece_spec] * (2 * pieces) + [cache_spec] * 4,
            out_specs=[out_spec] * pieces,
            scratch_shapes=[
                pltpu.VMEM((sources, BLK, width), jnp.bfloat16),
                pltpu.VMEM((sources, BLK, width), jnp.bfloat16),
                pltpu.VMEM((key_blocks, BLK, width), jnp.bfloat16),
                pltpu.VMEM((key_blocks, BLK, width), jnp.bfloat16),
            ],
        ),
        out_shape=[jax.ShapeDtypeStruct((per_piece, heads, BLK, width), jnp.bfloat16)] * pieces,
        compiler_params=pltpu.CompilerParams(vmem_limit_bytes=48 * 1024 * 1024),
        cost_estimate=pl.CostEstimate(
            flops=4 * work * width,
            bytes_accessed=2 * heads * width * BLK * (6 * sources + 2 * key_blocks),
            transcendentals=work,
        ),
    )(place, rand, *mine, *theirs, *caches)


def after(value, *earlier):
    return lax.optimization_barrier((value, *earlier))[0]


def per_device(queries, stretch_keys, stretch_values, cache_keys, cache_values, rand_blocks):
    heads, local_rows, width = queries.shape
    seq_devices = lax.axis_size("seq")
    here = lax.axis_index("seq")
    side = lax.axis_index("cache")
    owned = heads // seq_devices
    swap = [(0, 1), (1, 0)]
    assert local_rows == BLK and lax.axis_size("cache") == 2

    def own_rows(rows):
        return lax.dynamic_slice_in_dim(rows, side * local_rows, local_rows, axis=1)

    def by_owner(rows):
        return rows.reshape(seq_devices, owned, local_rows, width)

    caches = (
        cache_keys,
        lax.ppermute(cache_keys, "cache", swap),
        cache_values,
        lax.ppermute(cache_values, "cache", swap),
    )

    if seq_devices > 8 or seq_devices & (seq_devices - 1) or owned % CHUNKS:
        packed = jnp.stack(
            [by_owner(queries), by_owner(own_rows(stretch_keys)), by_owner(own_rows(stretch_values))], axis=1
        )
        place = jnp.concatenate([jnp.arange(seq_devices, dtype=jnp.int32), jnp.reshape(side, (1,)).astype(jnp.int32)])
        mine = lax.all_to_all(packed, "seq", split_axis=0, concat_axis=0, tiled=True)
        theirs = lax.ppermute(mine, "cache", swap)
        attended = attend(place, rand_blocks, [mine], [theirs], caches, 0)[0]
        returned = lax.all_to_all(attended, "seq", split_axis=0, concat_axis=0, tiled=True)
        return returned.reshape(heads, local_rows, width)

    partners = [here ^ step for step in range(seq_devices)]
    place = jnp.stack(partners + [side]).astype(jnp.int32)
    order = [4, 1, 5, 2, 6, 3, 7] if seq_devices == 8 else list(range(1, seq_devices))
    chunk = owned // CHUNKS

    def to_partner(value, step):
        return lax.ppermute(value, "seq", [(index, index ^ step) for index in range(seq_devices)])

    def packed(step, first):
        start = partners[step] * owned + first
        return jnp.stack(
            [
                lax.dynamic_slice(queries, (start, 0, 0), (chunk, local_rows, width)),
                lax.dynamic_slice(stretch_keys, (start, side * local_rows, 0), (chunk, local_rows, width)),
                lax.dynamic_slice(stretch_values, (start, side * local_rows, 0), (chunk, local_rows, width)),
            ]
        )[None]

    sent = []
    result = jnp.zeros((heads, local_rows, width), jnp.bfloat16)
    for first in range(0, owned, chunk):
        mine = [packed(0, first)] + [None] * (seq_devices - 1)
        for step in order:
            message = packed(step, first)
            if len(sent) >= WINDOW:
                message = after(message, sent[-WINDOW])
            mine[step] = to_partner(message, step)
            sent.append(mine[step])
        theirs = [lax.ppermute(piece, "cache", swap) for piece in mine]
        attended = attend(place, rand_blocks, mine, theirs, caches, first)
        for step in [0] + order:
            returned = attended[step][0] if step == 0 else to_partner(attended[step], step)[0]
            result = lax.dynamic_update_slice(result, returned, (partners[step] * owned + first, 0, 0))
    return result


def solution(mesh):
    placed = (
        P("groups", ("seq", "cache"), None),
        P("groups", "seq", None),
        P("groups", "seq", None),
        P(("groups", "seq"), "cache", None),
        P(("groups", "seq"), "cache", None),
        P("groups", None),
    )
    return jax.shard_map(
        per_device,
        mesh=mesh,
        in_specs=placed,
        out_specs=P("groups", ("seq", "cache"), None),
        check_vma=False,
    )
```

time: 252 us -> 266 us (1.056)
  blocking collectives: 108 us -> 0 us
  starting transfers between devices: 9.46 us -> 67.4 us
  waiting for transfers between devices: 67.6 us -> 123 us
  local copies, waits for them, and re-layouts: 12.3 us -> 19.3 us
    ppermute x2 -> x44, waiting for transfers between devices: 0.01 us -> 123 us  [the longest x28 123 us: to_partner(): lax.ppermute(value, 'seq', [(index, index ^ step) for index in range(seq_...]
    all_to_all x2 -> x0, blocking collectives: 108 us -> none  [the longest x1 77.9 us: per_device(): lax.all_to_all(packed[:, :, first:first + chunk], 'seq', split_axis=0, co...]
    all_to_all x2 -> x0, waiting for transfers between devices: 67.5 us -> none  [the longest x1 66 us: per_device(): lax.all_to_all(packed[:, :, first:first + chunk], 'seq', split_axis=0, co...]
    ppermute x2 -> x44, starting transfers between devices: 0.08 us -> 66.9 us  [the longest x28 64.7 us: to_partner(): lax.ppermute(value, 'seq', [(index, index ^ step) for index in range(seq_...]
    unnamed x7 -> x61, local copies, waits for them, and re-layouts: 0.26 us -> 12.6 us
    slice x3 -> x0, local copies, waits for them, and re-layouts: 9.37 us -> none  [the longest x2 6.3 us: per_device(): theirs = lax.ppermute(mine[:, 1:], 'cache', swap)]
    all_to_all x2 -> x0, starting transfers between devices: 8.81 us -> none  [the longest x1 4.57 us: per_device(): lax.all_to_all(packed[:, :, first:first + chunk], 'seq', split_axis=0, co...]
    another operation x0 -> x3, local copies, waits for them, and re-layouts: none -> 5.24 us  [the longest x2 5.16 us: packed(): jnp.stack([lax.dynamic_slice(queries, (start, 0, 0), (chunk, local_rows,...]
  transfers between devices with their start and end apart: 6 -> 46, of which waited for: 2 -> 15; matrix products, arithmetic and copies ran while one was open for 3% -> 1% of each run, Pallas kernels for 20% -> 20%
where the time goes in v2:
time: 266 us; the launch traced here: 265 us
  waiting for transfers between devices  123 us (46%)
  starting transfers between devices  67.4 us (25%)
  Pallas kernels  52.2 us (20%)
  local copies, waits for them, and re-layouts  19.3 us (7%)
    ppermute x28, waiting for transfers between devices, to_partner(): lax.ppermute(value, 'seq', [(index, index ^ step) for index in range(seq_...  123 us
    ppermute x28, starting transfers between devices, to_partner(): lax.ppermute(value, 'seq', [(index, index ^ step) for index in range(seq_...  64.7 us
    pallas_call x2, Pallas kernels, attend(): pl.pallas_call(kernel, grid_spec=pltpu.PrefetchScalarGridSpec(num_scalar_...  52.2 us
    unnamed x61, local copies, waits for them, and re-layouts  12.6 us
  transfers between devices with their start and end apart: 46, of which 15 were waited for; matrix products, arithmetic and copies ran while one was open for 1% of the time, Pallas kernels for 20%

profile of v2, /device:TPU:0, one launch (start us, length us, event | category | flops | bytes accessed | tf_op | source)
XLA Modules:
  0.0 264.8 jit_solution(12973365026695366728)
XLA Ops:
  0.0 2.1 dynamic-slice_bitcast_fusion.2
  2.1 0.8 copy-done.23
  2.9 3.0 %dynamic-slice_bitcast_fusion = (bf16[1,4,128,128]{3,2,1,0:T(8,128)(2,1)S(1)}, bf16[1,4,128,128]{3,2,1,0:T(8,128)(2,1)S(1)}, bf16[1,4,128,128]{3,2,1,0:T(8,128)(...) fusion(bf16[64,256,128]{2,1,0:T(8,128)(2,1)S(1)} %copy-done.23,, ...), kind=kLoop, calls=%fused_computation.32 | loop fusion | bytes 8388676 | tf_op jit(solution)/shard_map/stack | solution.py:170
  6.0 4.1 %collective-permute-start.3 = (bf16[1,3,4,128,128]{4,3,2,1,0:T(8,128)(2,1)S(1)}, bf16[1,3,4,128,128]{4,3,2,1,0:T(8,128)(2,1)S(1)}, u32[]{:S(2)}, u32[]{:S(2)}) collective-permute-start(bf16[1,3,4,128,128]{4,3,2,1,0:T(8,128)(2,1)S(1)} %maximum_bitcast_fusion.4), channel_id=1, source_target_pairs={{0,8},{2,10},{4,12},{6,14},{8,0},{10,2},{12,4},{14,6},{1,9},{3,11}... | collective-permute-start | bytes 1179656 | tf_op jit(solution)/shard_map/ppermute | solution.py:166
  10.2 1.6 collective-permute-start
  11.8 1.6 collective-permute-start.1
  13.5 0.4 collective-permute-start.4
  14.1 15.3 %collective-permute-done.3.refs_6_ = bf16[1,3,4,128,128]{4,3,2,1,0:T(8,128)(2,1)S(1)} collective-permute-done((bf16[1,3,4,128,128]{4,3,2,1,0:T(8,128)(2,1)S(1)}, bf16[1,3,4,128,128]{4,3,2,1,0:T(8,128)(2,1)S(1)}, u32[]{:S(2)}, u32[]{:S(2)}) %collective-permute-start.3) | collective-permute-done | bytes 393248 | tf_op jit(solution)/shard_map/ppermute | solution.py:166
  29.4 3.1 %collective-permute-start.5 = (bf16[1,3,4,128,128]{4,3,2,1,0:T(8,128)(2,1)S(1)}, bf16[1,3,4,128,128]{4,3,2,1,0:T(8,128)(2,1)S(1)}, u32[]{:S(2)}, u32[]{:S(2)}) collective-permute-start(bf16[1,3,4,128,128]{4,3,2,1,0:T(8,128)(2,1)S(1)} %maximum_bitcast_fusion.6), channel_id=1, source_target_pairs={{0,12},{2,14},{4,8},{6,10},{8,4},{10,6},{12,0},{14,2},{1,13},{3,15... | collective-permute-start | bytes 1179656 | tf_op jit(solution)/shard_map/ppermute | solution.py:166
  32.7 22.4 %collective-permute-done.4.refs_7_ = bf16[1,3,4,128,128]{4,3,2,1,0:T(8,128)(2,1)S(1)} collective-permute-done((bf16[1,3,4,128,128]{4,3,2,1,0:T(8,128)(2,1)S(1)}, bf16[1,3,4,128,128]{4,3,2,1,0:T(8,128)(2,1)S(1)}, u32[]{:S(2)}, u32[]{:S(2)}) %collective-permute-start.4) | collective-permute-done | bytes 393248 | tf_op jit(solution)/shard_map/ppermute | solution.py:166
  55.1 2.4 collective-permute-start.6
  57.6 0.5 collective-permute-start.16
  58.1 2.5 collective-permute-done.2.refs_5_
  60.6 27.0 %collective-permute-done.27.refs_6_ = bf16[1,3,4,128,128]{4,3,2,1,0:T(8,128)(2,1)S(1)} collective-permute-done((bf16[1,3,4,128,128]{4,3,2,1,0:T(8,128)(2,1)S(1)}, bf16[1,3,4,128,128]{4,3,2,1,0:T(8,128)(2,1)S(1)}, u32[]{:S(2)}, u32[]{:S(2)}) %collective-permute-start.27) | collective-permute-done | bytes 393248 | tf_op jit(solution)/shard_map/ppermute | solution.py:166
  87.6 0.5 collective-permute-start.9
  88.2 0.8 copy-done.10
  89.3 1.8 collective-permute-start.24
  91.1 0.8 copy-done.16
  91.9 10.4 %collective-permute-start.28 = (bf16[1,3,4,128,128]{4,3,2,1,0:T(8,128)(2,1)S(1)}, bf16[1,3,4,128,128]{4,3,2,1,0:T(8,128)(2,1)S(1)}, u32[]{:S(2)}, u32[]{:S(2)}) collective-permute-start(bf16[1,3,4,128,128]{4,3,2,1,0:T(8,128)(2,1)S(1)} %maximum_bitcast_fusion.13), channel_id=1, source_target_pairs={{0,10},{2,8},{4,14},{6,12},{8,2},{10,0},{12,6},{14,4},{1,11},{3,9}... | collective-permute-start | bytes 1179656 | tf_op jit(solution)/shard_map/ppermute | solution.py:166
  102.5 0.7 copy-done.18
  103.2 0.4 collective-permute-start.29
  103.6 14.1 %collective-permute-start.25 = (bf16[1,3,4,128,128]{4,3,2,1,0:T(8,128)(2,1)S(1)}, bf16[1,3,4,128,128]{4,3,2,1,0:T(8,128)(2,1)S(1)}, u32[]{:S(2)}, u32[]{:S(2)}) collective-permute-start(bf16[1,3,4,128,128]{4,3,2,1,0:T(8,128)(2,1)S(1)} %maximum_bitcast_fusion.10), channel_id=1, source_target_pairs={{0,4},{2,6},{4,0},{6,2},{8,12},{10,14},{12,8},{14,10},{1,5},{3,7},... | collective-permute-start | bytes 1179656 | tf_op jit(solution)/shard_map/ppermute | solution.py:166
  117.6 11.0 %collective-permute-done.28.refs_7_ = bf16[1,3,4,128,128]{4,3,2,1,0:T(8,128)(2,1)S(1)} collective-permute-done((bf16[1,3,4,128,128]{4,3,2,1,0:T(8,128)(2,1)S(1)}, bf16[1,3,4,128,128]{4,3,2,1,0:T(8,128)(2,1)S(1)}, u32[]{:S(2)}, u32[]{:S(2)}) %collective-permute-start.28) | collective-permute-done | bytes 393248 | tf_op jit(solution)/shard_map/ppermute | solution.py:166
  128.6 0.5 collective-permute-start.14
  129.1 6.8 %collective-permute-done.25.refs_4_ = bf16[1,3,4,128,128]{4,3,2,1,0:T(8,128)(2,1)S(1)} collective-permute-done((bf16[1,3,4,128,128]{4,3,2,1,0:T(8,128)(2,1)S(1)}, bf16[1,3,4,128,128]{4,3,2,1,0:T(8,128)(2,1)S(1)}, u32[]{:S(2)}, u32[]{:S(2)}) %collective-permute-start.25) | collective-permute-done | bytes 393248 | tf_op jit(solution)/shard_map/ppermute | solution.py:166
  135.9 0.7 copy-done.12
  136.6 0.7 copy-done.14
  137.4 0.8 maximum_bitcast_fusion.11
  138.2 0.8 maximum_bitcast_fusion.15
  139.0 2.1 collective-permute-start.26
  141.1 0.5 collective-permute-start.30
  141.9 0.7 copy-done.20
  142.8 13.5 %collective-permute-done.26.refs_5_ = bf16[1,3,4,128,128]{4,3,2,1,0:T(8,128)(2,1)} collective-permute-done((bf16[1,3,4,128,128]{4,3,2,1,0:T(8,128)(2,1)}, bf16[1,3,4,128,128]{4,3,2,1,0:T(8,128)(2,1)}, u32[]{:S(2)}, u32[]{:S(2)}) %collective-permute-start.26) | collective-permute-done | bytes 393248 | tf_op jit(solution)/shard_map/ppermute | solution.py:166
  156.3 7.8 %collective-permute-done.30.refs_9_ = bf16[1,3,4,128,128]{4,3,2,1,0:T(8,128)(2,1)} collective-permute-done((bf16[1,3,4,128,128]{4,3,2,1,0:T(8,128)(2,1)}, bf16[1,3,4,128,128]{4,3,2,1,0:T(8,128)(2,1)}, u32[]{:S(2)}, u32[]{:S(2)}) %collective-permute-start.30) | collective-permute-done | bytes 393248 | tf_op jit(solution)/shard_map/ppermute | solution.py:166
  164.0 0.5 collective-permute-start.33
  164.6 0.4 collective-permute-start.38
  165.1 1.0 copy-done.1
  166.1 1.0 copy-done.3
  167.1 1.0 copy-done.7
  168.1 1.0 copy-done.11
  169.1 1.0 copy-done.17
  170.1 1.0 copy-done.19
  171.1 1.0 copy-done.21
  172.0 26.1 %shard_map.64 = (bf16[1,4,128,128]{3,2,1,0:T(8,128)(2,1)S(1)}, bf16[1,4,128,128]{3,2,1,0:T(8,128)(2,1)S(1)}, bf16[1,4,128,128]{3,2,1,0:T(8,128)(2,1)S(1)}, bf16[...) custom-call(s32[9]{0:T(128)S(1)} %stack.231.refs_0_, ...), custom_call_target="tpu_custom_call" | custom-call | flops 2147483648 | bytes 14680064 | tf_op jit(solution)/shard_map/pallas_call | solution.py:99
  198.2 0.5 broadcast_in_dim.51
  198.7 3.4 %collective-permute-start.17 = (bf16[1,4,128,128]{3,2,1,0:T(8,128)(2,1)S(1)}, bf16[1,4,128,128]{3,2,1,0:T(8,128)(2,1)S(1)}, u32[]{:S(2)}, u32[]{:S(2)}) collective-permute-start(bf16[1,4,128,128]{3,2,1,0:T(8,128)(2,1)S(1)} %get-tuple-element.35), channel_id=1, source_target_pairs={{0,8},{2,10},{4,12},{6,14},{8,0},{10,2},{12,4},{14,6},{1,9},{3,11}... | collective-permute-start | bytes 393224 | tf_op jit(solution)/shard_map/ppermute | solution.py:166
  202.1 1.7 collective-permute-start.18
  203.9 2.2 collective-permute-start.20
  206.1 1.9 collective-permute-start.21
  208.0 26.1 %shard_map.65 = (bf16[1,4,128,128]{3,2,1,0:T(8,128)(2,1)S(1)}, bf16[1,4,128,128]{3,2,1,0:T(8,128)(2,1)S(1)}, bf16[1,4,128,128]{3,2,1,0:T(8,128)(2,1)S(1)}, bf16[...) custom-call(s32[9]{0:T(128)S(1)} %stack.231.refs_0_, ...), custom_call_target="tpu_custom_call" | custom-call | flops 2147483648 | bytes 14680064 | tf_op jit(solution)/shard_map/pallas_call | solution.py:99
  234.1 1.4 collective-permute-start.22
  235.6 1.2 collective-permute-start.23
  236.8 2.0 collective-permute-start.39
  238.8 1.8 collective-permute-start.40
  240.6 0.8 collective-permute-start.41
  241.6 1.4 collective-permute-start.42
  243.0 1.6 collective-permute-done.23
  244.6 1.8 collective-permute-start.43
  246.5 9.8 %collective-permute-done.39 = bf16[1,4,128,128]{3,2,1,0:T(8,128)(2,1)S(1)} collective-permute-done((bf16[1,4,128,128]{3,2,1,0:T(8,128)(2,1)S(1)}, bf16[1,4,128,128]{3,2,1,0:T(8,128)(2,1)S(1)}, u32[]{:S(2)}, u32[]{:S(2)}) %collective-permute-start.39) | collective-permute-done | bytes 131104 | tf_op jit(solution)/shard_map/ppermute | solution.py:166
  256.3 2.6 collective-permute-start.45
  258.8 2.1 collective-permute-done.41
  261.0 1.7 collective-permute-done.44
  262.7 1.4 collective-permute-done.45
  264.1 0.7 bitcast_dynamic-update-slice_fusion
  (127 shorter events, 2.2 us)
Async XLA Ops:
  0.0 2.9 %copy-start.23 = (bf16[64,256,128]{2,1,0:T(8,128)(2,1)S(1)}, bf16[64,256,128]{2,1,0:T(8,128)(2,1)}, u32[]{:S(2)}) copy-start(bf16[64,256,128]{2,1,0:T(8,128)(2,1)} %param.8) | copy-start | bytes 12582916
  6.0 23.4 %collective-permute-start.3 = (bf16[1,3,4,128,128]{4,3,2,1,0:T(8,128)(2,1)S(1)}, bf16[1,3,4,128,128]{4,3,2,1,0:T(8,128)(2,1)S(1)}, u32[]{:S(2)}, u32[]{:S(2)}) collective-permute-start(bf16[1,3,4,128,128]{4,3,2,1,0:T(8,128)(2,1)S(1)} %maximum_bitcast_fusion.4), channel_id=1, source_target_pairs={{0,8},{2,10},{4,12},{6,14},{8,0},{10,2},{12,4},{14,6},{1,9},{3,11}... | collective-permute-start | bytes 1179656 | tf_op jit(solution)/shard_map/ppermute | solution.py:166
  10.2 19.2 %collective-permute-start = (bf16[1,3,4,128,128]{4,3,2,1,0:T(8,128)(2,1)S(1)}, bf16[1,3,4,128,128]{4,3,2,1,0:T(8,128)(2,1)S(1)}, u32[]{:S(2)}, u32[]{:S(2)}) collective-permute-start(bf16[1,3,4,128,128]{4,3,2,1,0:T(8,128)(2,1)S(1)} %maximum_bitcast_fusion.1), channel_id=1, source_target_pairs={{0,2},{2,0},{4,6},{6,4},{8,10},{10,8},{12,14},{14,12},{1,3},{3,1},... | collective-permute-start | bytes 1179656 | tf_op jit(solution)/shard_map/ppermute | solution.py:166
  11.8 20.8 %collective-permute-start.1 = (bf16[1,3,4,128,128]{4,3,2,1,0:T(8,128)(2,1)S(1)}, bf16[1,3,4,128,128]{4,3,2,1,0:T(8,128)(2,1)S(1)}, u32[]{:S(2)}, u32[]{:S(2)}) collective-permute-start(bf16[1,3,4,128,128]{4,3,2,1,0:T(8,128)(2,1)S(1)} %maximum_bitcast_fusion.2), channel_id=1, source_target_pairs={{0,4},{2,6},{4,0},{6,2},{8,12},{10,14},{12,8},{14,10},{1,5},{3,7},... | collective-permute-start | bytes 1179656 | tf_op jit(solution)/shard_map/ppermute | solution.py:166
  13.5 41.7 %collective-permute-start.4 = (bf16[1,3,4,128,128]{4,3,2,1,0:T(8,128)(2,1)S(1)}, bf16[1,3,4,128,128]{4,3,2,1,0:T(8,128)(2,1)S(1)}, u32[]{:S(2)}, u32[]{:S(2)}) collective-permute-start(bf16[1,3,4,128,128]{4,3,2,1,0:T(8,128)(2,1)S(1)} %maximum_bitcast_fusion.5), channel_id=1, source_target_pairs={{0,10},{2,8},{4,14},{6,12},{8,2},{10,0},{12,6},{14,4},{1,11},{3,9}... | collective-permute-start | bytes 1179656 | tf_op jit(solution)/shard_map/ppermute | solution.py:166
  13.9 41.3 %collective-permute-start.31 = (bf16[1,3,4,128,128]{4,3,2,1,0:T(8,128)(2,1)S(1)}, bf16[1,3,4,128,128]{4,3,2,1,0:T(8,128)(2,1)S(1)}, u32[]{:S(2)}, u32[]{:S(2)}) collective-permute-start(bf16[1,3,4,128,128]{4,3,2,1,0:T(8,128)(2,1)S(1)} %maximum_bitcast_fusion.8.refs_2_), channel_id=1, source_target_pairs={{0,1},{1,0},{2,3},{3,2},{4,5},{5,4},{6,7},{7,6},{8,9},{9,8},{10,11... | collective-permute-start | bytes 1179656 | tf_op jit(solution)/shard_map/ppermute | solution.py:188
  29.4 28.2 %collective-permute-start.7 = (bf16[1,3,4,128,128]{4,3,2,1,0:T(8,128)(2,1)S(1)}, bf16[1,3,4,128,128]{4,3,2,1,0:T(8,128)(2,1)S(1)}, u32[]{:S(2)}, u32[]{:S(2)}) collective-permute-start(bf16[1,3,4,128,128]{4,3,2,1,0:T(8,128)(2,1)S(1)} %maximum_bitcast_fusion.refs_2_), channel_id=1, source_target_pairs={{0,1},{1,0},{2,3},{3,2},{4,5},{5,4},{6,7},{7,6},{8,9},{9,8},{10,11... | collective-permute-start | bytes 1179656 | tf_op jit(solution)/shard_map/ppermute | solution.py:188
  29.4 28.2 %collective-permute-start.5 = (bf16[1,3,4,128,128]{4,3,2,1,0:T(8,128)(2,1)S(1)}, bf16[1,3,4,128,128]{4,3,2,1,0:T(8,128)(2,1)S(1)}, u32[]{:S(2)}, u32[]{:S(2)}) collective-permute-start(bf16[1,3,4,128,128]{4,3,2,1,0:T(8,128)(2,1)S(1)} %maximum_bitcast_fusion.6), channel_id=1, source_target_pairs={{0,12},{2,14},{4,8},{6,10},{8,4},{10,6},{12,0},{14,2},{1,13},{3,15... | collective-permute-start | bytes 1179656 | tf_op jit(solution)/shard_map/ppermute | solution.py:166
  32.6 27.9 %collective-permute-start.2 = (bf16[1,3,4,128,128]{4,3,2,1,0:T(8,128)(2,1)S(1)}, bf16[1,3,4,128,128]{4,3,2,1,0:T(8,128)(2,1)S(1)}, u32[]{:S(2)}, u32[]{:S(2)}) collective-permute-start(bf16[1,3,4,128,128]{4,3,2,1,0:T(8,128)(2,1)S(1)} %maximum_bitcast_fusion.3), channel_id=1, source_target_pairs={{0,6},{2,4},{4,2},{6,0},{8,14},{10,12},{12,10},{14,8},{1,7},{3,5},... | collective-permute-start | bytes 1179656 | tf_op jit(solution)/shard_map/ppermute | solution.py:166
  55.1 32.4 %collective-permute-start.27 = (bf16[1,3,4,128,128]{4,3,2,1,0:T(8,128)(2,1)S(1)}, bf16[1,3,4,128,128]{4,3,2,1,0:T(8,128)(2,1)S(1)}, u32[]{:S(2)}, u32[]{:S(2)}) collective-permute-start(bf16[1,3,4,128,128]{4,3,2,1,0:T(8,128)(2,1)S(1)} %maximum_bitcast_fusion.12), channel_id=1, source_target_pairs={{0,8},{2,10},{4,12},{6,14},{8,0},{10,2},{12,4},{14,6},{1,9},{3,11}... | collective-permute-start | bytes 1179656 | tf_op jit(solution)/shard_map/ppermute | solution.py:166
  55.1 32.4 %collective-permute-start.6 = (bf16[1,3,4,128,128]{4,3,2,1,0:T(8,128)(2,1)S(1)}, bf16[1,3,4,128,128]{4,3,2,1,0:T(8,128)(2,1)S(1)}, u32[]{:S(2)}, u32[]{:S(2)}) collective-permute-start(bf16[1,3,4,128,128]{4,3,2,1,0:T(8,128)(2,1)S(1)} %maximum_bitcast_fusion.7), channel_id=1, source_target_pairs={{0,14},{2,12},{4,10},{6,8},{8,6},{10,4},{12,2},{14,0},{1,15},{3,13... | collective-permute-start | bytes 1179656 | tf_op jit(solution)/shard_map/ppermute | solution.py:166
  57.6 107.0 %collective-permute-start.15 = (bf16[8,1024,128]{2,1,0:T(8,128)(2,1)}, bf16[8,1024,128]{2,1,0:T(8,128)(2,1)}, u32[]{:S(2)}, u32[]{:S(2)}) collective-permute-start(bf16[8,1024,128]{2,1,0:T(8,128)(2,1)} %refs_18_.3), channel_id=1, source_target_pairs={{0,1},{1,0},{2,3},{3,2},{4,5},{5,4},{6,7},{7,6},{8,9},{9,8},{10,11... | collective-permute-start | bytes 6291464 | tf_op jit(solution)/shard_map/ppermute | solution.py:144
  57.6 81.4 %copy-start = (bf16[1,3,4,128,128]{4,3,2,1,0:T(8,128)(2,1)}, bf16[1,3,4,128,128]{4,3,2,1,0:T(8,128)(2,1)S(1)}, u32[]{:S(2)}) copy-start(bf16[1,3,4,128,128]{4,3,2,1,0:T(8,128)(2,1)S(1)} %collective-permute-done.5.refs_8_) | copy-start | bytes 1179652
  57.6 107.0 %collective-permute-start.16 = (bf16[8,1024,128]{2,1,0:T(8,128)(2,1)}, bf16[8,1024,128]{2,1,0:T(8,128)(2,1)}, u32[]{:S(2)}, u32[]{:S(2)}) collective-permute-start(bf16[8,1024,128]{2,1,0:T(8,128)(2,1)} %refs_20_.3), channel_id=1, source_target_pairs={{0,1},{1,0},{2,3},{3,2},{4,5},{5,4},{6,7},{7,6},{8,9},{9,8},{10,11... | collective-permute-start | bytes 6291464 | tf_op jit(solution)/shard_map/ppermute | solution.py:146
  60.6 78.5 %copy-start.2 = (bf16[1,3,4,128,128]{4,3,2,1,0:T(8,128)(2,1)}, bf16[1,3,4,128,128]{4,3,2,1,0:T(8,128)(2,1)S(1)}, u32[]{:S(2)}) copy-start(bf16[1,3,4,128,128]{4,3,2,1,0:T(8,128)(2,1)S(1)} %collective-permute-done.2.refs_5_) | copy-start | bytes 1179652
  60.6 27.6 %collective-permute-start.11 = (bf16[1,3,4,128,128]{4,3,2,1,0:T(8,128)(2,1)S(1)}, bf16[1,3,4,128,128]{4,3,2,1,0:T(8,128)(2,1)S(1)}, u32[]{:S(2)}, u32[]{:S(2)}) collective-permute-start(bf16[1,3,4,128,128]{4,3,2,1,0:T(8,128)(2,1)S(1)} %collective-permute-done.3.refs_6_), channel_id=1, source_target_pairs={{0,1},{1,0},{2,3},{3,2},{4,5},{5,4},{6,7},{7,6},{8,9},{9,8},{10,11... | collective-permute-start | bytes 1179656 | tf_op jit(solution)/shard_map/ppermute | solution.py:188
  87.6 1.7 collective-permute-start.12
  87.6 51.5 %copy-start.6 = (bf16[1,3,4,128,128]{4,3,2,1,0:T(8,128)(2,1)}, bf16[1,3,4,128,128]{4,3,2,1,0:T(8,128)(2,1)S(1)}, u32[]{:S(2)}) copy-start(bf16[1,3,4,128,128]{4,3,2,1,0:T(8,128)(2,1)S(1)} %collective-permute-done.6.refs_9_) | copy-start | bytes 1179652
  87.6 3.6 %collective-permute-start.9 = (bf16[1,3,4,128,128]{4,3,2,1,0:T(8,128)(2,1)S(1)}, bf16[1,3,4,128,128]{4,3,2,1,0:T(8,128)(2,1)S(1)}, u32[]{:S(2)}, u32[]{:S(2)}) collective-permute-start(bf16[1,3,4,128,128]{4,3,2,1,0:T(8,128)(2,1)S(1)} %collective-permute-done.1.refs_4_), channel_id=1, source_target_pairs={{0,1},{1,0},{2,3},{3,2},{4,5},{5,4},{6,7},{7,6},{8,9},{9,8},{10,11... | collective-permute-start | bytes 1179656 | tf_op jit(solution)/shard_map/ppermute | solution.py:188
  88.1 54.5 %copy-start.29 = (s32[16,3]{0,1:T(4,128)S(1)}, s32[16,3]{0,1:T(4,128)}, u32[]{:S(2)}) copy-start(s32[16,3]{0,1:T(4,128)} %param.11) | copy-start | bytes 580
  89.0 13.5 %collective-permute-start.8 = (bf16[1,3,4,128,128]{4,3,2,1,0:T(8,128)(2,1)S(1)}, bf16[1,3,4,128,128]{4,3,2,1,0:T(8,128)(2,1)S(1)}, u32[]{:S(2)}, u32[]{:S(2)}) collective-permute-start(bf16[1,3,4,128,128]{4,3,2,1,0:T(8,128)(2,1)S(1)} %collective-permute-done.refs_3_), channel_id=1, source_target_pairs={{0,1},{1,0},{2,3},{3,2},{4,5},{5,4},{6,7},{7,6},{8,9},{9,8},{10,11... | collective-permute-start | bytes 1179656 | tf_op jit(solution)/shard_map/ppermute | solution.py:188
  89.3 13.1 %copy-start.24 = (bf16[1,3,4,128,128]{4,3,2,1,0:T(8,128)(2,1)}, bf16[1,3,4,128,128]{4,3,2,1,0:T(8,128)(2,1)S(1)}, u32[]{:S(2)}) copy-start(bf16[1,3,4,128,128]{4,3,2,1,0:T(8,128)(2,1)S(1)} %collective-permute-done.12.refs_15_) | copy-start | bytes 1179652
  89.3 14.3 %collective-permute-start.24 = (bf16[1,3,4,128,128]{4,3,2,1,0:T(8,128)(2,1)S(1)}, bf16[1,3,4,128,128]{4,3,2,1,0:T(8,128)(2,1)S(1)}, u32[]{:S(2)}, u32[]{:S(2)}) collective-permute-start(bf16[1,3,4,128,128]{4,3,2,1,0:T(8,128)(2,1)S(1)} %maximum_bitcast_fusion.9), channel_id=1, source_target_pairs={{0,2},{2,0},{4,6},{6,4},{8,10},{10,8},{12,14},{14,12},{1,3},{3,1},... | collective-permute-start | bytes 1179656 | tf_op jit(solution)/shard_map/ppermute | solution.py:166
  91.9 36.7 %collective-permute-start.28 = (bf16[1,3,4,128,128]{4,3,2,1,0:T(8,128)(2,1)S(1)}, bf16[1,3,4,128,128]{4,3,2,1,0:T(8,128)(2,1)S(1)}, u32[]{:S(2)}, u32[]{:S(2)}) collective-permute-start(bf16[1,3,4,128,128]{4,3,2,1,0:T(8,128)(2,1)S(1)} %maximum_bitcast_fusion.13), channel_id=1, source_target_pairs={{0,10},{2,8},{4,14},{6,12},{8,2},{10,0},{12,6},{14,4},{1,11},{3,9}... | collective-permute-start | bytes 1179656 | tf_op jit(solution)/shard_map/ppermute | solution.py:166
  103.2 25.4 %collective-permute-start.29 = (bf16[1,3,4,128,128]{4,3,2,1,0:T(8,128)(2,1)S(1)}, bf16[1,3,4,128,128]{4,3,2,1,0:T(8,128)(2,1)}, u32[]{:S(2)}, u32[]{:S(2)}) collective-permute-start(bf16[1,3,4,128,128]{4,3,2,1,0:T(8,128)(2,1)S(1)} %maximum_bitcast_fusion.14), channel_id=1, source_target_pairs={{0,12},{2,14},{4,8},{6,10},{8,4},{10,6},{12,0},{14,2},{1,13},{3,15... | collective-permute-start | bytes 1179656 | tf_op jit(solution)/shard_map/ppermute | solution.py:166
  103.6 38.0 %copy-start.4 = (bf16[1,3,4,128,128]{4,3,2,1,0:T(8,128)(2,1)}, bf16[1,3,4,128,128]{4,3,2,1,0:T(8,128)(2,1)S(1)}, u32[]{:S(2)}) copy-start(bf16[1,3,4,128,128]{4,3,2,1,0:T(8,128)(2,1)S(1)} %collective-permute-done.24.refs_3_) | copy-start | bytes 1179652
  103.6 32.3 %collective-permute-start.25 = (bf16[1,3,4,128,128]{4,3,2,1,0:T(8,128)(2,1)S(1)}, bf16[1,3,4,128,128]{4,3,2,1,0:T(8,128)(2,1)S(1)}, u32[]{:S(2)}, u32[]{:S(2)}) collective-permute-start(bf16[1,3,4,128,128]{4,3,2,1,0:T(8,128)(2,1)S(1)} %maximum_bitcast_fusion.10), channel_id=1, source_target_pairs={{0,4},{2,6},{4,0},{6,2},{8,12},{10,14},{12,8},{14,10},{1,5},{3,7},... | collective-permute-start | bytes 1179656 | tf_op jit(solution)/shard_map/ppermute | solution.py:166
  128.6 13.0 %copy-start.8 = (bf16[1,3,4,128,128]{4,3,2,1,0:T(8,128)(2,1)}, bf16[1,3,4,128,128]{4,3,2,1,0:T(8,128)(2,1)S(1)}, u32[]{:S(2)}) copy-start(bf16[1,3,4,128,128]{4,3,2,1,0:T(8,128)(2,1)S(1)} %collective-permute-done.28.refs_7_) | copy-start | bytes 1179652
  128.6 7.3 %collective-permute-start.35 = (bf16[1,3,4,128,128]{4,3,2,1,0:T(8,128)(2,1)S(1)}, bf16[1,3,4,128,128]{4,3,2,1,0:T(8,128)(2,1)S(1)}, u32[]{:S(2)}, u32[]{:S(2)}) collective-permute-start(bf16[1,3,4,128,128]{4,3,2,1,0:T(8,128)(2,1)S(1)} %collective-permute-done.27.refs_6_), channel_id=1, source_target_pairs={{0,1},{1,0},{2,3},{3,2},{4,5},{5,4},{6,7},{7,6},{8,9},{9,8},{10,11... | collective-permute-start | bytes 1179656 | tf_op jit(solution)/shard_map/ppermute | solution.py:188
  128.6 10.4 %collective-permute-start.14 = (bf16[1,3,4,128,128]{4,3,2,1,0:T(8,128)(2,1)S(1)}, bf16[1,3,4,128,128]{4,3,2,1,0:T(8,128)(2,1)S(1)}, u32[]{:S(2)}, u32[]{:S(2)}) collective-permute-start(bf16[1,3,4,128,128]{4,3,2,1,0:T(8,128)(2,1)S(1)} %collective-permute-done.6.refs_9_), channel_id=1, source_target_pairs={{0,1},{1,0},{2,3},{3,2},{4,5},{5,4},{6,7},{7,6},{8,9},{9,8},{10,11... | collective-permute-start | bytes 1179656 | tf_op jit(solution)/shard_map/ppermute | solution.py:188
  135.9 5.2 %collective-permute-start.13 = (bf16[1,3,4,128,128]{4,3,2,1,0:T(8,128)(2,1)S(1)}, bf16[1,3,4,128,128]{4,3,2,1,0:T(8,128)(2,1)S(1)}, u32[]{:S(2)}, u32[]{:S(2)}) collective-permute-start(bf16[1,3,4,128,128]{4,3,2,1,0:T(8,128)(2,1)S(1)} %collective-permute-done.5.refs_8_), channel_id=1, source_target_pairs={{0,1},{1,0},{2,3},{3,2},{4,5},{5,4},{6,7},{7,6},{8,9},{9,8},{10,11... | collective-permute-start | bytes 1179656 | tf_op jit(solution)/shard_map/ppermute | solution.py:188
  137.4 4.2 %collective-permute-start.10 = (bf16[1,3,4,128,128]{4,3,2,1,0:T(8,128)(2,1)S(1)}, bf16[1,3,4,128,128]{4,3,2,1,0:T(8,128)(2,1)S(1)}, u32[]{:S(2)}, u32[]{:S(2)}) collective-permute-start(bf16[1,3,4,128,128]{4,3,2,1,0:T(8,128)(2,1)S(1)} %collective-permute-done.2.refs_5_), channel_id=1, source_target_pairs={{0,1},{1,0},{2,3},{3,2},{4,5},{5,4},{6,7},{7,6},{8,9},{9,8},{10,11... | collective-permute-start | bytes 1179656 | tf_op jit(solution)/shard_map/ppermute | solution.py:188
  139.0 2.6 copy-start.25
  139.0 17.2 %collective-permute-start.26 = (bf16[1,3,4,128,128]{4,3,2,1,0:T(8,128)(2,1)}, bf16[1,3,4,128,128]{4,3,2,1,0:T(8,128)(2,1)}, u32[]{:S(2)}, u32[]{:S(2)}) collective-permute-start(bf16[1,3,4,128,128]{4,3,2,1,0:T(8,128)(2,1)} %maximum_bitcast_fusion.11), channel_id=1, source_target_pairs={{0,6},{2,4},{4,2},{6,0},{8,14},{10,12},{12,10},{14,8},{1,7},{3,5},... | collective-permute-start | bytes 1179656 | tf_op jit(solution)/shard_map/ppermute | solution.py:166
  141.1 22.9 %collective-permute-start.30 = (bf16[1,3,4,128,128]{4,3,2,1,0:T(8,128)(2,1)}, bf16[1,3,4,128,128]{4,3,2,1,0:T(8,128)(2,1)}, u32[]{:S(2)}, u32[]{:S(2)}) collective-permute-start(bf16[1,3,4,128,128]{4,3,2,1,0:T(8,128)(2,1)} %maximum_bitcast_fusion.15), channel_id=1, source_target_pairs={{0,14},{2,12},{4,10},{6,8},{8,6},{10,4},{12,2},{14,0},{1,15},{3,13... | collective-permute-start | bytes 1179656 | tf_op jit(solution)/shard_map/ppermute | solution.py:166
  142.6 21.4 %collective-permute-start.37 = (bf16[1,3,4,128,128]{4,3,2,1,0:T(8,128)(2,1)}, bf16[1,3,4,128,128]{4,3,2,1,0:T(8,128)(2,1)}, u32[]{:S(2)}, u32[]{:S(2)}) collective-permute-start(bf16[1,3,4,128,128]{4,3,2,1,0:T(8,128)(2,1)} %collective-permute-done.29.refs_8_), channel_id=1, source_target_pairs={{0,1},{1,0},{2,3},{3,2},{4,5},{5,4},{6,7},{7,6},{8,9},{9,8},{10,11... | collective-permute-start | bytes 1179656 | tf_op jit(solution)/shard_map/ppermute | solution.py:188
  156.3 45.9 %collective-permute-start.32 = (bf16[1,3,4,128,128]{4,3,2,1,0:T(8,128)(2,1)}, bf16[1,3,4,128,128]{4,3,2,1,0:T(8,128)(2,1)S(1)}, u32[]{:S(2)}, u32[]{:S(2)}) collective-permute-start(bf16[1,3,4,128,128]{4,3,2,1,0:T(8,128)(2,1)} %copy-done.4), channel_id=1, source_target_pairs={{0,1},{1,0},{2,3},{3,2},{4,5},{5,4},{6,7},{7,6},{8,9},{9,8},{10,11... | collective-permute-start | bytes 1179656 | tf_op jit(solution)/shard_map/ppermute | solution.py:188
  164.0 39.8 %collective-permute-start.36 = (bf16[1,3,4,128,128]{4,3,2,1,0:T(8,128)(2,1)}, bf16[1,3,4,128,128]{4,3,2,1,0:T(8,128)(2,1)S(1)}, u32[]{:S(2)}, u32[]{:S(2)}) collective-permute-start(bf16[1,3,4,128,128]{4,3,2,1,0:T(8,128)(2,1)} %copy-done.8), channel_id=1, source_target_pairs={{0,1},{1,0},{2,3},{3,2},{4,5},{5,4},{6,7},{7,6},{8,9},{9,8},{10,11... | collective-permute-start | bytes 1179656 | tf_op jit(solution)/shard_map/ppermute | solution.py:188
  164.0 34.7 %collective-permute-start.33 = (bf16[1,3,4,128,128]{4,3,2,1,0:T(8,128)(2,1)}, bf16[1,3,4,128,128]{4,3,2,1,0:T(8,128)(2,1)S(1)}, u32[]{:S(2)}, u32[]{:S(2)}) collective-permute-start(bf16[1,3,4,128,128]{4,3,2,1,0:T(8,128)(2,1)} %copy-done.12), channel_id=1, source_target_pairs={{0,1},{1,0},{2,3},{3,2},{4,5},{5,4},{6,7},{7,6},{8,9},{9,8},{10,11... | collective-permute-start | bytes 1179656 | tf_op jit(solution)/shard_map/ppermute | solution.py:188
  164.6 39.3 %collective-permute-start.34 = (bf16[1,3,4,128,128]{4,3,2,1,0:T(8,128)(2,1)}, bf16[1,3,4,128,128]{4,3,2,1,0:T(8,128)(2,1)S(1)}, u32[]{:S(2)}, u32[]{:S(2)}) collective-permute-start(bf16[1,3,4,128,128]{4,3,2,1,0:T(8,128)(2,1)} %collective-permute-done.26.refs_5_), channel_id=1, source_target_pairs={{0,1},{1,0},{2,3},{3,2},{4,5},{5,4},{6,7},{7,6},{8,9},{9,8},{10,11... | collective-permute-start | bytes 1179656 | tf_op jit(solution)/shard_map/ppermute | solution.py:188
  164.6 41.4 %collective-permute-start.38 = (bf16[1,3,4,128,128]{4,3,2,1,0:T(8,128)(2,1)}, bf16[1,3,4,128,128]{4,3,2,1,0:T(8,128)(2,1)S(1)}, u32[]{:S(2)}, u32[]{:S(2)}) collective-permute-start(bf16[1,3,4,128,128]{4,3,2,1,0:T(8,128)(2,1)} %collective-permute-done.30.refs_9_), channel_id=1, source_target_pairs={{0,1},{1,0},{2,3},{3,2},{4,5},{5,4},{6,7},{7,6},{8,9},{9,8},{10,11... | collective-permute-start | bytes 1179656 | tf_op jit(solution)/shard_map/ppermute | solution.py:188
  165.1 1.0 copy-start.1
  169.1 1.0 copy-start.17
  198.2 9.8 %copy-start.5 = (bf16[1,3,4,128,128]{4,3,2,1,0:T(8,128)(2,1)S(1)}, bf16[1,3,4,128,128]{4,3,2,1,0:T(8,128)(2,1)}, u32[]{:S(2)}) copy-start(bf16[1,3,4,128,128]{4,3,2,1,0:T(8,128)(2,1)} %copy-done.4) | copy-start | bytes 1179652
  198.2 9.8 %copy-start.9 = (bf16[1,3,4,128,128]{4,3,2,1,0:T(8,128)(2,1)S(1)}, bf16[1,3,4,128,128]{4,3,2,1,0:T(8,128)(2,1)}, u32[]{:S(2)}) copy-start(bf16[1,3,4,128,128]{4,3,2,1,0:T(8,128)(2,1)} %copy-done.8) | copy-start | bytes 1179652
  198.2 9.8 %copy-start.13 = (bf16[1,3,4,128,128]{4,3,2,1,0:T(8,128)(2,1)S(1)}, bf16[1,3,4,128,128]{4,3,2,1,0:T(8,128)(2,1)}, u32[]{:S(2)}) copy-start(bf16[1,3,4,128,128]{4,3,2,1,0:T(8,128)(2,1)} %copy-done.12) | copy-start | bytes 1179652
  198.2 9.8 %copy-start.15 = (bf16[1,3,4,128,128]{4,3,2,1,0:T(8,128)(2,1)S(1)}, bf16[1,3,4,128,128]{4,3,2,1,0:T(8,128)(2,1)}, u32[]{:S(2)}) copy-start(bf16[1,3,4,128,128]{4,3,2,1,0:T(8,128)(2,1)} %copy-done.14) | copy-start | bytes 1179652
  198.7 35.4 %collective-permute-start.17 = (bf16[1,4,128,128]{3,2,1,0:T(8,128)(2,1)S(1)}, bf16[1,4,128,128]{3,2,1,0:T(8,128)(2,1)S(1)}, u32[]{:S(2)}, u32[]{:S(2)}) collective-permute-start(bf16[1,4,128,128]{3,2,1,0:T(8,128)(2,1)S(1)} %get-tuple-element.35), channel_id=1, source_target_pairs={{0,8},{2,10},{4,12},{6,14},{8,0},{10,2},{12,4},{14,6},{1,9},{3,11}... | collective-permute-start | bytes 393224 | tf_op jit(solution)/shard_map/ppermute | solution.py:166
  202.1 33.5 %collective-permute-start.18 = (bf16[1,4,128,128]{3,2,1,0:T(8,128)(2,1)S(1)}, bf16[1,4,128,128]{3,2,1,0:T(8,128)(2,1)S(1)}, u32[]{:S(2)}, u32[]{:S(2)}) collective-permute-start(bf16[1,4,128,128]{3,2,1,0:T(8,128)(2,1)S(1)} %get-tuple-element.36), channel_id=1, source_target_pairs={{0,2},{2,0},{4,6},{6,4},{8,10},{10,8},{12,14},{14,12},{1,3},{3,1},... | collective-permute-start | bytes 393224 | tf_op jit(solution)/shard_map/ppermute | solution.py:166
  203.8 4.1 %copy-start.26 = (bf16[1,3,4,128,128]{4,3,2,1,0:T(8,128)(2,1)}, bf16[1,3,4,128,128]{4,3,2,1,0:T(8,128)(2,1)S(1)}, u32[]{:S(2)}) copy-start(bf16[1,3,4,128,128]{4,3,2,1,0:T(8,128)(2,1)S(1)} %collective-permute-done.36.refs_15_) | copy-start | bytes 1179652
  203.8 33.0 %collective-permute-start.19 = (bf16[1,4,128,128]{3,2,1,0:T(8,128)(2,1)S(1)}, bf16[1,4,128,128]{3,2,1,0:T(8,128)(2,1)S(1)}, u32[]{:S(2)}, u32[]{:S(2)}) collective-permute-start(bf16[1,4,128,128]{3,2,1,0:T(8,128)(2,1)S(1)} %get-tuple-element.37), channel_id=1, source_target_pairs={{0,10},{2,8},{4,14},{6,12},{8,2},{10,0},{12,6},{14,4},{1,11},{3,9}... | collective-permute-start | bytes 393224 | tf_op jit(solution)/shard_map/ppermute | solution.py:166
  203.9 35.0 %collective-permute-start.20 = (bf16[1,4,128,128]{3,2,1,0:T(8,128)(2,1)S(1)}, bf16[1,4,128,128]{3,2,1,0:T(8,128)(2,1)S(1)}, u32[]{:S(2)}, u32[]{:S(2)}) collective-permute-start(bf16[1,4,128,128]{3,2,1,0:T(8,128)(2,1)S(1)} %get-tuple-element.38), channel_id=1, source_target_pairs={{0,4},{2,6},{4,0},{6,2},{8,12},{10,14},{12,8},{14,10},{1,5},{3,7},... | collective-permute-start | bytes 393224 | tf_op jit(solution)/shard_map/ppermute | solution.py:166
  206.1 1.9 copy-start.28
  206.1 34.6 %collective-permute-start.21 = (bf16[1,4,128,128]{3,2,1,0:T(8,128)(2,1)S(1)}, bf16[1,4,128,128]{3,2,1,0:T(8,128)(2,1)S(1)}, u32[]{:S(2)}, u32[]{:S(2)}) collective-permute-start(bf16[1,4,128,128]{3,2,1,0:T(8,128)(2,1)S(1)} %get-tuple-element.39), channel_id=1, source_target_pairs={{0,12},{2,14},{4,8},{6,10},{8,4},{10,6},{12,0},{14,2},{1,13},{3,15... | collective-permute-start | bytes 393224 | tf_op jit(solution)/shard_map/ppermute | solution.py:166
  234.1 7.4 %collective-permute-start.22 = (bf16[1,4,128,128]{3,2,1,0:T(8,128)(2,1)S(1)}, bf16[1,4,128,128]{3,2,1,0:T(8,128)(2,1)S(1)}, u32[]{:S(2)}, u32[]{:S(2)}) collective-permute-start(bf16[1,4,128,128]{3,2,1,0:T(8,128)(2,1)S(1)} %get-tuple-element.40), channel_id=1, source_target_pairs={{0,6},{2,4},{4,2},{6,0},{8,14},{10,12},{12,10},{14,8},{1,7},{3,5},... | collective-permute-start | bytes 393224 | tf_op jit(solution)/shard_map/ppermute | solution.py:166
  235.6 9.1 %collective-permute-start.23 = (bf16[1,4,128,128]{3,2,1,0:T(8,128)(2,1)S(1)}, bf16[1,4,128,128]{3,2,1,0:T(8,128)(2,1)S(1)}, u32[]{:S(2)}, u32[]{:S(2)}) collective-permute-start(bf16[1,4,128,128]{3,2,1,0:T(8,128)(2,1)S(1)} %get-tuple-element.41), channel_id=1, source_target_pairs={{0,14},{2,12},{4,10},{6,8},{8,6},{10,4},{12,2},{14,0},{1,15},{3,13... | collective-permute-start | bytes 393224 | tf_op jit(solution)/shard_map/ppermute | solution.py:166
  236.8 19.4 %collective-permute-start.39 = (bf16[1,4,128,128]{3,2,1,0:T(8,128)(2,1)S(1)}, bf16[1,4,128,128]{3,2,1,0:T(8,128)(2,1)S(1)}, u32[]{:S(2)}, u32[]{:S(2)}) collective-permute-start(bf16[1,4,128,128]{3,2,1,0:T(8,128)(2,1)S(1)} %get-tuple-element.50), channel_id=1, source_target_pairs={{0,8},{2,10},{4,12},{6,14},{8,0},{10,2},{12,4},{14,6},{1,9},{3,11}... | collective-permute-start | bytes 393224 | tf_op jit(solution)/shard_map/ppermute | solution.py:166
  238.8 17.4 %collective-permute-start.40 = (bf16[1,4,128,128]{3,2,1,0:T(8,128)(2,1)S(1)}, bf16[1,4,128,128]{3,2,1,0:T(8,128)(2,1)S(1)}, u32[]{:S(2)}, u32[]{:S(2)}) collective-permute-start(bf16[1,4,128,128]{3,2,1,0:T(8,128)(2,1)S(1)} %get-tuple-element.51), channel_id=1, source_target_pairs={{0,2},{2,0},{4,6},{6,4},{8,10},{10,8},{12,14},{14,12},{1,3},{3,1},... | collective-permute-start | bytes 393224 | tf_op jit(solution)/shard_map/ppermute | solution.py:166
  240.6 20.3 %collective-permute-start.41 = (bf16[1,4,128,128]{3,2,1,0:T(8,128)(2,1)S(1)}, bf16[1,4,128,128]{3,2,1,0:T(8,128)(2,1)S(1)}, u32[]{:S(2)}, u32[]{:S(2)}) collective-permute-start(bf16[1,4,128,128]{3,2,1,0:T(8,128)(2,1)S(1)} %get-tuple-element.52), channel_id=1, source_target_pairs={{0,10},{2,8},{4,14},{6,12},{8,2},{10,0},{12,6},{14,4},{1,11},{3,9}... | collective-permute-start | bytes 393224 | tf_op jit(solution)/shard_map/ppermute | solution.py:166
  241.6 19.3 %collective-permute-start.42 = (bf16[1,4,128,128]{3,2,1,0:T(8,128)(2,1)S(1)}, bf16[1,4,128,128]{3,2,1,0:T(8,128)(2,1)S(1)}, u32[]{:S(2)}, u32[]{:S(2)}) collective-permute-start(bf16[1,4,128,128]{3,2,1,0:T(8,128)(2,1)S(1)} %get-tuple-element.53), channel_id=1, source_target_pairs={{0,4},{2,6},{4,0},{6,2},{8,12},{10,14},{12,8},{14,10},{1,5},{3,7},... | collective-permute-start | bytes 393224 | tf_op jit(solution)/shard_map/ppermute | solution.py:166
  244.6 16.3 %collective-permute-start.43 = (bf16[1,4,128,128]{3,2,1,0:T(8,128)(2,1)S(1)}, bf16[1,4,128,128]{3,2,1,0:T(8,128)(2,1)S(1)}, u32[]{:S(2)}, u32[]{:S(2)}) collective-permute-start(bf16[1,4,128,128]{3,2,1,0:T(8,128)(2,1)S(1)} %get-tuple-element.54), channel_id=1, source_target_pairs={{0,12},{2,14},{4,8},{6,10},{8,4},{10,6},{12,0},{14,2},{1,13},{3,15... | collective-permute-start | bytes 393224 | tf_op jit(solution)/shard_map/ppermute | solution.py:166
  256.2 6.5 %collective-permute-start.44 = (bf16[1,4,128,128]{3,2,1,0:T(8,128)(2,1)S(1)}, bf16[1,4,128,128]{3,2,1,0:T(8,128)(2,1)S(1)}, u32[]{:S(2)}, u32[]{:S(2)}) collective-permute-start(bf16[1,4,128,128]{3,2,1,0:T(8,128)(2,1)S(1)} %get-tuple-element.55), channel_id=1, source_target_pairs={{0,6},{2,4},{4,2},{6,0},{8,14},{10,12},{12,10},{14,8},{1,7},{3,5},... | collective-permute-start | bytes 393224 | tf_op jit(solution)/shard_map/ppermute | solution.py:166
  256.3 7.8 %collective-permute-start.45 = (bf16[1,4,128,128]{3,2,1,0:T(8,128)(2,1)S(1)}, bf16[1,4,128,128]{3,2,1,0:T(8,128)(2,1)S(1)}, u32[]{:S(2)}, u32[]{:S(2)}) collective-permute-start(bf16[1,4,128,128]{3,2,1,0:T(8,128)(2,1)S(1)} %get-tuple-element.56), channel_id=1, source_target_pairs={{0,14},{2,12},{4,10},{6,8},{8,6},{10,4},{12,2},{14,0},{1,15},{3,13... | collective-permute-start | bytes 393224 | tf_op jit(solution)/shard_map/ppermute | solution.py:166
  262.7 1.4 copy-start.22
  (12 other events, 10.2 us)

commit v3 on v1

v3 whole, which is shorter than its diff:
```python
import math

import jax
import jax.numpy as jnp
from jax import lax
from jax.experimental import pallas as pl
from jax.experimental.pallas import tpu as pltpu
from jax.sharding import PartitionSpec as P

BLK = 128
LISTED = 8
PACK_VMEM = 60 * 1024 * 1024


def attention_kernel(
    place, rand, queries, keys_mine, values_mine, keys_theirs, values_theirs, ck_mine, ck_theirs, cv_mine, cv_theirs, out, keys, values
):
    sources = queries.shape[0]
    cached = ck_mine.shape[1] // BLK
    prefix = 2 * cached
    side = place[0]
    other = 1 - side
    for index in range(cached):
        rows = pl.ds(index * BLK, BLK)
        keys[side * cached + index] = ck_mine[0, rows, :]
        values[side * cached + index] = cv_mine[0, rows, :].T
        keys[other * cached + index] = ck_theirs[0, rows, :]
        values[other * cached + index] = cv_theirs[0, rows, :].T

    def place_source(source, carry):
        block = prefix + 2 * source
        keys[block + side] = keys_mine[source, 0, 0]
        values[block + side] = values_mine[source, 0, 0].T
        keys[block + other] = keys_theirs[source, 0, 0]
        values[block + other] = values_theirs[source, 0, 0].T
        return carry

    lax.fori_loop(0, sources, place_source, 0, unroll=min(8, sources))
    factor = math.log2(math.e) / math.sqrt(queries.shape[-1])
    key_slot = lax.broadcasted_iota(jnp.int32, (BLK, BLK), 0)
    query_slot = lax.broadcasted_iota(jnp.int32, (BLK, BLK), 1)
    blocked = key_slot > query_slot

    def one_block(source, carry):
        block = 2 * source + side
        own = prefix + block
        listed = [own - 2, own - 1, own, 0, 1] + [rand[block, column] for column in range(3)]
        chosen_keys = jnp.concatenate([keys[key_block] for key_block in listed], axis=0)
        chosen_values = jnp.concatenate([values[key_block] for key_block in listed], axis=1)
        scores = lax.dot_general(
            chosen_keys, queries[source, 0, 0], (((1,), (1,)), ((), ())), preferred_element_type=jnp.float32
        )
        diagonal = jnp.where(blocked, -jnp.inf, scores[2 * BLK : 3 * BLK])
        scores = jnp.concatenate([scores[: 2 * BLK], diagonal, scores[3 * BLK :]], axis=0)
        weights = jnp.exp2((scores - jnp.max(scores, axis=0, keepdims=True)) * factor)
        inverse = 1.0 / jnp.sum(weights, axis=0, keepdims=True)
        probs = (weights * inverse).astype(jnp.bfloat16)
        total = jnp.dot(chosen_values, probs, preferred_element_type=jnp.float32)
        out[source, 0] = total.T.astype(out.dtype)
        return carry

    lax.fori_loop(0, sources, one_block, 0, unroll=8 if sources % 8 == 0 else 1)


def attend(place, rand, parts, caches, first):
    sources, _, heads, _, width = parts[0][0].shape
    cached_rows = caches[0].shape[1]
    key_blocks = 2 * cached_rows // BLK + 2 * sources
    cache_spec = pl.BlockSpec((1, cached_rows, width), lambda head, *_: (first + head, 0, 0))

    def part_spec(index):
        return pl.BlockSpec((sources, 1, 1, BLK, width), lambda head, *_: (0, index, head, 0, 0))

    work = heads * sources * BLK * LISTED * BLK
    return pl.pallas_call(
        attention_kernel,
        grid_spec=pltpu.PrefetchScalarGridSpec(
            num_scalar_prefetch=2,
            grid=(heads,),
            in_specs=[part_spec(index) for _, index in parts] + [cache_spec] * 4,
            out_specs=pl.BlockSpec((sources, 1, BLK, width), lambda head, *_: (0, head, 0, 0)),
            scratch_shapes=[
                pltpu.VMEM((key_blocks, BLK, width), jnp.bfloat16),
                pltpu.VMEM((key_blocks, width, BLK), jnp.bfloat16),
            ],
        ),
        out_shape=jax.ShapeDtypeStruct((sources, heads, BLK, width), jnp.bfloat16),
        compiler_params=pltpu.CompilerParams(vmem_limit_bytes=48 * 1024 * 1024),
        cost_estimate=pl.CostEstimate(
            flops=4 * work * width,
            bytes_accessed=2 * heads * width * BLK * (6 * sources + 2 * key_blocks),
            transcendentals=work,
        ),
    )(place, rand, *[array for array, _ in parts], *caches)


def move(stage, groups, arrivals, departures):
    inward, outward = [], []
    for index, (sources, target) in enumerate(groups):
        slot = stage.at[index]
        inward.append(
            [
                pltpu.make_async_copy(source, slot.at[part], arrivals.at[index, part])
                for part, source in enumerate(sources)
            ]
        )
        outward.append(pltpu.make_async_copy(slot, target, departures.at[index]))
    for group in inward:
        for copy in group:
            copy.start()
    for group, departure in zip(inward, outward):
        for copy in group:
            copy.wait()
        departure.start()
    for departure in outward:
        departure.wait()


def move_call(kernel, stage, shape, place, *arrays, into=None):
    inputs = list(arrays) + ([] if into is None else [into])
    return pl.pallas_call(
        kernel,
        grid_spec=pltpu.PrefetchScalarGridSpec(
            num_scalar_prefetch=1,
            grid=(1,),
            in_specs=[pl.BlockSpec(memory_space=pl.ANY)] * len(inputs),
            out_specs=pl.BlockSpec(memory_space=pl.ANY),
            scratch_shapes=[
                pltpu.VMEM(stage, jnp.bfloat16),
                pltpu.SemaphoreType.DMA(stage[:2]),
                pltpu.SemaphoreType.DMA(stage[:1]),
            ],
        ),
        out_shape=jax.ShapeDtypeStruct(shape, jnp.bfloat16),
        input_output_aliases={} if into is None else {len(inputs): 0},
        compiler_params=pltpu.CompilerParams(vmem_limit_bytes=PACK_VMEM),
        cost_estimate=pl.CostEstimate(flops=0, bytes_accessed=4 * math.prod(stage), transcendentals=0),
    )(place, *inputs)


def pack(place, queries, stretch_keys, stretch_values, chunk, part):
    owners, _, local_rows, width = queries.shape
    heads = pl.ds(part * chunk, chunk)

    def kernel(place, queries, keys, values, out, stage, arrivals, departures):
        rows = pl.ds(place[0] * local_rows, local_rows)
        groups = [
            ((queries.at[owner, heads], keys.at[owner, heads, rows], values.at[owner, heads, rows]), out.at[owner])
            for owner in range(owners)
        ]
        move(stage, groups, arrivals, departures)

    shape = (owners, 3, chunk, local_rows, width)
    return move_call(kernel, shape, shape, place, queries, stretch_keys, stretch_values)


def collect(place, returned, owned, part, into):
    owners, chunk, local_rows, width = returned.shape
    heads = pl.ds(part * chunk, chunk)

    def kernel(place, returned, *refs):
        out, stage, arrivals, departures = refs[-4:]
        groups = [((returned.at[owner],), out.at[pl.ds(owner, 1), heads]) for owner in range(owners)]
        move(stage, groups, arrivals, departures)

    shape = (owners, owned, local_rows, width)
    return move_call(kernel, (owners, 1, chunk, local_rows, width), shape, place, returned, into=into)


def after(value, *earlier):
    return lax.optimization_barrier((value, *earlier))[0]


def per_device(queries, stretch_keys, stretch_values, cache_keys, cache_values, rand_blocks):
    heads, local_rows, width = queries.shape
    seq_devices = lax.axis_size("seq")
    side = lax.axis_index("cache")
    owned = heads // seq_devices
    swap = [(0, 1), (1, 0)]
    assert local_rows == BLK and lax.axis_size("cache") == 2

    def by_owner(rows):
        return rows.reshape(seq_devices, owned, rows.shape[1], width)

    def exchange(value):
        return lax.all_to_all(value, "seq", split_axis=0, concat_axis=0, tiled=True)

    place = jnp.reshape(side, (1,)).astype(jnp.int32)
    chunk = max(1, owned // 2)
    messages = [
        pack(place, by_owner(queries), by_owner(stretch_keys), by_owner(stretch_values), chunk, part)
        for part in range(owned // chunk)
    ]
    caches = (
        cache_keys,
        lax.ppermute(cache_keys, "cache", swap),
        cache_values,
        lax.ppermute(cache_values, "cache", swap),
    )
    result = attended = None
    for part, message in enumerate(messages):
        mine = exchange(message)
        if attended is not None:
            mine = after(mine, attended)
        theirs = lax.ppermute(mine, "cache", swap)
        parts = [(mine, 0), (mine, 1), (mine, 2), (theirs, 1), (theirs, 2)]
        attended = attend(place, rand_blocks, parts, caches, part * chunk)
        result = collect(place, exchange(attended), owned, part, result)
    return result.reshape(heads, local_rows, width)


def solution(mesh):
    placed = (
        P("groups", ("seq", "cache"), None),
        P("groups", "seq", None),
        P("groups", "seq", None),
        P(("groups", "seq"), "cache", None),
        P(("groups", "seq"), "cache", None),
        P("groups", None),
    )
    return jax.shard_map(
        per_device,
        mesh=mesh,
        in_specs=placed,
        out_specs=P("groups", ("seq", "cache"), None),
        check_vma=False,
    )
```

time: 252 us -> 219 us (0.87)
  blocking collectives: 108 us -> 0 us
  waiting for transfers between devices: 67.6 us -> 161 us
  Pallas kernels: 51 us -> 36.5 us
  local copies, waits for them, and re-layouts: 12.3 us -> 1.08 us
  starting transfers between devices: 9.46 us -> 19.6 us
  other arithmetic: 3.4 us -> 0 us
    all_to_all x2 -> x0, blocking collectives: 108 us -> none  [the longest x1 77.9 us: per_device(): lax.all_to_all(packed[:, :, first:first + chunk], 'seq', split_axis=0, co...]
    all_to_all x2 -> x4, waiting for transfers between devices: 67.5 us -> 148 us  [exchange(): return lax.all_to_all(value, 'seq', split_axis=0, concat_axis=0, tiled=True)]
    pallas_call x2, Pallas kernels: 51 us -> 26.3 us  [attend(): pl.pallas_call(attention_kernel, grid_spec=pltpu.PrefetchScalarGridSpec(n...]
    ppermute x1, waiting for transfers between devices: 0.01 us -> 10.7 us  [per_device(): lax.ppermute(cache_keys, 'cache', swap)]
    pallas_call x0 -> x4, Pallas kernels: none -> 10.2 us  [move_call(): pl.pallas_call(kernel, grid_spec=pltpu.PrefetchScalarGridSpec(num_scalar_...]
    all_to_all x2 -> x4, starting transfers between devices: 8.81 us -> 19 us  [exchange(): return lax.all_to_all(value, 'seq', split_axis=0, concat_axis=0, tiled=True)]
    slice x3 -> x0, local copies, waits for them, and re-layouts: 9.37 us -> none  [the longest x2 6.3 us: per_device(): theirs = lax.ppermute(mine[:, 1:], 'cache', swap)]
    concatenate x1 -> x0, other arithmetic: 2.73 us -> none  [per_device(): return jnp.concatenate(results, axis=1).reshape(heads, local_rows, width)]
  transfers between devices with their start and end apart: 6 -> 8, of which waited for: 2 -> 7; matrix products, arithmetic and copies ran while one was open for 3% -> 0% of each run, Pallas kernels for 20% -> 14%
where the time goes in v3:
time: 219 us
  waiting for transfers between devices  161 us (74%)
  Pallas kernels  36.5 us (17%)
  starting transfers between devices  19.6 us (9%)
    all_to_all x4, waiting for transfers between devices, exchange(): return lax.all_to_all(value, 'seq', split_axis=0, concat_axis=0, tiled=True)  148 us
    pallas_call x2, Pallas kernels, attend(): pl.pallas_call(attention_kernel, grid_spec=pltpu.PrefetchScalarGridSpec(n...  26.3 us
    all_to_all x4, starting transfers between devices, exchange(): return lax.all_to_all(value, 'seq', split_axis=0, concat_axis=0, tiled=True)  19 us
    ppermute x1, waiting for transfers between devices, per_device(): lax.ppermute(cache_keys, 'cache', swap)  10.7 us
    pallas_call x4, Pallas kernels, move_call(): pl.pallas_call(kernel, grid_spec=pltpu.PrefetchScalarGridSpec(num_scalar_...  10.2 us
  transfers between devices with their start and end apart: 8, of which 7 were waited for; matrix products, arithmetic and copies ran while one was open for 0% of the time, Pallas kernels for 14%

profile of v3, /device:TPU:0, one launch (start us, length us, event | category | flops | bytes accessed | tf_op | source)
XLA Modules:
  0.0 218.6 jit_solution(11601219468159819341)
XLA Ops:
  0.0 3.0 %shard_map.65 = bf16[8,3,4,128,128]{4,3,2,1,0:T(8,128)(2,1)} custom-call(s32[1]{0:T(128)} %bitcast.place, bf16[8,8,128,128]{3,2,1,0:T(8,128)(2,1)} %bitcast.9, bf16[8,8,256,128]{3,2,1,0:T(8,128)(2,1)} %bitcast.5, bf16[8,8,256,128]{3,2,1,0:T(8,128)(2,1)} %bitcast.7), custom_call_target="tpu_custom_call" | custom-call | bytes 6291456 | tf_op jit(solution)/shard_map/pallas_call | solution.py:121
  3.0 7.3 %all-to-all-start.1 = ((bf16[8,3,4,128,128]{4,3,2,1,0:T(8,128)(2,1)}), bf16[8,3,4,128,128]{4,3,2,1,0:T(8,128)(2,1)}, u32[]{:S(2)}, u32[]{:S(2)}) async-start(bf16[8,3,4,128,128]{4,3,2,1,0:T(8,128)(2,1)} %shard_map.65), calls=%async_computation.1 | async-start | bytes 6291456 | tf_op jit(solution)/shard_map/all_to_all | solution.py:186
  10.3 3.0 %shard_map.64 = bf16[8,3,4,128,128]{4,3,2,1,0:T(8,128)(2,1)} custom-call(s32[1]{0:T(128)} %bitcast.place, bf16[8,8,128,128]{3,2,1,0:T(8,128)(2,1)} %bitcast.10, bf16[8,8,256,128]{3,2,1,0:T(8,128)(2,1)} %bitcast.6, bf16[8,8,256,128]{3,2,1,0:T(8,128)(2,1)} %bitcast.8), custom_call_target="tpu_custom_call" | custom-call | bytes 6291456 | tf_op jit(solution)/shard_map/pallas_call | solution.py:121
  13.3 0.0 copy-start
  13.3 0.0 copy-start.3
  13.3 67.8 %all-to-all-done.1.queries.keys_mine.values_mine = bf16[8,3,4,128,128]{4,3,2,1,0:T(8,128)(2,1)} async-done(((bf16[8,3,4,128,128]{4,3,2,1,0:T(8,128)(2,1)}), bf16[8,3,4,128,128]{4,3,2,1,0:T(8,128)(2,1)}, u32[]{:S(2)}, u32[]{:S(2)}) %all-to-all-start.1) | async-done | bytes 3145760 | tf_op jit(solution)/shard_map/all_to_all | solution.py:186
  81.1 4.4 %all-to-all-start = ((bf16[8,3,4,128,128]{4,3,2,1,0:T(8,128)(2,1)}), bf16[8,3,4,128,128]{4,3,2,1,0:T(8,128)(2,1)}, u32[]{:S(2)}, u32[]{:S(2)}) async-start(bf16[8,3,4,128,128]{4,3,2,1,0:T(8,128)(2,1)} %shard_map.64), calls=%async_computation | async-start | bytes 6291456 | tf_op jit(solution)/shard_map/all_to_all | solution.py:186
  85.5 0.1 collective-permute-start
  85.6 0.0 copy-done
  85.6 0.5 collective-permute-start.1
  86.1 0.1 collective-permute-start.2
  86.2 0.0 copy-done.3
  86.2 0.1 copy.9.rand
  86.3 10.7 %collective-permute-done.1.ck_theirs = bf16[8,1024,128]{2,1,0:T(8,128)(2,1)} collective-permute-done((bf16[8,1024,128]{2,1,0:T(8,128)(2,1)S(1)}, bf16[8,1024,128]{2,1,0:T(8,128)(2,1)}, u32[]{:S(2)}, u32[]{:S(2)}) %collective-permute-start.1) | collective-permute-done | bytes 2097184 | tf_op jit(solution)/shard_map/ppermute | solution.py:196
  97.0 0.6 collective-permute-done.2.cv_theirs
  97.6 0.0 collective-permute-done.keys_theirs.values_theirs
  97.6 13.1 %shard_map.66 = bf16[8,4,128,128]{3,2,1,0:T(8,128)(2,1)} custom-call(s32[1]{0:T(128)} %bitcast.place, s32[16,3]{1,0:T(8,128)S(1)} %copy.9.rand, bf16[8,3,4,128,128]{4,3,2,1,0:T(8,128)(2,1)} %all-to-all-done.1.queries.keys_mine.values_mine, bf16[8,3,4,128,128]{4,3,2,1,0:T(8,128)(2,1)} %all-to-all-done.1.queries.keys_mine.values_mine, ...), custom_call_target="tpu_custom_call" | custom-call | flops 2147483648 | bytes 14680064 | tf_op jit(solution)/shard_map/pallas_call | solution.py:75
  110.8 45.0 %all-to-all-done.queries.keys_mine.values_mine = bf16[8,3,4,128,128]{4,3,2,1,0:T(8,128)(2,1)} async-done(((bf16[8,3,4,128,128]{4,3,2,1,0:T(8,128)(2,1)}), bf16[8,3,4,128,128]{4,3,2,1,0:T(8,128)(2,1)}, u32[]{:S(2)}, u32[]{:S(2)}) %all-to-all-start) | async-done | bytes 3145760 | tf_op jit(solution)/shard_map/all_to_all | solution.py:186
  155.7 0.0 collective-permute-start.3
  155.7 3.6 %all-to-all-start.3 = ((bf16[8,4,128,128]{3,2,1,0:T(8,128)(2,1)}), bf16[8,4,128,128]{3,2,1,0:T(8,128)(2,1)S(1)}, u32[]{:S(2)}, u32[]{:S(2)}) async-start(bf16[8,4,128,128]{3,2,1,0:T(8,128)(2,1)} %shard_map.66), calls=%async_computation.3 | async-start | bytes 2097152 | tf_op jit(solution)/shard_map/all_to_all | solution.py:186
  159.4 2.4 %collective-permute-done.3.keys_theirs.values_theirs = bf16[8,3,4,128,128]{4,3,2,1,0:T(8,128)(2,1)} collective-permute-done((bf16[8,3,4,128,128]{4,3,2,1,0:T(8,128)(2,1)}, bf16[8,3,4,128,128]{4,3,2,1,0:T(8,128)(2,1)}, u32[]{:S(2)}, u32[]{:S(2)}) %collective-permute-start.3) | collective-permute-done | bytes 3145760 | tf_op jit(solution)/shard_map/ppermute | solution.py:205
  161.7 13.2 %shard_map.67 = bf16[8,4,128,128]{3,2,1,0:T(8,128)(2,1)} custom-call(s32[1]{0:T(128)} %bitcast.place, s32[16,3]{1,0:T(8,128)S(1)} %copy.9.rand, bf16[8,3,4,128,128]{4,3,2,1,0:T(8,128)(2,1)} %all-to-all-done.queries.keys_mine.values_mine, bf16[8,3,4,128,128]{4,3,2,1,0:T(8,128)(2,1)} %all-to-all-done.queries.keys_mine.values_mine, ...), custom_call_target="tpu_custom_call" | custom-call | flops 2147483648 | bytes 14680064 | tf_op jit(solution)/shard_map/pallas_call | solution.py:75
  174.9 11.0 %all-to-all-done.3.returned = bf16[8,4,128,128]{3,2,1,0:T(8,128)(2,1)S(1)} async-done(((bf16[8,4,128,128]{3,2,1,0:T(8,128)(2,1)}), bf16[8,4,128,128]{3,2,1,0:T(8,128)(2,1)S(1)}, u32[]{:S(2)}, u32[]{:S(2)}) %all-to-all-start.3) | async-done | bytes 1048608 | tf_op jit(solution)/shard_map/all_to_all | solution.py:186
  185.9 0.0 copy-start.1
  185.9 3.6 %all-to-all-start.2 = ((bf16[8,4,128,128]{3,2,1,0:T(8,128)(2,1)}), bf16[8,4,128,128]{3,2,1,0:T(8,128)(2,1)S(1)}, u32[]{:S(2)}, u32[]{:S(2)}) async-start(bf16[8,4,128,128]{3,2,1,0:T(8,128)(2,1)} %shard_map.67), calls=%async_computation.2 | async-start | bytes 2097152 | tf_op jit(solution)/shard_map/all_to_all | solution.py:186
  189.6 0.0 copy-done.1
  189.6 2.1 shard_map.68.refs_0_
  191.7 23.9 %all-to-all-done.2.returned = bf16[8,4,128,128]{3,2,1,0:T(8,128)(2,1)S(1)} async-done(((bf16[8,4,128,128]{3,2,1,0:T(8,128)(2,1)}), bf16[8,4,128,128]{3,2,1,0:T(8,128)(2,1)S(1)}, u32[]{:S(2)}, u32[]{:S(2)}) %all-to-all-start.2) | async-done | bytes 1048608 | tf_op jit(solution)/shard_map/all_to_all | solution.py:186
  215.6 0.0 copy-start.2
  215.6 1.0 copy-done.2
  216.5 2.1 shard_map.69
Async XLA Ops:
  3.0 78.1 %all-to-all-start.1 = ((bf16[8,3,4,128,128]{4,3,2,1,0:T(8,128)(2,1)}), bf16[8,3,4,128,128]{4,3,2,1,0:T(8,128)(2,1)}, u32[]{:S(2)}, u32[]{:S(2)}) async-start(bf16[8,3,4,128,128]{4,3,2,1,0:T(8,128)(2,1)} %shard_map.65), calls=%async_computation.1 | async-start | bytes 6291456 | tf_op jit(solution)/shard_map/all_to_all | solution.py:186
  13.3 72.3 %copy-start = (bf16[8,1024,128]{2,1,0:T(8,128)(2,1)S(1)}, bf16[8,1024,128]{2,1,0:T(8,128)(2,1)}, u32[]{:S(2)}) copy-start(bf16[8,1024,128]{2,1,0:T(8,128)(2,1)} %ck_mine.3) | copy-start | bytes 6291460
  13.3 72.9 %copy-start.3 = (s32[16,3]{0,1:T(4,128)S(1)}, s32[16,3]{0,1:T(4,128)}, u32[]{:S(2)}) copy-start(s32[16,3]{0,1:T(4,128)} %param.11) | copy-start | bytes 580
  81.1 74.6 %all-to-all-start = ((bf16[8,3,4,128,128]{4,3,2,1,0:T(8,128)(2,1)}), bf16[8,3,4,128,128]{4,3,2,1,0:T(8,128)(2,1)}, u32[]{:S(2)}, u32[]{:S(2)}) async-start(bf16[8,3,4,128,128]{4,3,2,1,0:T(8,128)(2,1)} %shard_map.64), calls=%async_computation | async-start | bytes 6291456 | tf_op jit(solution)/shard_map/all_to_all | solution.py:186
  85.5 12.1 %collective-permute-start = (bf16[8,3,4,128,128]{4,3,2,1,0:T(8,128)(2,1)}, bf16[8,3,4,128,128]{4,3,2,1,0:T(8,128)(2,1)}, u32[]{:S(2)}, u32[]{:S(2)}) collective-permute-start(bf16[8,3,4,128,128]{4,3,2,1,0:T(8,128)(2,1)} %all-to-all-done.1.queries.keys_mine.values_mine), channel_id=1, source_target_pairs={{0,1},{1,0},{2,3},{3,2},{4,5},{5,4},{6,7},{7,6},{8,9},{9,8},{10,11... | collective-permute-start | bytes 9437192 | tf_op jit(solution)/shard_map/ppermute | solution.py:205
  85.6 11.4 %collective-permute-start.1 = (bf16[8,1024,128]{2,1,0:T(8,128)(2,1)S(1)}, bf16[8,1024,128]{2,1,0:T(8,128)(2,1)}, u32[]{:S(2)}, u32[]{:S(2)}) collective-permute-start(bf16[8,1024,128]{2,1,0:T(8,128)(2,1)S(1)} %copy-done), channel_id=1, source_target_pairs={{0,1},{1,0},{2,3},{3,2},{4,5},{5,4},{6,7},{7,6},{8,9},{9,8},{10,11... | collective-permute-start | bytes 6291464 | tf_op jit(solution)/shard_map/ppermute | solution.py:196
  86.1 11.5 %collective-permute-start.2 = (bf16[8,1024,128]{2,1,0:T(8,128)(2,1)}, bf16[8,1024,128]{2,1,0:T(8,128)(2,1)}, u32[]{:S(2)}, u32[]{:S(2)}) collective-permute-start(bf16[8,1024,128]{2,1,0:T(8,128)(2,1)} %cv_mine.3), channel_id=1, source_target_pairs={{0,1},{1,0},{2,3},{3,2},{4,5},{5,4},{6,7},{7,6},{8,9},{9,8},{10,11... | collective-permute-start | bytes 6291464 | tf_op jit(solution)/shard_map/ppermute | solution.py:198
  155.7 6.0 %collective-permute-start.3 = (bf16[8,3,4,128,128]{4,3,2,1,0:T(8,128)(2,1)}, bf16[8,3,4,128,128]{4,3,2,1,0:T(8,128)(2,1)}, u32[]{:S(2)}, u32[]{:S(2)}) collective-permute-start(bf16[8,3,4,128,128]{4,3,2,1,0:T(8,128)(2,1)} %all-to-all-done.queries.keys_mine.values_mine), channel_id=1, source_target_pairs={{0,1},{1,0},{2,3},{3,2},{4,5},{5,4},{6,7},{7,6},{8,9},{9,8},{10,11... | collective-permute-start | bytes 9437192 | tf_op jit(solution)/shard_map/ppermute | solution.py:205
  155.7 30.2 %all-to-all-start.3 = ((bf16[8,4,128,128]{3,2,1,0:T(8,128)(2,1)}), bf16[8,4,128,128]{3,2,1,0:T(8,128)(2,1)S(1)}, u32[]{:S(2)}, u32[]{:S(2)}) async-start(bf16[8,4,128,128]{3,2,1,0:T(8,128)(2,1)} %shard_map.66), calls=%async_computation.3 | async-start | bytes 2097152 | tf_op jit(solution)/shard_map/all_to_all | solution.py:186
  185.9 3.6 %copy-start.1 = (bf16[8,4,128,128]{3,2,1,0:T(8,128)(2,1)}, bf16[8,4,128,128]{3,2,1,0:T(8,128)(2,1)S(1)}, u32[]{:S(2)}) copy-start(bf16[8,4,128,128]{3,2,1,0:T(8,128)(2,1)S(1)} %all-to-all-done.3.returned) | copy-start | bytes 3145732
  185.9 29.6 %all-to-all-start.2 = ((bf16[8,4,128,128]{3,2,1,0:T(8,128)(2,1)}), bf16[8,4,128,128]{3,2,1,0:T(8,128)(2,1)S(1)}, u32[]{:S(2)}, u32[]{:S(2)}) async-start(bf16[8,4,128,128]{3,2,1,0:T(8,128)(2,1)} %shard_map.67), calls=%async_computation.2 | async-start | bytes 2097152 | tf_op jit(solution)/shard_map/all_to_all | solution.py:186
  215.6 1.0 copy-start.2

commit v4 on v1

v4 whole, which is shorter than its diff:
```python
import math

import jax
import jax.numpy as jnp
from jax import lax
from jax.experimental import pallas as pl
from jax.experimental.pallas import tpu as pltpu
from jax.sharding import PartitionSpec as P

BLK = 128
LISTED = 8
UNROLL = 16
OWNED = 4
EARLY = 3


def unroll_of(sources):
    return UNROLL if sources % UNROLL == 0 else 1


def listed_blocks(rand, prefix, block):
    own = prefix + block
    return [own - 2, own - 1, own, 0, 1] + [rand[block, column] for column in range(3)]


def fill(blocks, side, cached_mine, cached_theirs, sources, put):
    cached = cached_mine.shape[1] // BLK
    for index in range(cached):
        rows = pl.ds(index * BLK, BLK)
        blocks[side * cached + index] = put(cached_mine[0, rows, :])
        blocks[(1 - side) * cached + index] = put(cached_theirs[0, rows, :])
    for block, ref, index in sources:
        blocks[2 * cached + block] = put(ref[index, 0])


def turned(block):
    return block.T


def same(block):
    return block


def probabilities(query, keys, listed):
    factor = math.log2(math.e) / math.sqrt(query.shape[-1])
    key_slot = lax.broadcasted_iota(jnp.int32, (BLK, BLK), 0)
    query_slot = lax.broadcasted_iota(jnp.int32, (BLK, BLK), 1)
    chosen = jnp.concatenate([keys[key_block] for key_block in listed], axis=0)
    scores = lax.dot_general(chosen, query, (((1,), (1,)), ((), ())), preferred_element_type=jnp.float32)
    diagonal = jnp.where(key_slot > query_slot, -jnp.inf, scores[2 * BLK : 3 * BLK])
    scores = jnp.concatenate([scores[: 2 * BLK], diagonal, scores[3 * BLK :]], axis=0)
    weights = jnp.exp2((scores - jnp.max(scores, axis=0, keepdims=True)) * factor)
    inverse = 1.0 / jnp.sum(weights, axis=0, keepdims=True)
    return (weights * inverse).astype(jnp.bfloat16)


def weighted(probs, values, listed):
    chosen = jnp.concatenate([values[key_block] for key_block in listed], axis=1)
    return jnp.dot(chosen, probs, preferred_element_type=jnp.float32).T.astype(jnp.bfloat16)


def attention_kernel(paired, place, rand, queries, keys_mine, values_mine, ck_mine, ck_theirs, cv_mine, cv_theirs, *refs):
    theirs = refs[:2] if paired else None
    out, keys, values = refs[-3:]
    sources = queries.shape[0]
    prefix = 2 * ck_mine.shape[1] // BLK
    side = place[0]

    def block_of(source, which):
        return 2 * source + which if paired else source

    def rows_of(mine, part):
        rows = [(block_of(source, side), mine, source) for source in range(sources)]
        if paired:
            rows += [(block_of(source, 1 - side), theirs[part], source) for source in range(sources)]
        return rows

    fill(keys, side, ck_mine, ck_theirs, rows_of(keys_mine, 0), same)
    fill(values, side, cv_mine, cv_theirs, rows_of(values_mine, 1), turned)

    def one_block(source, carry):
        listed = listed_blocks(rand, prefix, block_of(source, side))
        out[source, 0] = weighted(probabilities(queries[source, 0], keys, listed), values, listed)
        return carry

    lax.fori_loop(0, sources, one_block, 0, unroll=unroll_of(sources))


def attend(place, rand, mine, theirs, caches, owned, first=0, into=None):
    sources, slabs, _, width = mine.shape
    heads = slabs // 3
    paired = theirs is not None
    cached_rows = caches[0].shape[1]
    key_blocks = 2 * cached_rows // BLK + (2 if paired else 1) * sources

    def slab(part):
        return pl.BlockSpec((sources, 1, BLK, width), lambda head, *_: (0, part * heads + head, 0, 0))

    def cache_index(head, place, rand):
        return ((0 if paired else place[0] * owned) + first + head, 0, 0)

    arrays = [in_hbm(array) for array in [mine] * 3 + list(caches) + ([theirs] * 2 if paired else [])]
    in_specs = [slab(0), slab(1), slab(2)] + [pl.BlockSpec((1, cached_rows, width), cache_index)] * 4
    in_specs += [slab(1), slab(2)] if paired else []
    aliases = {}
    if into is not None:
        aliases = {2 + len(arrays): 0}
        arrays.append(into)
        in_specs.append(pl.BlockSpec(memory_space=pl.ANY))
    work = heads * sources * BLK * LISTED * BLK
    return pl.pallas_call(
        lambda *refs: attention_kernel(paired, *refs),
        grid_spec=pltpu.PrefetchScalarGridSpec(
            num_scalar_prefetch=2,
            grid=(heads,),
            in_specs=in_specs,
            out_specs=pl.BlockSpec((sources, 1, BLK, width), lambda head, *_: (0, first + head, 0, 0)),
            scratch_shapes=[
                pltpu.VMEM((key_blocks, BLK, width), jnp.bfloat16),
                pltpu.VMEM((key_blocks, width, BLK), jnp.bfloat16),
            ],
        ),
        out_shape=jax.ShapeDtypeStruct((sources, owned, BLK, width), jnp.bfloat16),
        input_output_aliases=aliases,
        compiler_params=pltpu.CompilerParams(vmem_limit_bytes=48 * 1024 * 1024),
        cost_estimate=pl.CostEstimate(
            flops=4 * work * width,
            bytes_accessed=2 * heads * width * BLK * (4 * sources + 2 * key_blocks),
            transcendentals=work,
        ),
    )(place, rand, *arrays)


def in_hbm(array):
    return pltpu.with_memory_space_constraint(array, pltpu.HBM)


def pack(place, arrays, plan):
    owners, _, local_rows, width = arrays[0].shape
    slabs = sum(count for _, _, count in plan)
    group = 4 if owners % 4 == 0 else 1

    def kernel(place, *refs):
        sources, (out, stage, arrivals, departures) = refs[:-4], refs[-4:]
        rows = pl.ds(place[0] * local_rows, local_rows)
        inward = []
        for owner in range(owners):
            slab = 0
            for part, (index, first, count) in enumerate(plan):
                heads, whole = pl.ds(first, count), sources[index].shape[2] == local_rows
                source = sources[index].at[owner, heads] if whole else sources[index].at[owner, heads, rows]
                target = stage.at[owner, pl.ds(slab, count)]
                inward.append(pltpu.make_async_copy(source, target, arrivals.at[owner, part]))
                slab += count
        outward = []
        for index in range(owners // group):
            some = pl.ds(index * group, group)
            outward.append(pltpu.make_async_copy(stage.at[some], out.at[some], departures.at[index]))
        for copy in inward:
            copy.start()
        for index, departure in enumerate(outward):
            for copy in inward[index * group * len(plan) : (index + 1) * group * len(plan)]:
                copy.wait()
            departure.start()
        for departure in outward:
            departure.wait()

    shape = (owners, slabs, local_rows, width)
    return pl.pallas_call(
        kernel,
        grid_spec=pltpu.PrefetchScalarGridSpec(
            num_scalar_prefetch=1,
            grid=(1,),
            in_specs=[pl.BlockSpec(memory_space=pltpu.HBM)] * len(arrays),
            out_specs=pl.BlockSpec(memory_space=pltpu.HBM),
            scratch_shapes=[
                pltpu.VMEM(shape, jnp.bfloat16),
                pltpu.SemaphoreType.DMA((owners, len(plan))),
                pltpu.SemaphoreType.DMA((owners // group,)),
            ],
        ),
        out_shape=pltpu.HBM(shape, jnp.bfloat16),
        compiler_params=pltpu.CompilerParams(vmem_limit_bytes=48 * 1024 * 1024),
        cost_estimate=pl.CostEstimate(flops=0, bytes_accessed=4 * math.prod(shape), transcendentals=0),
    )(place, *[in_hbm(array) for array in arrays])


def after(value, *earlier):
    return lax.optimization_barrier((value, *earlier))[0]


def per_device(queries, stretch_keys, stretch_values, cache_keys, cache_values, rand_blocks):
    heads, local_rows, width = queries.shape
    side = lax.axis_index("cache")
    assert local_rows == BLK and lax.axis_size("cache") == 2
    place = jnp.reshape(side, (1,)).astype(jnp.int32)

    def to_sibling(value):
        return lax.ppermute(value, "cache", [(0, 1), (1, 0)])

    by_heads = heads % (2 * lax.axis_size("seq")) == 0
    axes = ("seq", "cache") if by_heads else "seq"
    owners = lax.axis_size(axes)
    owned = heads // owners
    arrays = [rows.reshape(owners, owned, rows.shape[1], width) for rows in (queries, stretch_keys, stretch_values)]
    caches = (cache_keys, to_sibling(cache_keys), cache_values, to_sibling(cache_values))

    def exchange(value):
        return lax.all_to_all(value, axes, split_axis=0, concat_axis=0, tiled=True)

    splits = [(0, EARLY), (EARLY, owned - EARLY)] if by_heads and owned == OWNED else [(0, owned)]
    attended = None
    for first, count in splits:
        mine = exchange(pack(place, arrays, [(index, first, count) for index in range(3)]))
        if attended is not None:
            mine = after(mine, attended)
        theirs = None if by_heads else to_sibling(mine)
        attended = attend(place, rand_blocks, mine, theirs, caches, owned, first, attended)
    return exchange(attended).reshape(heads, local_rows, width)


def solution(mesh):
    placed = (
        P("groups", ("seq", "cache"), None),
        P("groups", "seq", None),
        P("groups", "seq", None),
        P(("groups", "seq"), "cache", None),
        P(("groups", "seq"), "cache", None),
        P("groups", None),
    )
    return jax.shard_map(
        per_device,
        mesh=mesh,
        in_specs=placed,
        out_specs=P("groups", ("seq", "cache"), None),
        check_vma=False,
    )
```

time: 252 us -> 217 us (0.86)
  blocking collectives: 108 us -> 56.2 us
  waiting for transfers between devices: 67.6 us -> 101 us
  Pallas kernels: 51 us -> 28.3 us
  starting transfers between devices: 9.46 us -> 29.8 us
  local copies, waits for them, and re-layouts: 12.3 us -> 1.41 us
  other arithmetic: 3.4 us -> 0 us
    all_to_all x2 -> x1, blocking collectives: 108 us -> 56.2 us  [exchange(): return lax.all_to_all(value, axes, split_axis=0, concat_axis=0, tiled=True)]
    all_to_all x2, waiting for transfers between devices: 67.5 us -> 93.8 us  [exchange(): return lax.all_to_all(value, axes, split_axis=0, concat_axis=0, tiled=True)]
    pallas_call x2 -> x4, Pallas kernels: 51 us -> 28.3 us  [the longest x2 21.3 us: attend(): pl.pallas_call(lambda *refs: attention_kernel(paired, *refs), grid_spec=p...]
    all_to_all x2, starting transfers between devices: 8.81 us -> 29.2 us  [exchange(): return lax.all_to_all(value, axes, split_axis=0, concat_axis=0, tiled=True)]
    slice x3 -> x0, local copies, waits for them, and re-layouts: 9.37 us -> none  [the longest x2 6.3 us: per_device(): theirs = lax.ppermute(mine[:, 1:], 'cache', swap)]
    ppermute x4 -> x2, waiting for transfers between devices: 0.01 us -> 6.9 us  [to_sibling(): return lax.ppermute(value, 'cache', [(0, 1), (1, 0)])]
    concatenate x1 -> x0, other arithmetic: 2.73 us -> none  [per_device(): return jnp.concatenate(results, axis=1).reshape(heads, local_rows, width)]
    dynamic_slice x1 -> x0, local copies, waits for them, and re-layouts: 2.69 us -> none  [own_rows(): return lax.dynamic_slice_in_dim(rows, side * local_rows, local_rows, axis=1)]
  transfers between devices with their start and end apart: 6 -> 4, of which waited for: 2 -> 4; matrix products, arithmetic and copies ran while one was open for 3% -> 0% of each run, Pallas kernels for 20% -> 8%
where the time goes in v4:
time: 217 us
  waiting for transfers between devices  101 us (47%)
  blocking collectives  56.2 us (26%)
  starting transfers between devices  29.8 us (14%)
  Pallas kernels  28.3 us (13%)
    all_to_all x2, waiting for transfers between devices, exchange(): return lax.all_to_all(value, axes, split_axis=0, concat_axis=0, tiled=True)  93.8 us
    all_to_all x1, blocking collectives, exchange(): return lax.all_to_all(value, axes, split_axis=0, concat_axis=0, tiled=True)  56.2 us
    all_to_all x2, starting transfers between devices, exchange(): return lax.all_to_all(value, axes, split_axis=0, concat_axis=0, tiled=True)  29.2 us
    pallas_call x2, Pallas kernels, attend(): pl.pallas_call(lambda *refs: attention_kernel(paired, *refs), grid_spec=p...  21.3 us
    pallas_call x2, Pallas kernels, pack(): pl.pallas_call(kernel, grid_spec=pltpu.PrefetchScalarGridSpec(num_scalar_...  6.97 us
    ppermute x2, waiting for transfers between devices, to_sibling(): return lax.ppermute(value, 'cache', [(0, 1), (1, 0)])  6.9 us
  transfers between devices with their start and end apart: 4, of which 4 were waited for; matrix products, arithmetic and copies ran while one was open for 0% of the time, Pallas kernels for 8%

profile of v4, /device:TPU:0, one launch (start us, length us, event | category | flops | bytes accessed | tf_op | source)
XLA Modules:
  0.0 216.5 jit_solution(9488630994094799802)
XLA Ops:
  0.0 4.4 %shard_map.65 = bf16[16,9,128,128]{3,2,1,0:T(8,128)(2,1)} custom-call(s32[1]{0:T(128)} %bitcast.place.refs_0_, bf16[16,4,128,128]{3,2,1,0:T(8,128)(2,1)} %bitcast.10, bf16[16,4,256,128]{3,2,1,0:T(8,128)(2,1)} %bitcast.5, bf16[16,4,256,128]{3,2,1,0:T(8,128)(2,1)} %bitcast.7), custom_call_target="tpu_custom_call" | custom-call | bytes 9437184 | tf_op jit(solution)/shard_map/pallas_call | solution.py:169
  4.4 7.4 %all-to-all-start.1 = ((bf16[16,9,128,128]{3,2,1,0:T(8,128)(2,1)}), bf16[16,9,128,128]{3,2,1,0:T(8,128)(2,1)}, u32[]{:S(2)}, u32[]{:S(2)}) async-start(bf16[16,9,128,128]{3,2,1,0:T(8,128)(2,1)} %shard_map.65), calls=%async_computation.1 | async-start | bytes 9437184 | tf_op jit(solution)/shard_map/all_to_all | solution.py:209
  11.8 2.6 %shard_map.64 = bf16[16,3,128,128]{3,2,1,0:T(8,128)(2,1)} custom-call(s32[1]{0:T(128)} %bitcast.place.refs_0_, bf16[16,4,128,128]{3,2,1,0:T(8,128)(2,1)} %bitcast.11, bf16[16,4,256,128]{3,2,1,0:T(8,128)(2,1)} %bitcast.6, bf16[16,4,256,128]{3,2,1,0:T(8,128)(2,1)} %bitcast.8), custom_call_target="tpu_custom_call" | custom-call | bytes 3145728 | tf_op jit(solution)/shard_map/pallas_call | solution.py:169
  14.4 0.0 copy-start
  14.4 0.0 copy-start.1
  14.4 84.2 %all-to-all-done.1.refs_2_.refs_3_.refs_4_ = bf16[16,9,128,128]{3,2,1,0:T(8,128)(2,1)} async-done(((bf16[16,9,128,128]{3,2,1,0:T(8,128)(2,1)}), bf16[16,9,128,128]{3,2,1,0:T(8,128)(2,1)}, u32[]{:S(2)}, u32[]{:S(2)}) %all-to-all-start.1) | async-done | bytes 4718624 | tf_op jit(solution)/shard_map/all_to_all | solution.py:209
  98.7 21.8 %all-to-all-start = ((bf16[16,3,128,128]{3,2,1,0:T(8,128)(2,1)}), bf16[16,3,128,128]{3,2,1,0:T(8,128)(2,1)}, u32[]{:S(2)}, u32[]{:S(2)}) async-start(bf16[16,3,128,128]{3,2,1,0:T(8,128)(2,1)} %shard_map.64), calls=%async_computation | async-start | bytes 3145728 | tf_op jit(solution)/shard_map/all_to_all | solution.py:209
  120.5 0.0 copy-done
  120.5 0.4 collective-permute-start
  120.9 0.1 collective-permute-start.1
  121.0 0.0 copy-done.1
  121.0 0.1 copy.9.refs_1_
  121.1 5.2 %collective-permute-done.refs_6_ = bf16[8,1024,128]{2,1,0:T(8,128)(2,1)} collective-permute-done((bf16[8,1024,128]{2,1,0:T(8,128)(2,1)S(1)}, bf16[8,1024,128]{2,1,0:T(8,128)(2,1)}, u32[]{:S(2)}, u32[]{:S(2)}) %collective-permute-start) | collective-permute-done | bytes 2097184 | tf_op jit(solution)/shard_map/ppermute | solution.py:199
  126.3 1.7 collective-permute-done.1.refs_8_
  128.0 14.9 %shard_map.66.refs_9_ = bf16[16,4,128,128]{3,2,1,0:T(8,128)(2,1)S(1)} custom-call(s32[1]{0:T(128)} %bitcast.place.refs_0_, s32[16,3]{1,0:T(8,128)S(1)} %copy.9.refs_1_, bf16[16,9,128,128]{3,2,1,0:T(8,128)(2,1)} %all-to-all-done.1.refs_2_.refs_3_.refs_4_, bf16[16,9,128,128]{3,2,1,0:T(8,128)(2,1)} %all-to-all-done.1.refs_2_.refs_3_.refs_4_, ...), custom_call_target="tpu_custom_call" | custom-call | flops 3221225472 | bytes 12582912 | tf_op jit(solution)/shard_map/pallas_call | solution.py:111
  142.9 9.6 %all-to-all-done.refs_2_.refs_3_.refs_4_ = bf16[16,3,128,128]{3,2,1,0:T(8,128)(2,1)} async-done(((bf16[16,3,128,128]{3,2,1,0:T(8,128)(2,1)}), bf16[16,3,128,128]{3,2,1,0:T(8,128)(2,1)}, u32[]{:S(2)}, u32[]{:S(2)}) %all-to-all-start) | async-done | bytes 1572896 | tf_op jit(solution)/shard_map/all_to_all | solution.py:209
  152.5 6.5 %shard_map.67 = bf16[16,4,128,128]{3,2,1,0:T(8,128)(2,1)S(1)} custom-call(s32[1]{0:T(128)} %bitcast.place.refs_0_, s32[16,3]{1,0:T(8,128)S(1)} %copy.9.refs_1_, bf16[16,3,128,128]{3,2,1,0:T(8,128)(2,1)} %all-to-all-done.refs_2_.refs_3_.refs_4_, bf16[16,3,128,128]{3,2,1,0:T(8,128)(2,1)} %all-to-all-done.refs_2_.refs_3_.refs_4_, ...), custom_call_target="tpu_custom_call", output_to_operand_aliasing={{}: (9, {})} | custom-call | flops 1073741824 | bytes 4194304 | tf_op jit(solution)/shard_map/pallas_call | solution.py:111
  159.0 56.2 %all_to_all.15 = bf16[16,4,128,128]{3,2,1,0:T(8,128)(2,1)S(1)} all-to-all(bf16[16,4,128,128]{3,2,1,0:T(8,128)(2,1)S(1)} %shard_map.67), channel_id=1, replica_groups=mesh['groups'=2,'seq'=8,'cache'=2] {'seq','cache'}, dimensions={0} | all-to-all | bytes 4194304 | tf_op jit(solution)/shard_map/all_to_all | solution.py:209
  215.2 1.3 copy.12
Async XLA Ops:
  4.4 94.2 %all-to-all-start.1 = ((bf16[16,9,128,128]{3,2,1,0:T(8,128)(2,1)}), bf16[16,9,128,128]{3,2,1,0:T(8,128)(2,1)}, u32[]{:S(2)}, u32[]{:S(2)}) async-start(bf16[16,9,128,128]{3,2,1,0:T(8,128)(2,1)} %shard_map.65), calls=%async_computation.1 | async-start | bytes 9437184 | tf_op jit(solution)/shard_map/all_to_all | solution.py:209
  14.4 106.1 %copy-start = (bf16[8,1024,128]{2,1,0:T(8,128)(2,1)S(1)}, bf16[8,1024,128]{2,1,0:T(8,128)(2,1)}, u32[]{:S(2)}) copy-start(bf16[8,1024,128]{2,1,0:T(8,128)(2,1)} %refs_5_.3) | copy-start | bytes 6291460
  14.4 106.6 %copy-start.1 = (s32[16,3]{0,1:T(4,128)S(1)}, s32[16,3]{0,1:T(4,128)}, u32[]{:S(2)}) copy-start(s32[16,3]{0,1:T(4,128)} %param.11) | copy-start | bytes 580
  98.7 53.8 %all-to-all-start = ((bf16[16,3,128,128]{3,2,1,0:T(8,128)(2,1)}), bf16[16,3,128,128]{3,2,1,0:T(8,128)(2,1)}, u32[]{:S(2)}, u32[]{:S(2)}) async-start(bf16[16,3,128,128]{3,2,1,0:T(8,128)(2,1)} %shard_map.64), calls=%async_computation | async-start | bytes 3145728 | tf_op jit(solution)/shard_map/all_to_all | solution.py:209
  120.5 5.8 %collective-permute-start = (bf16[8,1024,128]{2,1,0:T(8,128)(2,1)S(1)}, bf16[8,1024,128]{2,1,0:T(8,128)(2,1)}, u32[]{:S(2)}, u32[]{:S(2)}) collective-permute-start(bf16[8,1024,128]{2,1,0:T(8,128)(2,1)S(1)} %copy-done), channel_id=1, source_target_pairs={{0,1},{1,0},{2,3},{3,2},{4,5},{5,4},{6,7},{7,6},{8,9},{9,8},{10,11... | collective-permute-start | bytes 6291464 | tf_op jit(solution)/shard_map/ppermute | solution.py:199
  120.9 7.1 %collective-permute-start.1 = (bf16[8,1024,128]{2,1,0:T(8,128)(2,1)}, bf16[8,1024,128]{2,1,0:T(8,128)(2,1)}, u32[]{:S(2)}, u32[]{:S(2)}) collective-permute-start(bf16[8,1024,128]{2,1,0:T(8,128)(2,1)} %refs_7_.3), channel_id=1, source_target_pairs={{0,1},{1,0},{2,3},{3,2},{4,5},{5,4},{6,7},{7,6},{8,9},{9,8},{10,11... | collective-permute-start | bytes 6291464 | tf_op jit(solution)/shard_map/ppermute | solution.py:199

commit v5 on v4

--- a/solution.py
+++ b/solution.py
@@ -11,7 +11,10 @@
 LISTED = 8
 UNROLL = 16
 OWNED = 4
-EARLY = 3
+EARLY = 2
+WINDOW = 5
+GATE = 6
+STEPS = (0, 8, 1, 9, 2, 10, 3, 11, 4, 12, 5, 13, 6, 14, 7, 15)
 
 
 def unroll_of(sources):
@@ -30,7 +33,7 @@
         blocks[side * cached + index] = put(cached_mine[0, rows, :])
         blocks[(1 - side) * cached + index] = put(cached_theirs[0, rows, :])
     for block, ref, index in sources:
-        blocks[2 * cached + block] = put(ref[index, 0])
+        blocks[2 * cached + block] = put(ref[index])
 
 
 def turned(block):
@@ -70,9 +73,9 @@
         return 2 * source + which if paired else source
 
     def rows_of(mine, part):
-        rows = [(block_of(source, side), mine, source) for source in range(sources)]
+        rows = [(block_of(source, side), mine, (source, 0)) for source in range(sources)]
         if paired:
-            rows += [(block_of(source, 1 - side), theirs[part], source) for source in range(sources)]
+            rows += [(block_of(source, 1 - side), theirs[part], (source, 0)) for source in range(sources)]
         return rows
 
     fill(keys, side, ck_mine, ck_theirs, rows_of(keys_mine, 0), same)
@@ -86,7 +89,7 @@
     lax.fori_loop(0, sources, one_block, 0, unroll=unroll_of(sources))
 
 
-def attend(place, rand, mine, theirs, caches, owned, first=0, into=None):
+def attend(place, rand, mine, theirs, caches, owned):
     sources, slabs, _, width = mine.shape
     heads = slabs // 3
     paired = theirs is not None
@@ -97,16 +100,11 @@
         return pl.BlockSpec((sources, 1, BLK, width), lambda head, *_: (0, part * heads + head, 0, 0))
 
     def cache_index(head, place, rand):
-        return ((0 if paired else place[0] * owned) + first + head, 0, 0)
+        return ((0 if paired else place[0] * owned) + head, 0, 0)
 
     arrays = [in_hbm(array) for array in [mine] * 3 + list(caches) + ([theirs] * 2 if paired else [])]
     in_specs = [slab(0), slab(1), slab(2)] + [pl.BlockSpec((1, cached_rows, width), cache_index)] * 4
     in_specs += [slab(1), slab(2)] if paired else []
-    aliases = {}
-    if into is not None:
-        aliases = {2 + len(arrays): 0}
-        arrays.append(into)
-        in_specs.append(pl.BlockSpec(memory_space=pl.ANY))
     work = heads * sources * BLK * LISTED * BLK
     return pl.pallas_call(
         lambda *refs: attention_kernel(paired, *refs),
@@ -114,18 +112,77 @@
             num_scalar_prefetch=2,
             grid=(heads,),
             in_specs=in_specs,
-            out_specs=pl.BlockSpec((sources, 1, BLK, width), lambda head, *_: (0, first + head, 0, 0)),
+            out_specs=pl.BlockSpec((sources, 1, BLK, width), lambda head, *_: (0, head, 0, 0)),
             scratch_shapes=[
                 pltpu.VMEM((key_blocks, BLK, width), jnp.bfloat16),
                 pltpu.VMEM((key_blocks, width, BLK), jnp.bfloat16),
             ],
         ),
         out_shape=jax.ShapeDtypeStruct((sources, owned, BLK, width), jnp.bfloat16),
-        input_output_aliases=aliases,
         compiler_params=pltpu.CompilerParams(vmem_limit_bytes=48 * 1024 * 1024),
         cost_estimate=pl.CostEstimate(
             flops=4 * work * width,
             bytes_accessed=2 * heads * width * BLK * (4 * sources + 2 * key_blocks),
+            transcendentals=work,
+        ),
+    )(place, rand, *arrays)
+
+
+def pieces_kernel(pieces, by_step, place, rand, *refs):
+    mine, (ck_mine, ck_theirs, cv_mine, cv_theirs) = refs[:pieces], refs[pieces : pieces + 4]
+    keys, values, queries, results = refs[-4:]
+    outs = refs[pieces + 4 : -4]
+    prefix = 2 * ck_mine.shape[1] // BLK
+    side = place[0]
+    rows = [(place[1 + index], ref) for index, ref in enumerate(mine)]
+    fill(keys, side, ck_mine, ck_theirs, [(source, ref, (0, 0, 1)) for source, ref in rows], same)
+    fill(values, side, cv_mine, cv_theirs, [(source, ref, (0, 0, 2)) for source, ref in rows], turned)
+    for source, ref in rows:
+        queries[source] = ref[0, 0, 0]
+
+    def one_block(source, carry):
+        listed = listed_blocks(rand, prefix, source)
+        results[source] = weighted(probabilities(queries[source], keys, listed), values, listed)
+        return carry
+
+    lax.fori_loop(0, pieces, one_block, 0, unroll=unroll_of(pieces))
+    if by_step:
+        for index, out in enumerate(outs):
+            out[0, 0] = results[place[1 + pieces + index]]
+    else:
+        outs[0][:, 0] = results[...]
+
+
+def attend_pieces(place, rand, mine, caches, owned, first, by_step=False):
+    pieces = len(mine)
+    _, heads, _, _, width = mine[0].shape
+    cached_rows = caches[0].shape[1]
+    key_blocks = 2 * cached_rows // BLK + pieces
+    piece_spec = pl.BlockSpec((1, 1, 3, BLK, width), lambda head, *_: (0, head, 0, 0, 0))
+    cache_spec = pl.BlockSpec((1, cached_rows, width), lambda head, place, rand: (place[0] * owned + first + head, 0, 0))
+    arrays = [in_hbm(array) for array in [*mine, *caches]]
+    in_specs = [piece_spec] * pieces + [cache_spec] * 4
+    outs = pieces if by_step else 1
+    work = heads * pieces * BLK * LISTED * BLK
+    return pl.pallas_call(
+        lambda *refs: pieces_kernel(pieces, by_step, *refs),
+        grid_spec=pltpu.PrefetchScalarGridSpec(
+            num_scalar_prefetch=2,
+            grid=(heads,),
+            in_specs=in_specs,
+            out_specs=[pl.BlockSpec((pieces // outs, 1, BLK, width), lambda head, *_: (0, head, 0, 0))] * outs,
+            scratch_shapes=[
+                pltpu.VMEM((key_blocks, BLK, width), jnp.bfloat16),
+                pltpu.VMEM((key_blocks, width, BLK), jnp.bfloat16),
+                pltpu.VMEM((pieces, BLK, width), jnp.bfloat16),
+                pltpu.VMEM((pieces, BLK, width), jnp.bfloat16),
+            ],
+        ),
+        out_shape=[jax.ShapeDtypeStruct((pieces // outs, heads, BLK, width), jnp.bfloat16)] * outs,
+        compiler_params=pltpu.CompilerParams(vmem_limit_bytes=48 * 1024 * 1024),
+        cost_estimate=pl.CostEstimate(
+            flops=24 * work * width,
+            bytes_accessed=2 * heads * width * BLK * (4 * pieces + 2 * key_blocks),
             transcendentals=work,
         ),
     )(place, rand, *arrays)
@@ -185,6 +242,96 @@
     )(place, *[in_hbm(array) for array in arrays])
 
 
+def pack_each(place, arrays, steps, first, count):
+    _, _, local_rows, width = arrays[0].shape
+    heads = pl.ds(first, count)
+    parts = len(arrays)
+
+    def kernel(place, *refs):
+        sources, outs, (stage, arrivals, departures) = refs[:parts], refs[parts:-3], refs[-3:]
+        rows = pl.ds(place[0] * local_rows, local_rows)
+        inward, outward = [], []
+        for index, step in enumerate(steps):
+            owner = place[1 + step]
+            for part, source in enumerate(sources):
+                piece = source.at[owner, heads] if source.shape[2] == local_rows else source.at[owner, heads, rows]
+                inward.append(pltpu.make_async_copy(piece, stage.at[index, :, part], arrivals.at[index, part]))
+            outward.append(pltpu.make_async_copy(stage.at[index], outs[index].at[0], departures.at[index]))
+        for copy in inward:
+            copy.start()
+        for index, departure in enumerate(outward):
+            for copy in inward[index * parts : (index + 1) * parts]:
+                copy.wait()
+            departure.start()
+        for departure in outward:
+            departure.wait()
+
+    shape = (count, parts, local_rows, width)
+    return pl.pallas_call(
+        kernel,
+        grid_spec=pltpu.PrefetchScalarGridSpec(
+            num_scalar_prefetch=1,
+            grid=(1,),
+            in_specs=[pl.BlockSpec(memory_space=pltpu.HBM)] * parts,
+            out_specs=[pl.BlockSpec(memory_space=pltpu.HBM)] * len(steps),
+            scratch_shapes=[
+                pltpu.VMEM((len(steps),) + shape, jnp.bfloat16),
+                pltpu.SemaphoreType.DMA((len(steps), parts)),
+                pltpu.SemaphoreType.DMA((len(steps),)),
+            ],
+        ),
+        out_shape=[pltpu.HBM((1,) + shape, jnp.bfloat16)] * len(steps),
+        compiler_params=pltpu.CompilerParams(vmem_limit_bytes=48 * 1024 * 1024),
+        cost_estimate=pl.CostEstimate(flops=0, bytes_accessed=4 * len(steps) * math.prod(shape), transcendentals=0),
+    )(place, *[in_hbm(array) for array in arrays])
+
+
+def collect(place, returned, owned, first, into=None):
+    apart = isinstance(returned, list)
+    arrays = returned if apart else [returned]
+    owners = len(arrays) if apart else returned.shape[0]
+    _, count, local_rows, width = arrays[0].shape
+    heads = pl.ds(first, count)
+    arrays = [in_hbm(array) for array in arrays] + ([] if into is None else [into])
+
+    def kernel(place, *refs):
+        sources, (out, stage, arrivals, departures) = refs[:-4], refs[-4:]
+        inward, outward = [], []
+        for index in range(owners):
+            source = sources[index].at[0] if apart else sources[0].at[index]
+            owner = place[1 + index] if apart else index
+            inward.append(pltpu.make_async_copy(source, stage.at[index], arrivals.at[index]))
+            outward.append(pltpu.make_async_copy(stage.at[index], out.at[owner, heads], departures.at[index]))
+        for copy in inward:
+            copy.start()
+        for copy, departure in zip(inward, outward):
+            copy.wait()
+            departure.start()
+        for departure in outward:
+            departure.wait()
+
+    return pl.pallas_call(
+        kernel,
+        grid_spec=pltpu.PrefetchScalarGridSpec(
+            num_scalar_prefetch=1,
+            grid=(1,),
+            in_specs=[pl.BlockSpec(memory_space=pl.ANY)] * len(arrays),
+            out_specs=pl.BlockSpec(memory_space=pl.ANY),
+            scratch_shapes=[
+                pltpu.VMEM((owners, count, local_rows, width), jnp.bfloat16),
+                pltpu.SemaphoreType.DMA((owners,)),
+                pltpu.SemaphoreType.DMA((owners,)),
+            ],
+        ),
+        out_shape=jax.ShapeDtypeStruct((owners, owned, local_rows, width), jnp.bfloat16),
+        input_output_aliases={} if into is None else {len(arrays): 0},
+        compiler_params=pltpu.CompilerParams(vmem_limit_bytes=48 * 1024 * 1024),
+        cost_estimate=pl.CostEstimate(
+            flops=0, bytes_accessed=4 * owners * count * local_rows * width, transcendentals=0
+        ),
+    )(place, *arrays)
+
+
 def after(value, *earlier):
     return lax.optimization_barrier((value, *earlier))[0]
 
@@ -208,15 +355,43 @@
     def exchange(value):
         return lax.all_to_all(value, axes, split_axis=0, concat_axis=0, tiled=True)
 
-    splits = [(0, EARLY), (EARLY, owned - EARLY)] if by_heads and owned == OWNED else [(0, owned)]
-    attended = None
-    for first, count in splits:
-        mine = exchange(pack(place, arrays, [(index, first, count) for index in range(3)]))
-        if attended is not None:
-            mine = after(mine, attended)
+    if owners != 16 or owned != OWNED:
+        mine = exchange(pack(place, arrays, [(index, 0, owned) for index in range(3)]))
         theirs = None if by_heads else to_sibling(mine)
-        attended = attend(place, rand_blocks, mine, theirs, caches, owned, first, attended)
-    return exchange(attended).reshape(heads, local_rows, width)
+        attended = attend(place, rand_blocks, mine, theirs, caches, owned)
+        return exchange(attended).reshape(heads, local_rows, width)
+
+    here = 2 * lax.axis_index("seq") + side
+    owner_at = jnp.stack([side] + [here ^ step ^ (8 * side) for step in range(owners)]).astype(jnp.int32)
+    source_at = jnp.stack([side] + [here ^ step ^ (8 * (side ^ (step & 1))) for step in range(owners)]).astype(jnp.int32)
+    sent = []
+
+    def pairs_of(step):
+        return [(index, index ^ step ^ (8 * (index & 1))) for index in range(owners)]
+
+    def send(message, step):
+        if len(sent) >= WINDOW:
+            message = after(message, sent[-WINDOW])
+        sent.append(lax.ppermute(message, axes, pairs_of(step)))
+        return sent[-1]
+
+    early, late = [None] * owners, [None] * owners
+    for step, message in zip(STEPS, pack_each(owner_at, arrays, STEPS, 0, EARLY)):
+        early[step] = send(message, step)
+    messages = pack_each(owner_at, arrays, STEPS, EARLY, owned - EARLY)
+    both = jnp.concatenate([source_at, owner_at[1:]])
+    attended = attend_pieces(both, rand_blocks, early, caches, owned, 0)[0]
+    for index, (step, message) in enumerate(zip(STEPS, messages)):
+        late[step] = send(message if index < GATE else after(message, attended), step)
+    attended = after(attended, *late)
+    taken = exchange(attended)
+    result = collect(source_at, taken, owned, 0)
+    parts = attend_pieces(both, rand_blocks, late, caches, owned, EARLY, True)
+    returned = [None] * owners
+    for index, step in enumerate(STEPS):
+        returned[step] = lax.ppermute(parts[step], axes, pairs_of(step))
+    result = collect(source_at, returned, owned, EARLY, result)
+    return result.reshape(heads, local_rows, width)
 
 
 def solution(mesh):

time: 217 us -> 215 us (level)
  starting transfers between devices: 29.8 us -> 124 us
  blocking collectives: 56.2 us -> 0 us
  waiting for transfers between devices: 101 us -> 50.2 us
  Pallas kernels: 28.3 us -> 36 us
    ppermute x0 -> x48, starting transfers between devices: none -> 116 us  [the longest x32 84.4 us: send(): sent.append(lax.ppermute(message, axes, pairs_of(step)))]
    all_to_all x2 -> x1, waiting for transfers between devices: 93.8 us -> 0.01 us  [exchange(): return lax.all_to_all(value, axes, split_axis=0, concat_axis=0, tiled=True)]
    all_to_all x1 -> x0, blocking collectives: 56.2 us -> none  [exchange(): return lax.all_to_all(value, axes, split_axis=0, concat_axis=0, tiled=True)]
    ppermute x0 -> x48, waiting for transfers between devices: none -> 50.2 us  [the longest x32 45.8 us: send(): sent.append(lax.ppermute(message, axes, pairs_of(step)))]
    all_to_all x2 -> x1, starting transfers between devices: 29.2 us -> 7.2 us  [exchange(): return lax.all_to_all(value, axes, split_axis=0, concat_axis=0, tiled=True)]
    pallas_call x4 -> x6, Pallas kernels: 28.3 us -> 36 us  [the longest x2 22.7 us: attend_pieces(): pl.pallas_call(lambda *refs: pieces_kernel(pieces, by_step, *refs), grid_...]
    ppermute x2, waiting for transfers between devices: 6.9 us -> 0.01 us  [to_sibling(): return lax.ppermute(value, 'cache', [(0, 1), (1, 0)])]
  transfers between devices with their start and end apart: 4 -> 51, of which waited for: 4 -> 18; matrix products, arithmetic and copies ran while one was open for 0% -> 0% of each run, Pallas kernels for 8% -> 16%
where the time goes in v5:
time: 215 us; the launch traced here: 214 us
  starting transfers between devices  124 us (58%)
  waiting for transfers between devices  50.2 us (23%)
  Pallas kernels  36 us (17%)
  local copies, waits for them, and re-layouts  2.85 us (1%)
    ppermute x32, starting transfers between devices, send(): sent.append(lax.ppermute(message, axes, pairs_of(step)))  84.4 us
    ppermute x32, waiting for transfers between devices, send(): sent.append(lax.ppermute(message, axes, pairs_of(step)))  45.8 us
    ppermute x16, starting transfers between devices, per_device(): returned[step] = lax.ppermute(parts[step], axes, pairs_of(step))  31.8 us
    pallas_call x2, Pallas kernels, attend_pieces(): pl.pallas_call(lambda *refs: pieces_kernel(pieces, by_step, *refs), grid_...  22.7 us
    pallas_call x2, Pallas kernels, pack_each(): pl.pallas_call(kernel, grid_spec=pltpu.PrefetchScalarGridSpec(num_scalar_...  7.93 us
    all_to_all x1, starting transfers between devices, exchange(): return lax.all_to_all(value, axes, split_axis=0, concat_axis=0, tiled=True)  7.2 us
    pallas_call x2, Pallas kernels, collect(): pl.pallas_call(kernel, grid_spec=pltpu.PrefetchScalarGridSpec(num_scalar_...  5.39 us
    ppermute x16, waiting for transfers between devices, per_device(): returned[step] = lax.ppermute(parts[step], axes, pairs_of(step))  4.37 us
  transfers between devices with their start and end apart: 51, of which 18 were waited for; matrix products, arithmetic and copies ran while one was open for 0% of the time, Pallas kernels for 16%

profile of v5, /device:TPU:0, one launch (start us, length us, event | category | flops | bytes accessed | tf_op | source)
XLA Modules:
  0.0 213.9 jit_solution(1275811377586366473)
XLA Ops:
  0.6 4.0 %shard_map.65 = (bf16[1,2,3,128,128]{4,3,2,1,0:T(8,128)(2,1)}, bf16[1,2,3,128,128]{4,3,2,1,0:T(8,128)(2,1)}, bf16[1,2,3,128,128]{4,3,2,1,0:T(8,128)(2,1)}, bf16[...) custom-call(s32[17]{0:T(128)S(1)} %stack.116.place, ...), custom_call_target="tpu_custom_call" | custom-call | bytes 6291456 | tf_op jit(solution)/shard_map/pallas_call | solution.py:270
  4.6 5.9 %collective-permute-start = (bf16[1,2,3,128,128]{4,3,2,1,0:T(8,128)(2,1)}, bf16[1,2,3,128,128]{4,3,2,1,0:T(8,128)(2,1)S(1)}, u32[]{:S(2)}, u32[]{:S(2)}) collective-permute-start(bf16[1,2,3,128,128]{4,3,2,1,0:T(8,128)(2,1)} %get-tuple-element.94), channel_id=1, source_target_pairs={{0,8},{1,1},{2,10},{3,3},{4,12},{5,5},{6,14},{7,7},{8,0},{9,9},{10... | collective-permute-start | bytes 589832 | tf_op jit(solution)/shard_map/ppermute | solution.py:375
  10.6 1.6 collective-permute-start.8
  12.2 9.1 %collective-permute-done.refs_10_ = bf16[1,2,3,128,128]{4,3,2,1,0:T(8,128)(2,1)S(1)} collective-permute-done((bf16[1,2,3,128,128]{4,3,2,1,0:T(8,128)(2,1)}, bf16[1,2,3,128,128]{4,3,2,1,0:T(8,128)(2,1)S(1)}, u32[]{:S(2)}, u32[]{:S(2)}) %collective-permute-start) | collective-permute-done | bytes 196640 | tf_op jit(solution)/shard_map/ppermute | solution.py:375
  21.3 2.2 %collective-permute-start.14 = (bf16[1,2,3,128,128]{4,3,2,1,0:T(8,128)(2,1)}, bf16[1,2,3,128,128]{4,3,2,1,0:T(8,128)(2,1)S(1)}, u32[]{:S(2)}, u32[]{:S(2)}) collective-permute-start(bf16[1,2,3,128,128]{4,3,2,1,0:T(8,128)(2,1)} %get-tuple-element.116), channel_id=1, source_target_pairs={{0,2},{1,11},{2,0},{3,9},{4,6},{5,15},{6,4},{7,13},{8,10},{9,3},{1... | collective-permute-start | bytes 589832 | tf_op jit(solution)/shard_map/ppermute | solution.py:375
  23.5 2.7 %collective-permute-start.1 = (bf16[1,2,3,128,128]{4,3,2,1,0:T(8,128)(2,1)}, bf16[1,2,3,128,128]{4,3,2,1,0:T(8,128)(2,1)S(1)}, u32[]{:S(2)}, u32[]{:S(2)}) collective-permute-start(bf16[1,2,3,128,128]{4,3,2,1,0:T(8,128)(2,1)} %get-tuple-element.95), channel_id=1, source_target_pairs={{0,3},{1,10},{2,1},{3,8},{4,7},{5,14},{6,5},{7,12},{8,11},{9,2},{1... | collective-permute-start | bytes 589832 | tf_op jit(solution)/shard_map/ppermute | solution.py:375
  26.2 1.3 collective-permute-done.13.refs_3_
  27.5 9.2 %collective-permute-start.5 = (bf16[1,2,3,128,128]{4,3,2,1,0:T(8,128)(2,1)}, bf16[1,2,3,128,128]{4,3,2,1,0:T(8,128)(2,1)S(1)}, u32[]{:S(2)}, u32[]{:S(2)}) collective-permute-start(bf16[1,2,3,128,128]{4,3,2,1,0:T(8,128)(2,1)} %get-tuple-element.102), channel_id=1, source_target_pairs={{0,4},{1,13},{2,6},{3,15},{4,0},{5,9},{6,2},{7,11},{8,12},{9,5},{1... | collective-permute-start | bytes 589832 | tf_op jit(solution)/shard_map/ppermute | solution.py:375
  36.7 2.0 collective-permute-start.9
  39.2 2.0 collective-permute-done.5.refs_6_
  41.2 8.1 %collective-permute-start.17 = (bf16[1,2,3,128,128]{4,3,2,1,0:T(8,128)(2,1)}, bf16[1,2,3,128,128]{4,3,2,1,0:T(8,128)(2,1)S(1)}, u32[]{:S(2)}, u32[]{:S(2)}) collective-permute-start(bf16[1,2,3,128,128]{4,3,2,1,0:T(8,128)(2,1)} %get-tuple-element.123), channel_id=1, source_target_pairs={{0,12},{1,5},{2,14},{3,7},{4,8},{5,1},{6,10},{7,3},{8,4},{9,13},{1... | collective-permute-start | bytes 589832 | tf_op jit(solution)/shard_map/ppermute | solution.py:375
  49.4 1.1 collective-permute-done.9.refs_12_
  50.5 7.9 %collective-permute-start.2 = (bf16[1,2,3,128,128]{4,3,2,1,0:T(8,128)(2,1)}, bf16[1,2,3,128,128]{4,3,2,1,0:T(8,128)(2,1)S(1)}, u32[]{:S(2)}, u32[]{:S(2)}) collective-permute-start(bf16[1,2,3,128,128]{4,3,2,1,0:T(8,128)(2,1)} %get-tuple-element.96), channel_id=1, source_target_pairs={{0,13},{1,4},{2,15},{3,6},{4,9},{5,0},{6,11},{7,2},{8,5},{9,12},{1... | collective-permute-start | bytes 589832 | tf_op jit(solution)/shard_map/ppermute | solution.py:375
  58.4 0.6 collective-permute-start.10
  59.1 3.9 %collective-permute-start.6 = (bf16[1,2,3,128,128]{4,3,2,1,0:T(8,128)(2,1)}, bf16[1,2,3,128,128]{4,3,2,1,0:T(8,128)(2,1)S(1)}, u32[]{:S(2)}, u32[]{:S(2)}) collective-permute-start(bf16[1,2,3,128,128]{4,3,2,1,0:T(8,128)(2,1)} %get-tuple-element.103), channel_id=1, source_target_pairs={{0,14},{1,7},{2,12},{3,5},{4,10},{5,3},{6,8},{7,1},{8,6},{9,15},{1... | collective-permute-start | bytes 589832 | tf_op jit(solution)/shard_map/ppermute | solution.py:375
  63.0 2.1 %collective-permute-done.2.refs_15_ = bf16[1,2,3,128,128]{4,3,2,1,0:T(8,128)(2,1)S(1)} collective-permute-done((bf16[1,2,3,128,128]{4,3,2,1,0:T(8,128)(2,1)}, bf16[1,2,3,128,128]{4,3,2,1,0:T(8,128)(2,1)S(1)}, u32[]{:S(2)}, u32[]{:S(2)}) %collective-permute-start.2) | collective-permute-done | bytes 196640 | tf_op jit(solution)/shard_map/ppermute | solution.py:375
  65.1 1.5 collective-permute-start.16
  66.6 4.0 %shard_map.64 = (bf16[1,2,3,128,128]{4,3,2,1,0:T(8,128)(2,1)}, bf16[1,2,3,128,128]{4,3,2,1,0:T(8,128)(2,1)}, bf16[1,2,3,128,128]{4,3,2,1,0:T(8,128)(2,1)}, bf16[...) custom-call(s32[17]{0:T(128)S(1)} %stack.116.place, ...), custom_call_target="tpu_custom_call" | custom-call | bytes 6291456 | tf_op jit(solution)/shard_map/pallas_call | solution.py:270
  70.6 0.8 collective-permute-done.10.refs_7_
  71.5 2.2 %collective-permute-start.18 = (bf16[1,2,3,128,128]{4,3,2,1,0:T(8,128)(2,1)S(1)}, bf16[1,2,3,128,128]{4,3,2,1,0:T(8,128)(2,1)S(1)}, u32[]{:S(2)}, u32[]{:S(2)}) collective-permute-start(bf16[1,2,3,128,128]{4,3,2,1,0:T(8,128)(2,1)S(1)} %copy-done.35), channel_id=1, source_target_pairs={{0,7},{1,14},{2,5},{3,12},{4,3},{5,10},{6,1},{7,8},{8,15},{9,6},{1... | collective-permute-start | bytes 589832 | tf_op jit(solution)/shard_map/ppermute | solution.py:375
  73.7 2.4 %collective-permute-done.6.refs_16_ = bf16[1,2,3,128,128]{4,3,2,1,0:T(8,128)(2,1)S(1)} collective-permute-done((bf16[1,2,3,128,128]{4,3,2,1,0:T(8,128)(2,1)}, bf16[1,2,3,128,128]{4,3,2,1,0:T(8,128)(2,1)S(1)}, u32[]{:S(2)}, u32[]{:S(2)}) %collective-permute-start.6) | collective-permute-done | bytes 196640 | tf_op jit(solution)/shard_map/ppermute | solution.py:375
  76.1 3.2 %collective-permute-start.11 = (bf16[1,2,3,128,128]{4,3,2,1,0:T(8,128)(2,1)S(1)}, bf16[1,2,3,128,128]{4,3,2,1,0:T(8,128)(2,1)}, u32[]{:S(2)}, u32[]{:S(2)}) collective-permute-start(bf16[1,2,3,128,128]{4,3,2,1,0:T(8,128)(2,1)S(1)} %copy-done.32), channel_id=1, source_target_pairs={{0,15},{1,6},{2,13},{3,4},{4,11},{5,2},{6,9},{7,0},{8,7},{9,14},{1... | collective-permute-start | bytes 589832 | tf_op jit(solution)/shard_map/ppermute | solution.py:375
  79.3 1.6 collective-permute-start.3
  81.1 0.5 collective-permute-done.18.refs_9_
  81.6 2.9 %collective-permute-start.23 = (bf16[1,2,3,128,128]{4,3,2,1,0:T(8,128)(2,1)}, bf16[1,2,3,128,128]{4,3,2,1,0:T(8,128)(2,1)S(1)}, u32[]{:S(2)}, u32[]{:S(2)}) collective-permute-start(bf16[1,2,3,128,128]{4,3,2,1,0:T(8,128)(2,1)} %get-tuple-element.132), channel_id=1, source_target_pairs={{0,9},{1,0},{2,11},{3,2},{4,13},{5,4},{6,15},{7,6},{8,1},{9,8},{10... | collective-permute-start | bytes 589832 | tf_op jit(solution)/shard_map/ppermute | solution.py:375
  84.5 1.3 collective-permute-done.11.refs_17_
  85.9 3.0 %collective-permute-start.21 = (bf16[1,2,3,128,128]{4,3,2,1,0:T(8,128)(2,1)}, bf16[1,2,3,128,128]{4,3,2,1,0:T(8,128)(2,1)S(1)}, u32[]{:S(2)}, u32[]{:S(2)}) collective-permute-start(bf16[1,2,3,128,128]{4,3,2,1,0:T(8,128)(2,1)} %get-tuple-element.127), channel_id=1, source_target_pairs={{0,8},{1,1},{2,10},{3,3},{4,12},{5,5},{6,14},{7,7},{8,0},{9,9},{10... | collective-permute-start | bytes 589832 | tf_op jit(solution)/shard_map/ppermute | solution.py:375
  88.9 4.2 %collective-permute-start.7 = (bf16[1,2,3,128,128]{4,3,2,1,0:T(8,128)(2,1)}, bf16[1,2,3,128,128]{4,3,2,1,0:T(8,128)(2,1)S(1)}, u32[]{:S(2)}, u32[]{:S(2)}) collective-permute-start(bf16[1,2,3,128,128]{4,3,2,1,0:T(8,128)(2,1)} %get-tuple-element.104), channel_id=1, source_target_pairs={{0,1},{1,8},{2,3},{3,10},{4,5},{5,12},{6,7},{7,14},{8,9},{9,0},{10... | collective-permute-start | bytes 589832 | tf_op jit(solution)/shard_map/ppermute | solution.py:375
  93.2 5.5 %collective-permute-start.12 = (bf16[1,2,3,128,128]{4,3,2,1,0:T(8,128)(2,1)}, bf16[1,2,3,128,128]{4,3,2,1,0:T(8,128)(2,1)S(1)}, u32[]{:S(2)}, u32[]{:S(2)}) collective-permute-start(bf16[1,2,3,128,128]{4,3,2,1,0:T(8,128)(2,1)} %get-tuple-element.113), channel_id=1, source_target_pairs={{0,2},{1,11},{2,0},{3,9},{4,6},{5,15},{6,4},{7,13},{8,10},{9,3},{1... | collective-permute-start | bytes 589832 | tf_op jit(solution)/shard_map/ppermute | solution.py:375
  98.7 11.7 %shard_map.66 = bf16[16,2,128,128]{3,2,1,0:T(8,128)(2,1)} custom-call(s32[33]{0:T(128)S(1)} %concatenate.6.refs_0_, s32[16,3]{1,0:T(8,128)S(1)} %copy.9.refs_1_, bf16[1,2,3,128,128]{4,3,2,1,0:T(8,128)(2,1)} %copy-done.24, bf16[1,2,3,128,128]{4,3,2,1,0:T(8,128)(2,1)} %copy-done.28, bf16[1,2,3,128,128]{4,3,2,1,0:T(8,128)(2,1)} %copy-done.30, ...), custom_call_target="tpu_custom_call" | custom-call | flops 12884901888 | bytes 8388608 | tf_op jit(solution)/shard_map/pallas_call | solution.py:167
  110.5 0.6 collective-permute-start.24
  111.5 3.6 %collective-permute-start.29 = (bf16[1,2,3,128,128]{4,3,2,1,0:T(8,128)(2,1)S(1)}, bf16[1,2,3,128,128]{4,3,2,1,0:T(8,128)(2,1)S(1)}, u32[]{:S(2)}, u32[]{:S(2)}) collective-permute-start(bf16[1,2,3,128,128]{4,3,2,1,0:T(8,128)(2,1)S(1)} %copy-done.34), channel_id=1, source_target_pairs={{0,12},{1,5},{2,14},{3,7},{4,8},{5,1},{6,10},{7,3},{8,4},{9,13},{1... | collective-permute-start | bytes 589832 | tf_op jit(solution)/shard_map/ppermute | solution.py:375
  115.1 1.0 collective-permute-start.27
  116.5 2.9 %collective-permute-done.24.refs_6_ = bf16[1,2,3,128,128]{4,3,2,1,0:T(8,128)(2,1)S(1)} collective-permute-done((bf16[1,2,3,128,128]{4,3,2,1,0:T(8,128)(2,1)S(1)}, bf16[1,2,3,128,128]{4,3,2,1,0:T(8,128)(2,1)S(1)}, u32[]{:S(2)}, u32[]{:S(2)}) %collective-permute-start.24) | collective-permute-done | bytes 196640 | tf_op jit(solution)/shard_map/ppermute | solution.py:375
  119.4 3.0 %collective-permute-start.32 = (bf16[1,2,3,128,128]{4,3,2,1,0:T(8,128)(2,1)S(1)}, bf16[1,2,3,128,128]{4,3,2,1,0:T(8,128)(2,1)S(1)}, u32[]{:S(2)}, u32[]{:S(2)}) collective-permute-start(bf16[1,2,3,128,128]{4,3,2,1,0:T(8,128)(2,1)S(1)} %copy-done.27), channel_id=1, source_target_pairs={{0,14},{1,7},{2,12},{3,5},{4,10},{5,3},{6,8},{7,1},{8,6},{9,15},{1... | collective-permute-start | bytes 589832 | tf_op jit(solution)/shard_map/ppermute | solution.py:375
  122.4 10.2 %collective-permute-done.22.refs_5_ = bf16[1,2,3,128,128]{4,3,2,1,0:T(8,128)(2,1)S(1)} collective-permute-done((bf16[1,2,3,128,128]{4,3,2,1,0:T(8,128)(2,1)S(1)}, bf16[1,2,3,128,128]{4,3,2,1,0:T(8,128)(2,1)S(1)}, u32[]{:S(2)}, u32[]{:S(2)}) %collective-permute-start.22) | collective-permute-done | bytes 196640 | tf_op jit(solution)/shard_map/ppermute | solution.py:375
  132.6 0.5 collective-permute-start.30
  133.2 1.8 collective-permute-start.28
  134.9 4.4 %collective-permute-start.33 = (bf16[1,2,3,128,128]{4,3,2,1,0:T(8,128)(2,1)S(1)}, bf16[1,2,3,128,128]{4,3,2,1,0:T(8,128)(2,1)S(1)}, u32[]{:S(2)}, u32[]{:S(2)}) collective-permute-start(bf16[1,2,3,128,128]{4,3,2,1,0:T(8,128)(2,1)S(1)} %copy-done.21), channel_id=1, source_target_pairs={{0,15},{1,6},{2,13},{3,4},{4,11},{5,2},{6,9},{7,0},{8,7},{9,14},{1... | collective-permute-start | bytes 589832 | tf_op jit(solution)/shard_map/ppermute | solution.py:375
  139.4 7.4 %collective-permute-done.31.refs_15_ = bf16[1,2,3,128,128]{4,3,2,1,0:T(8,128)(2,1)S(1)} collective-permute-done((bf16[1,2,3,128,128]{4,3,2,1,0:T(8,128)(2,1)S(1)}, bf16[1,2,3,128,128]{4,3,2,1,0:T(8,128)(2,1)S(1)}, u32[]{:S(2)}, u32[]{:S(2)}) %collective-permute-start.31) | collective-permute-done | bytes 196640 | tf_op jit(solution)/shard_map/ppermute | solution.py:375
  146.8 4.3 %collective-permute-done.28.refs_8_ = bf16[1,2,3,128,128]{4,3,2,1,0:T(8,128)(2,1)S(1)} collective-permute-done((bf16[1,2,3,128,128]{4,3,2,1,0:T(8,128)(2,1)S(1)}, bf16[1,2,3,128,128]{4,3,2,1,0:T(8,128)(2,1)S(1)}, u32[]{:S(2)}, u32[]{:S(2)}) %collective-permute-start.28) | collective-permute-done | bytes 196640 | tf_op jit(solution)/shard_map/ppermute | solution.py:375
  151.2 0.5 copy-done.60
  151.9 7.2 %all-to-all-start = ((bf16[16,2,128,128]{3,2,1,0:T(8,128)(2,1)}), bf16[16,2,128,128]{3,2,1,0:T(8,128)(2,1)S(1)}, u32[]{:S(2)}, u32[]{:S(2)}) async-start(bf16[16,2,128,128]{3,2,1,0:T(8,128)(2,1)} %shard_map.66), calls=%async_computation | async-start | bytes 2097152 | tf_op jit(solution)/shard_map/all_to_all | solution.py:356
  159.2 10.9 %shard_map.67 = (bf16[1,2,128,128]{3,2,1,0:T(8,128)(2,1)S(1)}, bf16[1,2,128,128]{3,2,1,0:T(8,128)(2,1)S(1)}, bf16[1,2,128,128]{3,2,1,0:T(8,128)(2,1)S(1)}, bf16[...) custom-call(s32[33]{0:T(128)S(1)} %concatenate.6.refs_0_, ...), custom_call_target="tpu_custom_call" | custom-call | flops 12884901888 | bytes 8388608 | tf_op jit(solution)/shard_map/pallas_call | solution.py:167
  170.1 0.7 collective-permute-start.34
  170.8 4.0 %collective-permute-start.35 = (bf16[1,2,128,128]{3,2,1,0:T(8,128)(2,1)S(1)}, bf16[1,2,128,128]{3,2,1,0:T(8,128)(2,1)S(1)}, u32[]{:S(2)}, u32[]{:S(2)}) collective-permute-start(bf16[1,2,128,128]{3,2,1,0:T(8,128)(2,1)S(1)} %get-tuple-element.161), channel_id=1, source_target_pairs={{0,1},{1,8},{2,3},{3,10},{4,5},{5,12},{6,7},{7,14},{8,9},{9,0},{10... | collective-permute-start | bytes 196616 | tf_op jit(solution)/shard_map/ppermute | solution.py:392
  174.8 1.5 collective-permute-start.36
  176.2 2.1 collective-permute-start.38
  178.3 10.4 %collective-permute-start.39 = (bf16[1,2,128,128]{3,2,1,0:T(8,128)(2,1)S(1)}, bf16[1,2,128,128]{3,2,1,0:T(8,128)(2,1)S(1)}, u32[]{:S(2)}, u32[]{:S(2)}) collective-permute-start(bf16[1,2,128,128]{3,2,1,0:T(8,128)(2,1)S(1)} %get-tuple-element.165), channel_id=1, source_target_pairs={{0,5},{1,12},{2,7},{3,14},{4,1},{5,8},{6,3},{7,10},{8,13},{9,4},{1... | collective-permute-start | bytes 196616 | tf_op jit(solution)/shard_map/ppermute | solution.py:392
  188.7 1.8 collective-permute-done.35.refs_1_
  190.6 1.7 collective-permute-start.40
  192.3 0.6 collective-permute-done.37.refs_3_
  192.9 3.4 %collective-permute-start.42 = (bf16[1,2,128,128]{3,2,1,0:T(8,128)(2,1)S(1)}, bf16[1,2,128,128]{3,2,1,0:T(8,128)(2,1)S(1)}, u32[]{:S(2)}, u32[]{:S(2)}) collective-permute-start(bf16[1,2,128,128]{3,2,1,0:T(8,128)(2,1)S(1)} %get-tuple-element.168), channel_id=1, source_target_pairs={{0,8},{1,1},{2,10},{3,3},{4,12},{5,5},{6,14},{7,7},{8,0},{9,9},{10... | collective-permute-start | bytes 196616 | tf_op jit(solution)/shard_map/ppermute | solution.py:392
  196.4 1.7 collective-permute-start.44
  198.1 1.0 collective-permute-start.45
  199.1 1.4 collective-permute-start.46
  200.5 0.8 collective-permute-done.42.refs_8_
  201.8 2.5 %collective-permute-start.48 = (bf16[1,2,128,128]{3,2,1,0:T(8,128)(2,1)S(1)}, bf16[1,2,128,128]{3,2,1,0:T(8,128)(2,1)S(1)}, u32[]{:S(2)}, u32[]{:S(2)}) collective-permute-start(bf16[1,2,128,128]{3,2,1,0:T(8,128)(2,1)S(1)} %get-tuple-element.174), channel_id=1, source_target_pairs={{0,14},{1,7},{2,12},{3,5},{4,10},{5,3},{6,8},{7,1},{8,6},{9,15},{1... | collective-permute-start | bytes 196616 | tf_op jit(solution)/shard_map/ppermute | solution.py:392
  204.3 1.0 collective-permute-start.49
  205.4 1.0 copy-done
  206.4 2.7 %shard_map.68.refs_16_ = bf16[16,4,128,128]{3,2,1,0:T(8,128)(2,1)} custom-call(s32[17]{0:T(128)S(1)} %stack.107.place, bf16[16,2,128,128]{3,2,1,0:T(8,128)(2,1)} %copy-done), custom_call_target="tpu_custom_call" | custom-call | bytes 2097152 | tf_op jit(solution)/shard_map/pallas_call | solution.py:313
  209.2 1.1 collective-permute-done.49.refs_15_
  210.4 0.6 copy-done.16
  211.0 2.7 %shard_map.69 = bf16[16,4,128,128]{3,2,1,0:T(8,128)(2,1)} custom-call(s32[17]{0:T(128)S(1)} %stack.107.place, bf16[1,2,128,128]{3,2,1,0:T(8,128)(2,1)} %copy-done.1, bf16[1,2,128,128]{3,2,1,0:T(8,128)(2,1)} %copy-done.2, bf16[1,2,128,128]{3,2,1,0:T(8,128)(2,1)} %copy-done.3, bf16[1,2,128,128]{3,2,1,0:T(8,128)(2,1)} %copy-done.4, ...), custom_call_target="tpu_custom_call", output_to_operand_aliasing={{}: (17, {})} | custom-call | bytes 2097152 | tf_op jit(solution)/shard_map/pallas_call | solution.py:313
  (172 shorter events, 3.3 us)
Async XLA Ops:
  0.0 93.2 %collective-permute-start.19 = (bf16[8,1024,128]{2,1,0:T(8,128)(2,1)}, bf16[8,1024,128]{2,1,0:T(8,128)(2,1)S(1)}, u32[]{:S(2)}, u32[]{:S(2)}) collective-permute-start(bf16[8,1024,128]{2,1,0:T(8,128)(2,1)} %refs_18_.3), channel_id=1, source_target_pairs={{0,1},{1,0},{2,3},{3,2},{4,5},{5,4},{6,7},{7,6},{8,9},{9,8},{10,11... | collective-permute-start | bytes 6291464 | tf_op jit(solution)/shard_map/ppermute | solution.py:346
  0.5 98.2 %collective-permute-start.20 = (bf16[8,1024,128]{2,1,0:T(8,128)(2,1)}, bf16[8,1024,128]{2,1,0:T(8,128)(2,1)}, u32[]{:S(2)}, u32[]{:S(2)}) collective-permute-start(bf16[8,1024,128]{2,1,0:T(8,128)(2,1)} %refs_20_.3), channel_id=1, source_target_pairs={{0,1},{1,0},{2,3},{3,2},{4,5},{5,4},{6,7},{7,6},{8,9},{9,8},{10,11... | collective-permute-start | bytes 6291464 | tf_op jit(solution)/shard_map/ppermute | solution.py:346
  4.6 16.7 %collective-permute-start = (bf16[1,2,3,128,128]{4,3,2,1,0:T(8,128)(2,1)}, bf16[1,2,3,128,128]{4,3,2,1,0:T(8,128)(2,1)S(1)}, u32[]{:S(2)}, u32[]{:S(2)}) collective-permute-start(bf16[1,2,3,128,128]{4,3,2,1,0:T(8,128)(2,1)} %get-tuple-element.94), channel_id=1, source_target_pairs={{0,8},{1,1},{2,10},{3,3},{4,12},{5,5},{6,14},{7,7},{8,0},{9,9},{10... | collective-permute-start | bytes 589832 | tf_op jit(solution)/shard_map/ppermute | solution.py:375
  10.5 10.8 %collective-permute-start.4 = (bf16[1,2,3,128,128]{4,3,2,1,0:T(8,128)(2,1)}, bf16[1,2,3,128,128]{4,3,2,1,0:T(8,128)(2,1)S(1)}, u32[]{:S(2)}, u32[]{:S(2)}) collective-permute-start(bf16[1,2,3,128,128]{4,3,2,1,0:T(8,128)(2,1)} %get-tuple-element.101), channel_id=1, source_target_pairs={{0,9},{1,0},{2,11},{3,2},{4,13},{5,4},{6,15},{7,6},{8,1},{9,8},{10... | collective-permute-start | bytes 589832 | tf_op jit(solution)/shard_map/ppermute | solution.py:375
  10.6 12.9 %collective-permute-start.8 = (bf16[1,2,3,128,128]{4,3,2,1,0:T(8,128)(2,1)}, bf16[1,2,3,128,128]{4,3,2,1,0:T(8,128)(2,1)S(1)}, u32[]{:S(2)}, u32[]{:S(2)}) collective-permute-start(bf16[1,2,3,128,128]{4,3,2,1,0:T(8,128)(2,1)} %get-tuple-element.109), channel_id=1, source_target_pairs={{0,0},{1,9},{2,2},{3,11},{4,4},{5,13},{6,6},{7,15},{8,8},{9,1},{10... | collective-permute-start | bytes 589832 | tf_op jit(solution)/shard_map/ppermute | solution.py:375
  21.3 49.3 %copy-start.20 = (bf16[1,2,3,128,128]{4,3,2,1,0:T(8,128)(2,1)}, bf16[1,2,3,128,128]{4,3,2,1,0:T(8,128)(2,1)S(1)}, u32[]{:S(2)}) copy-start(bf16[1,2,3,128,128]{4,3,2,1,0:T(8,128)(2,1)S(1)} %collective-permute-done.refs_10_) | copy-start | bytes 589828
  21.3 6.2 %collective-permute-start.13 = (bf16[1,2,3,128,128]{4,3,2,1,0:T(8,128)(2,1)}, bf16[1,2,3,128,128]{4,3,2,1,0:T(8,128)(2,1)S(1)}, u32[]{:S(2)}, u32[]{:S(2)}) collective-permute-start(bf16[1,2,3,128,128]{4,3,2,1,0:T(8,128)(2,1)} %get-tuple-element.115), channel_id=1, source_target_pairs={{0,1},{1,8},{2,3},{3,10},{4,5},{5,12},{6,7},{7,14},{8,9},{9,0},{10... | collective-permute-start | bytes 589832 | tf_op jit(solution)/shard_map/ppermute | solution.py:375
  21.3 49.3 %copy-start.22 = (bf16[1,2,3,128,128]{4,3,2,1,0:T(8,128)(2,1)}, bf16[1,2,3,128,128]{4,3,2,1,0:T(8,128)(2,1)S(1)}, u32[]{:S(2)}) copy-start(bf16[1,2,3,128,128]{4,3,2,1,0:T(8,128)(2,1)S(1)} %collective-permute-done.4.refs_11_) | copy-start | bytes 589828
  21.3 15.3 %collective-permute-start.14 = (bf16[1,2,3,128,128]{4,3,2,1,0:T(8,128)(2,1)}, bf16[1,2,3,128,128]{4,3,2,1,0:T(8,128)(2,1)S(1)}, u32[]{:S(2)}, u32[]{:S(2)}) collective-permute-start(bf16[1,2,3,128,128]{4,3,2,1,0:T(8,128)(2,1)} %get-tuple-element.116), channel_id=1, source_target_pairs={{0,2},{1,11},{2,0},{3,9},{4,6},{5,15},{6,4},{7,13},{8,10},{9,3},{1... | collective-permute-start | bytes 589832 | tf_op jit(solution)/shard_map/ppermute | solution.py:375
  23.5 47.1 %copy-start.24 = (bf16[1,2,3,128,128]{4,3,2,1,0:T(8,128)(2,1)}, bf16[1,2,3,128,128]{4,3,2,1,0:T(8,128)(2,1)S(1)}, u32[]{:S(2)}) copy-start(bf16[1,2,3,128,128]{4,3,2,1,0:T(8,128)(2,1)S(1)} %collective-permute-done.8.refs_2_) | copy-start | bytes 589828
  23.5 15.1 %collective-permute-start.1 = (bf16[1,2,3,128,128]{4,3,2,1,0:T(8,128)(2,1)}, bf16[1,2,3,128,128]{4,3,2,1,0:T(8,128)(2,1)S(1)}, u32[]{:S(2)}, u32[]{:S(2)}) collective-permute-start(bf16[1,2,3,128,128]{4,3,2,1,0:T(8,128)(2,1)} %get-tuple-element.95), channel_id=1, source_target_pairs={{0,3},{1,10},{2,1},{3,8},{4,7},{5,14},{6,5},{7,12},{8,11},{9,2},{1... | collective-permute-start | bytes 589832 | tf_op jit(solution)/shard_map/ppermute | solution.py:375
  27.5 43.1 %copy-start.28 = (bf16[1,2,3,128,128]{4,3,2,1,0:T(8,128)(2,1)}, bf16[1,2,3,128,128]{4,3,2,1,0:T(8,128)(2,1)S(1)}, u32[]{:S(2)}) copy-start(bf16[1,2,3,128,128]{4,3,2,1,0:T(8,128)(2,1)S(1)} %collective-permute-done.13.refs_3_) | copy-start | bytes 589828
  27.5 13.7 %collective-permute-start.5 = (bf16[1,2,3,128,128]{4,3,2,1,0:T(8,128)(2,1)}, bf16[1,2,3,128,128]{4,3,2,1,0:T(8,128)(2,1)S(1)}, u32[]{:S(2)}, u32[]{:S(2)}) collective-permute-start(bf16[1,2,3,128,128]{4,3,2,1,0:T(8,128)(2,1)} %get-tuple-element.102), channel_id=1, source_target_pairs={{0,4},{1,13},{2,6},{3,15},{4,0},{5,9},{6,2},{7,11},{8,12},{9,5},{1... | collective-permute-start | bytes 589832 | tf_op jit(solution)/shard_map/ppermute | solution.py:375
  36.7 13.8 %collective-permute-start.9 = (bf16[1,2,3,128,128]{4,3,2,1,0:T(8,128)(2,1)}, bf16[1,2,3,128,128]{4,3,2,1,0:T(8,128)(2,1)S(1)}, u32[]{:S(2)}, u32[]{:S(2)}) collective-permute-start(bf16[1,2,3,128,128]{4,3,2,1,0:T(8,128)(2,1)} %get-tuple-element.110), channel_id=1, source_target_pairs={{0,10},{1,3},{2,8},{3,1},{4,14},{5,7},{6,12},{7,5},{8,2},{9,11},{1... | collective-permute-start | bytes 589832 | tf_op jit(solution)/shard_map/ppermute | solution.py:375
  38.7 19.8 %collective-permute-start.15 = (bf16[1,2,3,128,128]{4,3,2,1,0:T(8,128)(2,1)}, bf16[1,2,3,128,128]{4,3,2,1,0:T(8,128)(2,1)S(1)}, u32[]{:S(2)}, u32[]{:S(2)}) collective-permute-start(bf16[1,2,3,128,128]{4,3,2,1,0:T(8,128)(2,1)} %get-tuple-element.119), channel_id=1, source_target_pairs={{0,11},{1,2},{2,9},{3,0},{4,15},{5,6},{6,13},{7,4},{8,3},{9,10},{1... | collective-permute-start | bytes 589832 | tf_op jit(solution)/shard_map/ppermute | solution.py:375
  41.2 17.9 %collective-permute-start.17 = (bf16[1,2,3,128,128]{4,3,2,1,0:T(8,128)(2,1)}, bf16[1,2,3,128,128]{4,3,2,1,0:T(8,128)(2,1)S(1)}, u32[]{:S(2)}, u32[]{:S(2)}) collective-permute-start(bf16[1,2,3,128,128]{4,3,2,1,0:T(8,128)(2,1)} %get-tuple-element.123), channel_id=1, source_target_pairs={{0,12},{1,5},{2,14},{3,7},{4,8},{5,1},{6,10},{7,3},{8,4},{9,13},{1... | collective-permute-start | bytes 589832 | tf_op jit(solution)/shard_map/ppermute | solution.py:375
  50.5 14.6 %collective-permute-start.2 = (bf16[1,2,3,128,128]{4,3,2,1,0:T(8,128)(2,1)}, bf16[1,2,3,128,128]{4,3,2,1,0:T(8,128)(2,1)S(1)}, u32[]{:S(2)}, u32[]{:S(2)}) collective-permute-start(bf16[1,2,3,128,128]{4,3,2,1,0:T(8,128)(2,1)} %get-tuple-element.96), channel_id=1, source_target_pairs={{0,13},{1,4},{2,15},{3,6},{4,9},{5,0},{6,11},{7,2},{8,5},{9,12},{1... | collective-permute-start | bytes 589832 | tf_op jit(solution)/shard_map/ppermute | solution.py:375
  58.4 13.0 %collective-permute-start.10 = (bf16[1,2,3,128,128]{4,3,2,1,0:T(8,128)(2,1)}, bf16[1,2,3,128,128]{4,3,2,1,0:T(8,128)(2,1)S(1)}, u32[]{:S(2)}, u32[]{:S(2)}) collective-permute-start(bf16[1,2,3,128,128]{4,3,2,1,0:T(8,128)(2,1)} %get-tuple-element.111), channel_id=1, source_target_pairs={{0,5},{1,12},{2,7},{3,14},{4,1},{5,8},{6,3},{7,10},{8,13},{9,4},{1... | collective-permute-start | bytes 589832 | tf_op jit(solution)/shard_map/ppermute | solution.py:375
  59.1 17.0 %collective-permute-start.6 = (bf16[1,2,3,128,128]{4,3,2,1,0:T(8,128)(2,1)}, bf16[1,2,3,128,128]{4,3,2,1,0:T(8,128)(2,1)S(1)}, u32[]{:S(2)}, u32[]{:S(2)}) collective-permute-start(bf16[1,2,3,128,128]{4,3,2,1,0:T(8,128)(2,1)} %get-tuple-element.103), channel_id=1, source_target_pairs={{0,14},{1,7},{2,12},{3,5},{4,10},{5,3},{6,8},{7,1},{8,6},{9,15},{1... | collective-permute-start | bytes 589832 | tf_op jit(solution)/shard_map/ppermute | solution.py:375
  65.1 14.1 %collective-permute-start.16 = (bf16[1,2,3,128,128]{4,3,2,1,0:T(8,128)(2,1)}, bf16[1,2,3,128,128]{4,3,2,1,0:T(8,128)(2,1)S(1)}, u32[]{:S(2)}, u32[]{:S(2)}) collective-permute-start(bf16[1,2,3,128,128]{4,3,2,1,0:T(8,128)(2,1)} %get-tuple-element.120), channel_id=1, source_target_pairs={{0,6},{1,15},{2,4},{3,13},{4,2},{5,11},{6,0},{7,9},{8,14},{9,7},{1... | collective-permute-start | bytes 589832 | tf_op jit(solution)/shard_map/ppermute | solution.py:375
  71.5 10.1 %collective-permute-start.18 = (bf16[1,2,3,128,128]{4,3,2,1,0:T(8,128)(2,1)S(1)}, bf16[1,2,3,128,128]{4,3,2,1,0:T(8,128)(2,1)S(1)}, u32[]{:S(2)}, u32[]{:S(2)}) collective-permute-start(bf16[1,2,3,128,128]{4,3,2,1,0:T(8,128)(2,1)S(1)} %copy-done.35), channel_id=1, source_target_pairs={{0,7},{1,14},{2,5},{3,12},{4,3},{5,10},{6,1},{7,8},{8,15},{9,6},{1... | collective-permute-start | bytes 589832 | tf_op jit(solution)/shard_map/ppermute | solution.py:375
  76.1 9.8 %collective-permute-start.11 = (bf16[1,2,3,128,128]{4,3,2,1,0:T(8,128)(2,1)S(1)}, bf16[1,2,3,128,128]{4,3,2,1,0:T(8,128)(2,1)}, u32[]{:S(2)}, u32[]{:S(2)}) collective-permute-start(bf16[1,2,3,128,128]{4,3,2,1,0:T(8,128)(2,1)S(1)} %copy-done.32), channel_id=1, source_target_pairs={{0,15},{1,6},{2,13},{3,4},{4,11},{5,2},{6,9},{7,0},{8,7},{9,14},{1... | collective-permute-start | bytes 589832 | tf_op jit(solution)/shard_map/ppermute | solution.py:375
  79.3 9.6 %collective-permute-start.3 = (bf16[1,2,3,128,128]{4,3,2,1,0:T(8,128)(2,1)}, bf16[1,2,3,128,128]{4,3,2,1,0:T(8,128)(2,1)S(1)}, u32[]{:S(2)}, u32[]{:S(2)}) collective-permute-start(bf16[1,2,3,128,128]{4,3,2,1,0:T(8,128)(2,1)} %get-tuple-element.97), channel_id=1, source_target_pairs={{0,0},{1,9},{2,2},{3,11},{4,4},{5,13},{6,6},{7,15},{8,8},{9,1},{10... | collective-permute-start | bytes 589832 | tf_op jit(solution)/shard_map/ppermute | solution.py:375
  81.6 28.9 %collective-permute-start.23 = (bf16[1,2,3,128,128]{4,3,2,1,0:T(8,128)(2,1)}, bf16[1,2,3,128,128]{4,3,2,1,0:T(8,128)(2,1)S(1)}, u32[]{:S(2)}, u32[]{:S(2)}) collective-permute-start(bf16[1,2,3,128,128]{4,3,2,1,0:T(8,128)(2,1)} %get-tuple-element.132), channel_id=1, source_target_pairs={{0,9},{1,0},{2,11},{3,2},{4,13},{5,4},{6,15},{7,6},{8,1},{9,8},{10... | collective-permute-start | bytes 589832 | tf_op jit(solution)/shard_map/ppermute | solution.py:375
  85.9 25.2 %collective-permute-start.21 = (bf16[1,2,3,128,128]{4,3,2,1,0:T(8,128)(2,1)}, bf16[1,2,3,128,128]{4,3,2,1,0:T(8,128)(2,1)S(1)}, u32[]{:S(2)}, u32[]{:S(2)}) collective-permute-start(bf16[1,2,3,128,128]{4,3,2,1,0:T(8,128)(2,1)} %get-tuple-element.127), channel_id=1, source_target_pairs={{0,8},{1,1},{2,10},{3,3},{4,12},{5,5},{6,14},{7,7},{8,0},{9,9},{10... | collective-permute-start | bytes 589832 | tf_op jit(solution)/shard_map/ppermute | solution.py:375
  88.9 26.1 %collective-permute-start.7 = (bf16[1,2,3,128,128]{4,3,2,1,0:T(8,128)(2,1)}, bf16[1,2,3,128,128]{4,3,2,1,0:T(8,128)(2,1)S(1)}, u32[]{:S(2)}, u32[]{:S(2)}) collective-permute-start(bf16[1,2,3,128,128]{4,3,2,1,0:T(8,128)(2,1)} %get-tuple-element.104), channel_id=1, source_target_pairs={{0,1},{1,8},{2,3},{3,10},{4,5},{5,12},{6,7},{7,14},{8,9},{9,0},{10... | collective-permute-start | bytes 589832 | tf_op jit(solution)/shard_map/ppermute | solution.py:375
  93.2 39.4 %copy-start.26 = (bf16[1,2,3,128,128]{4,3,2,1,0:T(8,128)(2,1)S(1)}, bf16[1,2,3,128,128]{4,3,2,1,0:T(8,128)(2,1)}, u32[]{:S(2)}) copy-start(bf16[1,2,3,128,128]{4,3,2,1,0:T(8,128)(2,1)} %get-tuple-element.153) | copy-start | bytes 589828
  93.2 39.4 %copy-start.25 = (bf16[1,2,3,128,128]{4,3,2,1,0:T(8,128)(2,1)S(1)}, bf16[1,2,3,128,128]{4,3,2,1,0:T(8,128)(2,1)}, u32[]{:S(2)}) copy-start(bf16[1,2,3,128,128]{4,3,2,1,0:T(8,128)(2,1)} %get-tuple-element.150) | copy-start | bytes 589828
  93.2 40.0 %copy-start.23 = (bf16[1,2,3,128,128]{4,3,2,1,0:T(8,128)(2,1)S(1)}, bf16[1,2,3,128,128]{4,3,2,1,0:T(8,128)(2,1)}, u32[]{:S(2)}) copy-start(bf16[1,2,3,128,128]{4,3,2,1,0:T(8,128)(2,1)} %get-tuple-element.144) | copy-start | bytes 589828
  93.2 41.8 %copy-start.21 = (bf16[1,2,3,128,128]{4,3,2,1,0:T(8,128)(2,1)S(1)}, bf16[1,2,3,128,128]{4,3,2,1,0:T(8,128)(2,1)}, u32[]{:S(2)}) copy-start(bf16[1,2,3,128,128]{4,3,2,1,0:T(8,128)(2,1)} %get-tuple-element.159) | copy-start | bytes 589828
  93.2 18.3 %collective-permute-start.12 = (bf16[1,2,3,128,128]{4,3,2,1,0:T(8,128)(2,1)}, bf16[1,2,3,128,128]{4,3,2,1,0:T(8,128)(2,1)S(1)}, u32[]{:S(2)}, u32[]{:S(2)}) collective-permute-start(bf16[1,2,3,128,128]{4,3,2,1,0:T(8,128)(2,1)} %get-tuple-element.113), channel_id=1, source_target_pairs={{0,2},{1,11},{2,0},{3,9},{4,6},{5,15},{6,4},{7,13},{8,10},{9,3},{1... | collective-permute-start | bytes 589832 | tf_op jit(solution)/shard_map/ppermute | solution.py:375
  98.7 17.4 %collective-permute-start.25 = (bf16[1,2,3,128,128]{4,3,2,1,0:T(8,128)(2,1)}, bf16[1,2,3,128,128]{4,3,2,1,0:T(8,128)(2,1)S(1)}, u32[]{:S(2)}, u32[]{:S(2)}) collective-permute-start(bf16[1,2,3,128,128]{4,3,2,1,0:T(8,128)(2,1)} %get-tuple-element.137), channel_id=1, source_target_pairs={{0,10},{1,3},{2,8},{3,1},{4,14},{5,7},{6,12},{7,5},{8,2},{9,11},{1... | collective-permute-start | bytes 589832 | tf_op jit(solution)/shard_map/ppermute | solution.py:375
  110.5 40.6 %copy-start.37 = (bf16[1,2,3,128,128]{4,3,2,1,0:T(8,128)(2,1)}, bf16[1,2,3,128,128]{4,3,2,1,0:T(8,128)(2,1)S(1)}, u32[]{:S(2)}) copy-start(bf16[1,2,3,128,128]{4,3,2,1,0:T(8,128)(2,1)S(1)} %collective-permute-done.23.refs_11_) | copy-start | bytes 589828
  110.5 8.9 %collective-permute-start.24 = (bf16[1,2,3,128,128]{4,3,2,1,0:T(8,128)(2,1)S(1)}, bf16[1,2,3,128,128]{4,3,2,1,0:T(8,128)(2,1)S(1)}, u32[]{:S(2)}, u32[]{:S(2)}) collective-permute-start(bf16[1,2,3,128,128]{4,3,2,1,0:T(8,128)(2,1)S(1)} %copy-done.41), channel_id=1, source_target_pairs={{0,4},{1,13},{2,6},{3,15},{4,0},{5,9},{6,2},{7,11},{8,12},{9,5},{1... | collective-permute-start | bytes 589832 | tf_op jit(solution)/shard_map/ppermute | solution.py:375
  111.1 40.0 %copy-start.40 = (bf16[1,2,3,128,128]{4,3,2,1,0:T(8,128)(2,1)}, bf16[1,2,3,128,128]{4,3,2,1,0:T(8,128)(2,1)S(1)}, u32[]{:S(2)}) copy-start(bf16[1,2,3,128,128]{4,3,2,1,0:T(8,128)(2,1)S(1)} %collective-permute-done.21.refs_10_) | copy-start | bytes 589828
  111.1 21.5 %collective-permute-start.22 = (bf16[1,2,3,128,128]{4,3,2,1,0:T(8,128)(2,1)S(1)}, bf16[1,2,3,128,128]{4,3,2,1,0:T(8,128)(2,1)S(1)}, u32[]{:S(2)}, u32[]{:S(2)}) collective-permute-start(bf16[1,2,3,128,128]{4,3,2,1,0:T(8,128)(2,1)S(1)} %copy-done.38), channel_id=1, source_target_pairs={{0,3},{1,10},{2,1},{3,8},{4,7},{5,14},{6,5},{7,12},{8,11},{9,2},{1... | collective-permute-start | bytes 589832 | tf_op jit(solution)/shard_map/ppermute | solution.py:375
  111.5 47.6 %copy-start.45 = (bf16[1,2,3,128,128]{4,3,2,1,0:T(8,128)(2,1)}, bf16[1,2,3,128,128]{4,3,2,1,0:T(8,128)(2,1)S(1)}, u32[]{:S(2)}) copy-start(bf16[1,2,3,128,128]{4,3,2,1,0:T(8,128)(2,1)S(1)} %collective-permute-done.12.refs_4_) | copy-start | bytes 589828
  111.5 21.1 %collective-permute-start.29 = (bf16[1,2,3,128,128]{4,3,2,1,0:T(8,128)(2,1)S(1)}, bf16[1,2,3,128,128]{4,3,2,1,0:T(8,128)(2,1)S(1)}, u32[]{:S(2)}, u32[]{:S(2)}) collective-permute-start(bf16[1,2,3,128,128]{4,3,2,1,0:T(8,128)(2,1)S(1)} %copy-done.34), channel_id=1, source_target_pairs={{0,12},{1,5},{2,14},{3,7},{4,8},{5,1},{6,10},{7,3},{8,4},{9,13},{1... | collective-permute-start | bytes 589832 | tf_op jit(solution)/shard_map/ppermute | solution.py:375
  115.1 18.1 %collective-permute-start.27 = (bf16[1,2,3,128,128]{4,3,2,1,0:T(8,128)(2,1)S(1)}, bf16[1,2,3,128,128]{4,3,2,1,0:T(8,128)(2,1)S(1)}, u32[]{:S(2)}, u32[]{:S(2)}) collective-permute-start(bf16[1,2,3,128,128]{4,3,2,1,0:T(8,128)(2,1)S(1)} %copy-done.31), channel_id=1, source_target_pairs={{0,11},{1,2},{2,9},{3,0},{4,15},{5,6},{6,13},{7,4},{8,3},{9,10},{1... | collective-permute-start | bytes 589832 | tf_op jit(solution)/shard_map/ppermute | solution.py:375
  116.1 43.1 %copy-start.46 = (bf16[1,2,3,128,128]{4,3,2,1,0:T(8,128)(2,1)}, bf16[1,2,3,128,128]{4,3,2,1,0:T(8,128)(2,1)S(1)}, u32[]{:S(2)}) copy-start(bf16[1,2,3,128,128]{4,3,2,1,0:T(8,128)(2,1)S(1)} %collective-permute-done.25.refs_12_) | copy-start | bytes 589828
  116.1 18.9 %collective-permute-start.26 = (bf16[1,2,3,128,128]{4,3,2,1,0:T(8,128)(2,1)S(1)}, bf16[1,2,3,128,128]{4,3,2,1,0:T(8,128)(2,1)S(1)}, u32[]{:S(2)}, u32[]{:S(2)}) collective-permute-start(bf16[1,2,3,128,128]{4,3,2,1,0:T(8,128)(2,1)S(1)} %copy-done.29), channel_id=1, source_target_pairs={{0,5},{1,12},{2,7},{3,14},{4,1},{5,8},{6,3},{7,10},{8,13},{9,4},{1... | collective-permute-start | bytes 589832 | tf_op jit(solution)/shard_map/ppermute | solution.py:375
  119.4 39.8 %copy-start.51 = (bf16[1,2,3,128,128]{4,3,2,1,0:T(8,128)(2,1)}, bf16[1,2,3,128,128]{4,3,2,1,0:T(8,128)(2,1)S(1)}, u32[]{:S(2)}) copy-start(bf16[1,2,3,128,128]{4,3,2,1,0:T(8,128)(2,1)S(1)} %collective-permute-done.24.refs_6_) | copy-start | bytes 589828
  119.4 20.0 %collective-permute-start.32 = (bf16[1,2,3,128,128]{4,3,2,1,0:T(8,128)(2,1)S(1)}, bf16[1,2,3,128,128]{4,3,2,1,0:T(8,128)(2,1)S(1)}, u32[]{:S(2)}, u32[]{:S(2)}) collective-permute-start(bf16[1,2,3,128,128]{4,3,2,1,0:T(8,128)(2,1)S(1)} %copy-done.27), channel_id=1, source_target_pairs={{0,14},{1,7},{2,12},{3,5},{4,10},{5,3},{6,8},{7,1},{8,6},{9,15},{1... | collective-permute-start | bytes 589832 | tf_op jit(solution)/shard_map/ppermute | solution.py:375
  132.6 14.2 %collective-permute-start.31 = (bf16[1,2,3,128,128]{4,3,2,1,0:T(8,128)(2,1)S(1)}, bf16[1,2,3,128,128]{4,3,2,1,0:T(8,128)(2,1)S(1)}, u32[]{:S(2)}, u32[]{:S(2)}) collective-permute-start(bf16[1,2,3,128,128]{4,3,2,1,0:T(8,128)(2,1)S(1)} %copy-done.26), channel_id=1, source_target_pairs={{0,13},{1,4},{2,15},{3,6},{4,9},{5,0},{6,11},{7,2},{8,5},{9,12},{1... | collective-permute-start | bytes 589832 | tf_op jit(solution)/shard_map/ppermute | solution.py:375
  132.6 14.2 %collective-permute-start.30 = (bf16[1,2,3,128,128]{4,3,2,1,0:T(8,128)(2,1)S(1)}, bf16[1,2,3,128,128]{4,3,2,1,0:T(8,128)(2,1)S(1)}, u32[]{:S(2)}, u32[]{:S(2)}) collective-permute-start(bf16[1,2,3,128,128]{4,3,2,1,0:T(8,128)(2,1)S(1)} %copy-done.25), channel_id=1, source_target_pairs={{0,7},{1,14},{2,5},{3,12},{4,3},{5,10},{6,1},{7,8},{8,15},{9,6},{1... | collective-permute-start | bytes 589832 | tf_op jit(solution)/shard_map/ppermute | solution.py:375
  133.2 17.9 %collective-permute-start.28 = (bf16[1,2,3,128,128]{4,3,2,1,0:T(8,128)(2,1)S(1)}, bf16[1,2,3,128,128]{4,3,2,1,0:T(8,128)(2,1)S(1)}, u32[]{:S(2)}, u32[]{:S(2)}) collective-permute-start(bf16[1,2,3,128,128]{4,3,2,1,0:T(8,128)(2,1)S(1)} %copy-done.23), channel_id=1, source_target_pairs={{0,6},{1,15},{2,4},{3,13},{4,2},{5,11},{6,0},{7,9},{8,14},{9,7},{1... | collective-permute-start | bytes 589832 | tf_op jit(solution)/shard_map/ppermute | solution.py:375
  134.9 16.3 %collective-permute-start.33 = (bf16[1,2,3,128,128]{4,3,2,1,0:T(8,128)(2,1)S(1)}, bf16[1,2,3,128,128]{4,3,2,1,0:T(8,128)(2,1)S(1)}, u32[]{:S(2)}, u32[]{:S(2)}) collective-permute-start(bf16[1,2,3,128,128]{4,3,2,1,0:T(8,128)(2,1)S(1)} %copy-done.21), channel_id=1, source_target_pairs={{0,15},{1,6},{2,13},{3,4},{4,11},{5,2},{6,9},{7,0},{8,7},{9,14},{1... | collective-permute-start | bytes 589832 | tf_op jit(solution)/shard_map/ppermute | solution.py:375
  151.9 53.5 %all-to-all-start = ((bf16[16,2,128,128]{3,2,1,0:T(8,128)(2,1)}), bf16[16,2,128,128]{3,2,1,0:T(8,128)(2,1)S(1)}, u32[]{:S(2)}, u32[]{:S(2)}) async-start(bf16[16,2,128,128]{3,2,1,0:T(8,128)(2,1)} %shard_map.66), calls=%async_computation | async-start | bytes 2097152 | tf_op jit(solution)/shard_map/all_to_all | solution.py:356
  170.1 8.2 %collective-permute-start.34 = (bf16[1,2,128,128]{3,2,1,0:T(8,128)(2,1)S(1)}, bf16[1,2,128,128]{3,2,1,0:T(8,128)(2,1)S(1)}, u32[]{:S(2)}, u32[]{:S(2)}) collective-permute-start(bf16[1,2,128,128]{3,2,1,0:T(8,128)(2,1)S(1)} %get-tuple-element.160), channel_id=1, source_target_pairs={{0,0},{1,9},{2,2},{3,11},{4,4},{5,13},{6,6},{7,15},{8,8},{9,1},{10... | collective-permute-start | bytes 196616 | tf_op jit(solution)/shard_map/ppermute | solution.py:392
  170.8 19.8 %collective-permute-start.35 = (bf16[1,2,128,128]{3,2,1,0:T(8,128)(2,1)S(1)}, bf16[1,2,128,128]{3,2,1,0:T(8,128)(2,1)S(1)}, u32[]{:S(2)}, u32[]{:S(2)}) collective-permute-start(bf16[1,2,128,128]{3,2,1,0:T(8,128)(2,1)S(1)} %get-tuple-element.161), channel_id=1, source_target_pairs={{0,1},{1,8},{2,3},{3,10},{4,5},{5,12},{6,7},{7,14},{8,9},{9,0},{10... | collective-permute-start | bytes 196616 | tf_op jit(solution)/shard_map/ppermute | solution.py:392
  174.8 17.5 %collective-permute-start.36 = (bf16[1,2,128,128]{3,2,1,0:T(8,128)(2,1)S(1)}, bf16[1,2,128,128]{3,2,1,0:T(8,128)(2,1)S(1)}, u32[]{:S(2)}, u32[]{:S(2)}) collective-permute-start(bf16[1,2,128,128]{3,2,1,0:T(8,128)(2,1)S(1)} %get-tuple-element.162), channel_id=1, source_target_pairs={{0,2},{1,11},{2,0},{3,9},{4,6},{5,15},{6,4},{7,13},{8,10},{9,3},{1... | collective-permute-start | bytes 196616 | tf_op jit(solution)/shard_map/ppermute | solution.py:392
  176.2 16.7 %collective-permute-start.37 = (bf16[1,2,128,128]{3,2,1,0:T(8,128)(2,1)S(1)}, bf16[1,2,128,128]{3,2,1,0:T(8,128)(2,1)S(1)}, u32[]{:S(2)}, u32[]{:S(2)}) collective-permute-start(bf16[1,2,128,128]{3,2,1,0:T(8,128)(2,1)S(1)} %get-tuple-element.163), channel_id=1, source_target_pairs={{0,3},{1,10},{2,1},{3,8},{4,7},{5,14},{6,5},{7,12},{8,11},{9,2},{1... | collective-permute-start | bytes 196616 | tf_op jit(solution)/shard_map/ppermute | solution.py:392
  176.2 20.1 %collective-permute-start.38 = (bf16[1,2,128,128]{3,2,1,0:T(8,128)(2,1)S(1)}, bf16[1,2,128,128]{3,2,1,0:T(8,128)(2,1)S(1)}, u32[]{:S(2)}, u32[]{:S(2)}) collective-permute-start(bf16[1,2,128,128]{3,2,1,0:T(8,128)(2,1)S(1)} %get-tuple-element.164), channel_id=1, source_target_pairs={{0,4},{1,13},{2,6},{3,15},{4,0},{5,9},{6,2},{7,11},{8,12},{9,5},{1... | collective-permute-start | bytes 196616 | tf_op jit(solution)/shard_map/ppermute | solution.py:392
  178.3 18.1 %collective-permute-start.39 = (bf16[1,2,128,128]{3,2,1,0:T(8,128)(2,1)S(1)}, bf16[1,2,128,128]{3,2,1,0:T(8,128)(2,1)S(1)}, u32[]{:S(2)}, u32[]{:S(2)}) collective-permute-start(bf16[1,2,128,128]{3,2,1,0:T(8,128)(2,1)S(1)} %get-tuple-element.165), channel_id=1, source_target_pairs={{0,5},{1,12},{2,7},{3,14},{4,1},{5,8},{6,3},{7,10},{8,13},{9,4},{1... | collective-permute-start | bytes 196616 | tf_op jit(solution)/shard_map/ppermute | solution.py:392
  190.6 7.5 %collective-permute-start.40 = (bf16[1,2,128,128]{3,2,1,0:T(8,128)(2,1)S(1)}, bf16[1,2,128,128]{3,2,1,0:T(8,128)(2,1)S(1)}, u32[]{:S(2)}, u32[]{:S(2)}) collective-permute-start(bf16[1,2,128,128]{3,2,1,0:T(8,128)(2,1)S(1)} %get-tuple-element.166), channel_id=1, source_target_pairs={{0,6},{1,15},{2,4},{3,13},{4,2},{5,11},{6,0},{7,9},{8,14},{9,7},{1... | collective-permute-start | bytes 196616 | tf_op jit(solution)/shard_map/ppermute | solution.py:392
  192.2 6.9 %collective-permute-start.41 = (bf16[1,2,128,128]{3,2,1,0:T(8,128)(2,1)S(1)}, bf16[1,2,128,128]{3,2,1,0:T(8,128)(2,1)S(1)}, u32[]{:S(2)}, u32[]{:S(2)}) collective-permute-start(bf16[1,2,128,128]{3,2,1,0:T(8,128)(2,1)S(1)} %get-tuple-element.167), channel_id=1, source_target_pairs={{0,7},{1,14},{2,5},{3,12},{4,3},{5,10},{6,1},{7,8},{8,15},{9,6},{1... | collective-permute-start | bytes 196616 | tf_op jit(solution)/shard_map/ppermute | solution.py:392
  192.9 8.5 %collective-permute-start.42 = (bf16[1,2,128,128]{3,2,1,0:T(8,128)(2,1)S(1)}, bf16[1,2,128,128]{3,2,1,0:T(8,128)(2,1)S(1)}, u32[]{:S(2)}, u32[]{:S(2)}) collective-permute-start(bf16[1,2,128,128]{3,2,1,0:T(8,128)(2,1)S(1)} %get-tuple-element.168), channel_id=1, source_target_pairs={{0,8},{1,1},{2,10},{3,3},{4,12},{5,5},{6,14},{7,7},{8,0},{9,9},{10... | collective-permute-start | bytes 196616 | tf_op jit(solution)/shard_map/ppermute | solution.py:392
  196.3 5.5 %collective-permute-start.43 = (bf16[1,2,128,128]{3,2,1,0:T(8,128)(2,1)S(1)}, bf16[1,2,128,128]{3,2,1,0:T(8,128)(2,1)S(1)}, u32[]{:S(2)}, u32[]{:S(2)}) collective-permute-start(bf16[1,2,128,128]{3,2,1,0:T(8,128)(2,1)S(1)} %get-tuple-element.169), channel_id=1, source_target_pairs={{0,9},{1,0},{2,11},{3,2},{4,13},{5,4},{6,15},{7,6},{8,1},{9,8},{10... | collective-permute-start | bytes 196616 | tf_op jit(solution)/shard_map/ppermute | solution.py:392
  196.4 7.9 %collective-permute-start.44 = (bf16[1,2,128,128]{3,2,1,0:T(8,128)(2,1)S(1)}, bf16[1,2,128,128]{3,2,1,0:T(8,128)(2,1)S(1)}, u32[]{:S(2)}, u32[]{:S(2)}) collective-permute-start(bf16[1,2,128,128]{3,2,1,0:T(8,128)(2,1)S(1)} %get-tuple-element.170), channel_id=1, source_target_pairs={{0,10},{1,3},{2,8},{3,1},{4,14},{5,7},{6,12},{7,5},{8,2},{9,11},{1... | collective-permute-start | bytes 196616 | tf_op jit(solution)/shard_map/ppermute | solution.py:392
  198.1 11.0 %collective-permute-start.45 = (bf16[1,2,128,128]{3,2,1,0:T(8,128)(2,1)S(1)}, bf16[1,2,128,128]{3,2,1,0:T(8,128)(2,1)S(1)}, u32[]{:S(2)}, u32[]{:S(2)}) collective-permute-start(bf16[1,2,128,128]{3,2,1,0:T(8,128)(2,1)S(1)} %get-tuple-element.171), channel_id=1, source_target_pairs={{0,11},{1,2},{2,9},{3,0},{4,15},{5,6},{6,13},{7,4},{8,3},{9,10},{1... | collective-permute-start | bytes 196616 | tf_op jit(solution)/shard_map/ppermute | solution.py:392
  199.1 10.0 %collective-permute-start.46 = (bf16[1,2,128,128]{3,2,1,0:T(8,128)(2,1)S(1)}, bf16[1,2,128,128]{3,2,1,0:T(8,128)(2,1)S(1)}, u32[]{:S(2)}, u32[]{:S(2)}) collective-permute-start(bf16[1,2,128,128]{3,2,1,0:T(8,128)(2,1)S(1)} %get-tuple-element.172), channel_id=1, source_target_pairs={{0,12},{1,5},{2,14},{3,7},{4,8},{5,1},{6,10},{7,3},{8,4},{9,13},{1... | collective-permute-start | bytes 196616 | tf_op jit(solution)/shard_map/ppermute | solution.py:392
  201.3 7.8 %collective-permute-start.47 = (bf16[1,2,128,128]{3,2,1,0:T(8,128)(2,1)S(1)}, bf16[1,2,128,128]{3,2,1,0:T(8,128)(2,1)S(1)}, u32[]{:S(2)}, u32[]{:S(2)}) collective-permute-start(bf16[1,2,128,128]{3,2,1,0:T(8,128)(2,1)S(1)} %get-tuple-element.173), channel_id=1, source_target_pairs={{0,13},{1,4},{2,15},{3,6},{4,9},{5,0},{6,11},{7,2},{8,5},{9,12},{1... | collective-permute-start | bytes 196616 | tf_op jit(solution)/shard_map/ppermute | solution.py:392
  201.8 7.4 %collective-permute-start.48 = (bf16[1,2,128,128]{3,2,1,0:T(8,128)(2,1)S(1)}, bf16[1,2,128,128]{3,2,1,0:T(8,128)(2,1)S(1)}, u32[]{:S(2)}, u32[]{:S(2)}) collective-permute-start(bf16[1,2,128,128]{3,2,1,0:T(8,128)(2,1)S(1)} %get-tuple-element.174), channel_id=1, source_target_pairs={{0,14},{1,7},{2,12},{3,5},{4,10},{5,3},{6,8},{7,1},{8,6},{9,15},{1... | collective-permute-start | bytes 196616 | tf_op jit(solution)/shard_map/ppermute | solution.py:392
  204.3 6.0 %collective-permute-start.49 = (bf16[1,2,128,128]{3,2,1,0:T(8,128)(2,1)S(1)}, bf16[1,2,128,128]{3,2,1,0:T(8,128)(2,1)S(1)}, u32[]{:S(2)}, u32[]{:S(2)}) collective-permute-start(bf16[1,2,128,128]{3,2,1,0:T(8,128)(2,1)S(1)} %get-tuple-element.175), channel_id=1, source_target_pairs={{0,15},{1,6},{2,13},{3,4},{4,11},{5,2},{6,9},{7,0},{8,7},{9,14},{1... | collective-permute-start | bytes 196616 | tf_op jit(solution)/shard_map/ppermute | solution.py:392
  (49 other events, 708.1 us)

commit v6 on v5

--- a/solution.py
+++ b/solution.py
@@ -13,7 +13,7 @@
 OWNED = 4
 EARLY = 2
 WINDOW = 5
-GATE = 6
+GATE = 5
 STEPS = (0, 8, 1, 9, 2, 10, 3, 11, 4, 12, 5, 13, 6, 14, 7, 15)
 
 
@@ -286,49 +286,37 @@
     )(place, *[in_hbm(array) for array in arrays])
 
 
-def collect(place, returned, owned, first, into=None):
-    apart = isinstance(returned, list)
-    arrays = returned if apart else [returned]
-    owners = len(arrays) if apart else returned.shape[0]
-    _, count, local_rows, width = arrays[0].shape
-    heads = pl.ds(first, count)
-    arrays = [in_hbm(array) for array in arrays] + ([] if into is None else [into])
-
-    def kernel(place, *refs):
-        sources, (out, stage, arrivals, departures) = refs[:-4], refs[-4:]
-        inward, outward = [], []
+def collect(place, early, late):
+    owners, first, local_rows, width = early.shape
+    count = late[0].shape[1]
+
+    def kernel(place, early, *refs):
+        late, (out, semaphores) = refs[:owners], refs[owners:]
+        copies = []
         for index in range(owners):
-            source = sources[index].at[0] if apart else sources[0].at[index]
-            owner = place[1 + index] if apart else index
-            inward.append(pltpu.make_async_copy(source, stage.at[index], arrivals.at[index]))
-            outward.append(pltpu.make_async_copy(stage.at[index], out.at[owner, heads], departures.at[index]))
-        for copy in inward:
+            target = out.at[index, pl.ds(0, first)]
+            copies.append(pltpu.make_async_copy(early.at[index], target, semaphores.at[0, index]))
+            target = out.at[place[1 + index], pl.ds(first, count)]
+            copies.append(pltpu.make_async_copy(late[index].at[0], target, semaphores.at[1, index]))
+        for copy in copies:
             copy.start()
-        for copy, departure in zip(inward, outward):
+        for copy in copies:
             copy.wait()
-            departure.start()
-        for departure in outward:
-            departure.wait()
-
+
+    shape = (owners, first + count, local_rows, width)
+    arrays = [pltpu.with_memory_space_constraint(array, pltpu.VMEM) for array in [early, *late]]
     return pl.pallas_call(
         kernel,
         grid_spec=pltpu.PrefetchScalarGridSpec(
             num_scalar_prefetch=1,
             grid=(1,),
             in_specs=[pl.BlockSpec(memory_space=pl.ANY)] * len(arrays),
-            out_specs=pl.BlockSpec(memory_space=pl.ANY),
-            scratch_shapes=[
-                pltpu.VMEM((owners, count, local_rows, width), jnp.bfloat16),
-                pltpu.SemaphoreType.DMA((owners,)),
-                pltpu.SemaphoreType.DMA((owners,)),
-            ],
-        ),
-        out_shape=jax.ShapeDtypeStruct((owners, owned, local_rows, width), jnp.bfloat16),
-        input_output_aliases={} if into is None else {len(arrays): 0},
-        compiler_params=pltpu.CompilerParams(vmem_limit_bytes=48 * 1024 * 1024),
-        cost_estimate=pl.CostEstimate(
-            flops=0, bytes_accessed=4 * owners * count * local_rows * width, transcendentals=0
-        ),
+            out_specs=pl.BlockSpec(memory_space=pltpu.HBM),
+            scratch_shapes=[pltpu.SemaphoreType.DMA((2, owners))],
+        ),
+        out_shape=pltpu.HBM(shape, jnp.bfloat16),
+        compiler_params=pltpu.CompilerParams(vmem_limit_bytes=16 * 1024 * 1024),
+        cost_estimate=pl.CostEstimate(flops=0, bytes_accessed=4 * math.prod(shape), transcendentals=0),
     )(place, *arrays)
 
 
@@ -364,14 +352,15 @@
     here = 2 * lax.axis_index("seq") + side
     owner_at = jnp.stack([side] + [here ^ step ^ (8 * side) for step in range(owners)]).astype(jnp.int32)
     source_at = jnp.stack([side] + [here ^ step ^ (8 * (side ^ (step & 1))) for step in range(owners)]).astype(jnp.int32)
-    sent = []
+    sent, started = [], []
 
     def pairs_of(step):
         return [(index, index ^ step ^ (8 * (index & 1))) for index in range(owners)]
 
     def send(message, step):
         if len(sent) >= WINDOW:
-            message = after(message, sent[-WINDOW])
+            message = after(message, sent[-WINDOW], *started[-1:])
+        started.append(message)
         sent.append(lax.ppermute(message, axes, pairs_of(step)))
         return sent[-1]
 
@@ -385,13 +374,11 @@
         late[step] = send(message if index < GATE else after(message, attended), step)
     attended = after(attended, *late)
     taken = exchange(attended)
-    result = collect(source_at, taken, owned, 0)
     parts = attend_pieces(both, rand_blocks, late, caches, owned, EARLY, True)
     returned = [None] * owners
-    for index, step in enumerate(STEPS):
+    for step in STEPS:
         returned[step] = lax.ppermute(parts[step], axes, pairs_of(step))
-    result = collect(source_at, returned, owned, EARLY, result)
-    return result.reshape(heads, local_rows, width)
+    return collect(source_at, taken, returned).reshape(heads, local_rows, width)
 
 
 def solution(mesh):

time: 215 us -> 210 us (0.977)
  waiting for transfers between devices: 50.2 us -> 59.8 us
  starting transfers between devices: 124 us -> 115 us
  Pallas kernels: 36 us -> 32.7 us
    ppermute x32, starting transfers between devices: 84.4 us -> 76.4 us  [send(): sent.append(lax.ppermute(message, axes, pairs_of(step)))]
    ppermute x32, waiting for transfers between devices: 45.8 us -> 51.6 us  [send(): sent.append(lax.ppermute(message, axes, pairs_of(step)))]
    ppermute x16, waiting for transfers between devices: 4.37 us -> 8.19 us  [per_device(): returned[step] = lax.ppermute(parts[step], axes, pairs_of(step))]
    pallas_call x2 -> x1, Pallas kernels: 5.39 us -> 2.11 us  [collect(): pl.pallas_call(kernel, grid_spec=pltpu.PrefetchScalarGridSpec(num_scalar_...]
  transfers between devices with their start and end apart: 51 -> 51, of which waited for: 18 -> 19; matrix products, arithmetic and copies ran while one was open for 0% -> 0% of each run, Pallas kernels for 16% -> 15%
where the time goes in v6:
time: 210 us
  starting transfers between devices  115 us (55%)
  waiting for transfers between devices  59.8 us (28%)
  Pallas kernels  32.7 us (16%)
    ppermute x32, starting transfers between devices, send(): sent.append(lax.ppermute(message, axes, pairs_of(step)))  76.4 us
    ppermute x32, waiting for transfers between devices, send(): sent.append(lax.ppermute(message, axes, pairs_of(step)))  51.6 us
    ppermute x16, starting transfers between devices, per_device(): returned[step] = lax.ppermute(parts[step], axes, pairs_of(step))  31.7 us
    pallas_call x2, Pallas kernels, attend_pieces(): pl.pallas_call(lambda *refs: pieces_kernel(pieces, by_step, *refs), grid_...  22.6 us
    ppermute x16, waiting for transfers between devices, per_device(): returned[step] = lax.ppermute(parts[step], axes, pairs_of(step))  8.19 us
    pallas_call x2, Pallas kernels, pack_each(): pl.pallas_call(kernel, grid_spec=pltpu.PrefetchScalarGridSpec(num_scalar_...  7.9 us
    all_to_all x1, starting transfers between devices, exchange(): return lax.all_to_all(value, axes, split_axis=0, concat_axis=0, tiled=True)  6.79 us
  transfers between devices with their start and end apart: 51, of which 19 were waited for; matrix products, arithmetic and copies ran while one was open for 0% of the time, Pallas kernels for 15%

profile of v6, /device:TPU:0, one launch (start us, length us, event | category | flops | bytes accessed | tf_op | source)
XLA Modules:
  0.0 209.7 jit_solution(1244550709077297998)
XLA Ops:
  0.0 0.5 collective-permute-start.16
  0.6 4.0 %shard_map.64 = (bf16[1,2,3,128,128]{4,3,2,1,0:T(8,128)(2,1)}, bf16[1,2,3,128,128]{4,3,2,1,0:T(8,128)(2,1)}, bf16[1,2,3,128,128]{4,3,2,1,0:T(8,128)(2,1)}, bf16[...) custom-call(s32[17]{0:T(128)S(1)} %stack.116.place, ...), custom_call_target="tpu_custom_call" | custom-call | bytes 6291456 | tf_op jit(solution)/shard_map/pallas_call | solution.py:270
  4.6 1.6 collective-permute-start
  6.2 5.9 %collective-permute-start.3 = (bf16[1,2,3,128,128]{4,3,2,1,0:T(8,128)(2,1)}, bf16[1,2,3,128,128]{4,3,2,1,0:T(8,128)(2,1)S(1)}, u32[]{:S(2)}, u32[]{:S(2)}) collective-permute-start(bf16[1,2,3,128,128]{4,3,2,1,0:T(8,128)(2,1)} %get-tuple-element.96), channel_id=1, source_target_pairs={{0,8},{1,1},{2,10},{3,3},{4,12},{5,5},{6,14},{7,7},{8,0},{9,9},{10... | collective-permute-start | bytes 589832 | tf_op jit(solution)/shard_map/ppermute | solution.py:364
  12.2 1.6 collective-permute-start.2
  13.7 9.6 %collective-permute-done.3.refs_10_ = bf16[1,2,3,128,128]{4,3,2,1,0:T(8,128)(2,1)S(1)} collective-permute-done((bf16[1,2,3,128,128]{4,3,2,1,0:T(8,128)(2,1)}, bf16[1,2,3,128,128]{4,3,2,1,0:T(8,128)(2,1)S(1)}, u32[]{:S(2)}, u32[]{:S(2)}) %collective-permute-start.3) | collective-permute-done | bytes 196640 | tf_op jit(solution)/shard_map/ppermute | solution.py:364
  23.3 0.9 collective-permute-start.5
  24.3 0.7 collective-permute-start.4
  24.9 0.9 collective-permute-start.7
  25.8 3.9 %collective-permute-done.5.refs_11_ = bf16[1,2,3,128,128]{4,3,2,1,0:T(8,128)(2,1)S(1)} collective-permute-done((bf16[1,2,3,128,128]{4,3,2,1,0:T(8,128)(2,1)}, bf16[1,2,3,128,128]{4,3,2,1,0:T(8,128)(2,1)S(1)}, u32[]{:S(2)}, u32[]{:S(2)}) %collective-permute-start.5) | collective-permute-done | bytes 196640 | tf_op jit(solution)/shard_map/ppermute | solution.py:364
  29.7 7.1 %collective-permute-start.9 = (bf16[1,2,3,128,128]{4,3,2,1,0:T(8,128)(2,1)}, bf16[1,2,3,128,128]{4,3,2,1,0:T(8,128)(2,1)}, u32[]{:S(2)}, u32[]{:S(2)}) collective-permute-start(bf16[1,2,3,128,128]{4,3,2,1,0:T(8,128)(2,1)} %get-tuple-element.103), channel_id=1, source_target_pairs={{0,11},{1,2},{2,9},{3,0},{4,15},{5,6},{6,13},{7,4},{8,3},{9,10},{1... | collective-permute-start | bytes 589832 | tf_op jit(solution)/shard_map/ppermute | solution.py:364
  36.8 2.9 %collective-permute-done.4.refs_5_ = bf16[1,2,3,128,128]{4,3,2,1,0:T(8,128)(2,1)S(1)} collective-permute-done((bf16[1,2,3,128,128]{4,3,2,1,0:T(8,128)(2,1)}, bf16[1,2,3,128,128]{4,3,2,1,0:T(8,128)(2,1)S(1)}, u32[]{:S(2)}, u32[]{:S(2)}) %collective-permute-start.4) | collective-permute-done | bytes 196640 | tf_op jit(solution)/shard_map/ppermute | solution.py:364
  39.7 2.9 %collective-permute-start.6 = (bf16[1,2,3,128,128]{4,3,2,1,0:T(8,128)(2,1)}, bf16[1,2,3,128,128]{4,3,2,1,0:T(8,128)(2,1)}, u32[]{:S(2)}, u32[]{:S(2)}) collective-permute-start(bf16[1,2,3,128,128]{4,3,2,1,0:T(8,128)(2,1)} %get-tuple-element.104), channel_id=1, source_target_pairs={{0,4},{1,13},{2,6},{3,15},{4,0},{5,9},{6,2},{7,11},{8,12},{9,5},{1... | collective-permute-start | bytes 589832 | tf_op jit(solution)/shard_map/ppermute | solution.py:364
  42.6 7.5 %collective-permute-start.11 = (bf16[1,2,3,128,128]{4,3,2,1,0:T(8,128)(2,1)}, bf16[1,2,3,128,128]{4,3,2,1,0:T(8,128)(2,1)}, u32[]{:S(2)}, u32[]{:S(2)}) collective-permute-start(bf16[1,2,3,128,128]{4,3,2,1,0:T(8,128)(2,1)} %get-tuple-element.107), channel_id=1, source_target_pairs={{0,12},{1,5},{2,14},{3,7},{4,8},{5,1},{6,10},{7,3},{8,4},{9,13},{1... | collective-permute-start | bytes 589832 | tf_op jit(solution)/shard_map/ppermute | solution.py:364
  50.1 0.2 collective-permute-done.6.refs_6_
  50.3 2.0 collective-permute-start.10
  52.3 3.1 %collective-permute-done.11.refs_14_ = bf16[1,2,3,128,128]{4,3,2,1,0:T(8,128)(2,1)} collective-permute-done((bf16[1,2,3,128,128]{4,3,2,1,0:T(8,128)(2,1)}, bf16[1,2,3,128,128]{4,3,2,1,0:T(8,128)(2,1)}, u32[]{:S(2)}, u32[]{:S(2)}) %collective-permute-start.11) | collective-permute-done | bytes 196640 | tf_op jit(solution)/shard_map/ppermute | solution.py:364
  55.4 5.3 %collective-permute-start.13 = (bf16[1,2,3,128,128]{4,3,2,1,0:T(8,128)(2,1)}, bf16[1,2,3,128,128]{4,3,2,1,0:T(8,128)(2,1)}, u32[]{:S(2)}, u32[]{:S(2)}) collective-permute-start(bf16[1,2,3,128,128]{4,3,2,1,0:T(8,128)(2,1)} %get-tuple-element.111), channel_id=1, source_target_pairs={{0,13},{1,4},{2,15},{3,6},{4,9},{5,0},{6,11},{7,2},{8,5},{9,12},{1... | collective-permute-start | bytes 589832 | tf_op jit(solution)/shard_map/ppermute | solution.py:364
  60.7 2.0 collective-permute-start.14
  62.6 3.6 %collective-permute-done.10.refs_8_ = bf16[1,2,3,128,128]{4,3,2,1,0:T(8,128)(2,1)} collective-permute-done((bf16[1,2,3,128,128]{4,3,2,1,0:T(8,128)(2,1)}, bf16[1,2,3,128,128]{4,3,2,1,0:T(8,128)(2,1)}, u32[]{:S(2)}, u32[]{:S(2)}) %collective-permute-start.10) | collective-permute-done | bytes 196640 | tf_op jit(solution)/shard_map/ppermute | solution.py:364
  66.3 0.6 collective-permute-done.13.refs_15_
  66.9 4.4 %collective-permute-start.15 = (bf16[1,2,3,128,128]{4,3,2,1,0:T(8,128)(2,1)}, bf16[1,2,3,128,128]{4,3,2,1,0:T(8,128)(2,1)}, u32[]{:S(2)}, u32[]{:S(2)}) collective-permute-start(bf16[1,2,3,128,128]{4,3,2,1,0:T(8,128)(2,1)} %get-tuple-element.118), channel_id=1, source_target_pairs={{0,15},{1,6},{2,13},{3,4},{4,11},{5,2},{6,9},{7,0},{8,7},{9,14},{1... | collective-permute-start | bytes 589832 | tf_op jit(solution)/shard_map/ppermute | solution.py:364
  71.3 3.9 %shard_map.66 = (bf16[1,2,3,128,128]{4,3,2,1,0:T(8,128)(2,1)}, bf16[1,2,3,128,128]{4,3,2,1,0:T(8,128)(2,1)}, bf16[1,2,3,128,128]{4,3,2,1,0:T(8,128)(2,1)}, bf16[...) custom-call(s32[17]{0:T(128)S(1)} %stack.116.place, ...), custom_call_target="tpu_custom_call" | custom-call | bytes 6291456 | tf_op jit(solution)/shard_map/pallas_call | solution.py:270
  75.4 0.1 concatenate.6.refs_0_
  75.5 1.6 collective-permute-start.18
  77.1 5.3 %collective-permute-start.19 = (bf16[1,2,3,128,128]{4,3,2,1,0:T(8,128)(2,1)}, bf16[1,2,3,128,128]{4,3,2,1,0:T(8,128)(2,1)S(1)}, u32[]{:S(2)}, u32[]{:S(2)}) collective-permute-start(bf16[1,2,3,128,128]{4,3,2,1,0:T(8,128)(2,1)} %get-tuple-element.124), channel_id=1, source_target_pairs={{0,1},{1,8},{2,3},{3,10},{4,5},{5,12},{6,7},{7,14},{8,9},{9,0},{10... | collective-permute-start | bytes 589832 | tf_op jit(solution)/shard_map/ppermute | solution.py:364
  82.4 4.3 %collective-permute-start.21 = (bf16[1,2,3,128,128]{4,3,2,1,0:T(8,128)(2,1)}, bf16[1,2,3,128,128]{4,3,2,1,0:T(8,128)(2,1)S(1)}, u32[]{:S(2)}, u32[]{:S(2)}) collective-permute-start(bf16[1,2,3,128,128]{4,3,2,1,0:T(8,128)(2,1)} %get-tuple-element.123), channel_id=1, source_target_pairs={{0,8},{1,1},{2,10},{3,3},{4,12},{5,5},{6,14},{7,7},{8,0},{9,9},{10... | collective-permute-start | bytes 589832 | tf_op jit(solution)/shard_map/ppermute | solution.py:364
  86.9 1.2 collective-permute-start.20
  88.1 11.7 %shard_map.65 = bf16[16,2,128,128]{3,2,1,0:T(8,128)(2,1)} custom-call(s32[33]{0:T(128)S(1)} %concatenate.6.refs_0_, s32[16,3]{1,0:T(8,128)S(1)} %copy.7.refs_1_, bf16[1,2,3,128,128]{4,3,2,1,0:T(8,128)(2,1)} %copy-done.2, bf16[1,2,3,128,128]{4,3,2,1,0:T(8,128)(2,1)} %copy-done.4, bf16[1,2,3,128,128]{4,3,2,1,0:T(8,128)(2,1)} %copy-done.5, ...), custom_call_target="tpu_custom_call" | custom-call | flops 12884901888 | bytes 8388608 | tf_op jit(solution)/shard_map/pallas_call | solution.py:167
  99.9 2.5 %collective-permute-start.25 = (bf16[1,2,3,128,128]{4,3,2,1,0:T(8,128)(2,1)S(1)}, bf16[1,2,3,128,128]{4,3,2,1,0:T(8,128)(2,1)S(1)}, u32[]{:S(2)}, u32[]{:S(2)}) collective-permute-start(bf16[1,2,3,128,128]{4,3,2,1,0:T(8,128)(2,1)S(1)} %copy-done.27), channel_id=1, source_target_pairs={{0,10},{1,3},{2,8},{3,1},{4,14},{5,7},{6,12},{7,5},{8,2},{9,11},{1... | collective-permute-start | bytes 589832 | tf_op jit(solution)/shard_map/ppermute | solution.py:364
  102.5 3.6 %collective-permute-start.27 = (bf16[1,2,3,128,128]{4,3,2,1,0:T(8,128)(2,1)S(1)}, bf16[1,2,3,128,128]{4,3,2,1,0:T(8,128)(2,1)S(1)}, u32[]{:S(2)}, u32[]{:S(2)}) collective-permute-start(bf16[1,2,3,128,128]{4,3,2,1,0:T(8,128)(2,1)S(1)} %copy-done.23), channel_id=1, source_target_pairs={{0,11},{1,2},{2,9},{3,0},{4,15},{5,6},{6,13},{7,4},{8,3},{9,10},{1... | collective-permute-start | bytes 589832 | tf_op jit(solution)/shard_map/ppermute | solution.py:364
  106.1 1.4 collective-permute-start.24
  107.5 1.2 collective-permute-start.29
  108.7 8.3 %collective-permute-done.25.refs_12_ = bf16[1,2,3,128,128]{4,3,2,1,0:T(8,128)(2,1)S(1)} collective-permute-done((bf16[1,2,3,128,128]{4,3,2,1,0:T(8,128)(2,1)S(1)}, bf16[1,2,3,128,128]{4,3,2,1,0:T(8,128)(2,1)S(1)}, u32[]{:S(2)}, u32[]{:S(2)}) %collective-permute-start.25) | collective-permute-done | bytes 196640 | tf_op jit(solution)/shard_map/ppermute | solution.py:364
  117.1 4.0 %collective-permute-done.22.refs_5_ = bf16[1,2,3,128,128]{4,3,2,1,0:T(8,128)(2,1)S(1)} collective-permute-done((bf16[1,2,3,128,128]{4,3,2,1,0:T(8,128)(2,1)S(1)}, bf16[1,2,3,128,128]{4,3,2,1,0:T(8,128)(2,1)S(1)}, u32[]{:S(2)}, u32[]{:S(2)}) %collective-permute-start.22) | collective-permute-done | bytes 196640 | tf_op jit(solution)/shard_map/ppermute | solution.py:364
  121.2 6.4 %collective-permute-start.28 = (bf16[1,2,3,128,128]{4,3,2,1,0:T(8,128)(2,1)S(1)}, bf16[1,2,3,128,128]{4,3,2,1,0:T(8,128)(2,1)S(1)}, u32[]{:S(2)}, u32[]{:S(2)}) collective-permute-start(bf16[1,2,3,128,128]{4,3,2,1,0:T(8,128)(2,1)S(1)} %copy-done.17), channel_id=1, source_target_pairs={{0,6},{1,15},{2,4},{3,13},{4,2},{5,11},{6,0},{7,9},{8,14},{9,7},{1... | collective-permute-start | bytes 589832 | tf_op jit(solution)/shard_map/ppermute | solution.py:364
  127.7 5.8 %collective-permute-start.30 = (bf16[1,2,3,128,128]{4,3,2,1,0:T(8,128)(2,1)S(1)}, bf16[1,2,3,128,128]{4,3,2,1,0:T(8,128)(2,1)S(1)}, u32[]{:S(2)}, u32[]{:S(2)}) collective-permute-start(bf16[1,2,3,128,128]{4,3,2,1,0:T(8,128)(2,1)S(1)} %copy-done.15), channel_id=1, source_target_pairs={{0,7},{1,14},{2,5},{3,12},{4,3},{5,10},{6,1},{7,8},{8,15},{9,6},{1... | collective-permute-start | bytes 589832 | tf_op jit(solution)/shard_map/ppermute | solution.py:364
  133.6 5.6 %collective-permute-done.28.refs_8_ = bf16[1,2,3,128,128]{4,3,2,1,0:T(8,128)(2,1)S(1)} collective-permute-done((bf16[1,2,3,128,128]{4,3,2,1,0:T(8,128)(2,1)S(1)}, bf16[1,2,3,128,128]{4,3,2,1,0:T(8,128)(2,1)S(1)}, u32[]{:S(2)}, u32[]{:S(2)}) %collective-permute-start.28) | collective-permute-done | bytes 196640 | tf_op jit(solution)/shard_map/ppermute | solution.py:364
  139.3 6.3 %collective-permute-done.30.refs_9_ = bf16[1,2,3,128,128]{4,3,2,1,0:T(8,128)(2,1)S(1)} collective-permute-done((bf16[1,2,3,128,128]{4,3,2,1,0:T(8,128)(2,1)S(1)}, bf16[1,2,3,128,128]{4,3,2,1,0:T(8,128)(2,1)S(1)}, u32[]{:S(2)}, u32[]{:S(2)}) %collective-permute-start.30) | collective-permute-done | bytes 196640 | tf_op jit(solution)/shard_map/ppermute | solution.py:364
  145.6 3.3 %collective-permute-done.33.refs_17_ = bf16[1,2,3,128,128]{4,3,2,1,0:T(8,128)(2,1)S(1)} collective-permute-done((bf16[1,2,3,128,128]{4,3,2,1,0:T(8,128)(2,1)S(1)}, bf16[1,2,3,128,128]{4,3,2,1,0:T(8,128)(2,1)S(1)}, u32[]{:S(2)}, u32[]{:S(2)}) %collective-permute-start.33) | collective-permute-done | bytes 196640 | tf_op jit(solution)/shard_map/ppermute | solution.py:364
  148.9 0.7 copy-done.35
  149.6 6.8 %all-to-all-start = ((bf16[16,2,128,128]{3,2,1,0:T(8,128)(2,1)}), bf16[16,2,128,128]{3,2,1,0:T(8,128)(2,1)S(1)}, u32[]{:S(2)}, u32[]{:S(2)}) async-start(bf16[16,2,128,128]{3,2,1,0:T(8,128)(2,1)} %shard_map.65), calls=%async_computation | async-start | bytes 2097152 | tf_op jit(solution)/shard_map/all_to_all | solution.py:344
  156.5 10.9 %shard_map.67 = (bf16[1,2,128,128]{3,2,1,0:T(8,128)(2,1)S(1)}, bf16[1,2,128,128]{3,2,1,0:T(8,128)(2,1)S(1)}, bf16[1,2,128,128]{3,2,1,0:T(8,128)(2,1)S(1)}, bf16[...) custom-call(s32[33]{0:T(128)S(1)} %concatenate.6.refs_0_, ...), custom_call_target="tpu_custom_call" | custom-call | flops 12884901888 | bytes 8388608 | tf_op jit(solution)/shard_map/pallas_call | solution.py:167
  167.4 0.7 collective-permute-start.34
  168.1 4.0 %collective-permute-start.35 = (bf16[1,2,128,128]{3,2,1,0:T(8,128)(2,1)S(1)}, bf16[1,2,128,128]{3,2,1,0:T(8,128)(2,1)S(1)}, u32[]{:S(2)}, u32[]{:S(2)}) collective-permute-start(bf16[1,2,128,128]{3,2,1,0:T(8,128)(2,1)S(1)} %get-tuple-element.164), channel_id=1, source_target_pairs={{0,1},{1,8},{2,3},{3,10},{4,5},{5,12},{6,7},{7,14},{8,9},{9,0},{10... | collective-permute-start | bytes 196616 | tf_op jit(solution)/shard_map/ppermute | solution.py:380
  172.1 1.5 collective-permute-start.36
  173.5 2.0 collective-permute-start.38
  175.5 10.4 %collective-permute-start.39 = (bf16[1,2,128,128]{3,2,1,0:T(8,128)(2,1)S(1)}, bf16[1,2,128,128]{3,2,1,0:T(8,128)(2,1)S(1)}, u32[]{:S(2)}, u32[]{:S(2)}) collective-permute-start(bf16[1,2,128,128]{3,2,1,0:T(8,128)(2,1)S(1)} %get-tuple-element.168), channel_id=1, source_target_pairs={{0,5},{1,12},{2,7},{3,14},{4,1},{5,8},{6,3},{7,10},{8,13},{9,4},{1... | collective-permute-start | bytes 196616 | tf_op jit(solution)/shard_map/ppermute | solution.py:380
  185.9 2.0 collective-permute-done.35.refs_1_
  187.9 1.7 collective-permute-start.40
  189.5 0.6 collective-permute-done.37.refs_3_
  190.2 3.3 %collective-permute-start.42 = (bf16[1,2,128,128]{3,2,1,0:T(8,128)(2,1)S(1)}, bf16[1,2,128,128]{3,2,1,0:T(8,128)(2,1)S(1)}, u32[]{:S(2)}, u32[]{:S(2)}) collective-permute-start(bf16[1,2,128,128]{3,2,1,0:T(8,128)(2,1)S(1)} %get-tuple-element.171), channel_id=1, source_target_pairs={{0,8},{1,1},{2,10},{3,3},{4,12},{5,5},{6,14},{7,7},{8,0},{9,9},{10... | collective-permute-start | bytes 196616 | tf_op jit(solution)/shard_map/ppermute | solution.py:380
  193.6 1.7 collective-permute-start.44
  195.3 1.1 collective-permute-start.45
  196.4 1.4 collective-permute-start.46
  197.8 0.8 collective-permute-done.42.refs_8_
  198.6 0.3 collective-permute-start.47
  199.0 2.6 %collective-permute-start.48 = (bf16[1,2,128,128]{3,2,1,0:T(8,128)(2,1)S(1)}, bf16[1,2,128,128]{3,2,1,0:T(8,128)(2,1)S(1)}, u32[]{:S(2)}, u32[]{:S(2)}) collective-permute-start(bf16[1,2,128,128]{3,2,1,0:T(8,128)(2,1)S(1)} %get-tuple-element.177), channel_id=1, source_target_pairs={{0,14},{1,7},{2,12},{3,5},{4,10},{5,3},{6,8},{7,1},{8,6},{9,15},{1... | collective-permute-start | bytes 196616 | tf_op jit(solution)/shard_map/ppermute | solution.py:380
  201.6 1.0 collective-permute-start.49
  202.7 0.2 collective-permute-done.46.refs_12_
  202.9 1.3 collective-permute-done.47.refs_13_
  204.3 1.9 collective-permute-done.48.refs_14_
  206.1 1.3 collective-permute-done.49.refs_15_
  207.4 2.1 %shard_map.68 = bf16[16,4,128,128]{3,2,1,0:T(8,128)(2,1)} custom-call(s32[17]{0:T(128)S(1)} %stack.107.place, bf16[16,2,128,128]{3,2,1,0:T(8,128)(2,1)S(1)} %all-to-all-done.early, bf16[1,2,128,128]{3,2,1,0:T(8,128)(2,1)S(1)} %collective-permute-done.34.refs_0_, bf16[1,2,128,128]{3,2,1,0:T(8,128)(2,1)S(1)} %collective-permute-done.35.refs_1_, ...), custom_call_target="tpu_custom_call" | custom-call | bytes 4194304 | tf_op jit(solution)/shard_map/pallas_call | solution.py:308
  (119 shorter events, 0.9 us)
Async XLA Ops:
  0.0 86.8 %collective-permute-start.16 = (bf16[8,1024,128]{2,1,0:T(8,128)(2,1)}, bf16[8,1024,128]{2,1,0:T(8,128)(2,1)S(1)}, u32[]{:S(2)}, u32[]{:S(2)}) collective-permute-start(bf16[8,1024,128]{2,1,0:T(8,128)(2,1)} %refs_18_.3), channel_id=1, source_target_pairs={{0,1},{1,0},{2,3},{3,2},{4,5},{5,4},{6,7},{7,6},{8,9},{9,8},{10,11... | collective-permute-start | bytes 6291464 | tf_op jit(solution)/shard_map/ppermute | solution.py:334
  0.5 86.4 %collective-permute-start.17 = (bf16[8,1024,128]{2,1,0:T(8,128)(2,1)}, bf16[8,1024,128]{2,1,0:T(8,128)(2,1)}, u32[]{:S(2)}, u32[]{:S(2)}) collective-permute-start(bf16[8,1024,128]{2,1,0:T(8,128)(2,1)} %refs_20_.3), channel_id=1, source_target_pairs={{0,1},{1,0},{2,3},{3,2},{4,5},{5,4},{6,7},{7,6},{8,9},{9,8},{10,11... | collective-permute-start | bytes 6291464 | tf_op jit(solution)/shard_map/ppermute | solution.py:334
  4.6 7.6 %collective-permute-start = (bf16[1,2,3,128,128]{4,3,2,1,0:T(8,128)(2,1)}, bf16[1,2,3,128,128]{4,3,2,1,0:T(8,128)(2,1)S(1)}, u32[]{:S(2)}, u32[]{:S(2)}) collective-permute-start(bf16[1,2,3,128,128]{4,3,2,1,0:T(8,128)(2,1)} %get-tuple-element.92), channel_id=1, source_target_pairs={{0,0},{1,9},{2,2},{3,11},{4,4},{5,13},{6,6},{7,15},{8,8},{9,1},{10... | collective-permute-start | bytes 589832 | tf_op jit(solution)/shard_map/ppermute | solution.py:364
  6.2 17.2 %collective-permute-start.3 = (bf16[1,2,3,128,128]{4,3,2,1,0:T(8,128)(2,1)}, bf16[1,2,3,128,128]{4,3,2,1,0:T(8,128)(2,1)S(1)}, u32[]{:S(2)}, u32[]{:S(2)}) collective-permute-start(bf16[1,2,3,128,128]{4,3,2,1,0:T(8,128)(2,1)} %get-tuple-element.96), channel_id=1, source_target_pairs={{0,8},{1,1},{2,10},{3,3},{4,12},{5,5},{6,14},{7,7},{8,0},{9,9},{10... | collective-permute-start | bytes 589832 | tf_op jit(solution)/shard_map/ppermute | solution.py:364
  12.1 12.2 %collective-permute-start.1 = (bf16[1,2,3,128,128]{4,3,2,1,0:T(8,128)(2,1)}, bf16[1,2,3,128,128]{4,3,2,1,0:T(8,128)(2,1)S(1)}, u32[]{:S(2)}, u32[]{:S(2)}) collective-permute-start(bf16[1,2,3,128,128]{4,3,2,1,0:T(8,128)(2,1)} %get-tuple-element.93), channel_id=1, source_target_pairs={{0,1},{1,8},{2,3},{3,10},{4,5},{5,12},{6,7},{7,14},{8,9},{9,0},{10... | collective-permute-start | bytes 589832 | tf_op jit(solution)/shard_map/ppermute | solution.py:364
  12.2 63.1 %copy-start.2 = (bf16[1,2,3,128,128]{4,3,2,1,0:T(8,128)(2,1)}, bf16[1,2,3,128,128]{4,3,2,1,0:T(8,128)(2,1)S(1)}, u32[]{:S(2)}) copy-start(bf16[1,2,3,128,128]{4,3,2,1,0:T(8,128)(2,1)S(1)} %collective-permute-done.refs_2_) | copy-start | bytes 589828
  12.2 12.8 %collective-permute-start.2 = (bf16[1,2,3,128,128]{4,3,2,1,0:T(8,128)(2,1)}, bf16[1,2,3,128,128]{4,3,2,1,0:T(8,128)(2,1)S(1)}, u32[]{:S(2)}, u32[]{:S(2)}) collective-permute-start(bf16[1,2,3,128,128]{4,3,2,1,0:T(8,128)(2,1)} %get-tuple-element.94), channel_id=1, source_target_pairs={{0,2},{1,11},{2,0},{3,9},{4,6},{5,15},{6,4},{7,13},{8,10},{9,3},{1... | collective-permute-start | bytes 589832 | tf_op jit(solution)/shard_map/ppermute | solution.py:364
  23.3 51.9 %copy-start.3 = (bf16[1,2,3,128,128]{4,3,2,1,0:T(8,128)(2,1)}, bf16[1,2,3,128,128]{4,3,2,1,0:T(8,128)(2,1)S(1)}, u32[]{:S(2)}) copy-start(bf16[1,2,3,128,128]{4,3,2,1,0:T(8,128)(2,1)S(1)} %collective-permute-done.3.refs_10_) | copy-start | bytes 589828
  23.3 6.4 %collective-permute-start.5 = (bf16[1,2,3,128,128]{4,3,2,1,0:T(8,128)(2,1)}, bf16[1,2,3,128,128]{4,3,2,1,0:T(8,128)(2,1)S(1)}, u32[]{:S(2)}, u32[]{:S(2)}) collective-permute-start(bf16[1,2,3,128,128]{4,3,2,1,0:T(8,128)(2,1)} %get-tuple-element.101), channel_id=1, source_target_pairs={{0,9},{1,0},{2,11},{3,2},{4,13},{5,4},{6,15},{7,6},{8,1},{9,8},{10... | collective-permute-start | bytes 589832 | tf_op jit(solution)/shard_map/ppermute | solution.py:364
  24.3 51.0 %copy-start.4 = (bf16[1,2,3,128,128]{4,3,2,1,0:T(8,128)(2,1)}, bf16[1,2,3,128,128]{4,3,2,1,0:T(8,128)(2,1)S(1)}, u32[]{:S(2)}) copy-start(bf16[1,2,3,128,128]{4,3,2,1,0:T(8,128)(2,1)S(1)} %collective-permute-done.1.refs_3_) | copy-start | bytes 589828
  24.3 15.4 %collective-permute-start.4 = (bf16[1,2,3,128,128]{4,3,2,1,0:T(8,128)(2,1)}, bf16[1,2,3,128,128]{4,3,2,1,0:T(8,128)(2,1)S(1)}, u32[]{:S(2)}, u32[]{:S(2)}) collective-permute-start(bf16[1,2,3,128,128]{4,3,2,1,0:T(8,128)(2,1)} %get-tuple-element.99), channel_id=1, source_target_pairs={{0,3},{1,10},{2,1},{3,8},{4,7},{5,14},{6,5},{7,12},{8,11},{9,2},{1... | collective-permute-start | bytes 589832 | tf_op jit(solution)/shard_map/ppermute | solution.py:364
  24.9 50.3 %copy-start.5 = (bf16[1,2,3,128,128]{4,3,2,1,0:T(8,128)(2,1)}, bf16[1,2,3,128,128]{4,3,2,1,0:T(8,128)(2,1)S(1)}, u32[]{:S(2)}) copy-start(bf16[1,2,3,128,128]{4,3,2,1,0:T(8,128)(2,1)S(1)} %collective-permute-done.2.refs_4_) | copy-start | bytes 589828
  24.9 17.7 %collective-permute-start.7 = (bf16[1,2,3,128,128]{4,3,2,1,0:T(8,128)(2,1)}, bf16[1,2,3,128,128]{4,3,2,1,0:T(8,128)(2,1)S(1)}, u32[]{:S(2)}, u32[]{:S(2)}) collective-permute-start(bf16[1,2,3,128,128]{4,3,2,1,0:T(8,128)(2,1)} %get-tuple-element.98), channel_id=1, source_target_pairs={{0,10},{1,3},{2,8},{3,1},{4,14},{5,7},{6,12},{7,5},{8,2},{9,11},{1... | collective-permute-start | bytes 589832 | tf_op jit(solution)/shard_map/ppermute | solution.py:364
  29.7 45.6 %copy-start.6 = (bf16[1,2,3,128,128]{4,3,2,1,0:T(8,128)(2,1)}, bf16[1,2,3,128,128]{4,3,2,1,0:T(8,128)(2,1)S(1)}, u32[]{:S(2)}) copy-start(bf16[1,2,3,128,128]{4,3,2,1,0:T(8,128)(2,1)S(1)} %collective-permute-done.5.refs_11_) | copy-start | bytes 589828
  29.7 20.4 %collective-permute-start.9 = (bf16[1,2,3,128,128]{4,3,2,1,0:T(8,128)(2,1)}, bf16[1,2,3,128,128]{4,3,2,1,0:T(8,128)(2,1)}, u32[]{:S(2)}, u32[]{:S(2)}) collective-permute-start(bf16[1,2,3,128,128]{4,3,2,1,0:T(8,128)(2,1)} %get-tuple-element.103), channel_id=1, source_target_pairs={{0,11},{1,2},{2,9},{3,0},{4,15},{5,6},{6,13},{7,4},{8,3},{9,10},{1... | collective-permute-start | bytes 589832 | tf_op jit(solution)/shard_map/ppermute | solution.py:364
  39.7 10.6 %collective-permute-start.6 = (bf16[1,2,3,128,128]{4,3,2,1,0:T(8,128)(2,1)}, bf16[1,2,3,128,128]{4,3,2,1,0:T(8,128)(2,1)}, u32[]{:S(2)}, u32[]{:S(2)}) collective-permute-start(bf16[1,2,3,128,128]{4,3,2,1,0:T(8,128)(2,1)} %get-tuple-element.104), channel_id=1, source_target_pairs={{0,4},{1,13},{2,6},{3,15},{4,0},{5,9},{6,2},{7,11},{8,12},{9,5},{1... | collective-permute-start | bytes 589832 | tf_op jit(solution)/shard_map/ppermute | solution.py:364
  42.6 12.8 %collective-permute-start.11 = (bf16[1,2,3,128,128]{4,3,2,1,0:T(8,128)(2,1)}, bf16[1,2,3,128,128]{4,3,2,1,0:T(8,128)(2,1)}, u32[]{:S(2)}, u32[]{:S(2)}) collective-permute-start(bf16[1,2,3,128,128]{4,3,2,1,0:T(8,128)(2,1)} %get-tuple-element.107), channel_id=1, source_target_pairs={{0,12},{1,5},{2,14},{3,7},{4,8},{5,1},{6,10},{7,3},{8,4},{9,13},{1... | collective-permute-start | bytes 589832 | tf_op jit(solution)/shard_map/ppermute | solution.py:364
  50.1 10.6 %collective-permute-start.8 = (bf16[1,2,3,128,128]{4,3,2,1,0:T(8,128)(2,1)}, bf16[1,2,3,128,128]{4,3,2,1,0:T(8,128)(2,1)}, u32[]{:S(2)}, u32[]{:S(2)}) collective-permute-start(bf16[1,2,3,128,128]{4,3,2,1,0:T(8,128)(2,1)} %get-tuple-element.108), channel_id=1, source_target_pairs={{0,5},{1,12},{2,7},{3,14},{4,1},{5,8},{6,3},{7,10},{8,13},{9,4},{1... | collective-permute-start | bytes 589832 | tf_op jit(solution)/shard_map/ppermute | solution.py:364
  50.3 16.0 %collective-permute-start.10 = (bf16[1,2,3,128,128]{4,3,2,1,0:T(8,128)(2,1)}, bf16[1,2,3,128,128]{4,3,2,1,0:T(8,128)(2,1)}, u32[]{:S(2)}, u32[]{:S(2)}) collective-permute-start(bf16[1,2,3,128,128]{4,3,2,1,0:T(8,128)(2,1)} %get-tuple-element.112), channel_id=1, source_target_pairs={{0,6},{1,15},{2,4},{3,13},{4,2},{5,11},{6,0},{7,9},{8,14},{9,7},{1... | collective-permute-start | bytes 589832 | tf_op jit(solution)/shard_map/ppermute | solution.py:364
  55.4 11.5 %collective-permute-start.13 = (bf16[1,2,3,128,128]{4,3,2,1,0:T(8,128)(2,1)}, bf16[1,2,3,128,128]{4,3,2,1,0:T(8,128)(2,1)}, u32[]{:S(2)}, u32[]{:S(2)}) collective-permute-start(bf16[1,2,3,128,128]{4,3,2,1,0:T(8,128)(2,1)} %get-tuple-element.111), channel_id=1, source_target_pairs={{0,13},{1,4},{2,15},{3,6},{4,9},{5,0},{6,11},{7,2},{8,5},{9,12},{1... | collective-permute-start | bytes 589832 | tf_op jit(solution)/shard_map/ppermute | solution.py:364
  60.7 14.9 %collective-permute-start.14 = (bf16[1,2,3,128,128]{4,3,2,1,0:T(8,128)(2,1)}, bf16[1,2,3,128,128]{4,3,2,1,0:T(8,128)(2,1)}, u32[]{:S(2)}, u32[]{:S(2)}) collective-permute-start(bf16[1,2,3,128,128]{4,3,2,1,0:T(8,128)(2,1)} %get-tuple-element.115), channel_id=1, source_target_pairs={{0,14},{1,7},{2,12},{3,5},{4,10},{5,3},{6,8},{7,1},{8,6},{9,15},{1... | collective-permute-start | bytes 589832 | tf_op jit(solution)/shard_map/ppermute | solution.py:364
  66.3 10.8 %collective-permute-start.12 = (bf16[1,2,3,128,128]{4,3,2,1,0:T(8,128)(2,1)}, bf16[1,2,3,128,128]{4,3,2,1,0:T(8,128)(2,1)}, u32[]{:S(2)}, u32[]{:S(2)}) collective-permute-start(bf16[1,2,3,128,128]{4,3,2,1,0:T(8,128)(2,1)} %get-tuple-element.116), channel_id=1, source_target_pairs={{0,7},{1,14},{2,5},{3,12},{4,3},{5,10},{6,1},{7,8},{8,15},{9,6},{1... | collective-permute-start | bytes 589832 | tf_op jit(solution)/shard_map/ppermute | solution.py:364
  66.9 15.5 %collective-permute-start.15 = (bf16[1,2,3,128,128]{4,3,2,1,0:T(8,128)(2,1)}, bf16[1,2,3,128,128]{4,3,2,1,0:T(8,128)(2,1)}, u32[]{:S(2)}, u32[]{:S(2)}) collective-permute-start(bf16[1,2,3,128,128]{4,3,2,1,0:T(8,128)(2,1)} %get-tuple-element.118), channel_id=1, source_target_pairs={{0,15},{1,6},{2,13},{3,4},{4,11},{5,2},{6,9},{7,0},{8,7},{9,14},{1... | collective-permute-start | bytes 589832 | tf_op jit(solution)/shard_map/ppermute | solution.py:364
  75.5 24.3 %collective-permute-start.18 = (bf16[1,2,3,128,128]{4,3,2,1,0:T(8,128)(2,1)}, bf16[1,2,3,128,128]{4,3,2,1,0:T(8,128)(2,1)S(1)}, u32[]{:S(2)}, u32[]{:S(2)}) collective-permute-start(bf16[1,2,3,128,128]{4,3,2,1,0:T(8,128)(2,1)} %get-tuple-element.120), channel_id=1, source_target_pairs={{0,0},{1,9},{2,2},{3,11},{4,4},{5,13},{6,6},{7,15},{8,8},{9,1},{10... | collective-permute-start | bytes 589832 | tf_op jit(solution)/shard_map/ppermute | solution.py:364
  77.1 25.4 %collective-permute-start.19 = (bf16[1,2,3,128,128]{4,3,2,1,0:T(8,128)(2,1)}, bf16[1,2,3,128,128]{4,3,2,1,0:T(8,128)(2,1)S(1)}, u32[]{:S(2)}, u32[]{:S(2)}) collective-permute-start(bf16[1,2,3,128,128]{4,3,2,1,0:T(8,128)(2,1)} %get-tuple-element.124), channel_id=1, source_target_pairs={{0,1},{1,8},{2,3},{3,10},{4,5},{5,12},{6,7},{7,14},{8,9},{9,0},{10... | collective-permute-start | bytes 589832 | tf_op jit(solution)/shard_map/ppermute | solution.py:364
  82.4 20.0 %collective-permute-start.21 = (bf16[1,2,3,128,128]{4,3,2,1,0:T(8,128)(2,1)}, bf16[1,2,3,128,128]{4,3,2,1,0:T(8,128)(2,1)S(1)}, u32[]{:S(2)}, u32[]{:S(2)}) collective-permute-start(bf16[1,2,3,128,128]{4,3,2,1,0:T(8,128)(2,1)} %get-tuple-element.123), channel_id=1, source_target_pairs={{0,8},{1,1},{2,10},{3,3},{4,12},{5,5},{6,14},{7,7},{8,0},{9,9},{10... | collective-permute-start | bytes 589832 | tf_op jit(solution)/shard_map/ppermute | solution.py:364
  86.8 40.9 %copy-start.12 = (bf16[1,2,3,128,128]{4,3,2,1,0:T(8,128)(2,1)S(1)}, bf16[1,2,3,128,128]{4,3,2,1,0:T(8,128)(2,1)}, u32[]{:S(2)}) copy-start(bf16[1,2,3,128,128]{4,3,2,1,0:T(8,128)(2,1)} %get-tuple-element.157) | copy-start | bytes 589828
  86.8 40.9 %copy-start.15 = (bf16[1,2,3,128,128]{4,3,2,1,0:T(8,128)(2,1)S(1)}, bf16[1,2,3,128,128]{4,3,2,1,0:T(8,128)(2,1)}, u32[]{:S(2)}) copy-start(bf16[1,2,3,128,128]{4,3,2,1,0:T(8,128)(2,1)} %get-tuple-element.158) | copy-start | bytes 589828
  86.8 46.8 %copy-start.10 = (bf16[1,2,3,128,128]{4,3,2,1,0:T(8,128)(2,1)S(1)}, bf16[1,2,3,128,128]{4,3,2,1,0:T(8,128)(2,1)}, u32[]{:S(2)}) copy-start(bf16[1,2,3,128,128]{4,3,2,1,0:T(8,128)(2,1)} %get-tuple-element.161) | copy-start | bytes 589828
  86.8 19.2 %collective-permute-start.23 = (bf16[1,2,3,128,128]{4,3,2,1,0:T(8,128)(2,1)}, bf16[1,2,3,128,128]{4,3,2,1,0:T(8,128)(2,1)S(1)}, u32[]{:S(2)}, u32[]{:S(2)}) collective-permute-start(bf16[1,2,3,128,128]{4,3,2,1,0:T(8,128)(2,1)} %get-tuple-element.127), channel_id=1, source_target_pairs={{0,9},{1,0},{2,11},{3,2},{4,13},{5,4},{6,15},{7,6},{8,1},{9,8},{10... | collective-permute-start | bytes 589832 | tf_op jit(solution)/shard_map/ppermute | solution.py:364
  86.9 20.6 %collective-permute-start.20 = (bf16[1,2,3,128,128]{4,3,2,1,0:T(8,128)(2,1)}, bf16[1,2,3,128,128]{4,3,2,1,0:T(8,128)(2,1)S(1)}, u32[]{:S(2)}, u32[]{:S(2)}) collective-permute-start(bf16[1,2,3,128,128]{4,3,2,1,0:T(8,128)(2,1)} %get-tuple-element.128), channel_id=1, source_target_pairs={{0,2},{1,11},{2,0},{3,9},{4,6},{5,15},{6,4},{7,13},{8,10},{9,3},{1... | collective-permute-start | bytes 589832 | tf_op jit(solution)/shard_map/ppermute | solution.py:364
  99.9 56.5 %copy-start.7 = (bf16[1,2,3,128,128]{4,3,2,1,0:T(8,128)(2,1)}, bf16[1,2,3,128,128]{4,3,2,1,0:T(8,128)(2,1)S(1)}, u32[]{:S(2)}) copy-start(bf16[1,2,3,128,128]{4,3,2,1,0:T(8,128)(2,1)S(1)} %collective-permute-done.18.refs_2_) | copy-start | bytes 589828
  99.9 17.2 %collective-permute-start.25 = (bf16[1,2,3,128,128]{4,3,2,1,0:T(8,128)(2,1)S(1)}, bf16[1,2,3,128,128]{4,3,2,1,0:T(8,128)(2,1)S(1)}, u32[]{:S(2)}, u32[]{:S(2)}) collective-permute-start(bf16[1,2,3,128,128]{4,3,2,1,0:T(8,128)(2,1)S(1)} %copy-done.27), channel_id=1, source_target_pairs={{0,10},{1,3},{2,8},{3,1},{4,14},{5,7},{6,12},{7,5},{8,2},{9,11},{1... | collective-permute-start | bytes 589832 | tf_op jit(solution)/shard_map/ppermute | solution.py:364
  102.4 43.1 %copy-start.13 = (bf16[1,2,3,128,128]{4,3,2,1,0:T(8,128)(2,1)}, bf16[1,2,3,128,128]{4,3,2,1,0:T(8,128)(2,1)S(1)}, u32[]{:S(2)}) copy-start(bf16[1,2,3,128,128]{4,3,2,1,0:T(8,128)(2,1)S(1)} %collective-permute-done.21.refs_10_) | copy-start | bytes 589828
  102.4 18.7 %collective-permute-start.22 = (bf16[1,2,3,128,128]{4,3,2,1,0:T(8,128)(2,1)S(1)}, bf16[1,2,3,128,128]{4,3,2,1,0:T(8,128)(2,1)S(1)}, u32[]{:S(2)}, u32[]{:S(2)}) collective-permute-start(bf16[1,2,3,128,128]{4,3,2,1,0:T(8,128)(2,1)S(1)} %copy-done.25), channel_id=1, source_target_pairs={{0,3},{1,10},{2,1},{3,8},{4,7},{5,14},{6,5},{7,12},{8,11},{9,2},{1... | collective-permute-start | bytes 589832 | tf_op jit(solution)/shard_map/ppermute | solution.py:364
  102.5 53.9 %copy-start.9 = (bf16[1,2,3,128,128]{4,3,2,1,0:T(8,128)(2,1)}, bf16[1,2,3,128,128]{4,3,2,1,0:T(8,128)(2,1)S(1)}, u32[]{:S(2)}) copy-start(bf16[1,2,3,128,128]{4,3,2,1,0:T(8,128)(2,1)S(1)} %collective-permute-done.19.refs_3_) | copy-start | bytes 589828
  102.5 18.6 %collective-permute-start.27 = (bf16[1,2,3,128,128]{4,3,2,1,0:T(8,128)(2,1)S(1)}, bf16[1,2,3,128,128]{4,3,2,1,0:T(8,128)(2,1)S(1)}, u32[]{:S(2)}, u32[]{:S(2)}) collective-permute-start(bf16[1,2,3,128,128]{4,3,2,1,0:T(8,128)(2,1)S(1)} %copy-done.23), channel_id=1, source_target_pairs={{0,11},{1,2},{2,9},{3,0},{4,15},{5,6},{6,13},{7,4},{8,3},{9,10},{1... | collective-permute-start | bytes 589832 | tf_op jit(solution)/shard_map/ppermute | solution.py:364
  106.1 39.5 %copy-start.16 = (bf16[1,2,3,128,128]{4,3,2,1,0:T(8,128)(2,1)}, bf16[1,2,3,128,128]{4,3,2,1,0:T(8,128)(2,1)S(1)}, u32[]{:S(2)}) copy-start(bf16[1,2,3,128,128]{4,3,2,1,0:T(8,128)(2,1)S(1)} %collective-permute-done.23.refs_11_) | copy-start | bytes 589828
  106.1 21.5 %collective-permute-start.24 = (bf16[1,2,3,128,128]{4,3,2,1,0:T(8,128)(2,1)S(1)}, bf16[1,2,3,128,128]{4,3,2,1,0:T(8,128)(2,1)S(1)}, u32[]{:S(2)}, u32[]{:S(2)}) collective-permute-start(bf16[1,2,3,128,128]{4,3,2,1,0:T(8,128)(2,1)S(1)} %copy-done.21), channel_id=1, source_target_pairs={{0,4},{1,13},{2,6},{3,15},{4,0},{5,9},{6,2},{7,11},{8,12},{9,5},{1... | collective-permute-start | bytes 589832 | tf_op jit(solution)/shard_map/ppermute | solution.py:364
  107.5 20.2 %collective-permute-start.29 = (bf16[1,2,3,128,128]{4,3,2,1,0:T(8,128)(2,1)S(1)}, bf16[1,2,3,128,128]{4,3,2,1,0:T(8,128)(2,1)S(1)}, u32[]{:S(2)}, u32[]{:S(2)}) collective-permute-start(bf16[1,2,3,128,128]{4,3,2,1,0:T(8,128)(2,1)S(1)} %copy-done.20), channel_id=1, source_target_pairs={{0,12},{1,5},{2,14},{3,7},{4,8},{5,1},{6,10},{7,3},{8,4},{9,13},{1... | collective-permute-start | bytes 589832 | tf_op jit(solution)/shard_map/ppermute | solution.py:364
  117.1 39.3 %copy-start.22 = (bf16[1,2,3,128,128]{4,3,2,1,0:T(8,128)(2,1)}, bf16[1,2,3,128,128]{4,3,2,1,0:T(8,128)(2,1)S(1)}, u32[]{:S(2)}) copy-start(bf16[1,2,3,128,128]{4,3,2,1,0:T(8,128)(2,1)S(1)} %collective-permute-done.25.refs_12_) | copy-start | bytes 589828
  117.1 16.5 %collective-permute-start.26 = (bf16[1,2,3,128,128]{4,3,2,1,0:T(8,128)(2,1)S(1)}, bf16[1,2,3,128,128]{4,3,2,1,0:T(8,128)(2,1)S(1)}, u32[]{:S(2)}, u32[]{:S(2)}) collective-permute-start(bf16[1,2,3,128,128]{4,3,2,1,0:T(8,128)(2,1)S(1)} %copy-done.19), channel_id=1, source_target_pairs={{0,5},{1,12},{2,7},{3,14},{4,1},{5,8},{6,3},{7,10},{8,13},{9,4},{1... | collective-permute-start | bytes 589832 | tf_op jit(solution)/shard_map/ppermute | solution.py:364
  121.1 24.4 %collective-permute-start.31 = (bf16[1,2,3,128,128]{4,3,2,1,0:T(8,128)(2,1)S(1)}, bf16[1,2,3,128,128]{4,3,2,1,0:T(8,128)(2,1)S(1)}, u32[]{:S(2)}, u32[]{:S(2)}) collective-permute-start(bf16[1,2,3,128,128]{4,3,2,1,0:T(8,128)(2,1)S(1)} %copy-done.14), channel_id=1, source_target_pairs={{0,13},{1,4},{2,15},{3,6},{4,9},{5,0},{6,11},{7,2},{8,5},{9,12},{1... | collective-permute-start | bytes 589832 | tf_op jit(solution)/shard_map/ppermute | solution.py:364
  121.2 18.1 %collective-permute-start.28 = (bf16[1,2,3,128,128]{4,3,2,1,0:T(8,128)(2,1)S(1)}, bf16[1,2,3,128,128]{4,3,2,1,0:T(8,128)(2,1)S(1)}, u32[]{:S(2)}, u32[]{:S(2)}) collective-permute-start(bf16[1,2,3,128,128]{4,3,2,1,0:T(8,128)(2,1)S(1)} %copy-done.17), channel_id=1, source_target_pairs={{0,6},{1,15},{2,4},{3,13},{4,2},{5,11},{6,0},{7,9},{8,14},{9,7},{1... | collective-permute-start | bytes 589832 | tf_op jit(solution)/shard_map/ppermute | solution.py:364
  127.6 17.9 %collective-permute-start.32 = (bf16[1,2,3,128,128]{4,3,2,1,0:T(8,128)(2,1)S(1)}, bf16[1,2,3,128,128]{4,3,2,1,0:T(8,128)(2,1)S(1)}, u32[]{:S(2)}, u32[]{:S(2)}) collective-permute-start(bf16[1,2,3,128,128]{4,3,2,1,0:T(8,128)(2,1)S(1)} %copy-done.12), channel_id=1, source_target_pairs={{0,14},{1,7},{2,12},{3,5},{4,10},{5,3},{6,8},{7,1},{8,6},{9,15},{1... | collective-permute-start | bytes 589832 | tf_op jit(solution)/shard_map/ppermute | solution.py:364
  127.7 17.8 %collective-permute-start.30 = (bf16[1,2,3,128,128]{4,3,2,1,0:T(8,128)(2,1)S(1)}, bf16[1,2,3,128,128]{4,3,2,1,0:T(8,128)(2,1)S(1)}, u32[]{:S(2)}, u32[]{:S(2)}) collective-permute-start(bf16[1,2,3,128,128]{4,3,2,1,0:T(8,128)(2,1)S(1)} %copy-done.15), channel_id=1, source_target_pairs={{0,7},{1,14},{2,5},{3,12},{4,3},{5,10},{6,1},{7,8},{8,15},{9,6},{1... | collective-permute-start | bytes 589832 | tf_op jit(solution)/shard_map/ppermute | solution.py:364
  133.6 15.3 %collective-permute-start.33 = (bf16[1,2,3,128,128]{4,3,2,1,0:T(8,128)(2,1)S(1)}, bf16[1,2,3,128,128]{4,3,2,1,0:T(8,128)(2,1)S(1)}, u32[]{:S(2)}, u32[]{:S(2)}) collective-permute-start(bf16[1,2,3,128,128]{4,3,2,1,0:T(8,128)(2,1)S(1)} %copy-done.10), channel_id=1, source_target_pairs={{0,15},{1,6},{2,13},{3,4},{4,11},{5,2},{6,9},{7,0},{8,7},{9,14},{1... | collective-permute-start | bytes 589832 | tf_op jit(solution)/shard_map/ppermute | solution.py:364
  149.6 57.8 %all-to-all-start = ((bf16[16,2,128,128]{3,2,1,0:T(8,128)(2,1)}), bf16[16,2,128,128]{3,2,1,0:T(8,128)(2,1)S(1)}, u32[]{:S(2)}, u32[]{:S(2)}) async-start(bf16[16,2,128,128]{3,2,1,0:T(8,128)(2,1)} %shard_map.65), calls=%async_computation | async-start | bytes 2097152 | tf_op jit(solution)/shard_map/all_to_all | solution.py:344
  167.4 8.1 %collective-permute-start.34 = (bf16[1,2,128,128]{3,2,1,0:T(8,128)(2,1)S(1)}, bf16[1,2,128,128]{3,2,1,0:T(8,128)(2,1)S(1)}, u32[]{:S(2)}, u32[]{:S(2)}) collective-permute-start(bf16[1,2,128,128]{3,2,1,0:T(8,128)(2,1)S(1)} %get-tuple-element.163), channel_id=1, source_target_pairs={{0,0},{1,9},{2,2},{3,11},{4,4},{5,13},{6,6},{7,15},{8,8},{9,1},{10... | collective-permute-start | bytes 196616 | tf_op jit(solution)/shard_map/ppermute | solution.py:380
  168.1 19.8 %collective-permute-start.35 = (bf16[1,2,128,128]{3,2,1,0:T(8,128)(2,1)S(1)}, bf16[1,2,128,128]{3,2,1,0:T(8,128)(2,1)S(1)}, u32[]{:S(2)}, u32[]{:S(2)}) collective-permute-start(bf16[1,2,128,128]{3,2,1,0:T(8,128)(2,1)S(1)} %get-tuple-element.164), channel_id=1, source_target_pairs={{0,1},{1,8},{2,3},{3,10},{4,5},{5,12},{6,7},{7,14},{8,9},{9,0},{10... | collective-permute-start | bytes 196616 | tf_op jit(solution)/shard_map/ppermute | solution.py:380
  172.1 17.5 %collective-permute-start.36 = (bf16[1,2,128,128]{3,2,1,0:T(8,128)(2,1)S(1)}, bf16[1,2,128,128]{3,2,1,0:T(8,128)(2,1)S(1)}, u32[]{:S(2)}, u32[]{:S(2)}) collective-permute-start(bf16[1,2,128,128]{3,2,1,0:T(8,128)(2,1)S(1)} %get-tuple-element.165), channel_id=1, source_target_pairs={{0,2},{1,11},{2,0},{3,9},{4,6},{5,15},{6,4},{7,13},{8,10},{9,3},{1... | collective-permute-start | bytes 196616 | tf_op jit(solution)/shard_map/ppermute | solution.py:380
  173.5 16.6 %collective-permute-start.37 = (bf16[1,2,128,128]{3,2,1,0:T(8,128)(2,1)S(1)}, bf16[1,2,128,128]{3,2,1,0:T(8,128)(2,1)S(1)}, u32[]{:S(2)}, u32[]{:S(2)}) collective-permute-start(bf16[1,2,128,128]{3,2,1,0:T(8,128)(2,1)S(1)} %get-tuple-element.166), channel_id=1, source_target_pairs={{0,3},{1,10},{2,1},{3,8},{4,7},{5,14},{6,5},{7,12},{8,11},{9,2},{1... | collective-permute-start | bytes 196616 | tf_op jit(solution)/shard_map/ppermute | solution.py:380
  173.5 20.0 %collective-permute-start.38 = (bf16[1,2,128,128]{3,2,1,0:T(8,128)(2,1)S(1)}, bf16[1,2,128,128]{3,2,1,0:T(8,128)(2,1)S(1)}, u32[]{:S(2)}, u32[]{:S(2)}) collective-permute-start(bf16[1,2,128,128]{3,2,1,0:T(8,128)(2,1)S(1)} %get-tuple-element.167), channel_id=1, source_target_pairs={{0,4},{1,13},{2,6},{3,15},{4,0},{5,9},{6,2},{7,11},{8,12},{9,5},{1... | collective-permute-start | bytes 196616 | tf_op jit(solution)/shard_map/ppermute | solution.py:380
  175.5 18.1 %collective-permute-start.39 = (bf16[1,2,128,128]{3,2,1,0:T(8,128)(2,1)S(1)}, bf16[1,2,128,128]{3,2,1,0:T(8,128)(2,1)S(1)}, u32[]{:S(2)}, u32[]{:S(2)}) collective-permute-start(bf16[1,2,128,128]{3,2,1,0:T(8,128)(2,1)S(1)} %get-tuple-element.168), channel_id=1, source_target_pairs={{0,5},{1,12},{2,7},{3,14},{4,1},{5,8},{6,3},{7,10},{8,13},{9,4},{1... | collective-permute-start | bytes 196616 | tf_op jit(solution)/shard_map/ppermute | solution.py:380
  187.9 7.4 %collective-permute-start.40 = (bf16[1,2,128,128]{3,2,1,0:T(8,128)(2,1)S(1)}, bf16[1,2,128,128]{3,2,1,0:T(8,128)(2,1)S(1)}, u32[]{:S(2)}, u32[]{:S(2)}) collective-permute-start(bf16[1,2,128,128]{3,2,1,0:T(8,128)(2,1)S(1)} %get-tuple-element.169), channel_id=1, source_target_pairs={{0,6},{1,15},{2,4},{3,13},{4,2},{5,11},{6,0},{7,9},{8,14},{9,7},{1... | collective-permute-start | bytes 196616 | tf_op jit(solution)/shard_map/ppermute | solution.py:380
  189.5 6.8 %collective-permute-start.41 = (bf16[1,2,128,128]{3,2,1,0:T(8,128)(2,1)S(1)}, bf16[1,2,128,128]{3,2,1,0:T(8,128)(2,1)S(1)}, u32[]{:S(2)}, u32[]{:S(2)}) collective-permute-start(bf16[1,2,128,128]{3,2,1,0:T(8,128)(2,1)S(1)} %get-tuple-element.170), channel_id=1, source_target_pairs={{0,7},{1,14},{2,5},{3,12},{4,3},{5,10},{6,1},{7,8},{8,15},{9,6},{1... | collective-permute-start | bytes 196616 | tf_op jit(solution)/shard_map/ppermute | solution.py:380
  190.2 8.5 %collective-permute-start.42 = (bf16[1,2,128,128]{3,2,1,0:T(8,128)(2,1)S(1)}, bf16[1,2,128,128]{3,2,1,0:T(8,128)(2,1)S(1)}, u32[]{:S(2)}, u32[]{:S(2)}) collective-permute-start(bf16[1,2,128,128]{3,2,1,0:T(8,128)(2,1)S(1)} %get-tuple-element.171), channel_id=1, source_target_pairs={{0,8},{1,1},{2,10},{3,3},{4,12},{5,5},{6,14},{7,7},{8,0},{9,9},{10... | collective-permute-start | bytes 196616 | tf_op jit(solution)/shard_map/ppermute | solution.py:380
  193.5 5.4 %collective-permute-start.43 = (bf16[1,2,128,128]{3,2,1,0:T(8,128)(2,1)S(1)}, bf16[1,2,128,128]{3,2,1,0:T(8,128)(2,1)S(1)}, u32[]{:S(2)}, u32[]{:S(2)}) collective-permute-start(bf16[1,2,128,128]{3,2,1,0:T(8,128)(2,1)S(1)} %get-tuple-element.172), channel_id=1, source_target_pairs={{0,9},{1,0},{2,11},{3,2},{4,13},{5,4},{6,15},{7,6},{8,1},{9,8},{10... | collective-permute-start | bytes 196616 | tf_op jit(solution)/shard_map/ppermute | solution.py:380
  193.6 8.0 %collective-permute-start.44 = (bf16[1,2,128,128]{3,2,1,0:T(8,128)(2,1)S(1)}, bf16[1,2,128,128]{3,2,1,0:T(8,128)(2,1)S(1)}, u32[]{:S(2)}, u32[]{:S(2)}) collective-permute-start(bf16[1,2,128,128]{3,2,1,0:T(8,128)(2,1)S(1)} %get-tuple-element.173), channel_id=1, source_target_pairs={{0,10},{1,3},{2,8},{3,1},{4,14},{5,7},{6,12},{7,5},{8,2},{9,11},{1... | collective-permute-start | bytes 196616 | tf_op jit(solution)/shard_map/ppermute | solution.py:380
  195.3 7.4 %collective-permute-start.45 = (bf16[1,2,128,128]{3,2,1,0:T(8,128)(2,1)S(1)}, bf16[1,2,128,128]{3,2,1,0:T(8,128)(2,1)S(1)}, u32[]{:S(2)}, u32[]{:S(2)}) collective-permute-start(bf16[1,2,128,128]{3,2,1,0:T(8,128)(2,1)S(1)} %get-tuple-element.174), channel_id=1, source_target_pairs={{0,11},{1,2},{2,9},{3,0},{4,15},{5,6},{6,13},{7,4},{8,3},{9,10},{1... | collective-permute-start | bytes 196616 | tf_op jit(solution)/shard_map/ppermute | solution.py:380
  196.4 6.5 %collective-permute-start.46 = (bf16[1,2,128,128]{3,2,1,0:T(8,128)(2,1)S(1)}, bf16[1,2,128,128]{3,2,1,0:T(8,128)(2,1)S(1)}, u32[]{:S(2)}, u32[]{:S(2)}) collective-permute-start(bf16[1,2,128,128]{3,2,1,0:T(8,128)(2,1)S(1)} %get-tuple-element.175), channel_id=1, source_target_pairs={{0,12},{1,5},{2,14},{3,7},{4,8},{5,1},{6,10},{7,3},{8,4},{9,13},{1... | collective-permute-start | bytes 196616 | tf_op jit(solution)/shard_map/ppermute | solution.py:380
  198.6 5.6 %collective-permute-start.47 = (bf16[1,2,128,128]{3,2,1,0:T(8,128)(2,1)S(1)}, bf16[1,2,128,128]{3,2,1,0:T(8,128)(2,1)S(1)}, u32[]{:S(2)}, u32[]{:S(2)}) collective-permute-start(bf16[1,2,128,128]{3,2,1,0:T(8,128)(2,1)S(1)} %get-tuple-element.176), channel_id=1, source_target_pairs={{0,13},{1,4},{2,15},{3,6},{4,9},{5,0},{6,11},{7,2},{8,5},{9,12},{1... | collective-permute-start | bytes 196616 | tf_op jit(solution)/shard_map/ppermute | solution.py:380
  199.0 7.2 %collective-permute-start.48 = (bf16[1,2,128,128]{3,2,1,0:T(8,128)(2,1)S(1)}, bf16[1,2,128,128]{3,2,1,0:T(8,128)(2,1)S(1)}, u32[]{:S(2)}, u32[]{:S(2)}) collective-permute-start(bf16[1,2,128,128]{3,2,1,0:T(8,128)(2,1)S(1)} %get-tuple-element.177), channel_id=1, source_target_pairs={{0,14},{1,7},{2,12},{3,5},{4,10},{5,3},{6,8},{7,1},{8,6},{9,15},{1... | collective-permute-start | bytes 196616 | tf_op jit(solution)/shard_map/ppermute | solution.py:380
  201.6 5.9 %collective-permute-start.49 = (bf16[1,2,128,128]{3,2,1,0:T(8,128)(2,1)S(1)}, bf16[1,2,128,128]{3,2,1,0:T(8,128)(2,1)S(1)}, u32[]{:S(2)}, u32[]{:S(2)}) collective-permute-start(bf16[1,2,128,128]{3,2,1,0:T(8,128)(2,1)S(1)} %get-tuple-element.178), channel_id=1, source_target_pairs={{0,15},{1,6},{2,13},{3,4},{4,11},{5,2},{6,9},{7,0},{8,7},{9,14},{1... | collective-permute-start | bytes 196616 | tf_op jit(solution)/shard_map/ppermute | solution.py:380
  (23 other events, 467.1 us)

commit v7 on v6

--- a/solution.py
+++ b/solution.py
@@ -12,8 +12,8 @@
 UNROLL = 16
 OWNED = 4
 EARLY = 2
-WINDOW = 5
-GATE = 5
+WINDOW = 7
+GATE = 6
 STEPS = (0, 8, 1, 9, 2, 10, 3, 11, 4, 12, 5, 13, 6, 14, 7, 15)
 
 

time: 210 us -> 209 us (level)
  waiting for transfers between devices: 59.8 us -> 52.2 us
  starting transfers between devices: 115 us -> 122 us
    ppermute x32, starting transfers between devices: 76.4 us -> 85 us  [send(): sent.append(lax.ppermute(message, axes, pairs_of(step)))]
    ppermute x32, waiting for transfers between devices: 51.6 us -> 43.4 us  [send(): sent.append(lax.ppermute(message, axes, pairs_of(step)))]
where the time goes in v7:
time: 209 us
  starting transfers between devices  122 us (58%)
  waiting for transfers between devices  52.2 us (25%)
  Pallas kernels  32.7 us (16%)
    ppermute x32, starting transfers between devices, send(): sent.append(lax.ppermute(message, axes, pairs_of(step)))  85 us
    ppermute x32, waiting for transfers between devices, send(): sent.append(lax.ppermute(message, axes, pairs_of(step)))  43.4 us
    ppermute x16, starting transfers between devices, per_device(): returned[step] = lax.ppermute(parts[step], axes, pairs_of(step))  31.3 us
    pallas_call x2, Pallas kernels, attend_pieces(): pl.pallas_call(lambda *refs: pieces_kernel(pieces, by_step, *refs), grid_...  22.7 us
    ppermute x16, waiting for transfers between devices, per_device(): returned[step] = lax.ppermute(parts[step], axes, pairs_of(step))  8.76 us
    pallas_call x2, Pallas kernels, pack_each(): pl.pallas_call(kernel, grid_spec=pltpu.PrefetchScalarGridSpec(num_scalar_...  7.9 us
    all_to_all x1, starting transfers between devices, exchange(): return lax.all_to_all(value, axes, split_axis=0, concat_axis=0, tiled=True)  4.83 us
  transfers between devices with their start and end apart: 51, of which 19 were waited for; matrix products, arithmetic and copies ran while one was open for 0% of the time, Pallas kernels for 15%

profile of v7, /device:TPU:0, one launch (start us, length us, event | category | flops | bytes accessed | tf_op | source)
XLA Modules:
  0.0 208.5 jit_solution(11586119156787532007)
XLA Ops:
  0.0 0.5 collective-permute-start.16
  0.6 4.0 %shard_map.64 = (bf16[1,2,3,128,128]{4,3,2,1,0:T(8,128)(2,1)}, bf16[1,2,3,128,128]{4,3,2,1,0:T(8,128)(2,1)}, bf16[1,2,3,128,128]{4,3,2,1,0:T(8,128)(2,1)}, bf16[...) custom-call(s32[17]{0:T(128)S(1)} %stack.116.place, ...), custom_call_target="tpu_custom_call" | custom-call | bytes 6291456 | tf_op jit(solution)/shard_map/pallas_call | solution.py:270
  4.6 1.6 collective-permute-start
  6.2 4.1 %collective-permute-start.1 = (bf16[1,2,3,128,128]{4,3,2,1,0:T(8,128)(2,1)}, bf16[1,2,3,128,128]{4,3,2,1,0:T(8,128)(2,1)S(1)}, u32[]{:S(2)}, u32[]{:S(2)}) collective-permute-start(bf16[1,2,3,128,128]{4,3,2,1,0:T(8,128)(2,1)} %get-tuple-element.90), channel_id=1, source_target_pairs={{0,1},{1,8},{2,3},{3,10},{4,5},{5,12},{6,7},{7,14},{8,9},{9,0},{10... | collective-permute-start | bytes 589832 | tf_op jit(solution)/shard_map/ppermute | solution.py:364
  10.3 2.2 %collective-permute-start.4 = (bf16[1,2,3,128,128]{4,3,2,1,0:T(8,128)(2,1)}, bf16[1,2,3,128,128]{4,3,2,1,0:T(8,128)(2,1)S(1)}, u32[]{:S(2)}, u32[]{:S(2)}) collective-permute-start(bf16[1,2,3,128,128]{4,3,2,1,0:T(8,128)(2,1)} %get-tuple-element.94), channel_id=1, source_target_pairs={{0,8},{1,1},{2,10},{3,3},{4,12},{5,5},{6,14},{7,7},{8,0},{9,9},{10... | collective-permute-start | bytes 589832 | tf_op jit(solution)/shard_map/ppermute | solution.py:364
  12.5 1.6 collective-permute-start.2
  14.1 10.1 %collective-permute-done.1.refs_3_ = bf16[1,2,3,128,128]{4,3,2,1,0:T(8,128)(2,1)S(1)} collective-permute-done((bf16[1,2,3,128,128]{4,3,2,1,0:T(8,128)(2,1)}, bf16[1,2,3,128,128]{4,3,2,1,0:T(8,128)(2,1)S(1)}, u32[]{:S(2)}, u32[]{:S(2)}) %collective-permute-start.1) | collective-permute-done | bytes 196640 | tf_op jit(solution)/shard_map/ppermute | solution.py:364
  24.3 0.3 collective-permute-start.8
  24.6 12.8 %collective-permute-start.3 = (bf16[1,2,3,128,128]{4,3,2,1,0:T(8,128)(2,1)}, bf16[1,2,3,128,128]{4,3,2,1,0:T(8,128)(2,1)S(1)}, u32[]{:S(2)}, u32[]{:S(2)}) collective-permute-start(bf16[1,2,3,128,128]{4,3,2,1,0:T(8,128)(2,1)} %get-tuple-element.92), channel_id=1, source_target_pairs={{0,3},{1,10},{2,1},{3,8},{4,7},{5,14},{6,5},{7,12},{8,11},{9,2},{1... | collective-permute-start | bytes 589832 | tf_op jit(solution)/shard_map/ppermute | solution.py:364
  37.4 0.2 collective-permute-start.5
  37.7 2.5 %collective-permute-done.8.refs_12_ = bf16[1,2,3,128,128]{4,3,2,1,0:T(8,128)(2,1)S(1)} collective-permute-done((bf16[1,2,3,128,128]{4,3,2,1,0:T(8,128)(2,1)}, bf16[1,2,3,128,128]{4,3,2,1,0:T(8,128)(2,1)S(1)}, u32[]{:S(2)}, u32[]{:S(2)}) %collective-permute-start.8) | collective-permute-done | bytes 196640 | tf_op jit(solution)/shard_map/ppermute | solution.py:364
  40.2 1.1 collective-permute-done.3.refs_5_
  41.2 2.4 %collective-permute-start.9 = (bf16[1,2,3,128,128]{4,3,2,1,0:T(8,128)(2,1)}, bf16[1,2,3,128,128]{4,3,2,1,0:T(8,128)(2,1)S(1)}, u32[]{:S(2)}, u32[]{:S(2)}) collective-permute-start(bf16[1,2,3,128,128]{4,3,2,1,0:T(8,128)(2,1)} %get-tuple-element.107), channel_id=1, source_target_pairs={{0,6},{1,15},{2,4},{3,13},{4,2},{5,11},{6,0},{7,9},{8,14},{9,7},{1... | collective-permute-start | bytes 589832 | tf_op jit(solution)/shard_map/ppermute | solution.py:364
  43.7 2.6 %collective-permute-done.5.refs_6_ = bf16[1,2,3,128,128]{4,3,2,1,0:T(8,128)(2,1)S(1)} collective-permute-done((bf16[1,2,3,128,128]{4,3,2,1,0:T(8,128)(2,1)}, bf16[1,2,3,128,128]{4,3,2,1,0:T(8,128)(2,1)S(1)}, u32[]{:S(2)}, u32[]{:S(2)}) %collective-permute-start.5) | collective-permute-done | bytes 196640 | tf_op jit(solution)/shard_map/ppermute | solution.py:364
  46.3 1.7 collective-permute-start.10
  48.0 1.5 collective-permute-done.7.refs_7_
  49.5 4.5 %collective-permute-start.12 = (bf16[1,2,3,128,128]{4,3,2,1,0:T(8,128)(2,1)}, bf16[1,2,3,128,128]{4,3,2,1,0:T(8,128)(2,1)S(1)}, u32[]{:S(2)}, u32[]{:S(2)}) collective-permute-start(bf16[1,2,3,128,128]{4,3,2,1,0:T(8,128)(2,1)} %get-tuple-element.101), channel_id=1, source_target_pairs={{0,12},{1,5},{2,14},{3,7},{4,8},{5,1},{6,10},{7,3},{8,4},{9,13},{1... | collective-permute-start | bytes 589832 | tf_op jit(solution)/shard_map/ppermute | solution.py:364
  54.0 2.4 %collective-permute-start.13 = (bf16[1,2,3,128,128]{4,3,2,1,0:T(8,128)(2,1)}, bf16[1,2,3,128,128]{4,3,2,1,0:T(8,128)(2,1)S(1)}, u32[]{:S(2)}, u32[]{:S(2)}) collective-permute-start(bf16[1,2,3,128,128]{4,3,2,1,0:T(8,128)(2,1)} %get-tuple-element.106), channel_id=1, source_target_pairs={{0,13},{1,4},{2,15},{3,6},{4,9},{5,0},{6,11},{7,2},{8,5},{9,12},{1... | collective-permute-start | bytes 589832 | tf_op jit(solution)/shard_map/ppermute | solution.py:364
  56.5 3.1 %collective-permute-start.14 = (bf16[1,2,3,128,128]{4,3,2,1,0:T(8,128)(2,1)}, bf16[1,2,3,128,128]{4,3,2,1,0:T(8,128)(2,1)}, u32[]{:S(2)}, u32[]{:S(2)}) collective-permute-start(bf16[1,2,3,128,128]{4,3,2,1,0:T(8,128)(2,1)} %get-tuple-element.110), channel_id=1, source_target_pairs={{0,14},{1,7},{2,12},{3,5},{4,10},{5,3},{6,8},{7,1},{8,6},{9,15},{1... | collective-permute-start | bytes 589832 | tf_op jit(solution)/shard_map/ppermute | solution.py:364
  59.6 3.9 %shard_map.66 = (bf16[1,2,3,128,128]{4,3,2,1,0:T(8,128)(2,1)}, bf16[1,2,3,128,128]{4,3,2,1,0:T(8,128)(2,1)}, bf16[1,2,3,128,128]{4,3,2,1,0:T(8,128)(2,1)}, bf16[...) custom-call(s32[17]{0:T(128)S(1)} %stack.116.place, ...), custom_call_target="tpu_custom_call" | custom-call | bytes 6291456 | tf_op jit(solution)/shard_map/pallas_call | solution.py:270
  63.6 3.7 %collective-permute-start.11 = (bf16[1,2,3,128,128]{4,3,2,1,0:T(8,128)(2,1)}, bf16[1,2,3,128,128]{4,3,2,1,0:T(8,128)(2,1)S(1)}, u32[]{:S(2)}, u32[]{:S(2)}) collective-permute-start(bf16[1,2,3,128,128]{4,3,2,1,0:T(8,128)(2,1)} %get-tuple-element.111), channel_id=1, source_target_pairs={{0,7},{1,14},{2,5},{3,12},{4,3},{5,10},{6,1},{7,8},{8,15},{9,6},{1... | collective-permute-start | bytes 589832 | tf_op jit(solution)/shard_map/ppermute | solution.py:364
  67.3 2.6 %collective-permute-start.15 = (bf16[1,2,3,128,128]{4,3,2,1,0:T(8,128)(2,1)S(1)}, bf16[1,2,3,128,128]{4,3,2,1,0:T(8,128)(2,1)S(1)}, u32[]{:S(2)}, u32[]{:S(2)}) collective-permute-start(bf16[1,2,3,128,128]{4,3,2,1,0:T(8,128)(2,1)S(1)} %copy-done.15), channel_id=1, source_target_pairs={{0,15},{1,6},{2,13},{3,4},{4,11},{5,2},{6,9},{7,0},{8,7},{9,14},{1... | collective-permute-start | bytes 589832 | tf_op jit(solution)/shard_map/ppermute | solution.py:364
  69.9 1.1 collective-permute-done.14.refs_16_
  71.0 1.6 collective-permute-start.18
  72.8 0.6 collective-permute-done.11.refs_9_
  73.4 3.8 %collective-permute-start.19 = (bf16[1,2,3,128,128]{4,3,2,1,0:T(8,128)(2,1)}, bf16[1,2,3,128,128]{4,3,2,1,0:T(8,128)(2,1)S(1)}, u32[]{:S(2)}, u32[]{:S(2)}) collective-permute-start(bf16[1,2,3,128,128]{4,3,2,1,0:T(8,128)(2,1)} %get-tuple-element.119), channel_id=1, source_target_pairs={{0,1},{1,8},{2,3},{3,10},{4,5},{5,12},{6,7},{7,14},{8,9},{9,0},{10... | collective-permute-start | bytes 589832 | tf_op jit(solution)/shard_map/ppermute | solution.py:364
  77.3 0.8 collective-permute-done.15.refs_17_
  78.1 1.0 collective-permute-start.20
  79.1 12.1 %collective-permute-start.22 = (bf16[1,2,3,128,128]{4,3,2,1,0:T(8,128)(2,1)}, bf16[1,2,3,128,128]{4,3,2,1,0:T(8,128)(2,1)S(1)}, u32[]{:S(2)}, u32[]{:S(2)}) collective-permute-start(bf16[1,2,3,128,128]{4,3,2,1,0:T(8,128)(2,1)} %get-tuple-element.118), channel_id=1, source_target_pairs={{0,8},{1,1},{2,10},{3,3},{4,12},{5,5},{6,14},{7,7},{8,0},{9,9},{10... | collective-permute-start | bytes 589832 | tf_op jit(solution)/shard_map/ppermute | solution.py:364
  91.3 3.0 %collective-permute-start.26 = (bf16[1,2,3,128,128]{4,3,2,1,0:T(8,128)(2,1)}, bf16[1,2,3,128,128]{4,3,2,1,0:T(8,128)(2,1)S(1)}, u32[]{:S(2)}, u32[]{:S(2)}) collective-permute-start(bf16[1,2,3,128,128]{4,3,2,1,0:T(8,128)(2,1)} %get-tuple-element.127), channel_id=1, source_target_pairs={{0,10},{1,3},{2,8},{3,1},{4,14},{5,7},{6,12},{7,5},{8,2},{9,11},{1... | collective-permute-start | bytes 589832 | tf_op jit(solution)/shard_map/ppermute | solution.py:364
  94.3 11.7 %shard_map.65 = bf16[16,2,128,128]{3,2,1,0:T(8,128)(2,1)} custom-call(s32[33]{0:T(128)S(1)} %concatenate.6.refs_0_, s32[16,3]{1,0:T(8,128)S(1)} %copy.7.refs_1_, bf16[1,2,3,128,128]{4,3,2,1,0:T(8,128)(2,1)} %copy-done.3, bf16[1,2,3,128,128]{4,3,2,1,0:T(8,128)(2,1)} %copy-done.5, bf16[1,2,3,128,128]{4,3,2,1,0:T(8,128)(2,1)} %copy-done.11, ...), custom_call_target="tpu_custom_call" | custom-call | flops 12884901888 | bytes 8388608 | tf_op jit(solution)/shard_map/pallas_call | solution.py:167
  106.3 4.8 %collective-permute-start.28 = (bf16[1,2,3,128,128]{4,3,2,1,0:T(8,128)(2,1)S(1)}, bf16[1,2,3,128,128]{4,3,2,1,0:T(8,128)(2,1)S(1)}, u32[]{:S(2)}, u32[]{:S(2)}) collective-permute-start(bf16[1,2,3,128,128]{4,3,2,1,0:T(8,128)(2,1)S(1)} %copy-done.20), channel_id=1, source_target_pairs={{0,11},{1,2},{2,9},{3,0},{4,15},{5,6},{6,13},{7,4},{8,3},{9,10},{1... | collective-permute-start | bytes 589832 | tf_op jit(solution)/shard_map/ppermute | solution.py:364
  111.2 0.9 collective-permute-start.27
  112.1 8.3 %collective-permute-done.21.refs_5_ = bf16[1,2,3,128,128]{4,3,2,1,0:T(8,128)(2,1)S(1)} collective-permute-done((bf16[1,2,3,128,128]{4,3,2,1,0:T(8,128)(2,1)S(1)}, bf16[1,2,3,128,128]{4,3,2,1,0:T(8,128)(2,1)S(1)}, u32[]{:S(2)}, u32[]{:S(2)}) %collective-permute-start.21) | collective-permute-done | bytes 196640 | tf_op jit(solution)/shard_map/ppermute | solution.py:364
  120.4 3.0 %collective-permute-start.30 = (bf16[1,2,3,128,128]{4,3,2,1,0:T(8,128)(2,1)S(1)}, bf16[1,2,3,128,128]{4,3,2,1,0:T(8,128)(2,1)S(1)}, u32[]{:S(2)}, u32[]{:S(2)}) collective-permute-start(bf16[1,2,3,128,128]{4,3,2,1,0:T(8,128)(2,1)S(1)} %copy-done.10), channel_id=1, source_target_pairs={{0,12},{1,5},{2,14},{3,7},{4,8},{5,1},{6,10},{7,3},{8,4},{9,13},{1... | collective-permute-start | bytes 589832 | tf_op jit(solution)/shard_map/ppermute | solution.py:364
  123.4 4.1 %collective-permute-start.31 = (bf16[1,2,3,128,128]{4,3,2,1,0:T(8,128)(2,1)S(1)}, bf16[1,2,3,128,128]{4,3,2,1,0:T(8,128)(2,1)S(1)}, u32[]{:S(2)}, u32[]{:S(2)}) collective-permute-start(bf16[1,2,3,128,128]{4,3,2,1,0:T(8,128)(2,1)S(1)} %copy-done.9), channel_id=1, source_target_pairs={{0,13},{1,4},{2,15},{3,6},{4,9},{5,0},{6,11},{7,2},{8,5},{9,12},{1... | collective-permute-start | bytes 589832 | tf_op jit(solution)/shard_map/ppermute | solution.py:364
  127.6 1.7 collective-permute-start.32
  129.3 3.4 %collective-permute-done.27.refs_8_ = bf16[1,2,3,128,128]{4,3,2,1,0:T(8,128)(2,1)S(1)} collective-permute-done((bf16[1,2,3,128,128]{4,3,2,1,0:T(8,128)(2,1)S(1)}, bf16[1,2,3,128,128]{4,3,2,1,0:T(8,128)(2,1)S(1)}, u32[]{:S(2)}, u32[]{:S(2)}) %collective-permute-start.27) | collective-permute-done | bytes 196640 | tf_op jit(solution)/shard_map/ppermute | solution.py:364
  132.7 5.3 %collective-permute-start.33 = (bf16[1,2,3,128,128]{4,3,2,1,0:T(8,128)(2,1)S(1)}, bf16[1,2,3,128,128]{4,3,2,1,0:T(8,128)(2,1)S(1)}, u32[]{:S(2)}, u32[]{:S(2)}) collective-permute-start(bf16[1,2,3,128,128]{4,3,2,1,0:T(8,128)(2,1)S(1)} %copy-done.4), channel_id=1, source_target_pairs={{0,15},{1,6},{2,13},{3,4},{4,11},{5,2},{6,9},{7,0},{8,7},{9,14},{1... | collective-permute-start | bytes 589832 | tf_op jit(solution)/shard_map/ppermute | solution.py:364
  138.1 2.9 %collective-permute-done.32.refs_16_ = bf16[1,2,3,128,128]{4,3,2,1,0:T(8,128)(2,1)S(1)} collective-permute-done((bf16[1,2,3,128,128]{4,3,2,1,0:T(8,128)(2,1)S(1)}, bf16[1,2,3,128,128]{4,3,2,1,0:T(8,128)(2,1)S(1)}, u32[]{:S(2)}, u32[]{:S(2)}) %collective-permute-start.32) | collective-permute-done | bytes 196640 | tf_op jit(solution)/shard_map/ppermute | solution.py:364
  141.0 8.5 %collective-permute-done.33.refs_17_ = bf16[1,2,3,128,128]{4,3,2,1,0:T(8,128)(2,1)S(1)} collective-permute-done((bf16[1,2,3,128,128]{4,3,2,1,0:T(8,128)(2,1)S(1)}, bf16[1,2,3,128,128]{4,3,2,1,0:T(8,128)(2,1)S(1)}, u32[]{:S(2)}, u32[]{:S(2)}) %collective-permute-start.33) | collective-permute-done | bytes 196640 | tf_op jit(solution)/shard_map/ppermute | solution.py:364
  149.5 0.6 copy-done.43
  150.2 4.8 %all-to-all-start = ((bf16[16,2,128,128]{3,2,1,0:T(8,128)(2,1)}), bf16[16,2,128,128]{3,2,1,0:T(8,128)(2,1)S(1)}, u32[]{:S(2)}, u32[]{:S(2)}) async-start(bf16[16,2,128,128]{3,2,1,0:T(8,128)(2,1)} %shard_map.65), calls=%async_computation | async-start | bytes 2097152 | tf_op jit(solution)/shard_map/all_to_all | solution.py:344
  155.1 10.9 %shard_map.67 = (bf16[1,2,128,128]{3,2,1,0:T(8,128)(2,1)S(1)}, bf16[1,2,128,128]{3,2,1,0:T(8,128)(2,1)S(1)}, bf16[1,2,128,128]{3,2,1,0:T(8,128)(2,1)S(1)}, bf16[...) custom-call(s32[33]{0:T(128)S(1)} %concatenate.6.refs_0_, ...), custom_call_target="tpu_custom_call" | custom-call | flops 12884901888 | bytes 8388608 | tf_op jit(solution)/shard_map/pallas_call | solution.py:167
  166.0 0.7 collective-permute-start.34
  166.7 4.0 %collective-permute-start.35 = (bf16[1,2,128,128]{3,2,1,0:T(8,128)(2,1)S(1)}, bf16[1,2,128,128]{3,2,1,0:T(8,128)(2,1)S(1)}, u32[]{:S(2)}, u32[]{:S(2)}) collective-permute-start(bf16[1,2,128,128]{3,2,1,0:T(8,128)(2,1)S(1)} %get-tuple-element.158), channel_id=1, source_target_pairs={{0,1},{1,8},{2,3},{3,10},{4,5},{5,12},{6,7},{7,14},{8,9},{9,0},{10... | collective-permute-start | bytes 196616 | tf_op jit(solution)/shard_map/ppermute | solution.py:380
  170.7 1.5 collective-permute-start.36
  172.1 1.5 collective-permute-start.38
  173.6 10.5 %collective-permute-start.39 = (bf16[1,2,128,128]{3,2,1,0:T(8,128)(2,1)S(1)}, bf16[1,2,128,128]{3,2,1,0:T(8,128)(2,1)S(1)}, u32[]{:S(2)}, u32[]{:S(2)}) collective-permute-start(bf16[1,2,128,128]{3,2,1,0:T(8,128)(2,1)S(1)} %get-tuple-element.162), channel_id=1, source_target_pairs={{0,5},{1,12},{2,7},{3,14},{4,1},{5,8},{6,3},{7,10},{8,13},{9,4},{1... | collective-permute-start | bytes 196616 | tf_op jit(solution)/shard_map/ppermute | solution.py:380
  184.1 2.3 %collective-permute-done.35.refs_1_ = bf16[1,2,128,128]{3,2,1,0:T(8,128)(2,1)S(1)} collective-permute-done((bf16[1,2,128,128]{3,2,1,0:T(8,128)(2,1)S(1)}, bf16[1,2,128,128]{3,2,1,0:T(8,128)(2,1)S(1)}, u32[]{:S(2)}, u32[]{:S(2)}) %collective-permute-start.35) | collective-permute-done | bytes 65568 | tf_op jit(solution)/shard_map/ppermute | solution.py:380
  186.5 1.7 collective-permute-start.40
  188.1 0.6 collective-permute-done.37.refs_3_
  188.8 3.3 %collective-permute-start.42 = (bf16[1,2,128,128]{3,2,1,0:T(8,128)(2,1)S(1)}, bf16[1,2,128,128]{3,2,1,0:T(8,128)(2,1)S(1)}, u32[]{:S(2)}, u32[]{:S(2)}) collective-permute-start(bf16[1,2,128,128]{3,2,1,0:T(8,128)(2,1)S(1)} %get-tuple-element.165), channel_id=1, source_target_pairs={{0,8},{1,1},{2,10},{3,3},{4,12},{5,5},{6,14},{7,7},{8,0},{9,9},{10... | collective-permute-start | bytes 196616 | tf_op jit(solution)/shard_map/ppermute | solution.py:380
  192.2 1.7 collective-permute-start.44
  193.9 1.1 collective-permute-start.45
  195.0 1.4 collective-permute-start.46
  196.4 0.8 collective-permute-done.42.refs_8_
  197.3 0.3 collective-permute-start.47
  197.6 2.9 %collective-permute-start.48 = (bf16[1,2,128,128]{3,2,1,0:T(8,128)(2,1)S(1)}, bf16[1,2,128,128]{3,2,1,0:T(8,128)(2,1)S(1)}, u32[]{:S(2)}, u32[]{:S(2)}) collective-permute-start(bf16[1,2,128,128]{3,2,1,0:T(8,128)(2,1)S(1)} %get-tuple-element.171), channel_id=1, source_target_pairs={{0,14},{1,7},{2,12},{3,5},{4,10},{5,3},{6,8},{7,1},{8,6},{9,15},{1... | collective-permute-start | bytes 196616 | tf_op jit(solution)/shard_map/ppermute | solution.py:380
  200.5 0.7 collective-permute-start.49
  201.5 1.3 collective-permute-done.47.refs_13_
  202.9 2.1 %collective-permute-done.48.refs_14_ = bf16[1,2,128,128]{3,2,1,0:T(8,128)(2,1)S(1)} collective-permute-done((bf16[1,2,128,128]{3,2,1,0:T(8,128)(2,1)S(1)}, bf16[1,2,128,128]{3,2,1,0:T(8,128)(2,1)S(1)}, u32[]{:S(2)}, u32[]{:S(2)}) %collective-permute-start.48) | collective-permute-done | bytes 65568 | tf_op jit(solution)/shard_map/ppermute | solution.py:380
  205.0 1.2 collective-permute-done.49.refs_15_
  206.2 2.1 %shard_map.68 = bf16[16,4,128,128]{3,2,1,0:T(8,128)(2,1)} custom-call(s32[17]{0:T(128)S(1)} %stack.107.place, bf16[16,2,128,128]{3,2,1,0:T(8,128)(2,1)S(1)} %all-to-all-done.early, bf16[1,2,128,128]{3,2,1,0:T(8,128)(2,1)S(1)} %collective-permute-done.34.refs_0_, bf16[1,2,128,128]{3,2,1,0:T(8,128)(2,1)S(1)} %collective-permute-done.35.refs_1_, ...), custom_call_target="tpu_custom_call" | custom-call | bytes 4194304 | tf_op jit(solution)/shard_map/pallas_call | solution.py:308
  (135 shorter events, 1.3 us)
Async XLA Ops:
  0.0 91.2 %collective-permute-start.16 = (bf16[8,1024,128]{2,1,0:T(8,128)(2,1)}, bf16[8,1024,128]{2,1,0:T(8,128)(2,1)S(1)}, u32[]{:S(2)}, u32[]{:S(2)}) collective-permute-start(bf16[8,1024,128]{2,1,0:T(8,128)(2,1)} %refs_18_.3), channel_id=1, source_target_pairs={{0,1},{1,0},{2,3},{3,2},{4,5},{5,4},{6,7},{7,6},{8,9},{9,8},{10,11... | collective-permute-start | bytes 6291464 | tf_op jit(solution)/shard_map/ppermute | solution.py:334
  0.5 90.9 %collective-permute-start.17 = (bf16[8,1024,128]{2,1,0:T(8,128)(2,1)}, bf16[8,1024,128]{2,1,0:T(8,128)(2,1)}, u32[]{:S(2)}, u32[]{:S(2)}) collective-permute-start(bf16[8,1024,128]{2,1,0:T(8,128)(2,1)} %refs_20_.3), channel_id=1, source_target_pairs={{0,1},{1,0},{2,3},{3,2},{4,5},{5,4},{6,7},{7,6},{8,9},{9,8},{10,11... | collective-permute-start | bytes 6291464 | tf_op jit(solution)/shard_map/ppermute | solution.py:334
  4.6 7.9 %collective-permute-start = (bf16[1,2,3,128,128]{4,3,2,1,0:T(8,128)(2,1)}, bf16[1,2,3,128,128]{4,3,2,1,0:T(8,128)(2,1)S(1)}, u32[]{:S(2)}, u32[]{:S(2)}) collective-permute-start(bf16[1,2,3,128,128]{4,3,2,1,0:T(8,128)(2,1)} %get-tuple-element.89), channel_id=1, source_target_pairs={{0,0},{1,9},{2,2},{3,11},{4,4},{5,13},{6,6},{7,15},{8,8},{9,1},{10... | collective-permute-start | bytes 589832 | tf_op jit(solution)/shard_map/ppermute | solution.py:364
  6.2 18.1 %collective-permute-start.1 = (bf16[1,2,3,128,128]{4,3,2,1,0:T(8,128)(2,1)}, bf16[1,2,3,128,128]{4,3,2,1,0:T(8,128)(2,1)S(1)}, u32[]{:S(2)}, u32[]{:S(2)}) collective-permute-start(bf16[1,2,3,128,128]{4,3,2,1,0:T(8,128)(2,1)} %get-tuple-element.90), channel_id=1, source_target_pairs={{0,1},{1,8},{2,3},{3,10},{4,5},{5,12},{6,7},{7,14},{8,9},{9,0},{10... | collective-permute-start | bytes 589832 | tf_op jit(solution)/shard_map/ppermute | solution.py:364
  10.3 14.0 %collective-permute-start.4 = (bf16[1,2,3,128,128]{4,3,2,1,0:T(8,128)(2,1)}, bf16[1,2,3,128,128]{4,3,2,1,0:T(8,128)(2,1)S(1)}, u32[]{:S(2)}, u32[]{:S(2)}) collective-permute-start(bf16[1,2,3,128,128]{4,3,2,1,0:T(8,128)(2,1)} %get-tuple-element.94), channel_id=1, source_target_pairs={{0,8},{1,1},{2,10},{3,3},{4,12},{5,5},{6,14},{7,7},{8,0},{9,9},{10... | collective-permute-start | bytes 589832 | tf_op jit(solution)/shard_map/ppermute | solution.py:364
  12.5 51.0 %copy-start.3 = (bf16[1,2,3,128,128]{4,3,2,1,0:T(8,128)(2,1)}, bf16[1,2,3,128,128]{4,3,2,1,0:T(8,128)(2,1)S(1)}, u32[]{:S(2)}) copy-start(bf16[1,2,3,128,128]{4,3,2,1,0:T(8,128)(2,1)S(1)} %collective-permute-done.refs_2_) | copy-start | bytes 589828
  12.5 12.1 %collective-permute-start.2 = (bf16[1,2,3,128,128]{4,3,2,1,0:T(8,128)(2,1)}, bf16[1,2,3,128,128]{4,3,2,1,0:T(8,128)(2,1)S(1)}, u32[]{:S(2)}, u32[]{:S(2)}) collective-permute-start(bf16[1,2,3,128,128]{4,3,2,1,0:T(8,128)(2,1)} %get-tuple-element.91), channel_id=1, source_target_pairs={{0,2},{1,11},{2,0},{3,9},{4,6},{5,15},{6,4},{7,13},{8,10},{9,3},{1... | collective-permute-start | bytes 589832 | tf_op jit(solution)/shard_map/ppermute | solution.py:364
  24.2 39.3 %copy-start.5 = (bf16[1,2,3,128,128]{4,3,2,1,0:T(8,128)(2,1)}, bf16[1,2,3,128,128]{4,3,2,1,0:T(8,128)(2,1)S(1)}, u32[]{:S(2)}) copy-start(bf16[1,2,3,128,128]{4,3,2,1,0:T(8,128)(2,1)S(1)} %collective-permute-done.1.refs_3_) | copy-start | bytes 589828
  24.2 13.2 %collective-permute-start.6 = (bf16[1,2,3,128,128]{4,3,2,1,0:T(8,128)(2,1)}, bf16[1,2,3,128,128]{4,3,2,1,0:T(8,128)(2,1)S(1)}, u32[]{:S(2)}, u32[]{:S(2)}) collective-permute-start(bf16[1,2,3,128,128]{4,3,2,1,0:T(8,128)(2,1)} %get-tuple-element.99), channel_id=1, source_target_pairs={{0,9},{1,0},{2,11},{3,2},{4,13},{5,4},{6,15},{7,6},{8,1},{9,8},{10... | collective-permute-start | bytes 589832 | tf_op jit(solution)/shard_map/ppermute | solution.py:364
  24.3 39.3 %copy-start.7 = (bf16[1,2,3,128,128]{4,3,2,1,0:T(8,128)(2,1)}, bf16[1,2,3,128,128]{4,3,2,1,0:T(8,128)(2,1)S(1)}, u32[]{:S(2)}) copy-start(bf16[1,2,3,128,128]{4,3,2,1,0:T(8,128)(2,1)S(1)} %collective-permute-done.4.refs_10_) | copy-start | bytes 589828
  24.3 15.9 %collective-permute-start.8 = (bf16[1,2,3,128,128]{4,3,2,1,0:T(8,128)(2,1)}, bf16[1,2,3,128,128]{4,3,2,1,0:T(8,128)(2,1)S(1)}, u32[]{:S(2)}, u32[]{:S(2)}) collective-permute-start(bf16[1,2,3,128,128]{4,3,2,1,0:T(8,128)(2,1)} %get-tuple-element.104), channel_id=1, source_target_pairs={{0,10},{1,3},{2,8},{3,1},{4,14},{5,7},{6,12},{7,5},{8,2},{9,11},{1... | collective-permute-start | bytes 589832 | tf_op jit(solution)/shard_map/ppermute | solution.py:364
  24.6 38.9 %copy-start.11 = (bf16[1,2,3,128,128]{4,3,2,1,0:T(8,128)(2,1)}, bf16[1,2,3,128,128]{4,3,2,1,0:T(8,128)(2,1)S(1)}, u32[]{:S(2)}) copy-start(bf16[1,2,3,128,128]{4,3,2,1,0:T(8,128)(2,1)S(1)} %collective-permute-done.2.refs_4_) | copy-start | bytes 589828
  24.6 16.6 %collective-permute-start.3 = (bf16[1,2,3,128,128]{4,3,2,1,0:T(8,128)(2,1)}, bf16[1,2,3,128,128]{4,3,2,1,0:T(8,128)(2,1)S(1)}, u32[]{:S(2)}, u32[]{:S(2)}) collective-permute-start(bf16[1,2,3,128,128]{4,3,2,1,0:T(8,128)(2,1)} %get-tuple-element.92), channel_id=1, source_target_pairs={{0,3},{1,10},{2,1},{3,8},{4,7},{5,14},{6,5},{7,12},{8,11},{9,2},{1... | collective-permute-start | bytes 589832 | tf_op jit(solution)/shard_map/ppermute | solution.py:364
  37.4 8.8 %collective-permute-start.5 = (bf16[1,2,3,128,128]{4,3,2,1,0:T(8,128)(2,1)}, bf16[1,2,3,128,128]{4,3,2,1,0:T(8,128)(2,1)S(1)}, u32[]{:S(2)}, u32[]{:S(2)}) collective-permute-start(bf16[1,2,3,128,128]{4,3,2,1,0:T(8,128)(2,1)} %get-tuple-element.97), channel_id=1, source_target_pairs={{0,4},{1,13},{2,6},{3,15},{4,0},{5,9},{6,2},{7,11},{8,12},{9,5},{1... | collective-permute-start | bytes 589832 | tf_op jit(solution)/shard_map/ppermute | solution.py:364
  40.2 9.3 %collective-permute-start.7 = (bf16[1,2,3,128,128]{4,3,2,1,0:T(8,128)(2,1)}, bf16[1,2,3,128,128]{4,3,2,1,0:T(8,128)(2,1)S(1)}, u32[]{:S(2)}, u32[]{:S(2)}) collective-permute-start(bf16[1,2,3,128,128]{4,3,2,1,0:T(8,128)(2,1)} %get-tuple-element.102), channel_id=1, source_target_pairs={{0,5},{1,12},{2,7},{3,14},{4,1},{5,8},{6,3},{7,10},{8,13},{9,4},{1... | collective-permute-start | bytes 589832 | tf_op jit(solution)/shard_map/ppermute | solution.py:364
  41.2 12.8 %collective-permute-start.9 = (bf16[1,2,3,128,128]{4,3,2,1,0:T(8,128)(2,1)}, bf16[1,2,3,128,128]{4,3,2,1,0:T(8,128)(2,1)S(1)}, u32[]{:S(2)}, u32[]{:S(2)}) collective-permute-start(bf16[1,2,3,128,128]{4,3,2,1,0:T(8,128)(2,1)} %get-tuple-element.107), channel_id=1, source_target_pairs={{0,6},{1,15},{2,4},{3,13},{4,2},{5,11},{6,0},{7,9},{8,14},{9,7},{1... | collective-permute-start | bytes 589832 | tf_op jit(solution)/shard_map/ppermute | solution.py:364
  46.3 10.2 %collective-permute-start.10 = (bf16[1,2,3,128,128]{4,3,2,1,0:T(8,128)(2,1)}, bf16[1,2,3,128,128]{4,3,2,1,0:T(8,128)(2,1)S(1)}, u32[]{:S(2)}, u32[]{:S(2)}) collective-permute-start(bf16[1,2,3,128,128]{4,3,2,1,0:T(8,128)(2,1)} %get-tuple-element.96), channel_id=1, source_target_pairs={{0,11},{1,2},{2,9},{3,0},{4,15},{5,6},{6,13},{7,4},{8,3},{9,10},{1... | collective-permute-start | bytes 589832 | tf_op jit(solution)/shard_map/ppermute | solution.py:364
  49.5 14.1 %collective-permute-start.12 = (bf16[1,2,3,128,128]{4,3,2,1,0:T(8,128)(2,1)}, bf16[1,2,3,128,128]{4,3,2,1,0:T(8,128)(2,1)S(1)}, u32[]{:S(2)}, u32[]{:S(2)}) collective-permute-start(bf16[1,2,3,128,128]{4,3,2,1,0:T(8,128)(2,1)} %get-tuple-element.101), channel_id=1, source_target_pairs={{0,12},{1,5},{2,14},{3,7},{4,8},{5,1},{6,10},{7,3},{8,4},{9,13},{1... | collective-permute-start | bytes 589832 | tf_op jit(solution)/shard_map/ppermute | solution.py:364
  54.0 13.3 %collective-permute-start.13 = (bf16[1,2,3,128,128]{4,3,2,1,0:T(8,128)(2,1)}, bf16[1,2,3,128,128]{4,3,2,1,0:T(8,128)(2,1)S(1)}, u32[]{:S(2)}, u32[]{:S(2)}) collective-permute-start(bf16[1,2,3,128,128]{4,3,2,1,0:T(8,128)(2,1)} %get-tuple-element.106), channel_id=1, source_target_pairs={{0,13},{1,4},{2,15},{3,6},{4,9},{5,0},{6,11},{7,2},{8,5},{9,12},{1... | collective-permute-start | bytes 589832 | tf_op jit(solution)/shard_map/ppermute | solution.py:364
  56.5 14.6 %collective-permute-start.14 = (bf16[1,2,3,128,128]{4,3,2,1,0:T(8,128)(2,1)}, bf16[1,2,3,128,128]{4,3,2,1,0:T(8,128)(2,1)}, u32[]{:S(2)}, u32[]{:S(2)}) collective-permute-start(bf16[1,2,3,128,128]{4,3,2,1,0:T(8,128)(2,1)} %get-tuple-element.110), channel_id=1, source_target_pairs={{0,14},{1,7},{2,12},{3,5},{4,10},{5,3},{6,8},{7,1},{8,6},{9,15},{1... | collective-permute-start | bytes 589832 | tf_op jit(solution)/shard_map/ppermute | solution.py:364
  63.6 9.8 %collective-permute-start.11 = (bf16[1,2,3,128,128]{4,3,2,1,0:T(8,128)(2,1)}, bf16[1,2,3,128,128]{4,3,2,1,0:T(8,128)(2,1)S(1)}, u32[]{:S(2)}, u32[]{:S(2)}) collective-permute-start(bf16[1,2,3,128,128]{4,3,2,1,0:T(8,128)(2,1)} %get-tuple-element.111), channel_id=1, source_target_pairs={{0,7},{1,14},{2,5},{3,12},{4,3},{5,10},{6,1},{7,8},{8,15},{9,6},{1... | collective-permute-start | bytes 589832 | tf_op jit(solution)/shard_map/ppermute | solution.py:364
  67.3 10.7 %collective-permute-start.15 = (bf16[1,2,3,128,128]{4,3,2,1,0:T(8,128)(2,1)S(1)}, bf16[1,2,3,128,128]{4,3,2,1,0:T(8,128)(2,1)S(1)}, u32[]{:S(2)}, u32[]{:S(2)}) collective-permute-start(bf16[1,2,3,128,128]{4,3,2,1,0:T(8,128)(2,1)S(1)} %copy-done.15), channel_id=1, source_target_pairs={{0,15},{1,6},{2,13},{3,4},{4,11},{5,2},{6,9},{7,0},{8,7},{9,14},{1... | collective-permute-start | bytes 589832 | tf_op jit(solution)/shard_map/ppermute | solution.py:364
  71.0 8.1 %collective-permute-start.18 = (bf16[1,2,3,128,128]{4,3,2,1,0:T(8,128)(2,1)}, bf16[1,2,3,128,128]{4,3,2,1,0:T(8,128)(2,1)S(1)}, u32[]{:S(2)}, u32[]{:S(2)}) collective-permute-start(bf16[1,2,3,128,128]{4,3,2,1,0:T(8,128)(2,1)} %get-tuple-element.115), channel_id=1, source_target_pairs={{0,0},{1,9},{2,2},{3,11},{4,4},{5,13},{6,6},{7,15},{8,8},{9,1},{10... | collective-permute-start | bytes 589832 | tf_op jit(solution)/shard_map/ppermute | solution.py:364
  73.4 32.8 %collective-permute-start.19 = (bf16[1,2,3,128,128]{4,3,2,1,0:T(8,128)(2,1)}, bf16[1,2,3,128,128]{4,3,2,1,0:T(8,128)(2,1)S(1)}, u32[]{:S(2)}, u32[]{:S(2)}) collective-permute-start(bf16[1,2,3,128,128]{4,3,2,1,0:T(8,128)(2,1)} %get-tuple-element.119), channel_id=1, source_target_pairs={{0,1},{1,8},{2,3},{3,10},{4,5},{5,12},{6,7},{7,14},{8,9},{9,0},{10... | collective-permute-start | bytes 589832 | tf_op jit(solution)/shard_map/ppermute | solution.py:364
  77.2 43.2 %copy-start.10 = (bf16[1,2,3,128,128]{4,3,2,1,0:T(8,128)(2,1)S(1)}, bf16[1,2,3,128,128]{4,3,2,1,0:T(8,128)(2,1)}, u32[]{:S(2)}) copy-start(bf16[1,2,3,128,128]{4,3,2,1,0:T(8,128)(2,1)} %get-tuple-element.139) | copy-start | bytes 589828
  77.2 46.2 %copy-start.9 = (bf16[1,2,3,128,128]{4,3,2,1,0:T(8,128)(2,1)S(1)}, bf16[1,2,3,128,128]{4,3,2,1,0:T(8,128)(2,1)}, u32[]{:S(2)}) copy-start(bf16[1,2,3,128,128]{4,3,2,1,0:T(8,128)(2,1)} %get-tuple-element.145) | copy-start | bytes 589828
  77.2 50.3 %copy-start.8 = (bf16[1,2,3,128,128]{4,3,2,1,0:T(8,128)(2,1)S(1)}, bf16[1,2,3,128,128]{4,3,2,1,0:T(8,128)(2,1)}, u32[]{:S(2)}) copy-start(bf16[1,2,3,128,128]{4,3,2,1,0:T(8,128)(2,1)} %get-tuple-element.152) | copy-start | bytes 589828
  77.2 50.4 %copy-start.6 = (bf16[1,2,3,128,128]{4,3,2,1,0:T(8,128)(2,1)S(1)}, bf16[1,2,3,128,128]{4,3,2,1,0:T(8,128)(2,1)}, u32[]{:S(2)}) copy-start(bf16[1,2,3,128,128]{4,3,2,1,0:T(8,128)(2,1)} %get-tuple-element.151) | copy-start | bytes 589828
  77.2 55.5 %copy-start.4 = (bf16[1,2,3,128,128]{4,3,2,1,0:T(8,128)(2,1)S(1)}, bf16[1,2,3,128,128]{4,3,2,1,0:T(8,128)(2,1)}, u32[]{:S(2)}) copy-start(bf16[1,2,3,128,128]{4,3,2,1,0:T(8,128)(2,1)} %get-tuple-element.155) | copy-start | bytes 589828
  78.1 33.0 %collective-permute-start.20 = (bf16[1,2,3,128,128]{4,3,2,1,0:T(8,128)(2,1)}, bf16[1,2,3,128,128]{4,3,2,1,0:T(8,128)(2,1)S(1)}, u32[]{:S(2)}, u32[]{:S(2)}) collective-permute-start(bf16[1,2,3,128,128]{4,3,2,1,0:T(8,128)(2,1)} %get-tuple-element.123), channel_id=1, source_target_pairs={{0,2},{1,11},{2,0},{3,9},{4,6},{5,15},{6,4},{7,13},{8,10},{9,3},{1... | collective-permute-start | bytes 589832 | tf_op jit(solution)/shard_map/ppermute | solution.py:364
  79.1 26.9 %collective-permute-start.22 = (bf16[1,2,3,128,128]{4,3,2,1,0:T(8,128)(2,1)}, bf16[1,2,3,128,128]{4,3,2,1,0:T(8,128)(2,1)S(1)}, u32[]{:S(2)}, u32[]{:S(2)}) collective-permute-start(bf16[1,2,3,128,128]{4,3,2,1,0:T(8,128)(2,1)} %get-tuple-element.118), channel_id=1, source_target_pairs={{0,8},{1,1},{2,10},{3,3},{4,12},{5,5},{6,14},{7,7},{8,0},{9,9},{10... | collective-permute-start | bytes 589832 | tf_op jit(solution)/shard_map/ppermute | solution.py:364
  91.3 15.0 %collective-permute-start.24 = (bf16[1,2,3,128,128]{4,3,2,1,0:T(8,128)(2,1)}, bf16[1,2,3,128,128]{4,3,2,1,0:T(8,128)(2,1)S(1)}, u32[]{:S(2)}, u32[]{:S(2)}) collective-permute-start(bf16[1,2,3,128,128]{4,3,2,1,0:T(8,128)(2,1)} %get-tuple-element.122), channel_id=1, source_target_pairs={{0,9},{1,0},{2,11},{3,2},{4,13},{5,4},{6,15},{7,6},{8,1},{9,8},{10... | collective-permute-start | bytes 589832 | tf_op jit(solution)/shard_map/ppermute | solution.py:364
  91.3 19.8 %collective-permute-start.26 = (bf16[1,2,3,128,128]{4,3,2,1,0:T(8,128)(2,1)}, bf16[1,2,3,128,128]{4,3,2,1,0:T(8,128)(2,1)S(1)}, u32[]{:S(2)}, u32[]{:S(2)}) collective-permute-start(bf16[1,2,3,128,128]{4,3,2,1,0:T(8,128)(2,1)} %get-tuple-element.127), channel_id=1, source_target_pairs={{0,10},{1,3},{2,8},{3,1},{4,14},{5,7},{6,12},{7,5},{8,2},{9,11},{1... | collective-permute-start | bytes 589832 | tf_op jit(solution)/shard_map/ppermute | solution.py:364
  106.1 34.9 %copy-start.25 = (bf16[1,2,3,128,128]{4,3,2,1,0:T(8,128)(2,1)}, bf16[1,2,3,128,128]{4,3,2,1,0:T(8,128)(2,1)S(1)}, u32[]{:S(2)}) copy-start(bf16[1,2,3,128,128]{4,3,2,1,0:T(8,128)(2,1)S(1)} %collective-permute-done.22.refs_10_) | copy-start | bytes 589828
  106.1 14.3 %collective-permute-start.21 = (bf16[1,2,3,128,128]{4,3,2,1,0:T(8,128)(2,1)S(1)}, bf16[1,2,3,128,128]{4,3,2,1,0:T(8,128)(2,1)S(1)}, u32[]{:S(2)}, u32[]{:S(2)}) collective-permute-start(bf16[1,2,3,128,128]{4,3,2,1,0:T(8,128)(2,1)S(1)} %copy-done.23), channel_id=1, source_target_pairs={{0,3},{1,10},{2,1},{3,8},{4,7},{5,14},{6,5},{7,12},{8,11},{9,2},{1... | collective-permute-start | bytes 589832 | tf_op jit(solution)/shard_map/ppermute | solution.py:364
  106.2 21.3 %collective-permute-start.23 = (bf16[1,2,3,128,128]{4,3,2,1,0:T(8,128)(2,1)S(1)}, bf16[1,2,3,128,128]{4,3,2,1,0:T(8,128)(2,1)S(1)}, u32[]{:S(2)}, u32[]{:S(2)}) collective-permute-start(bf16[1,2,3,128,128]{4,3,2,1,0:T(8,128)(2,1)S(1)} %copy-done.17), channel_id=1, source_target_pairs={{0,4},{1,13},{2,6},{3,15},{4,0},{5,9},{6,2},{7,11},{8,12},{9,5},{1... | collective-permute-start | bytes 589832 | tf_op jit(solution)/shard_map/ppermute | solution.py:364
  106.3 48.7 %copy-start.27 = (bf16[1,2,3,128,128]{4,3,2,1,0:T(8,128)(2,1)}, bf16[1,2,3,128,128]{4,3,2,1,0:T(8,128)(2,1)S(1)}, u32[]{:S(2)}) copy-start(bf16[1,2,3,128,128]{4,3,2,1,0:T(8,128)(2,1)S(1)} %collective-permute-done.24.refs_11_) | copy-start | bytes 589828
  106.3 17.1 %collective-permute-start.28 = (bf16[1,2,3,128,128]{4,3,2,1,0:T(8,128)(2,1)S(1)}, bf16[1,2,3,128,128]{4,3,2,1,0:T(8,128)(2,1)S(1)}, u32[]{:S(2)}, u32[]{:S(2)}) collective-permute-start(bf16[1,2,3,128,128]{4,3,2,1,0:T(8,128)(2,1)S(1)} %copy-done.20), channel_id=1, source_target_pairs={{0,11},{1,2},{2,9},{3,0},{4,15},{5,6},{6,13},{7,4},{8,3},{9,10},{1... | collective-permute-start | bytes 589832 | tf_op jit(solution)/shard_map/ppermute | solution.py:364
  111.1 43.9 %copy-start.22 = (bf16[1,2,3,128,128]{4,3,2,1,0:T(8,128)(2,1)}, bf16[1,2,3,128,128]{4,3,2,1,0:T(8,128)(2,1)S(1)}, u32[]{:S(2)}) copy-start(bf16[1,2,3,128,128]{4,3,2,1,0:T(8,128)(2,1)S(1)} %collective-permute-done.20.refs_4_) | copy-start | bytes 589828
  111.1 16.5 %collective-permute-start.25 = (bf16[1,2,3,128,128]{4,3,2,1,0:T(8,128)(2,1)S(1)}, bf16[1,2,3,128,128]{4,3,2,1,0:T(8,128)(2,1)S(1)}, u32[]{:S(2)}, u32[]{:S(2)}) collective-permute-start(bf16[1,2,3,128,128]{4,3,2,1,0:T(8,128)(2,1)S(1)} %copy-done.14), channel_id=1, source_target_pairs={{0,5},{1,12},{2,7},{3,14},{4,1},{5,8},{6,3},{7,10},{8,13},{9,4},{1... | collective-permute-start | bytes 589832 | tf_op jit(solution)/shard_map/ppermute | solution.py:364
  111.2 43.8 %copy-start.28 = (bf16[1,2,3,128,128]{4,3,2,1,0:T(8,128)(2,1)}, bf16[1,2,3,128,128]{4,3,2,1,0:T(8,128)(2,1)S(1)}, u32[]{:S(2)}) copy-start(bf16[1,2,3,128,128]{4,3,2,1,0:T(8,128)(2,1)S(1)} %collective-permute-done.26.refs_12_) | copy-start | bytes 589828
  111.2 21.5 %collective-permute-start.27 = (bf16[1,2,3,128,128]{4,3,2,1,0:T(8,128)(2,1)S(1)}, bf16[1,2,3,128,128]{4,3,2,1,0:T(8,128)(2,1)S(1)}, u32[]{:S(2)}, u32[]{:S(2)}) collective-permute-start(bf16[1,2,3,128,128]{4,3,2,1,0:T(8,128)(2,1)S(1)} %copy-done.12), channel_id=1, source_target_pairs={{0,6},{1,15},{2,4},{3,13},{4,2},{5,11},{6,0},{7,9},{8,14},{9,7},{1... | collective-permute-start | bytes 589832 | tf_op jit(solution)/shard_map/ppermute | solution.py:364
  120.4 17.7 %collective-permute-start.30 = (bf16[1,2,3,128,128]{4,3,2,1,0:T(8,128)(2,1)S(1)}, bf16[1,2,3,128,128]{4,3,2,1,0:T(8,128)(2,1)S(1)}, u32[]{:S(2)}, u32[]{:S(2)}) collective-permute-start(bf16[1,2,3,128,128]{4,3,2,1,0:T(8,128)(2,1)S(1)} %copy-done.10), channel_id=1, source_target_pairs={{0,12},{1,5},{2,14},{3,7},{4,8},{5,1},{6,10},{7,3},{8,4},{9,13},{1... | collective-permute-start | bytes 589832 | tf_op jit(solution)/shard_map/ppermute | solution.py:364
  123.4 14.6 %collective-permute-start.31 = (bf16[1,2,3,128,128]{4,3,2,1,0:T(8,128)(2,1)S(1)}, bf16[1,2,3,128,128]{4,3,2,1,0:T(8,128)(2,1)S(1)}, u32[]{:S(2)}, u32[]{:S(2)}) collective-permute-start(bf16[1,2,3,128,128]{4,3,2,1,0:T(8,128)(2,1)S(1)} %copy-done.9), channel_id=1, source_target_pairs={{0,13},{1,4},{2,15},{3,6},{4,9},{5,0},{6,11},{7,2},{8,5},{9,12},{1... | collective-permute-start | bytes 589832 | tf_op jit(solution)/shard_map/ppermute | solution.py:364
  127.5 10.5 %collective-permute-start.29 = (bf16[1,2,3,128,128]{4,3,2,1,0:T(8,128)(2,1)S(1)}, bf16[1,2,3,128,128]{4,3,2,1,0:T(8,128)(2,1)S(1)}, u32[]{:S(2)}, u32[]{:S(2)}) collective-permute-start(bf16[1,2,3,128,128]{4,3,2,1,0:T(8,128)(2,1)S(1)} %copy-done.8), channel_id=1, source_target_pairs={{0,7},{1,14},{2,5},{3,12},{4,3},{5,10},{6,1},{7,8},{8,15},{9,6},{1... | collective-permute-start | bytes 589832 | tf_op jit(solution)/shard_map/ppermute | solution.py:364
  127.6 13.4 %collective-permute-start.32 = (bf16[1,2,3,128,128]{4,3,2,1,0:T(8,128)(2,1)S(1)}, bf16[1,2,3,128,128]{4,3,2,1,0:T(8,128)(2,1)S(1)}, u32[]{:S(2)}, u32[]{:S(2)}) collective-permute-start(bf16[1,2,3,128,128]{4,3,2,1,0:T(8,128)(2,1)S(1)} %copy-done.6), channel_id=1, source_target_pairs={{0,14},{1,7},{2,12},{3,5},{4,10},{5,3},{6,8},{7,1},{8,6},{9,15},{1... | collective-permute-start | bytes 589832 | tf_op jit(solution)/shard_map/ppermute | solution.py:364
  132.7 16.8 %collective-permute-start.33 = (bf16[1,2,3,128,128]{4,3,2,1,0:T(8,128)(2,1)S(1)}, bf16[1,2,3,128,128]{4,3,2,1,0:T(8,128)(2,1)S(1)}, u32[]{:S(2)}, u32[]{:S(2)}) collective-permute-start(bf16[1,2,3,128,128]{4,3,2,1,0:T(8,128)(2,1)S(1)} %copy-done.4), channel_id=1, source_target_pairs={{0,15},{1,6},{2,13},{3,4},{4,11},{5,2},{6,9},{7,0},{8,7},{9,14},{1... | collective-permute-start | bytes 589832 | tf_op jit(solution)/shard_map/ppermute | solution.py:364
  150.2 56.1 %all-to-all-start = ((bf16[16,2,128,128]{3,2,1,0:T(8,128)(2,1)}), bf16[16,2,128,128]{3,2,1,0:T(8,128)(2,1)S(1)}, u32[]{:S(2)}, u32[]{:S(2)}) async-start(bf16[16,2,128,128]{3,2,1,0:T(8,128)(2,1)} %shard_map.65), calls=%async_computation | async-start | bytes 2097152 | tf_op jit(solution)/shard_map/all_to_all | solution.py:344
  166.0 7.6 %collective-permute-start.34 = (bf16[1,2,128,128]{3,2,1,0:T(8,128)(2,1)S(1)}, bf16[1,2,128,128]{3,2,1,0:T(8,128)(2,1)S(1)}, u32[]{:S(2)}, u32[]{:S(2)}) collective-permute-start(bf16[1,2,128,128]{3,2,1,0:T(8,128)(2,1)S(1)} %get-tuple-element.157), channel_id=1, source_target_pairs={{0,0},{1,9},{2,2},{3,11},{4,4},{5,13},{6,6},{7,15},{8,8},{9,1},{10... | collective-permute-start | bytes 196616 | tf_op jit(solution)/shard_map/ppermute | solution.py:380
  166.7 19.8 %collective-permute-start.35 = (bf16[1,2,128,128]{3,2,1,0:T(8,128)(2,1)S(1)}, bf16[1,2,128,128]{3,2,1,0:T(8,128)(2,1)S(1)}, u32[]{:S(2)}, u32[]{:S(2)}) collective-permute-start(bf16[1,2,128,128]{3,2,1,0:T(8,128)(2,1)S(1)} %get-tuple-element.158), channel_id=1, source_target_pairs={{0,1},{1,8},{2,3},{3,10},{4,5},{5,12},{6,7},{7,14},{8,9},{9,0},{10... | collective-permute-start | bytes 196616 | tf_op jit(solution)/shard_map/ppermute | solution.py:380
  170.7 17.5 %collective-permute-start.36 = (bf16[1,2,128,128]{3,2,1,0:T(8,128)(2,1)S(1)}, bf16[1,2,128,128]{3,2,1,0:T(8,128)(2,1)S(1)}, u32[]{:S(2)}, u32[]{:S(2)}) collective-permute-start(bf16[1,2,128,128]{3,2,1,0:T(8,128)(2,1)S(1)} %get-tuple-element.159), channel_id=1, source_target_pairs={{0,2},{1,11},{2,0},{3,9},{4,6},{5,15},{6,4},{7,13},{8,10},{9,3},{1... | collective-permute-start | bytes 196616 | tf_op jit(solution)/shard_map/ppermute | solution.py:380
  172.1 16.7 %collective-permute-start.37 = (bf16[1,2,128,128]{3,2,1,0:T(8,128)(2,1)S(1)}, bf16[1,2,128,128]{3,2,1,0:T(8,128)(2,1)S(1)}, u32[]{:S(2)}, u32[]{:S(2)}) collective-permute-start(bf16[1,2,128,128]{3,2,1,0:T(8,128)(2,1)S(1)} %get-tuple-element.160), channel_id=1, source_target_pairs={{0,3},{1,10},{2,1},{3,8},{4,7},{5,14},{6,5},{7,12},{8,11},{9,2},{1... | collective-permute-start | bytes 196616 | tf_op jit(solution)/shard_map/ppermute | solution.py:380
  172.1 20.0 %collective-permute-start.38 = (bf16[1,2,128,128]{3,2,1,0:T(8,128)(2,1)S(1)}, bf16[1,2,128,128]{3,2,1,0:T(8,128)(2,1)S(1)}, u32[]{:S(2)}, u32[]{:S(2)}) collective-permute-start(bf16[1,2,128,128]{3,2,1,0:T(8,128)(2,1)S(1)} %get-tuple-element.161), channel_id=1, source_target_pairs={{0,4},{1,13},{2,6},{3,15},{4,0},{5,9},{6,2},{7,11},{8,12},{9,5},{1... | collective-permute-start | bytes 196616 | tf_op jit(solution)/shard_map/ppermute | solution.py:380
  173.6 18.6 %collective-permute-start.39 = (bf16[1,2,128,128]{3,2,1,0:T(8,128)(2,1)S(1)}, bf16[1,2,128,128]{3,2,1,0:T(8,128)(2,1)S(1)}, u32[]{:S(2)}, u32[]{:S(2)}) collective-permute-start(bf16[1,2,128,128]{3,2,1,0:T(8,128)(2,1)S(1)} %get-tuple-element.162), channel_id=1, source_target_pairs={{0,5},{1,12},{2,7},{3,14},{4,1},{5,8},{6,3},{7,10},{8,13},{9,4},{1... | collective-permute-start | bytes 196616 | tf_op jit(solution)/shard_map/ppermute | solution.py:380
  186.5 7.4 %collective-permute-start.40 = (bf16[1,2,128,128]{3,2,1,0:T(8,128)(2,1)S(1)}, bf16[1,2,128,128]{3,2,1,0:T(8,128)(2,1)S(1)}, u32[]{:S(2)}, u32[]{:S(2)}) collective-permute-start(bf16[1,2,128,128]{3,2,1,0:T(8,128)(2,1)S(1)} %get-tuple-element.163), channel_id=1, source_target_pairs={{0,6},{1,15},{2,4},{3,13},{4,2},{5,11},{6,0},{7,9},{8,14},{9,7},{1... | collective-permute-start | bytes 196616 | tf_op jit(solution)/shard_map/ppermute | solution.py:380
  188.1 6.9 %collective-permute-start.41 = (bf16[1,2,128,128]{3,2,1,0:T(8,128)(2,1)S(1)}, bf16[1,2,128,128]{3,2,1,0:T(8,128)(2,1)S(1)}, u32[]{:S(2)}, u32[]{:S(2)}) collective-permute-start(bf16[1,2,128,128]{3,2,1,0:T(8,128)(2,1)S(1)} %get-tuple-element.164), channel_id=1, source_target_pairs={{0,7},{1,14},{2,5},{3,12},{4,3},{5,10},{6,1},{7,8},{8,15},{9,6},{1... | collective-permute-start | bytes 196616 | tf_op jit(solution)/shard_map/ppermute | solution.py:380
  188.8 8.5 %collective-permute-start.42 = (bf16[1,2,128,128]{3,2,1,0:T(8,128)(2,1)S(1)}, bf16[1,2,128,128]{3,2,1,0:T(8,128)(2,1)S(1)}, u32[]{:S(2)}, u32[]{:S(2)}) collective-permute-start(bf16[1,2,128,128]{3,2,1,0:T(8,128)(2,1)S(1)} %get-tuple-element.165), channel_id=1, source_target_pairs={{0,8},{1,1},{2,10},{3,3},{4,12},{5,5},{6,14},{7,7},{8,0},{9,9},{10... | collective-permute-start | bytes 196616 | tf_op jit(solution)/shard_map/ppermute | solution.py:380
  192.1 5.4 %collective-permute-start.43 = (bf16[1,2,128,128]{3,2,1,0:T(8,128)(2,1)S(1)}, bf16[1,2,128,128]{3,2,1,0:T(8,128)(2,1)S(1)}, u32[]{:S(2)}, u32[]{:S(2)}) collective-permute-start(bf16[1,2,128,128]{3,2,1,0:T(8,128)(2,1)S(1)} %get-tuple-element.166), channel_id=1, source_target_pairs={{0,9},{1,0},{2,11},{3,2},{4,13},{5,4},{6,15},{7,6},{8,1},{9,8},{10... | collective-permute-start | bytes 196616 | tf_op jit(solution)/shard_map/ppermute | solution.py:380
  192.2 8.3 %collective-permute-start.44 = (bf16[1,2,128,128]{3,2,1,0:T(8,128)(2,1)S(1)}, bf16[1,2,128,128]{3,2,1,0:T(8,128)(2,1)S(1)}, u32[]{:S(2)}, u32[]{:S(2)}) collective-permute-start(bf16[1,2,128,128]{3,2,1,0:T(8,128)(2,1)S(1)} %get-tuple-element.167), channel_id=1, source_target_pairs={{0,10},{1,3},{2,8},{3,1},{4,14},{5,7},{6,12},{7,5},{8,2},{9,11},{1... | collective-permute-start | bytes 196616 | tf_op jit(solution)/shard_map/ppermute | solution.py:380
  193.9 7.4 %collective-permute-start.45 = (bf16[1,2,128,128]{3,2,1,0:T(8,128)(2,1)S(1)}, bf16[1,2,128,128]{3,2,1,0:T(8,128)(2,1)S(1)}, u32[]{:S(2)}, u32[]{:S(2)}) collective-permute-start(bf16[1,2,128,128]{3,2,1,0:T(8,128)(2,1)S(1)} %get-tuple-element.168), channel_id=1, source_target_pairs={{0,11},{1,2},{2,9},{3,0},{4,15},{5,6},{6,13},{7,4},{8,3},{9,10},{1... | collective-permute-start | bytes 196616 | tf_op jit(solution)/shard_map/ppermute | solution.py:380
  195.0 6.5 %collective-permute-start.46 = (bf16[1,2,128,128]{3,2,1,0:T(8,128)(2,1)S(1)}, bf16[1,2,128,128]{3,2,1,0:T(8,128)(2,1)S(1)}, u32[]{:S(2)}, u32[]{:S(2)}) collective-permute-start(bf16[1,2,128,128]{3,2,1,0:T(8,128)(2,1)S(1)} %get-tuple-element.169), channel_id=1, source_target_pairs={{0,12},{1,5},{2,14},{3,7},{4,8},{5,1},{6,10},{7,3},{8,4},{9,13},{1... | collective-permute-start | bytes 196616 | tf_op jit(solution)/shard_map/ppermute | solution.py:380
  197.3 5.6 %collective-permute-start.47 = (bf16[1,2,128,128]{3,2,1,0:T(8,128)(2,1)S(1)}, bf16[1,2,128,128]{3,2,1,0:T(8,128)(2,1)S(1)}, u32[]{:S(2)}, u32[]{:S(2)}) collective-permute-start(bf16[1,2,128,128]{3,2,1,0:T(8,128)(2,1)S(1)} %get-tuple-element.170), channel_id=1, source_target_pairs={{0,13},{1,4},{2,15},{3,6},{4,9},{5,0},{6,11},{7,2},{8,5},{9,12},{1... | collective-permute-start | bytes 196616 | tf_op jit(solution)/shard_map/ppermute | solution.py:380
  197.6 7.4 %collective-permute-start.48 = (bf16[1,2,128,128]{3,2,1,0:T(8,128)(2,1)S(1)}, bf16[1,2,128,128]{3,2,1,0:T(8,128)(2,1)S(1)}, u32[]{:S(2)}, u32[]{:S(2)}) collective-permute-start(bf16[1,2,128,128]{3,2,1,0:T(8,128)(2,1)S(1)} %get-tuple-element.171), channel_id=1, source_target_pairs={{0,14},{1,7},{2,12},{3,5},{4,10},{5,3},{6,8},{7,1},{8,6},{9,15},{1... | collective-permute-start | bytes 196616 | tf_op jit(solution)/shard_map/ppermute | solution.py:380
  200.5 5.8 %collective-permute-start.49 = (bf16[1,2,128,128]{3,2,1,0:T(8,128)(2,1)S(1)}, bf16[1,2,128,128]{3,2,1,0:T(8,128)(2,1)S(1)}, u32[]{:S(2)}, u32[]{:S(2)}) collective-permute-start(bf16[1,2,128,128]{3,2,1,0:T(8,128)(2,1)S(1)} %get-tuple-element.172), channel_id=1, source_target_pairs={{0,15},{1,6},{2,13},{3,4},{4,11},{5,2},{6,9},{7,0},{8,7},{9,14},{1... | collective-permute-start | bytes 196616 | tf_op jit(solution)/shard_map/ppermute | solution.py:380
  (31 other events, 609.0 us)

commit v8 on v7

--- a/solution.py
+++ b/solution.py
@@ -12,8 +12,8 @@
 UNROLL = 16
 OWNED = 4
 EARLY = 2
-WINDOW = 7
-GATE = 6
+WINDOW = 8
+GATE = 7
 STEPS = (0, 8, 1, 9, 2, 10, 3, 11, 4, 12, 5, 13, 6, 14, 7, 15)
 
 

time: 209 us -> 220 us (1.053); the launches traced: 209 us -> 217 us
  starting transfers between devices: 122 us -> 129 us
    ppermute x32, starting transfers between devices: 85 us -> 92.6 us  [send(): sent.append(lax.ppermute(message, axes, pairs_of(step)))]
  transfers between devices with their start and end apart: 51 -> 51, of which waited for: 19 -> 20; matrix products, arithmetic and copies ran while one was open for 0% -> 0% of each run, Pallas kernels for 15% -> 14%
where the time goes in v8:
time: 220 us; the launch traced here: 217 us
  starting transfers between devices  129 us (59%)
  waiting for transfers between devices  53.8 us (24%)
  Pallas kernels  32.7 us (15%)
    ppermute x32, starting transfers between devices, send(): sent.append(lax.ppermute(message, axes, pairs_of(step)))  92.6 us
    ppermute x32, waiting for transfers between devices, send(): sent.append(lax.ppermute(message, axes, pairs_of(step)))  45.1 us
    ppermute x16, starting transfers between devices, per_device(): returned[step] = lax.ppermute(parts[step], axes, pairs_of(step))  31.3 us
    pallas_call x2, Pallas kernels, attend_pieces(): pl.pallas_call(lambda *refs: pieces_kernel(pieces, by_step, *refs), grid_...  22.7 us
    ppermute x16, waiting for transfers between devices, per_device(): returned[step] = lax.ppermute(parts[step], axes, pairs_of(step))  8.76 us
    pallas_call x2, Pallas kernels, pack_each(): pl.pallas_call(kernel, grid_spec=pltpu.PrefetchScalarGridSpec(num_scalar_...  7.9 us
  transfers between devices with their start and end apart: 51, of which 20 were waited for; matrix products, arithmetic and copies ran while one was open for 0% of the time, Pallas kernels for 14%

profile of v8, /device:TPU:0, one launch (start us, length us, event | category | flops | bytes accessed | tf_op | source)
XLA Modules:
  0.0 217.0 jit_solution(5642484402789742121)
XLA Ops:
  0.0 0.5 collective-permute-start.16
  0.6 4.0 %shard_map.64 = (bf16[1,2,3,128,128]{4,3,2,1,0:T(8,128)(2,1)}, bf16[1,2,3,128,128]{4,3,2,1,0:T(8,128)(2,1)}, bf16[1,2,3,128,128]{4,3,2,1,0:T(8,128)(2,1)}, bf16[...) custom-call(s32[17]{0:T(128)S(1)} %stack.116.place, ...), custom_call_target="tpu_custom_call" | custom-call | bytes 6291456 | tf_op jit(solution)/shard_map/pallas_call | solution.py:270
  4.6 1.6 collective-permute-start
  6.2 4.1 %collective-permute-start.1 = (bf16[1,2,3,128,128]{4,3,2,1,0:T(8,128)(2,1)}, bf16[1,2,3,128,128]{4,3,2,1,0:T(8,128)(2,1)S(1)}, u32[]{:S(2)}, u32[]{:S(2)}) collective-permute-start(bf16[1,2,3,128,128]{4,3,2,1,0:T(8,128)(2,1)} %get-tuple-element.88), channel_id=1, source_target_pairs={{0,1},{1,8},{2,3},{3,10},{4,5},{5,12},{6,7},{7,14},{8,9},{9,0},{10... | collective-permute-start | bytes 589832 | tf_op jit(solution)/shard_map/ppermute | solution.py:364
  10.3 1.5 collective-permute-start.2
  11.8 2.2 %collective-permute-start.5 = (bf16[1,2,3,128,128]{4,3,2,1,0:T(8,128)(2,1)}, bf16[1,2,3,128,128]{4,3,2,1,0:T(8,128)(2,1)S(1)}, u32[]{:S(2)}, u32[]{:S(2)}) collective-permute-start(bf16[1,2,3,128,128]{4,3,2,1,0:T(8,128)(2,1)} %get-tuple-element.96), channel_id=1, source_target_pairs={{0,8},{1,1},{2,10},{3,3},{4,12},{5,5},{6,14},{7,7},{8,0},{9,9},{10... | collective-permute-start | bytes 589832 | tf_op jit(solution)/shard_map/ppermute | solution.py:364
  14.0 12.3 %collective-permute-done.1.refs_3_ = bf16[1,2,3,128,128]{4,3,2,1,0:T(8,128)(2,1)S(1)} collective-permute-done((bf16[1,2,3,128,128]{4,3,2,1,0:T(8,128)(2,1)}, bf16[1,2,3,128,128]{4,3,2,1,0:T(8,128)(2,1)S(1)}, u32[]{:S(2)}, u32[]{:S(2)}) %collective-permute-start.1) | collective-permute-done | bytes 196640 | tf_op jit(solution)/shard_map/ppermute | solution.py:364
  26.3 3.0 %collective-permute-start.3 = (bf16[1,2,3,128,128]{4,3,2,1,0:T(8,128)(2,1)}, bf16[1,2,3,128,128]{4,3,2,1,0:T(8,128)(2,1)S(1)}, u32[]{:S(2)}, u32[]{:S(2)}) collective-permute-start(bf16[1,2,3,128,128]{4,3,2,1,0:T(8,128)(2,1)} %get-tuple-element.90), channel_id=1, source_target_pairs={{0,3},{1,10},{2,1},{3,8},{4,7},{5,14},{6,5},{7,12},{8,11},{9,2},{1... | collective-permute-start | bytes 589832 | tf_op jit(solution)/shard_map/ppermute | solution.py:364
  29.3 0.5 collective-permute-done.7.refs_11_
  29.8 4.9 %collective-permute-start.11 = (bf16[1,2,3,128,128]{4,3,2,1,0:T(8,128)(2,1)}, bf16[1,2,3,128,128]{4,3,2,1,0:T(8,128)(2,1)S(1)}, u32[]{:S(2)}, u32[]{:S(2)}) collective-permute-start(bf16[1,2,3,128,128]{4,3,2,1,0:T(8,128)(2,1)} %get-tuple-element.92), channel_id=1, source_target_pairs={{0,11},{1,2},{2,9},{3,0},{4,15},{5,6},{6,13},{7,4},{8,3},{9,10},{1... | collective-permute-start | bytes 589832 | tf_op jit(solution)/shard_map/ppermute | solution.py:364
  34.7 9.5 %collective-permute-done.3.refs_5_ = bf16[1,2,3,128,128]{4,3,2,1,0:T(8,128)(2,1)S(1)} collective-permute-done((bf16[1,2,3,128,128]{4,3,2,1,0:T(8,128)(2,1)}, bf16[1,2,3,128,128]{4,3,2,1,0:T(8,128)(2,1)S(1)}, u32[]{:S(2)}, u32[]{:S(2)}) %collective-permute-start.3) | collective-permute-done | bytes 196640 | tf_op jit(solution)/shard_map/ppermute | solution.py:364
  44.2 1.6 collective-permute-start.4
  45.8 2.9 %collective-permute-done.11.refs_13_ = bf16[1,2,3,128,128]{4,3,2,1,0:T(8,128)(2,1)S(1)} collective-permute-done((bf16[1,2,3,128,128]{4,3,2,1,0:T(8,128)(2,1)}, bf16[1,2,3,128,128]{4,3,2,1,0:T(8,128)(2,1)S(1)}, u32[]{:S(2)}, u32[]{:S(2)}) %collective-permute-start.11) | collective-permute-done | bytes 196640 | tf_op jit(solution)/shard_map/ppermute | solution.py:364
  48.7 6.3 %collective-permute-start.8 = (bf16[1,2,3,128,128]{4,3,2,1,0:T(8,128)(2,1)}, bf16[1,2,3,128,128]{4,3,2,1,0:T(8,128)(2,1)S(1)}, u32[]{:S(2)}, u32[]{:S(2)}) collective-permute-start(bf16[1,2,3,128,128]{4,3,2,1,0:T(8,128)(2,1)} %get-tuple-element.103), channel_id=1, source_target_pairs={{0,6},{1,15},{2,4},{3,13},{4,2},{5,11},{6,0},{7,9},{8,14},{9,7},{1... | collective-permute-start | bytes 589832 | tf_op jit(solution)/shard_map/ppermute | solution.py:364
  55.0 2.7 %collective-permute-start.12 = (bf16[1,2,3,128,128]{4,3,2,1,0:T(8,128)(2,1)}, bf16[1,2,3,128,128]{4,3,2,1,0:T(8,128)(2,1)S(1)}, u32[]{:S(2)}, u32[]{:S(2)}) collective-permute-start(bf16[1,2,3,128,128]{4,3,2,1,0:T(8,128)(2,1)} %get-tuple-element.97), channel_id=1, source_target_pairs={{0,12},{1,5},{2,14},{3,7},{4,8},{5,1},{6,10},{7,3},{8,4},{9,13},{1... | collective-permute-start | bytes 589832 | tf_op jit(solution)/shard_map/ppermute | solution.py:364
  57.8 1.8 collective-permute-start.13
  59.6 4.5 %collective-permute-start.14 = (bf16[1,2,3,128,128]{4,3,2,1,0:T(8,128)(2,1)}, bf16[1,2,3,128,128]{4,3,2,1,0:T(8,128)(2,1)}, u32[]{:S(2)}, u32[]{:S(2)}) collective-permute-start(bf16[1,2,3,128,128]{4,3,2,1,0:T(8,128)(2,1)} %get-tuple-element.107), channel_id=1, source_target_pairs={{0,14},{1,7},{2,12},{3,5},{4,10},{5,3},{6,8},{7,1},{8,6},{9,15},{1... | collective-permute-start | bytes 589832 | tf_op jit(solution)/shard_map/ppermute | solution.py:364
  64.1 3.9 %shard_map.66 = (bf16[1,2,3,128,128]{4,3,2,1,0:T(8,128)(2,1)}, bf16[1,2,3,128,128]{4,3,2,1,0:T(8,128)(2,1)}, bf16[1,2,3,128,128]{4,3,2,1,0:T(8,128)(2,1)}, bf16[...) custom-call(s32[17]{0:T(128)S(1)} %stack.116.place, ...), custom_call_target="tpu_custom_call" | custom-call | bytes 6291456 | tf_op jit(solution)/shard_map/pallas_call | solution.py:270
  68.1 1.4 collective-permute-start.10
  69.5 0.5 collective-permute-done.13.refs_15_
  70.0 2.7 %collective-permute-start.15 = (bf16[1,2,3,128,128]{4,3,2,1,0:T(8,128)(2,1)S(1)}, bf16[1,2,3,128,128]{4,3,2,1,0:T(8,128)(2,1)S(1)}, u32[]{:S(2)}, u32[]{:S(2)}) collective-permute-start(bf16[1,2,3,128,128]{4,3,2,1,0:T(8,128)(2,1)S(1)} %copy-done.15), channel_id=1, source_target_pairs={{0,15},{1,6},{2,13},{3,4},{4,11},{5,2},{6,9},{7,0},{8,7},{9,14},{1... | collective-permute-start | bytes 589832 | tf_op jit(solution)/shard_map/ppermute | solution.py:364
  72.7 1.7 collective-permute-done.14.refs_16_
  74.4 1.6 collective-permute-start.18
  76.1 0.8 collective-permute-done.10.refs_9_
  76.9 4.0 %collective-permute-start.19 = (bf16[1,2,3,128,128]{4,3,2,1,0:T(8,128)(2,1)}, bf16[1,2,3,128,128]{4,3,2,1,0:T(8,128)(2,1)S(1)}, u32[]{:S(2)}, u32[]{:S(2)}) collective-permute-start(bf16[1,2,3,128,128]{4,3,2,1,0:T(8,128)(2,1)} %get-tuple-element.116), channel_id=1, source_target_pairs={{0,1},{1,8},{2,3},{3,10},{4,5},{5,12},{6,7},{7,14},{8,9},{9,0},{10... | collective-permute-start | bytes 589832 | tf_op jit(solution)/shard_map/ppermute | solution.py:364
  81.0 1.0 collective-permute-start.20
  82.0 4.3 %collective-permute-start.23 = (bf16[1,2,3,128,128]{4,3,2,1,0:T(8,128)(2,1)}, bf16[1,2,3,128,128]{4,3,2,1,0:T(8,128)(2,1)S(1)}, u32[]{:S(2)}, u32[]{:S(2)}) collective-permute-start(bf16[1,2,3,128,128]{4,3,2,1,0:T(8,128)(2,1)} %get-tuple-element.115), channel_id=1, source_target_pairs={{0,8},{1,1},{2,10},{3,3},{4,12},{5,5},{6,14},{7,7},{8,0},{9,9},{10... | collective-permute-start | bytes 589832 | tf_op jit(solution)/shard_map/ppermute | solution.py:364
  86.3 12.5 %collective-permute-start.25 = (bf16[1,2,3,128,128]{4,3,2,1,0:T(8,128)(2,1)}, bf16[1,2,3,128,128]{4,3,2,1,0:T(8,128)(2,1)S(1)}, u32[]{:S(2)}, u32[]{:S(2)}) collective-permute-start(bf16[1,2,3,128,128]{4,3,2,1,0:T(8,128)(2,1)} %get-tuple-element.119), channel_id=1, source_target_pairs={{0,9},{1,0},{2,11},{3,2},{4,13},{5,4},{6,15},{7,6},{8,1},{9,8},{10... | collective-permute-start | bytes 589832 | tf_op jit(solution)/shard_map/ppermute | solution.py:364
  98.8 1.9 collective-permute-start.27
  100.8 11.7 %shard_map.65 = bf16[16,2,128,128]{3,2,1,0:T(8,128)(2,1)} custom-call(s32[33]{0:T(128)S(1)} %concatenate.6.refs_0_, s32[16,3]{1,0:T(8,128)S(1)} %copy.7.refs_1_, bf16[1,2,3,128,128]{4,3,2,1,0:T(8,128)(2,1)} %copy-done.3, bf16[1,2,3,128,128]{4,3,2,1,0:T(8,128)(2,1)} %copy-done.5, bf16[1,2,3,128,128]{4,3,2,1,0:T(8,128)(2,1)} %copy-done.7, ...), custom_call_target="tpu_custom_call" | custom-call | flops 12884901888 | bytes 8388608 | tf_op jit(solution)/shard_map/pallas_call | solution.py:167
  113.1 3.2 %collective-permute-start.29 = (bf16[1,2,3,128,128]{4,3,2,1,0:T(8,128)(2,1)S(1)}, bf16[1,2,3,128,128]{4,3,2,1,0:T(8,128)(2,1)S(1)}, u32[]{:S(2)}, u32[]{:S(2)}) collective-permute-start(bf16[1,2,3,128,128]{4,3,2,1,0:T(8,128)(2,1)S(1)} %copy-done.20), channel_id=1, source_target_pairs={{0,11},{1,2},{2,9},{3,0},{4,15},{5,6},{6,13},{7,4},{8,3},{9,10},{1... | collective-permute-start | bytes 589832 | tf_op jit(solution)/shard_map/ppermute | solution.py:364
  116.4 1.8 collective-permute-start.24
  118.2 1.4 collective-permute-start.26
  119.7 1.4 collective-permute-start.30
  121.2 2.1 collective-permute-done.29.refs_13_
  123.3 2.4 %collective-permute-start.28 = (bf16[1,2,3,128,128]{4,3,2,1,0:T(8,128)(2,1)S(1)}, bf16[1,2,3,128,128]{4,3,2,1,0:T(8,128)(2,1)S(1)}, u32[]{:S(2)}, u32[]{:S(2)}) collective-permute-start(bf16[1,2,3,128,128]{4,3,2,1,0:T(8,128)(2,1)S(1)} %copy-done.10), channel_id=1, source_target_pairs={{0,7},{1,14},{2,5},{3,12},{4,3},{5,10},{6,1},{7,8},{8,15},{9,6},{1... | collective-permute-start | bytes 589832 | tf_op jit(solution)/shard_map/ppermute | solution.py:364
  125.8 10.1 %collective-permute-start.31 = (bf16[1,2,3,128,128]{4,3,2,1,0:T(8,128)(2,1)S(1)}, bf16[1,2,3,128,128]{4,3,2,1,0:T(8,128)(2,1)S(1)}, u32[]{:S(2)}, u32[]{:S(2)}) collective-permute-start(bf16[1,2,3,128,128]{4,3,2,1,0:T(8,128)(2,1)S(1)} %copy-done.8), channel_id=1, source_target_pairs={{0,13},{1,4},{2,15},{3,6},{4,9},{5,0},{6,11},{7,2},{8,5},{9,12},{1... | collective-permute-start | bytes 589832 | tf_op jit(solution)/shard_map/ppermute | solution.py:364
  136.2 1.2 collective-permute-done.26.refs_8_
  137.5 7.8 %collective-permute-start.33 = (bf16[1,2,3,128,128]{4,3,2,1,0:T(8,128)(2,1)S(1)}, bf16[1,2,3,128,128]{4,3,2,1,0:T(8,128)(2,1)S(1)}, u32[]{:S(2)}, u32[]{:S(2)}) collective-permute-start(bf16[1,2,3,128,128]{4,3,2,1,0:T(8,128)(2,1)S(1)} %copy-done.4), channel_id=1, source_target_pairs={{0,15},{1,6},{2,13},{3,4},{4,11},{5,2},{6,9},{7,0},{8,7},{9,14},{1... | collective-permute-start | bytes 589832 | tf_op jit(solution)/shard_map/ppermute | solution.py:364
  145.3 1.8 collective-permute-done.31.refs_15_
  147.1 6.7 %collective-permute-done.32.refs_16_ = bf16[1,2,3,128,128]{4,3,2,1,0:T(8,128)(2,1)S(1)} collective-permute-done((bf16[1,2,3,128,128]{4,3,2,1,0:T(8,128)(2,1)S(1)}, bf16[1,2,3,128,128]{4,3,2,1,0:T(8,128)(2,1)S(1)}, u32[]{:S(2)}, u32[]{:S(2)}) %collective-permute-start.32) | collective-permute-done | bytes 196640 | tf_op jit(solution)/shard_map/ppermute | solution.py:364
  153.8 4.8 %collective-permute-done.33.refs_17_ = bf16[1,2,3,128,128]{4,3,2,1,0:T(8,128)(2,1)S(1)} collective-permute-done((bf16[1,2,3,128,128]{4,3,2,1,0:T(8,128)(2,1)S(1)}, bf16[1,2,3,128,128]{4,3,2,1,0:T(8,128)(2,1)S(1)}, u32[]{:S(2)}, u32[]{:S(2)}) %collective-permute-start.33) | collective-permute-done | bytes 196640 | tf_op jit(solution)/shard_map/ppermute | solution.py:364
  158.7 0.6 copy-done.43
  159.3 4.2 %all-to-all-start = ((bf16[16,2,128,128]{3,2,1,0:T(8,128)(2,1)}), bf16[16,2,128,128]{3,2,1,0:T(8,128)(2,1)S(1)}, u32[]{:S(2)}, u32[]{:S(2)}) async-start(bf16[16,2,128,128]{3,2,1,0:T(8,128)(2,1)} %shard_map.65), calls=%async_computation | async-start | bytes 2097152 | tf_op jit(solution)/shard_map/all_to_all | solution.py:344
  163.5 10.9 %shard_map.67 = (bf16[1,2,128,128]{3,2,1,0:T(8,128)(2,1)S(1)}, bf16[1,2,128,128]{3,2,1,0:T(8,128)(2,1)S(1)}, bf16[1,2,128,128]{3,2,1,0:T(8,128)(2,1)S(1)}, bf16[...) custom-call(s32[33]{0:T(128)S(1)} %concatenate.6.refs_0_, ...), custom_call_target="tpu_custom_call" | custom-call | flops 12884901888 | bytes 8388608 | tf_op jit(solution)/shard_map/pallas_call | solution.py:167
  174.5 0.7 collective-permute-start.34
  175.2 4.0 %collective-permute-start.35 = (bf16[1,2,128,128]{3,2,1,0:T(8,128)(2,1)S(1)}, bf16[1,2,128,128]{3,2,1,0:T(8,128)(2,1)S(1)}, u32[]{:S(2)}, u32[]{:S(2)}) collective-permute-start(bf16[1,2,128,128]{3,2,1,0:T(8,128)(2,1)S(1)} %get-tuple-element.154), channel_id=1, source_target_pairs={{0,1},{1,8},{2,3},{3,10},{4,5},{5,12},{6,7},{7,14},{8,9},{9,0},{10... | collective-permute-start | bytes 196616 | tf_op jit(solution)/shard_map/ppermute | solution.py:380
  179.1 1.5 collective-permute-start.36
  180.6 1.5 collective-permute-start.38
  182.1 10.5 %collective-permute-start.39 = (bf16[1,2,128,128]{3,2,1,0:T(8,128)(2,1)S(1)}, bf16[1,2,128,128]{3,2,1,0:T(8,128)(2,1)S(1)}, u32[]{:S(2)}, u32[]{:S(2)}) collective-permute-start(bf16[1,2,128,128]{3,2,1,0:T(8,128)(2,1)S(1)} %get-tuple-element.158), channel_id=1, source_target_pairs={{0,5},{1,12},{2,7},{3,14},{4,1},{5,8},{6,3},{7,10},{8,13},{9,4},{1... | collective-permute-start | bytes 196616 | tf_op jit(solution)/shard_map/ppermute | solution.py:380
  192.6 2.3 %collective-permute-done.35.refs_1_ = bf16[1,2,128,128]{3,2,1,0:T(8,128)(2,1)S(1)} collective-permute-done((bf16[1,2,128,128]{3,2,1,0:T(8,128)(2,1)S(1)}, bf16[1,2,128,128]{3,2,1,0:T(8,128)(2,1)S(1)}, u32[]{:S(2)}, u32[]{:S(2)}) %collective-permute-start.35) | collective-permute-done | bytes 65568 | tf_op jit(solution)/shard_map/ppermute | solution.py:380
  194.9 1.7 collective-permute-start.40
  196.6 0.6 collective-permute-done.37.refs_3_
  197.3 3.3 %collective-permute-start.42 = (bf16[1,2,128,128]{3,2,1,0:T(8,128)(2,1)S(1)}, bf16[1,2,128,128]{3,2,1,0:T(8,128)(2,1)S(1)}, u32[]{:S(2)}, u32[]{:S(2)}) collective-permute-start(bf16[1,2,128,128]{3,2,1,0:T(8,128)(2,1)S(1)} %get-tuple-element.161), channel_id=1, source_target_pairs={{0,8},{1,1},{2,10},{3,3},{4,12},{5,5},{6,14},{7,7},{8,0},{9,9},{10... | collective-permute-start | bytes 196616 | tf_op jit(solution)/shard_map/ppermute | solution.py:380
  200.7 1.7 collective-permute-start.44
  202.3 1.1 collective-permute-start.45
  203.5 1.4 collective-permute-start.46
  204.9 0.8 collective-permute-done.42.refs_8_
  206.0 2.9 %collective-permute-start.48 = (bf16[1,2,128,128]{3,2,1,0:T(8,128)(2,1)S(1)}, bf16[1,2,128,128]{3,2,1,0:T(8,128)(2,1)S(1)}, u32[]{:S(2)}, u32[]{:S(2)}) collective-permute-start(bf16[1,2,128,128]{3,2,1,0:T(8,128)(2,1)S(1)} %get-tuple-element.167), channel_id=1, source_target_pairs={{0,14},{1,7},{2,12},{3,5},{4,10},{5,3},{6,8},{7,1},{8,6},{9,15},{1... | collective-permute-start | bytes 196616 | tf_op jit(solution)/shard_map/ppermute | solution.py:380
  208.9 0.7 collective-permute-start.49
  210.0 1.3 collective-permute-done.47.refs_13_
  211.3 2.1 collective-permute-done.48.refs_14_
  213.5 1.2 collective-permute-done.49.refs_15_
  214.7 2.1 shard_map.68
  (135 shorter events, 2.4 us)
Async XLA Ops:
  0.0 86.3 %collective-permute-start.16 = (bf16[8,1024,128]{2,1,0:T(8,128)(2,1)}, bf16[8,1024,128]{2,1,0:T(8,128)(2,1)S(1)}, u32[]{:S(2)}, u32[]{:S(2)}) collective-permute-start(bf16[8,1024,128]{2,1,0:T(8,128)(2,1)} %refs_18_.3), channel_id=1, source_target_pairs={{0,1},{1,0},{2,3},{3,2},{4,5},{5,4},{6,7},{7,6},{8,9},{9,8},{10,11... | collective-permute-start | bytes 6291464 | tf_op jit(solution)/shard_map/ppermute | solution.py:334
  0.5 98.4 %collective-permute-start.17 = (bf16[8,1024,128]{2,1,0:T(8,128)(2,1)}, bf16[8,1024,128]{2,1,0:T(8,128)(2,1)}, u32[]{:S(2)}, u32[]{:S(2)}) collective-permute-start(bf16[8,1024,128]{2,1,0:T(8,128)(2,1)} %refs_20_.3), channel_id=1, source_target_pairs={{0,1},{1,0},{2,3},{3,2},{4,5},{5,4},{6,7},{7,6},{8,9},{9,8},{10,11... | collective-permute-start | bytes 6291464 | tf_op jit(solution)/shard_map/ppermute | solution.py:334
  4.6 7.2 %collective-permute-start = (bf16[1,2,3,128,128]{4,3,2,1,0:T(8,128)(2,1)}, bf16[1,2,3,128,128]{4,3,2,1,0:T(8,128)(2,1)S(1)}, u32[]{:S(2)}, u32[]{:S(2)}) collective-permute-start(bf16[1,2,3,128,128]{4,3,2,1,0:T(8,128)(2,1)} %get-tuple-element.87), channel_id=1, source_target_pairs={{0,0},{1,9},{2,2},{3,11},{4,4},{5,13},{6,6},{7,15},{8,8},{9,1},{10... | collective-permute-start | bytes 589832 | tf_op jit(solution)/shard_map/ppermute | solution.py:364
  6.2 20.2 %collective-permute-start.1 = (bf16[1,2,3,128,128]{4,3,2,1,0:T(8,128)(2,1)}, bf16[1,2,3,128,128]{4,3,2,1,0:T(8,128)(2,1)S(1)}, u32[]{:S(2)}, u32[]{:S(2)}) collective-permute-start(bf16[1,2,3,128,128]{4,3,2,1,0:T(8,128)(2,1)} %get-tuple-element.88), channel_id=1, source_target_pairs={{0,1},{1,8},{2,3},{3,10},{4,5},{5,12},{6,7},{7,14},{8,9},{9,0},{10... | collective-permute-start | bytes 589832 | tf_op jit(solution)/shard_map/ppermute | solution.py:364
  10.3 16.0 %collective-permute-start.2 = (bf16[1,2,3,128,128]{4,3,2,1,0:T(8,128)(2,1)}, bf16[1,2,3,128,128]{4,3,2,1,0:T(8,128)(2,1)S(1)}, u32[]{:S(2)}, u32[]{:S(2)}) collective-permute-start(bf16[1,2,3,128,128]{4,3,2,1,0:T(8,128)(2,1)} %get-tuple-element.89), channel_id=1, source_target_pairs={{0,2},{1,11},{2,0},{3,9},{4,6},{5,15},{6,4},{7,13},{8,10},{9,3},{1... | collective-permute-start | bytes 589832 | tf_op jit(solution)/shard_map/ppermute | solution.py:364
  11.8 56.2 %copy-start.3 = (bf16[1,2,3,128,128]{4,3,2,1,0:T(8,128)(2,1)}, bf16[1,2,3,128,128]{4,3,2,1,0:T(8,128)(2,1)S(1)}, u32[]{:S(2)}) copy-start(bf16[1,2,3,128,128]{4,3,2,1,0:T(8,128)(2,1)S(1)} %collective-permute-done.refs_2_) | copy-start | bytes 589828
  11.8 17.5 %collective-permute-start.5 = (bf16[1,2,3,128,128]{4,3,2,1,0:T(8,128)(2,1)}, bf16[1,2,3,128,128]{4,3,2,1,0:T(8,128)(2,1)S(1)}, u32[]{:S(2)}, u32[]{:S(2)}) collective-permute-start(bf16[1,2,3,128,128]{4,3,2,1,0:T(8,128)(2,1)} %get-tuple-element.96), channel_id=1, source_target_pairs={{0,8},{1,1},{2,10},{3,3},{4,12},{5,5},{6,14},{7,7},{8,0},{9,9},{10... | collective-permute-start | bytes 589832 | tf_op jit(solution)/shard_map/ppermute | solution.py:364
  26.3 41.7 %copy-start.5 = (bf16[1,2,3,128,128]{4,3,2,1,0:T(8,128)(2,1)}, bf16[1,2,3,128,128]{4,3,2,1,0:T(8,128)(2,1)S(1)}, u32[]{:S(2)}) copy-start(bf16[1,2,3,128,128]{4,3,2,1,0:T(8,128)(2,1)S(1)} %collective-permute-done.1.refs_3_) | copy-start | bytes 589828
  26.3 3.5 %collective-permute-start.7 = (bf16[1,2,3,128,128]{4,3,2,1,0:T(8,128)(2,1)}, bf16[1,2,3,128,128]{4,3,2,1,0:T(8,128)(2,1)S(1)}, u32[]{:S(2)}, u32[]{:S(2)}) collective-permute-start(bf16[1,2,3,128,128]{4,3,2,1,0:T(8,128)(2,1)} %get-tuple-element.101), channel_id=1, source_target_pairs={{0,9},{1,0},{2,11},{3,2},{4,13},{5,4},{6,15},{7,6},{8,1},{9,8},{10... | collective-permute-start | bytes 589832 | tf_op jit(solution)/shard_map/ppermute | solution.py:364
  26.3 41.7 %copy-start.7 = (bf16[1,2,3,128,128]{4,3,2,1,0:T(8,128)(2,1)}, bf16[1,2,3,128,128]{4,3,2,1,0:T(8,128)(2,1)S(1)}, u32[]{:S(2)}) copy-start(bf16[1,2,3,128,128]{4,3,2,1,0:T(8,128)(2,1)S(1)} %collective-permute-done.2.refs_4_) | copy-start | bytes 589828
  26.3 17.8 %collective-permute-start.3 = (bf16[1,2,3,128,128]{4,3,2,1,0:T(8,128)(2,1)}, bf16[1,2,3,128,128]{4,3,2,1,0:T(8,128)(2,1)S(1)}, u32[]{:S(2)}, u32[]{:S(2)}) collective-permute-start(bf16[1,2,3,128,128]{4,3,2,1,0:T(8,128)(2,1)} %get-tuple-element.90), channel_id=1, source_target_pairs={{0,3},{1,10},{2,1},{3,8},{4,7},{5,14},{6,5},{7,12},{8,11},{9,2},{1... | collective-permute-start | bytes 589832 | tf_op jit(solution)/shard_map/ppermute | solution.py:364
  29.3 16.5 %collective-permute-start.9 = (bf16[1,2,3,128,128]{4,3,2,1,0:T(8,128)(2,1)}, bf16[1,2,3,128,128]{4,3,2,1,0:T(8,128)(2,1)S(1)}, u32[]{:S(2)}, u32[]{:S(2)}) collective-permute-start(bf16[1,2,3,128,128]{4,3,2,1,0:T(8,128)(2,1)} %get-tuple-element.106), channel_id=1, source_target_pairs={{0,10},{1,3},{2,8},{3,1},{4,14},{5,7},{6,12},{7,5},{8,2},{9,11},{1... | collective-permute-start | bytes 589832 | tf_op jit(solution)/shard_map/ppermute | solution.py:364
  29.8 18.9 %collective-permute-start.11 = (bf16[1,2,3,128,128]{4,3,2,1,0:T(8,128)(2,1)}, bf16[1,2,3,128,128]{4,3,2,1,0:T(8,128)(2,1)S(1)}, u32[]{:S(2)}, u32[]{:S(2)}) collective-permute-start(bf16[1,2,3,128,128]{4,3,2,1,0:T(8,128)(2,1)} %get-tuple-element.92), channel_id=1, source_target_pairs={{0,11},{1,2},{2,9},{3,0},{4,15},{5,6},{6,13},{7,4},{8,3},{9,10},{1... | collective-permute-start | bytes 589832 | tf_op jit(solution)/shard_map/ppermute | solution.py:364
  44.2 10.8 %collective-permute-start.4 = (bf16[1,2,3,128,128]{4,3,2,1,0:T(8,128)(2,1)}, bf16[1,2,3,128,128]{4,3,2,1,0:T(8,128)(2,1)S(1)}, u32[]{:S(2)}, u32[]{:S(2)}) collective-permute-start(bf16[1,2,3,128,128]{4,3,2,1,0:T(8,128)(2,1)} %get-tuple-element.93), channel_id=1, source_target_pairs={{0,4},{1,13},{2,6},{3,15},{4,0},{5,9},{6,2},{7,11},{8,12},{9,5},{1... | collective-permute-start | bytes 589832 | tf_op jit(solution)/shard_map/ppermute | solution.py:364
  45.8 11.9 %collective-permute-start.6 = (bf16[1,2,3,128,128]{4,3,2,1,0:T(8,128)(2,1)}, bf16[1,2,3,128,128]{4,3,2,1,0:T(8,128)(2,1)S(1)}, u32[]{:S(2)}, u32[]{:S(2)}) collective-permute-start(bf16[1,2,3,128,128]{4,3,2,1,0:T(8,128)(2,1)} %get-tuple-element.98), channel_id=1, source_target_pairs={{0,5},{1,12},{2,7},{3,14},{4,1},{5,8},{6,3},{7,10},{8,13},{9,4},{1... | collective-permute-start | bytes 589832 | tf_op jit(solution)/shard_map/ppermute | solution.py:364
  48.7 10.9 %collective-permute-start.8 = (bf16[1,2,3,128,128]{4,3,2,1,0:T(8,128)(2,1)}, bf16[1,2,3,128,128]{4,3,2,1,0:T(8,128)(2,1)S(1)}, u32[]{:S(2)}, u32[]{:S(2)}) collective-permute-start(bf16[1,2,3,128,128]{4,3,2,1,0:T(8,128)(2,1)} %get-tuple-element.103), channel_id=1, source_target_pairs={{0,6},{1,15},{2,4},{3,13},{4,2},{5,11},{6,0},{7,9},{8,14},{9,7},{1... | collective-permute-start | bytes 589832 | tf_op jit(solution)/shard_map/ppermute | solution.py:364
  55.0 13.1 %collective-permute-start.12 = (bf16[1,2,3,128,128]{4,3,2,1,0:T(8,128)(2,1)}, bf16[1,2,3,128,128]{4,3,2,1,0:T(8,128)(2,1)S(1)}, u32[]{:S(2)}, u32[]{:S(2)}) collective-permute-start(bf16[1,2,3,128,128]{4,3,2,1,0:T(8,128)(2,1)} %get-tuple-element.97), channel_id=1, source_target_pairs={{0,12},{1,5},{2,14},{3,7},{4,8},{5,1},{6,10},{7,3},{8,4},{9,13},{1... | collective-permute-start | bytes 589832 | tf_op jit(solution)/shard_map/ppermute | solution.py:364
  57.8 12.2 %collective-permute-start.13 = (bf16[1,2,3,128,128]{4,3,2,1,0:T(8,128)(2,1)}, bf16[1,2,3,128,128]{4,3,2,1,0:T(8,128)(2,1)S(1)}, u32[]{:S(2)}, u32[]{:S(2)}) collective-permute-start(bf16[1,2,3,128,128]{4,3,2,1,0:T(8,128)(2,1)} %get-tuple-element.102), channel_id=1, source_target_pairs={{0,13},{1,4},{2,15},{3,6},{4,9},{5,0},{6,11},{7,2},{8,5},{9,12},{1... | collective-permute-start | bytes 589832 | tf_op jit(solution)/shard_map/ppermute | solution.py:364
  59.6 14.8 %collective-permute-start.14 = (bf16[1,2,3,128,128]{4,3,2,1,0:T(8,128)(2,1)}, bf16[1,2,3,128,128]{4,3,2,1,0:T(8,128)(2,1)}, u32[]{:S(2)}, u32[]{:S(2)}) collective-permute-start(bf16[1,2,3,128,128]{4,3,2,1,0:T(8,128)(2,1)} %get-tuple-element.107), channel_id=1, source_target_pairs={{0,14},{1,7},{2,12},{3,5},{4,10},{5,3},{6,8},{7,1},{8,6},{9,15},{1... | collective-permute-start | bytes 589832 | tf_op jit(solution)/shard_map/ppermute | solution.py:364
  68.1 8.8 %collective-permute-start.10 = (bf16[1,2,3,128,128]{4,3,2,1,0:T(8,128)(2,1)}, bf16[1,2,3,128,128]{4,3,2,1,0:T(8,128)(2,1)S(1)}, u32[]{:S(2)}, u32[]{:S(2)}) collective-permute-start(bf16[1,2,3,128,128]{4,3,2,1,0:T(8,128)(2,1)} %get-tuple-element.108), channel_id=1, source_target_pairs={{0,7},{1,14},{2,5},{3,12},{4,3},{5,10},{6,1},{7,8},{8,15},{9,6},{1... | collective-permute-start | bytes 589832 | tf_op jit(solution)/shard_map/ppermute | solution.py:364
  70.0 11.1 %collective-permute-start.15 = (bf16[1,2,3,128,128]{4,3,2,1,0:T(8,128)(2,1)S(1)}, bf16[1,2,3,128,128]{4,3,2,1,0:T(8,128)(2,1)S(1)}, u32[]{:S(2)}, u32[]{:S(2)}) collective-permute-start(bf16[1,2,3,128,128]{4,3,2,1,0:T(8,128)(2,1)S(1)} %copy-done.15), channel_id=1, source_target_pairs={{0,15},{1,6},{2,13},{3,4},{4,11},{5,2},{6,9},{7,0},{8,7},{9,14},{1... | collective-permute-start | bytes 589832 | tf_op jit(solution)/shard_map/ppermute | solution.py:364
  74.4 7.6 %collective-permute-start.18 = (bf16[1,2,3,128,128]{4,3,2,1,0:T(8,128)(2,1)}, bf16[1,2,3,128,128]{4,3,2,1,0:T(8,128)(2,1)S(1)}, u32[]{:S(2)}, u32[]{:S(2)}) collective-permute-start(bf16[1,2,3,128,128]{4,3,2,1,0:T(8,128)(2,1)} %get-tuple-element.112), channel_id=1, source_target_pairs={{0,0},{1,9},{2,2},{3,11},{4,4},{5,13},{6,6},{7,15},{8,8},{9,1},{10... | collective-permute-start | bytes 589832 | tf_op jit(solution)/shard_map/ppermute | solution.py:364
  76.9 36.1 %collective-permute-start.19 = (bf16[1,2,3,128,128]{4,3,2,1,0:T(8,128)(2,1)}, bf16[1,2,3,128,128]{4,3,2,1,0:T(8,128)(2,1)S(1)}, u32[]{:S(2)}, u32[]{:S(2)}) collective-permute-start(bf16[1,2,3,128,128]{4,3,2,1,0:T(8,128)(2,1)} %get-tuple-element.116), channel_id=1, source_target_pairs={{0,1},{1,8},{2,3},{3,10},{4,5},{5,12},{6,7},{7,14},{8,9},{9,0},{10... | collective-permute-start | bytes 589832 | tf_op jit(solution)/shard_map/ppermute | solution.py:364
  81.0 42.3 %copy-start.10 = (bf16[1,2,3,128,128]{4,3,2,1,0:T(8,128)(2,1)S(1)}, bf16[1,2,3,128,128]{4,3,2,1,0:T(8,128)(2,1)}, u32[]{:S(2)}) copy-start(bf16[1,2,3,128,128]{4,3,2,1,0:T(8,128)(2,1)} %get-tuple-element.148) | copy-start | bytes 589828
  81.0 44.8 %copy-start.8 = (bf16[1,2,3,128,128]{4,3,2,1,0:T(8,128)(2,1)S(1)}, bf16[1,2,3,128,128]{4,3,2,1,0:T(8,128)(2,1)}, u32[]{:S(2)}) copy-start(bf16[1,2,3,128,128]{4,3,2,1,0:T(8,128)(2,1)} %get-tuple-element.141) | copy-start | bytes 589828
  81.0 54.9 %copy-start.6 = (bf16[1,2,3,128,128]{4,3,2,1,0:T(8,128)(2,1)S(1)}, bf16[1,2,3,128,128]{4,3,2,1,0:T(8,128)(2,1)}, u32[]{:S(2)}) copy-start(bf16[1,2,3,128,128]{4,3,2,1,0:T(8,128)(2,1)} %get-tuple-element.147) | copy-start | bytes 589828
  81.0 56.5 %copy-start.4 = (bf16[1,2,3,128,128]{4,3,2,1,0:T(8,128)(2,1)S(1)}, bf16[1,2,3,128,128]{4,3,2,1,0:T(8,128)(2,1)}, u32[]{:S(2)}) copy-start(bf16[1,2,3,128,128]{4,3,2,1,0:T(8,128)(2,1)} %get-tuple-element.151) | copy-start | bytes 589828
  81.0 35.3 %collective-permute-start.20 = (bf16[1,2,3,128,128]{4,3,2,1,0:T(8,128)(2,1)}, bf16[1,2,3,128,128]{4,3,2,1,0:T(8,128)(2,1)S(1)}, u32[]{:S(2)}, u32[]{:S(2)}) collective-permute-start(bf16[1,2,3,128,128]{4,3,2,1,0:T(8,128)(2,1)} %get-tuple-element.120), channel_id=1, source_target_pairs={{0,2},{1,11},{2,0},{3,9},{4,6},{5,15},{6,4},{7,13},{8,10},{9,3},{1... | collective-permute-start | bytes 589832 | tf_op jit(solution)/shard_map/ppermute | solution.py:364
  82.0 30.5 %collective-permute-start.23 = (bf16[1,2,3,128,128]{4,3,2,1,0:T(8,128)(2,1)}, bf16[1,2,3,128,128]{4,3,2,1,0:T(8,128)(2,1)S(1)}, u32[]{:S(2)}, u32[]{:S(2)}) collective-permute-start(bf16[1,2,3,128,128]{4,3,2,1,0:T(8,128)(2,1)} %get-tuple-element.115), channel_id=1, source_target_pairs={{0,8},{1,1},{2,10},{3,3},{4,12},{5,5},{6,14},{7,7},{8,0},{9,9},{10... | collective-permute-start | bytes 589832 | tf_op jit(solution)/shard_map/ppermute | solution.py:364
  86.3 26.8 %collective-permute-start.25 = (bf16[1,2,3,128,128]{4,3,2,1,0:T(8,128)(2,1)}, bf16[1,2,3,128,128]{4,3,2,1,0:T(8,128)(2,1)S(1)}, u32[]{:S(2)}, u32[]{:S(2)}) collective-permute-start(bf16[1,2,3,128,128]{4,3,2,1,0:T(8,128)(2,1)} %get-tuple-element.119), channel_id=1, source_target_pairs={{0,9},{1,0},{2,11},{3,2},{4,13},{5,4},{6,15},{7,6},{8,1},{9,8},{10... | collective-permute-start | bytes 589832 | tf_op jit(solution)/shard_map/ppermute | solution.py:364
  98.8 19.3 %collective-permute-start.27 = (bf16[1,2,3,128,128]{4,3,2,1,0:T(8,128)(2,1)}, bf16[1,2,3,128,128]{4,3,2,1,0:T(8,128)(2,1)S(1)}, u32[]{:S(2)}, u32[]{:S(2)}) collective-permute-start(bf16[1,2,3,128,128]{4,3,2,1,0:T(8,128)(2,1)} %get-tuple-element.123), channel_id=1, source_target_pairs={{0,10},{1,3},{2,8},{3,1},{4,14},{5,7},{6,12},{7,5},{8,2},{9,11},{1... | collective-permute-start | bytes 589832 | tf_op jit(solution)/shard_map/ppermute | solution.py:364
  112.6 41.2 %copy-start.25 = (bf16[1,2,3,128,128]{4,3,2,1,0:T(8,128)(2,1)}, bf16[1,2,3,128,128]{4,3,2,1,0:T(8,128)(2,1)S(1)}, u32[]{:S(2)}) copy-start(bf16[1,2,3,128,128]{4,3,2,1,0:T(8,128)(2,1)S(1)} %collective-permute-done.23.refs_10_) | copy-start | bytes 589828
  112.6 7.1 %collective-permute-start.21 = (bf16[1,2,3,128,128]{4,3,2,1,0:T(8,128)(2,1)S(1)}, bf16[1,2,3,128,128]{4,3,2,1,0:T(8,128)(2,1)S(1)}, u32[]{:S(2)}, u32[]{:S(2)}) collective-permute-start(bf16[1,2,3,128,128]{4,3,2,1,0:T(8,128)(2,1)S(1)} %copy-done.23), channel_id=1, source_target_pairs={{0,3},{1,10},{2,1},{3,8},{4,7},{5,14},{6,5},{7,12},{8,11},{9,2},{1... | collective-permute-start | bytes 589832 | tf_op jit(solution)/shard_map/ppermute | solution.py:364
  113.0 40.8 %copy-start.19 = (bf16[1,2,3,128,128]{4,3,2,1,0:T(8,128)(2,1)}, bf16[1,2,3,128,128]{4,3,2,1,0:T(8,128)(2,1)S(1)}, u32[]{:S(2)}) copy-start(bf16[1,2,3,128,128]{4,3,2,1,0:T(8,128)(2,1)S(1)} %collective-permute-done.19.refs_3_) | copy-start | bytes 589828
  113.0 12.7 %collective-permute-start.22 = (bf16[1,2,3,128,128]{4,3,2,1,0:T(8,128)(2,1)S(1)}, bf16[1,2,3,128,128]{4,3,2,1,0:T(8,128)(2,1)S(1)}, u32[]{:S(2)}, u32[]{:S(2)}) collective-permute-start(bf16[1,2,3,128,128]{4,3,2,1,0:T(8,128)(2,1)S(1)} %copy-done.17), channel_id=1, source_target_pairs={{0,4},{1,13},{2,6},{3,15},{4,0},{5,9},{6,2},{7,11},{8,12},{9,5},{1... | collective-permute-start | bytes 589832 | tf_op jit(solution)/shard_map/ppermute | solution.py:364
  113.1 50.4 %copy-start.27 = (bf16[1,2,3,128,128]{4,3,2,1,0:T(8,128)(2,1)}, bf16[1,2,3,128,128]{4,3,2,1,0:T(8,128)(2,1)S(1)}, u32[]{:S(2)}) copy-start(bf16[1,2,3,128,128]{4,3,2,1,0:T(8,128)(2,1)S(1)} %collective-permute-done.25.refs_11_) | copy-start | bytes 589828
  113.1 10.2 %collective-permute-start.29 = (bf16[1,2,3,128,128]{4,3,2,1,0:T(8,128)(2,1)S(1)}, bf16[1,2,3,128,128]{4,3,2,1,0:T(8,128)(2,1)S(1)}, u32[]{:S(2)}, u32[]{:S(2)}) collective-permute-start(bf16[1,2,3,128,128]{4,3,2,1,0:T(8,128)(2,1)S(1)} %copy-done.20), channel_id=1, source_target_pairs={{0,11},{1,2},{2,9},{3,0},{4,15},{5,6},{6,13},{7,4},{8,3},{9,10},{1... | collective-permute-start | bytes 589832 | tf_op jit(solution)/shard_map/ppermute | solution.py:364
  116.4 47.1 %copy-start.22 = (bf16[1,2,3,128,128]{4,3,2,1,0:T(8,128)(2,1)}, bf16[1,2,3,128,128]{4,3,2,1,0:T(8,128)(2,1)S(1)}, u32[]{:S(2)}) copy-start(bf16[1,2,3,128,128]{4,3,2,1,0:T(8,128)(2,1)S(1)} %collective-permute-done.20.refs_4_) | copy-start | bytes 589828
  116.4 19.5 %collective-permute-start.24 = (bf16[1,2,3,128,128]{4,3,2,1,0:T(8,128)(2,1)S(1)}, bf16[1,2,3,128,128]{4,3,2,1,0:T(8,128)(2,1)S(1)}, u32[]{:S(2)}, u32[]{:S(2)}) collective-permute-start(bf16[1,2,3,128,128]{4,3,2,1,0:T(8,128)(2,1)S(1)} %copy-done.14), channel_id=1, source_target_pairs={{0,5},{1,12},{2,7},{3,14},{4,1},{5,8},{6,3},{7,10},{8,13},{9,4},{1... | collective-permute-start | bytes 589832 | tf_op jit(solution)/shard_map/ppermute | solution.py:364
  118.2 45.3 %copy-start.28 = (bf16[1,2,3,128,128]{4,3,2,1,0:T(8,128)(2,1)}, bf16[1,2,3,128,128]{4,3,2,1,0:T(8,128)(2,1)S(1)}, u32[]{:S(2)}) copy-start(bf16[1,2,3,128,128]{4,3,2,1,0:T(8,128)(2,1)S(1)} %collective-permute-done.27.refs_12_) | copy-start | bytes 589828
  118.2 19.3 %collective-permute-start.26 = (bf16[1,2,3,128,128]{4,3,2,1,0:T(8,128)(2,1)S(1)}, bf16[1,2,3,128,128]{4,3,2,1,0:T(8,128)(2,1)S(1)}, u32[]{:S(2)}, u32[]{:S(2)}) collective-permute-start(bf16[1,2,3,128,128]{4,3,2,1,0:T(8,128)(2,1)S(1)} %copy-done.12), channel_id=1, source_target_pairs={{0,6},{1,15},{2,4},{3,13},{4,2},{5,11},{6,0},{7,9},{8,14},{9,7},{1... | collective-permute-start | bytes 589832 | tf_op jit(solution)/shard_map/ppermute | solution.py:364
  119.7 43.8 %copy-start.32 = (bf16[1,2,3,128,128]{4,3,2,1,0:T(8,128)(2,1)}, bf16[1,2,3,128,128]{4,3,2,1,0:T(8,128)(2,1)S(1)}, u32[]{:S(2)}) copy-start(bf16[1,2,3,128,128]{4,3,2,1,0:T(8,128)(2,1)S(1)} %collective-permute-done.21.refs_5_) | copy-start | bytes 589828
  119.7 25.6 %collective-permute-start.30 = (bf16[1,2,3,128,128]{4,3,2,1,0:T(8,128)(2,1)S(1)}, bf16[1,2,3,128,128]{4,3,2,1,0:T(8,128)(2,1)S(1)}, u32[]{:S(2)}, u32[]{:S(2)}) collective-permute-start(bf16[1,2,3,128,128]{4,3,2,1,0:T(8,128)(2,1)S(1)} %copy-done.9), channel_id=1, source_target_pairs={{0,12},{1,5},{2,14},{3,7},{4,8},{5,1},{6,10},{7,3},{8,4},{9,13},{1... | collective-permute-start | bytes 589832 | tf_op jit(solution)/shard_map/ppermute | solution.py:364
  123.3 22.0 %collective-permute-start.28 = (bf16[1,2,3,128,128]{4,3,2,1,0:T(8,128)(2,1)S(1)}, bf16[1,2,3,128,128]{4,3,2,1,0:T(8,128)(2,1)S(1)}, u32[]{:S(2)}, u32[]{:S(2)}) collective-permute-start(bf16[1,2,3,128,128]{4,3,2,1,0:T(8,128)(2,1)S(1)} %copy-done.10), channel_id=1, source_target_pairs={{0,7},{1,14},{2,5},{3,12},{4,3},{5,10},{6,1},{7,8},{8,15},{9,6},{1... | collective-permute-start | bytes 589832 | tf_op jit(solution)/shard_map/ppermute | solution.py:364
  125.8 21.4 %collective-permute-start.31 = (bf16[1,2,3,128,128]{4,3,2,1,0:T(8,128)(2,1)S(1)}, bf16[1,2,3,128,128]{4,3,2,1,0:T(8,128)(2,1)S(1)}, u32[]{:S(2)}, u32[]{:S(2)}) collective-permute-start(bf16[1,2,3,128,128]{4,3,2,1,0:T(8,128)(2,1)S(1)} %copy-done.8), channel_id=1, source_target_pairs={{0,13},{1,4},{2,15},{3,6},{4,9},{5,0},{6,11},{7,2},{8,5},{9,12},{1... | collective-permute-start | bytes 589832 | tf_op jit(solution)/shard_map/ppermute | solution.py:364
  135.9 18.0 %collective-permute-start.32 = (bf16[1,2,3,128,128]{4,3,2,1,0:T(8,128)(2,1)S(1)}, bf16[1,2,3,128,128]{4,3,2,1,0:T(8,128)(2,1)S(1)}, u32[]{:S(2)}, u32[]{:S(2)}) collective-permute-start(bf16[1,2,3,128,128]{4,3,2,1,0:T(8,128)(2,1)S(1)} %copy-done.6), channel_id=1, source_target_pairs={{0,14},{1,7},{2,12},{3,5},{4,10},{5,3},{6,8},{7,1},{8,6},{9,15},{1... | collective-permute-start | bytes 589832 | tf_op jit(solution)/shard_map/ppermute | solution.py:364
  137.5 21.1 %collective-permute-start.33 = (bf16[1,2,3,128,128]{4,3,2,1,0:T(8,128)(2,1)S(1)}, bf16[1,2,3,128,128]{4,3,2,1,0:T(8,128)(2,1)S(1)}, u32[]{:S(2)}, u32[]{:S(2)}) collective-permute-start(bf16[1,2,3,128,128]{4,3,2,1,0:T(8,128)(2,1)S(1)} %copy-done.4), channel_id=1, source_target_pairs={{0,15},{1,6},{2,13},{3,4},{4,11},{5,2},{6,9},{7,0},{8,7},{9,14},{1... | collective-permute-start | bytes 589832 | tf_op jit(solution)/shard_map/ppermute | solution.py:364
  159.3 55.4 %all-to-all-start = ((bf16[16,2,128,128]{3,2,1,0:T(8,128)(2,1)}), bf16[16,2,128,128]{3,2,1,0:T(8,128)(2,1)S(1)}, u32[]{:S(2)}, u32[]{:S(2)}) async-start(bf16[16,2,128,128]{3,2,1,0:T(8,128)(2,1)} %shard_map.65), calls=%async_computation | async-start | bytes 2097152 | tf_op jit(solution)/shard_map/all_to_all | solution.py:344
  174.5 7.6 %collective-permute-start.34 = (bf16[1,2,128,128]{3,2,1,0:T(8,128)(2,1)S(1)}, bf16[1,2,128,128]{3,2,1,0:T(8,128)(2,1)S(1)}, u32[]{:S(2)}, u32[]{:S(2)}) collective-permute-start(bf16[1,2,128,128]{3,2,1,0:T(8,128)(2,1)S(1)} %get-tuple-element.153), channel_id=1, source_target_pairs={{0,0},{1,9},{2,2},{3,11},{4,4},{5,13},{6,6},{7,15},{8,8},{9,1},{10... | collective-permute-start | bytes 196616 | tf_op jit(solution)/shard_map/ppermute | solution.py:380
  175.2 19.8 %collective-permute-start.35 = (bf16[1,2,128,128]{3,2,1,0:T(8,128)(2,1)S(1)}, bf16[1,2,128,128]{3,2,1,0:T(8,128)(2,1)S(1)}, u32[]{:S(2)}, u32[]{:S(2)}) collective-permute-start(bf16[1,2,128,128]{3,2,1,0:T(8,128)(2,1)S(1)} %get-tuple-element.154), channel_id=1, source_target_pairs={{0,1},{1,8},{2,3},{3,10},{4,5},{5,12},{6,7},{7,14},{8,9},{9,0},{10... | collective-permute-start | bytes 196616 | tf_op jit(solution)/shard_map/ppermute | solution.py:380
  179.1 17.5 %collective-permute-start.36 = (bf16[1,2,128,128]{3,2,1,0:T(8,128)(2,1)S(1)}, bf16[1,2,128,128]{3,2,1,0:T(8,128)(2,1)S(1)}, u32[]{:S(2)}, u32[]{:S(2)}) collective-permute-start(bf16[1,2,128,128]{3,2,1,0:T(8,128)(2,1)S(1)} %get-tuple-element.155), channel_id=1, source_target_pairs={{0,2},{1,11},{2,0},{3,9},{4,6},{5,15},{6,4},{7,13},{8,10},{9,3},{1... | collective-permute-start | bytes 196616 | tf_op jit(solution)/shard_map/ppermute | solution.py:380
  180.6 16.7 %collective-permute-start.37 = (bf16[1,2,128,128]{3,2,1,0:T(8,128)(2,1)S(1)}, bf16[1,2,128,128]{3,2,1,0:T(8,128)(2,1)S(1)}, u32[]{:S(2)}, u32[]{:S(2)}) collective-permute-start(bf16[1,2,128,128]{3,2,1,0:T(8,128)(2,1)S(1)} %get-tuple-element.156), channel_id=1, source_target_pairs={{0,3},{1,10},{2,1},{3,8},{4,7},{5,14},{6,5},{7,12},{8,11},{9,2},{1... | collective-permute-start | bytes 196616 | tf_op jit(solution)/shard_map/ppermute | solution.py:380
  180.6 20.0 %collective-permute-start.38 = (bf16[1,2,128,128]{3,2,1,0:T(8,128)(2,1)S(1)}, bf16[1,2,128,128]{3,2,1,0:T(8,128)(2,1)S(1)}, u32[]{:S(2)}, u32[]{:S(2)}) collective-permute-start(bf16[1,2,128,128]{3,2,1,0:T(8,128)(2,1)S(1)} %get-tuple-element.157), channel_id=1, source_target_pairs={{0,4},{1,13},{2,6},{3,15},{4,0},{5,9},{6,2},{7,11},{8,12},{9,5},{1... | collective-permute-start | bytes 196616 | tf_op jit(solution)/shard_map/ppermute | solution.py:380
  182.1 18.6 %collective-permute-start.39 = (bf16[1,2,128,128]{3,2,1,0:T(8,128)(2,1)S(1)}, bf16[1,2,128,128]{3,2,1,0:T(8,128)(2,1)S(1)}, u32[]{:S(2)}, u32[]{:S(2)}) collective-permute-start(bf16[1,2,128,128]{3,2,1,0:T(8,128)(2,1)S(1)} %get-tuple-element.158), channel_id=1, source_target_pairs={{0,5},{1,12},{2,7},{3,14},{4,1},{5,8},{6,3},{7,10},{8,13},{9,4},{1... | collective-permute-start | bytes 196616 | tf_op jit(solution)/shard_map/ppermute | solution.py:380
  194.9 7.4 %collective-permute-start.40 = (bf16[1,2,128,128]{3,2,1,0:T(8,128)(2,1)S(1)}, bf16[1,2,128,128]{3,2,1,0:T(8,128)(2,1)S(1)}, u32[]{:S(2)}, u32[]{:S(2)}) collective-permute-start(bf16[1,2,128,128]{3,2,1,0:T(8,128)(2,1)S(1)} %get-tuple-element.159), channel_id=1, source_target_pairs={{0,6},{1,15},{2,4},{3,13},{4,2},{5,11},{6,0},{7,9},{8,14},{9,7},{1... | collective-permute-start | bytes 196616 | tf_op jit(solution)/shard_map/ppermute | solution.py:380
  196.6 6.9 %collective-permute-start.41 = (bf16[1,2,128,128]{3,2,1,0:T(8,128)(2,1)S(1)}, bf16[1,2,128,128]{3,2,1,0:T(8,128)(2,1)S(1)}, u32[]{:S(2)}, u32[]{:S(2)}) collective-permute-start(bf16[1,2,128,128]{3,2,1,0:T(8,128)(2,1)S(1)} %get-tuple-element.160), channel_id=1, source_target_pairs={{0,7},{1,14},{2,5},{3,12},{4,3},{5,10},{6,1},{7,8},{8,15},{9,6},{1... | collective-permute-start | bytes 196616 | tf_op jit(solution)/shard_map/ppermute | solution.py:380
  197.3 8.5 %collective-permute-start.42 = (bf16[1,2,128,128]{3,2,1,0:T(8,128)(2,1)S(1)}, bf16[1,2,128,128]{3,2,1,0:T(8,128)(2,1)S(1)}, u32[]{:S(2)}, u32[]{:S(2)}) collective-permute-start(bf16[1,2,128,128]{3,2,1,0:T(8,128)(2,1)S(1)} %get-tuple-element.161), channel_id=1, source_target_pairs={{0,8},{1,1},{2,10},{3,3},{4,12},{5,5},{6,14},{7,7},{8,0},{9,9},{10... | collective-permute-start | bytes 196616 | tf_op jit(solution)/shard_map/ppermute | solution.py:380
  200.6 5.4 %collective-permute-start.43 = (bf16[1,2,128,128]{3,2,1,0:T(8,128)(2,1)S(1)}, bf16[1,2,128,128]{3,2,1,0:T(8,128)(2,1)S(1)}, u32[]{:S(2)}, u32[]{:S(2)}) collective-permute-start(bf16[1,2,128,128]{3,2,1,0:T(8,128)(2,1)S(1)} %get-tuple-element.162), channel_id=1, source_target_pairs={{0,9},{1,0},{2,11},{3,2},{4,13},{5,4},{6,15},{7,6},{8,1},{9,8},{10... | collective-permute-start | bytes 196616 | tf_op jit(solution)/shard_map/ppermute | solution.py:380
  200.7 8.3 %collective-permute-start.44 = (bf16[1,2,128,128]{3,2,1,0:T(8,128)(2,1)S(1)}, bf16[1,2,128,128]{3,2,1,0:T(8,128)(2,1)S(1)}, u32[]{:S(2)}, u32[]{:S(2)}) collective-permute-start(bf16[1,2,128,128]{3,2,1,0:T(8,128)(2,1)S(1)} %get-tuple-element.163), channel_id=1, source_target_pairs={{0,10},{1,3},{2,8},{3,1},{4,14},{5,7},{6,12},{7,5},{8,2},{9,11},{1... | collective-permute-start | bytes 196616 | tf_op jit(solution)/shard_map/ppermute | solution.py:380
  202.3 7.4 %collective-permute-start.45 = (bf16[1,2,128,128]{3,2,1,0:T(8,128)(2,1)S(1)}, bf16[1,2,128,128]{3,2,1,0:T(8,128)(2,1)S(1)}, u32[]{:S(2)}, u32[]{:S(2)}) collective-permute-start(bf16[1,2,128,128]{3,2,1,0:T(8,128)(2,1)S(1)} %get-tuple-element.164), channel_id=1, source_target_pairs={{0,11},{1,2},{2,9},{3,0},{4,15},{5,6},{6,13},{7,4},{8,3},{9,10},{1... | collective-permute-start | bytes 196616 | tf_op jit(solution)/shard_map/ppermute | solution.py:380
  203.5 6.5 %collective-permute-start.46 = (bf16[1,2,128,128]{3,2,1,0:T(8,128)(2,1)S(1)}, bf16[1,2,128,128]{3,2,1,0:T(8,128)(2,1)S(1)}, u32[]{:S(2)}, u32[]{:S(2)}) collective-permute-start(bf16[1,2,128,128]{3,2,1,0:T(8,128)(2,1)S(1)} %get-tuple-element.165), channel_id=1, source_target_pairs={{0,12},{1,5},{2,14},{3,7},{4,8},{5,1},{6,10},{7,3},{8,4},{9,13},{1... | collective-permute-start | bytes 196616 | tf_op jit(solution)/shard_map/ppermute | solution.py:380
  205.7 5.6 %collective-permute-start.47 = (bf16[1,2,128,128]{3,2,1,0:T(8,128)(2,1)S(1)}, bf16[1,2,128,128]{3,2,1,0:T(8,128)(2,1)S(1)}, u32[]{:S(2)}, u32[]{:S(2)}) collective-permute-start(bf16[1,2,128,128]{3,2,1,0:T(8,128)(2,1)S(1)} %get-tuple-element.166), channel_id=1, source_target_pairs={{0,13},{1,4},{2,15},{3,6},{4,9},{5,0},{6,11},{7,2},{8,5},{9,12},{1... | collective-permute-start | bytes 196616 | tf_op jit(solution)/shard_map/ppermute | solution.py:380
  206.0 7.4 %collective-permute-start.48 = (bf16[1,2,128,128]{3,2,1,0:T(8,128)(2,1)S(1)}, bf16[1,2,128,128]{3,2,1,0:T(8,128)(2,1)S(1)}, u32[]{:S(2)}, u32[]{:S(2)}) collective-permute-start(bf16[1,2,128,128]{3,2,1,0:T(8,128)(2,1)S(1)} %get-tuple-element.167), channel_id=1, source_target_pairs={{0,14},{1,7},{2,12},{3,5},{4,10},{5,3},{6,8},{7,1},{8,6},{9,15},{1... | collective-permute-start | bytes 196616 | tf_op jit(solution)/shard_map/ppermute | solution.py:380
  208.9 5.8 %collective-permute-start.49 = (bf16[1,2,128,128]{3,2,1,0:T(8,128)(2,1)S(1)}, bf16[1,2,128,128]{3,2,1,0:T(8,128)(2,1)S(1)}, u32[]{:S(2)}, u32[]{:S(2)}) collective-permute-start(bf16[1,2,128,128]{3,2,1,0:T(8,128)(2,1)S(1)} %get-tuple-element.168), channel_id=1, source_target_pairs={{0,15},{1,6},{2,13},{3,4},{4,11},{5,2},{6,9},{7,0},{8,7},{9,14},{1... | collective-permute-start | bytes 196616 | tf_op jit(solution)/shard_map/ppermute | solution.py:380
  (31 other events, 680.6 us)
